TPU v7x, 32 devices: a whole 2x2x4 slice. The times are simulated.
32 devices in a mesh: gx: 4 (over x, core), gy: 4 (over z), gz: 2 (over y).
Axes of the slice: x: 2, y: 2, z: 4, core: 2. Of those that a mesh axis runs over, the one named last changes fastest.
Arguments:
- probes: float32 [8, 32, 64, 512], P(None, 'gx', 'gy', 'gz'), may hold values from -0.011 to 0.011
- kappa2: float32 [32, 64, 512], P('gx', 'gy', 'gz'), may hold values from 0.25 to 4
- cotangents: float32 [5, 8], replicated, may hold values from -0.4375 to 0.4375
Outputs:
- kappa_grad: float32 [32, 64, 512], P('gx', 'gy', 'gz')
All inputs are finite; a program needn't handle non-finite values.
Results may differ from a plain program's by a relative error of at most 0.02.
Values sent between devices are 32-bit elements; how exact they have to be, the bound alone decides.
No kernel may reach another device: no remote copies, remote signals or barrier semaphores. Data moves between devices by JAX's collectives and lax.ppermute only.
A program may use at most 64 MiB of HBM per device.

v0:
```python
import jax
import jax.numpy as jnp
from jax import lax
from jax.sharding import PartitionSpec as P

EPSILON = 1e-06


def with_halo(block, sides, width):
    for axis, dim in sides:
        count = lax.axis_size(axis)
        forward = [(i, i + 1) for i in range(count - 1)]
        backward = [(target, source) for source, target in forward]
        low = lax.ppermute(
            lax.slice_in_dim(block, block.shape[dim] - width, None, axis=dim), axis, forward
        )
        high = lax.ppermute(lax.slice_in_dim(block, 0, width, axis=dim), axis, backward)
        block = jnp.concatenate([low, block, high], axis=dim)
    return block


def neighbours(padded):
    total = padded[:, 2:, 1:-1, 1:-1] + padded[:, :-2, 1:-1, 1:-1]
    total = total + padded[:, 1:-1, 2:, 1:-1] + padded[:, 1:-1, :-2, 1:-1]
    return total + padded[:, 1:-1, 1:-1, 2:] + padded[:, 1:-1, 1:-1, :-2]


def stencil(field, kappa2):
    padded = with_halo(field, (("gx", 1), ("gy", 2), ("gz", 3)), 1)
    return (6.0 + kappa2) * field - neighbours(padded)


def squared(field, kappa2):
    single = stencil(field, kappa2)
    return (single, stencil(single, kappa2))


def local_sum(first, second):
    return jnp.sum(first * second, axis=(1, 2, 3))


def column(values):
    return values[:, None, None, None]


def orthogonalize(basis, image, inverse_count):
    alpha = lax.psum(local_sum(basis, image), ("gx", "gy", "gz")) * inverse_count
    rest = image - column(alpha) * basis
    square = lax.psum(local_sum(rest, rest), ("gx", "gy", "gz")) * inverse_count
    return (alpha, rest, jnp.sqrt(square + EPSILON))


def body(probes, kappa2, cotangents):
    cells = (
        probes.shape[1]
        * probes.shape[2]
        * probes.shape[3]
        * lax.axis_size("gx")
        * lax.axis_size("gy")
        * lax.axis_size("gz")
    )
    inverse_count = 1.0 / cells
    start_norm = lax.psum(local_sum(probes, probes), ("gx", "gy", "gz")) * inverse_count
    first_basis = probes / column(jnp.sqrt(start_norm + EPSILON))
    first_stencil, first_image = squared(first_basis, kappa2)
    first_alpha, first_rest, first_beta = orthogonalize(first_basis, first_image, inverse_count)
    second_basis = first_rest / column(first_beta)
    second_stencil, second_applied = squared(second_basis, kappa2)
    second_image = second_applied - column(first_beta) * first_basis
    second_alpha, second_rest, second_beta = orthogonalize(
        second_basis, second_image, inverse_count
    )
    third_basis = second_rest / column(second_beta)
    third_stencil, third_applied = squared(third_basis, kappa2)
    third_image = third_applied - column(second_beta) * second_basis
    weight_three = column(cotangents[2])
    back_third_image = weight_three * third_basis
    back_third_stencil = weight_three * third_stencil
    back_third_applied = weight_three * third_applied
    back_third_basis = weight_three * third_image + back_third_applied
    gradient = back_third_image * third_stencil + back_third_stencil * third_basis
    cross_one, cross_two = lax.psum(
        (local_sum(second_basis, back_third_image), local_sum(back_third_basis, third_basis)),
        ("gx", "gy", "gz"),
    )
    back_second_beta = (
        cotangents[4] - cross_one * inverse_count - cross_two * inverse_count / second_beta
    )
    back_second_rest = (
        back_third_basis / column(second_beta) + column(back_second_beta) * third_basis
    )
    cross_three = lax.psum(local_sum(second_basis, back_second_rest), ("gx", "gy", "gz"))
    back_second_alpha = cotangents[1] - cross_three * inverse_count
    back_second_image = back_second_rest + column(back_second_alpha) * second_basis
    back_second_stencil, back_second_applied = squared(back_second_image, kappa2)
    back_second_basis = (
        back_second_applied
        - column(second_beta) * back_third_image
        - column(second_alpha) * back_second_rest
        + column(back_second_alpha) * second_image
    )
    gradient = gradient + back_second_image * second_stencil + back_second_stencil * second_basis
    cross_four, cross_five = lax.psum(
        (local_sum(first_basis, back_second_image), local_sum(back_second_basis, second_basis)),
        ("gx", "gy", "gz"),
    )
    back_first_beta = (
        cotangents[3] - cross_four * inverse_count - cross_five * inverse_count / first_beta
    )
    back_first_rest = (
        back_second_basis / column(first_beta) + column(back_first_beta) * second_basis
    )
    cross_six = lax.psum(local_sum(first_basis, back_first_rest), ("gx", "gy", "gz"))
    back_first_alpha = cotangents[0] - cross_six * inverse_count
    back_first_image = back_first_rest + column(back_first_alpha) * first_basis
    back_first_stencil = stencil(back_first_image, kappa2)
    gradient = gradient + back_first_image * first_stencil + back_first_stencil * first_basis
    return jnp.sum(gradient, axis=0)


def solution(mesh):
    return jax.shard_map(
        body,
        mesh=mesh,
        in_specs=(P(None, "gx", "gy", "gz"), P("gx", "gy", "gz"), P()),
        out_specs=P("gx", "gy", "gz"),
        check_vma=False,
    )
```

profile of v0, /device:TPU:0, one launch (start us, length us, event | category | flops | bytes accessed | tf_op | source)
XLA Modules:
  0.0 744.1 jit_solution(4515255613234515883)
XLA Ops:
  1.5 42.0 %psum.77 = f32[8]{0:T(128)S(1)} all-reduce(f32[8]{0:T(128)S(1)} %multiply_reduce_fusion.10), channel_id=1, replica_groups=mesh['gx'=4,'gy'=4,'gz'=2] {'gx','gy','gz'}, use_global_device_ids=true, to_apply=%region_1.0 | all-reduce | flops 8 | bytes 64 | tf_op jit(solution)/shard_map/psum | solution.py:63
  46.8 4.4 collective-permute-done
  68.9 4.6 collective-permute-done.4
  103.1 4.5 collective-permute-start.11
  114.7 41.8 %psum.78 = f32[8]{0:T(128)S(1)} all-reduce(f32[8]{0:T(128)S(1)} %get-tuple-element.18), channel_id=1, replica_groups=mesh['gx'=4,'gy'=4,'gz'=2] {'gx','gy','gz'}, use_global_device_ids=true, to_apply=%region_3.0 | all-reduce | flops 8 | bytes 64 | tf_op jit(solution)/shard_map/psum | solution.py:47
  157.3 39.8 %psum.79 = f32[8]{0:T(128)S(1)} all-reduce(f32[8]{0:T(128)S(1)} %multiply_reduce_fusion.8), channel_id=1, replica_groups=mesh['gx'=4,'gy'=4,'gz'=2] {'gx','gy','gz'}, use_global_device_ids=true, to_apply=%region_5.0 | all-reduce | flops 8 | bytes 64 | tf_op jit(solution)/shard_map/psum | solution.py:49
  220.2 4.5 collective-permute-start.17
  255.6 5.8 collective-permute-start.23
  265.8 4.8 multiply_reduce_fusion.7
  270.5 42.1 %psum.80 = f32[8]{0:T(128)S(1)} all-reduce(f32[8]{0:T(128)S(1)} %get-tuple-element.16), channel_id=1, replica_groups=mesh['gx'=4,'gy'=4,'gz'=2] {'gx','gy','gz'}, use_global_device_ids=true, to_apply=%region_7.0 | all-reduce | flops 8 | bytes 64 | tf_op jit(solution)/shard_map/psum | solution.py:47
  314.3 39.0 %psum.81 = f32[8]{0:T(128)S(1)} all-reduce(f32[8]{0:T(128)S(1)} %multiply_reduce_fusion.6), channel_id=1, replica_groups=mesh['gx'=4,'gy'=4,'gz'=2] {'gx','gy','gz'}, use_global_device_ids=true, to_apply=%region_9.0 | all-reduce | flops 8 | bytes 64 | tf_op jit(solution)/shard_map/psum | solution.py:49
  357.9 4.4 collective-permute-done.24
  379.6 5.8 collective-permute-start.29
  430.8 6.7 multiply_reduce_fusion.5
  437.4 39.8 %all-reduce.1 = (f32[8]{0:T(128)}, f32[8]{0:T(128)}) all-reduce(f32[8]{0:T(128)} %get-tuple-element.6, f32[8]{0:T(128)} %get-tuple-element.5), channel_id=1, replica_groups=mesh['gx'=4,'gy'=4,'gz'=2] {'gx','gy','gz'}, use_global_device_ids=true, to_apply=%region_13.0 | all-reduce | flops 16 | bytes 128 | tf_op jit(solution)/shard_map/psum | solution.py:82
  480.2 42.0 %psum.84 = f32[8]{0:T(128)} all-reduce(f32[8]{0:T(128)} %multiply_reduce_fusion.3), channel_id=1, replica_groups=mesh['gx'=4,'gy'=4,'gz'=2] {'gx','gy','gz'}, use_global_device_ids=true, to_apply=%region_15.0 | all-reduce | flops 8 | bytes 64 | tf_op jit(solution)/shard_map/psum | solution.py:92
  548.9 5.8 collective-permute-start.41
  559.2 4.9 fusion.20
  588.5 6.0 collective-permute-start.47
  599.0 7.4 %multiply_reduce_fusion.1 = (f32[8]{0:T(128)}, f32[8,8,16,256]{3,0,2,1:T(8,128)}) fusion(f32[8,8,16,256]{3,0,2,1:T(8,128)S(1)} %broadcast_divide_fusion.1, f32[8,8,16,256]{3,0,2,1:T(8,128)} %get-tuple-element.17, f32[8]{0:T(128)} %copy-done.46, f32[8,8,16,256]{3,0,2,1:T(8,128)S(1)} %broadcast_divide_fusion, f32[8]{0:T(128)S(1)} %fusion.63, ...), kind=kLoop, calls=%fused_computation.238 | loop fusion | flops 9699320 | bytes 6860224 | tf_op jit(solution)/shard_map/reduce_sum | solution.py:39
  606.4 42.0 %all-reduce = (f32[8]{0:T(128)S(1)}, f32[8]{0:T(128)}) all-reduce(f32[8]{0:T(128)} %get-tuple-element.13, f32[8]{0:T(128)} %get-tuple-element.11), channel_id=1, replica_groups=mesh['gx'=4,'gy'=4,'gz'=2] {'gx','gy','gz'}, use_global_device_ids=true, to_apply=%region_19.0 | all-reduce | flops 16 | bytes 128 | tf_op jit(solution)/shard_map/psum | solution.py:103
  651.2 39.5 %psum.87 = f32[8]{0:T(128)} all-reduce(f32[8]{0:T(128)S(1)} %multiply_reduce_fusion), channel_id=1, replica_groups=mesh['gx'=4,'gy'=4,'gz'=2] {'gx','gy','gz'}, use_global_device_ids=true, to_apply=%region_21.0 | all-reduce | flops 8 | bytes 64 | tf_op jit(solution)/shard_map/psum | solution.py:113
  717.8 5.7 collective-permute-start.53
  728.1 15.6 %fusion.5 = f32[8,16,256]{2,1,0:T(8,128)} fusion(f32[8,8,16,256]{3,0,2,1:T(8,128)S(1)} %copy-done.2, f32[8,10,18,1]{3,0,2,1:T(8,128)} %copy.40, f32[8,10,1,256]{3,0,2,1:T(8,128)} %copy-done.33, f32[8,10,1,256]{3,0,2,1:T(8,128)} %copy-done.32, f32[8,1,16,256]{3,0,2,1:T(8,128)} %copy-done.15, f32[8,8,16,256]{3,0,2,1:T(8,128)} %copy-done.4, ...), kind=kLoop, calls=%fused_computation.16 | loop fusion | flops 36405248 | bytes 7692576 | tf_op jit(solution)/shard_map/reduce_sum | solution.py:118
  (293 shorter events, 283.7 us)
Async XLA Ops:
  54.7 6.3 collective-permute-start.2
  65.1 9.9 %collective-permute-start.5 = (f32[8,10,18,1]{2,0,3,1:T(8,128)S(1)}, f32[8,10,18,1]{2,0,3,1:T(8,128)S(1)}, u32[]{:S(2)}, u32[]{:S(2)}) collective-permute-start(f32[8,10,18,1]{2,0,3,1:T(8,128)S(1)} %copy.7), channel_id=1, source_target_pairs={{0,1},{2,3},{4,5},{6,7},{8,9},{10,11},{12,13},{14,15},{16,17},{18,... | collective-permute-start | bytes 17288 | tf_op jit(solution)/shard_map/ppermute | solution.py:14
  91.4 6.3 collective-permute-start.8
  101.3 6.4 collective-permute-start.10
  208.5 6.3 collective-permute-start.14
  218.3 6.4 collective-permute-start.16
  241.9 6.3 collective-permute-start.20
  252.0 9.3 %collective-permute-start.22 = (f32[8,10,18,1]{2,0,3,1:T(8,128)}, f32[8,10,18,1]{2,0,3,1:T(8,128)}, u32[]{:S(2)}, u32[]{:S(2)}) collective-permute-start(f32[8,10,18,1]{2,0,3,1:T(8,128)} %copy.17), channel_id=1, source_target_pairs={{1,0},{3,2},{5,4},{7,6},{9,8},{11,10},{13,12},{15,14},{17,16},{19,... | collective-permute-start | bytes 17288 | tf_op jit(solution)/shard_map/ppermute | solution.py:17
  255.6 8.0 %collective-permute-start.23 = (f32[8,10,18,1]{2,0,3,1:T(8,128)}, f32[8,10,18,1]{2,0,3,1:T(8,128)}, u32[]{:S(2)}, u32[]{:S(2)}) collective-permute-start(f32[8,10,18,1]{2,0,3,1:T(8,128)} %copy.19), channel_id=1, source_target_pairs={{0,1},{2,3},{4,5},{6,7},{8,9},{10,11},{12,13},{14,15},{16,17},{18,... | collective-permute-start | bytes 17288 | tf_op jit(solution)/shard_map/ppermute | solution.py:14
  365.9 6.3 collective-permute-start.26
  376.0 9.3 %collective-permute-start.28 = (f32[8,10,18,1]{2,0,3,1:T(8,128)}, f32[8,10,18,1]{2,0,3,1:T(8,128)}, u32[]{:S(2)}, u32[]{:S(2)}) collective-permute-start(f32[8,10,18,1]{2,0,3,1:T(8,128)} %copy.21), channel_id=1, source_target_pairs={{1,0},{3,2},{5,4},{7,6},{9,8},{11,10},{13,12},{15,14},{17,16},{19,... | collective-permute-start | bytes 17288 | tf_op jit(solution)/shard_map/ppermute | solution.py:17
  379.6 8.0 %collective-permute-start.29 = (f32[8,10,18,1]{2,0,3,1:T(8,128)}, f32[8,10,18,1]{2,0,3,1:T(8,128)}, u32[]{:S(2)}, u32[]{:S(2)}) collective-permute-start(f32[8,10,18,1]{2,0,3,1:T(8,128)} %copy.23), channel_id=1, source_target_pairs={{0,1},{2,3},{4,5},{6,7},{8,9},{10,11},{12,13},{14,15},{16,17},{18,... | collective-permute-start | bytes 17288 | tf_op jit(solution)/shard_map/ppermute | solution.py:14
  403.7 6.3 collective-permute-start.32
  416.1 12.4 %collective-permute-start.35 = (f32[8,10,18,1]{2,0,3,1:T(8,128)}, f32[8,10,18,1]{2,0,3,1:T(8,128)}, u32[]{:S(2)}, u32[]{:S(2)}) collective-permute-start(f32[8,10,18,1]{2,0,3,1:T(8,128)} %copy.27), channel_id=1, source_target_pairs={{0,1},{2,3},{4,5},{6,7},{8,9},{10,11},{12,13},{14,15},{16,17},{18,... | collective-permute-start | bytes 17288 | tf_op jit(solution)/shard_map/ppermute | solution.py:14
  420.1 6.2 collective-permute-start.34
  535.1 6.3 collective-permute-start.38
  545.3 9.3 %collective-permute-start.40 = (f32[8,10,18,1]{2,0,3,1:T(8,128)}, f32[8,10,18,1]{2,0,3,1:T(8,128)}, u32[]{:S(2)}, u32[]{:S(2)}) collective-permute-start(f32[8,10,18,1]{2,0,3,1:T(8,128)} %copy.29), channel_id=1, source_target_pairs={{1,0},{3,2},{5,4},{7,6},{9,8},{11,10},{13,12},{15,14},{17,16},{19,... | collective-permute-start | bytes 17288 | tf_op jit(solution)/shard_map/ppermute | solution.py:17
  548.9 8.0 %collective-permute-start.41 = (f32[8,10,18,1]{2,0,3,1:T(8,128)}, f32[8,10,18,1]{2,0,3,1:T(8,128)}, u32[]{:S(2)}, u32[]{:S(2)}) collective-permute-start(f32[8,10,18,1]{2,0,3,1:T(8,128)} %copy.31), channel_id=1, source_target_pairs={{0,1},{2,3},{4,5},{6,7},{8,9},{10,11},{12,13},{14,15},{16,17},{18,... | collective-permute-start | bytes 17288 | tf_op jit(solution)/shard_map/ppermute | solution.py:14
  574.8 6.3 collective-permute-start.44
  585.0 9.6 %collective-permute-start.46 = (f32[8,10,18,1]{2,0,3,1:T(8,128)}, f32[8,10,18,1]{2,0,3,1:T(8,128)}, u32[]{:S(2)}, u32[]{:S(2)}) collective-permute-start(f32[8,10,18,1]{2,0,3,1:T(8,128)} %copy.33), channel_id=1, source_target_pairs={{1,0},{3,2},{5,4},{7,6},{9,8},{11,10},{13,12},{15,14},{17,16},{19,... | collective-permute-start | bytes 17288 | tf_op jit(solution)/shard_map/ppermute | solution.py:17
  588.5 8.2 %collective-permute-start.47 = (f32[8,10,18,1]{2,0,3,1:T(8,128)}, f32[8,10,18,1]{2,0,3,1:T(8,128)}, u32[]{:S(2)}, u32[]{:S(2)}) collective-permute-start(f32[8,10,18,1]{2,0,3,1:T(8,128)} %copy.35), channel_id=1, source_target_pairs={{0,1},{2,3},{4,5},{6,7},{8,9},{10,11},{12,13},{14,15},{16,17},{18,... | collective-permute-start | bytes 17288 | tf_op jit(solution)/shard_map/ppermute | solution.py:14
  704.0 6.3 collective-permute-start.50
  714.2 9.3 %collective-permute-start.52 = (f32[8,10,18,1]{2,0,3,1:T(8,128)}, f32[8,10,18,1]{2,0,3,1:T(8,128)}, u32[]{:S(2)}, u32[]{:S(2)}) collective-permute-start(f32[8,10,18,1]{2,0,3,1:T(8,128)} %copy.37), channel_id=1, source_target_pairs={{1,0},{3,2},{5,4},{7,6},{9,8},{11,10},{13,12},{15,14},{17,16},{19,... | collective-permute-start | bytes 17288 | tf_op jit(solution)/shard_map/ppermute | solution.py:17
  717.8 8.0 %collective-permute-start.53 = (f32[8,10,18,1]{2,0,3,1:T(8,128)}, f32[8,10,18,1]{2,0,3,1:T(8,128)}, u32[]{:S(2)}, u32[]{:S(2)}) collective-permute-start(f32[8,10,18,1]{2,0,3,1:T(8,128)} %copy.39), channel_id=1, source_target_pairs={{0,1},{2,3},{4,5},{6,7},{8,9},{10,11},{12,13},{14,15},{16,17},{18,... | collective-permute-start | bytes 17288 | tf_op jit(solution)/shard_map/ppermute | solution.py:14
  (79 other events, 708.3 us)
where the time goes:
time: 757 us; the launch traced here: 744 us
  blocking collectives  368 us (49%)
  starting transfers between devices  125 us (17%)
  waiting for transfers between devices  90.4 us (12%)
  local copies, waits for them, and re-layouts  84.7 us (11%)
  other arithmetic  74.6 us (10%)
    ppermute x27, starting transfers between devices, with_halo(): lax.ppermute(lax.slice_in_dim(block, block.shape[dim] - width, None, axis...  89.8 us
    psum x2, blocking collectives, orthogonalize(): lax.psum(local_sum(basis, image), ('gx', 'gy', 'gz')) * inverse_count  83.8 us
    ppermute x27, waiting for transfers between devices, with_halo(): lax.ppermute(lax.slice_in_dim(block, 0, width, axis=dim), axis, backward)  83.8 us
    psum x2, blocking collectives, orthogonalize(): square = lax.psum(local_sum(rest, rest), ('gx', 'gy', 'gz')) * inverse_count  78.7 us
    psum x1, blocking collectives, body(): lax.psum((local_sum(first_basis, back_second_image), local_sum(back_secon...  42 us
    psum x1, blocking collectives, body(): lax.psum(local_sum(probes, probes), ('gx', 'gy', 'gz')) * inverse_count  42 us
    psum x1, blocking collectives, body(): lax.psum(local_sum(second_basis, back_second_rest), ('gx', 'gy', 'gz'))  42 us
    psum x1, blocking collectives, body(): lax.psum((local_sum(second_basis, back_third_image), local_sum(back_third...  39.8 us
  transfers between devices with their start and end apart: 54, of which 31 were waited for; matrix products, arithmetic and copies ran while one was open for 4% of the time, Pallas kernels for 0%

commit v1 on v0

v1 whole, which is shorter than its diff:
```python
import functools

import jax
import jax.numpy as jnp
from jax import lax
from jax.experimental import pallas as pl
from jax.experimental.pallas import tpu as pltpu
from jax.sharding import PartitionSpec as P

EPSILON = 1e-06
SHIFT = 64.0
DEPTH = 9
KAPPA_HALO = 8
MIB = 1024 * 1024


def loss_of_moments(moments, weights):
    m0, m1, m2, m3, m4, m5 = moments
    norm = m0 + EPSILON
    alpha1 = (m1 + SHIFT * m0) / norm
    e1 = SHIFT - alpha1
    rest1 = jnp.maximum(m2 + 2.0 * e1 * m1 + e1 * e1 * m0, 0.0)
    beta1_square = rest1 / norm + EPSILON
    beta1 = jnp.sqrt(beta1_square)
    scale = 1.0 / (norm * beta1_square)
    alpha2 = scale * (m3 + 2.0 * e1 * m2 + e1 * e1 * m1 + SHIFT * rest1) - (m1 + e1 * m0) / norm
    e2 = SHIFT - alpha2
    f1 = e1 + e2
    f0 = e1 * e2 - beta1_square
    g = f1 * f1 + 2.0 * f0
    rest2 = jnp.maximum(m4 + 2.0 * f1 * m3 + g * m2 + 2.0 * f1 * f0 * m1 + f0 * f0 * m0, 0.0)
    beta2_square = scale * rest2 + EPSILON
    beta2 = jnp.sqrt(beta2_square)
    image2 = m5 + 2.0 * f1 * m4 + g * m3 + 2.0 * f1 * f0 * m2 + f0 * f0 * m1
    cross = m3 + f1 * m2 + f0 * m1 + e1 * (m2 + f1 * m1 + f0 * m0)
    alpha3 = scale * ((image2 + SHIFT * rest2) / beta2_square - cross)
    return (
        weights[0] * alpha1
        + weights[1] * alpha2
        + weights[2] * alpha3
        + weights[3] * beta1
        + weights[4] * beta2
    )


def shifted(value, step, axis):
    tile = (8, 128)[axis]
    size = value.shape[axis]
    rolled = pltpu.roll(value, step % size, axis)
    at = 0 if step > 0 else size - tile
    edge = lax.slice_in_dim(rolled, at, at + tile, axis=axis)
    index = lax.broadcasted_iota(jnp.int32, edge.shape, axis)
    edge = jnp.where(index == (0 if step > 0 else tile - 1), 0.0, edge)
    if step > 0:
        parts = [edge, lax.slice_in_dim(rolled, tile, size, axis=axis)]
    else:
        parts = [lax.slice_in_dim(rolled, 0, size - tile, axis=axis), edge]
    return jnp.concatenate(parts, axis=axis)


def stencil_row(ref, at, diagonal):
    centre = ref[at]
    total = ref[at - 1] + ref[at + 1]
    total = total + shifted(centre, 1, 0) + shifted(centre, -1, 0)
    total = total + shifted(centre, 1, 1) + shifted(centre, -1, 1)
    return diagonal * centre - total


class Field:
    def __init__(self, ref, halo):
        self.ref = ref
        self.halo = halo

    def row(self, at):
        return self.ref[at + self.halo]

    def rows(self, own, halo):
        return self.ref.at[pl.ds(self.halo - halo, own + 2 * halo)]


def apply_steps(bounds_ref, own, target, source, diagonal, minus=None):
    halo = target.halo
    first = jnp.maximum(-halo, bounds_ref[0])
    last = jnp.minimum(own + halo, bounds_ref[1])
    if halo:
        zero = jnp.zeros(target.ref.shape[1:], jnp.float32)
        target.ref[halo - 1] = zero
        target.ref[halo + own] = zero

    def body(row, carry):
        value = stencil_row(source.ref, row + source.halo, diagonal.row(row))
        if minus is not None:
            value = value - SHIFT * minus.row(row)
        target.ref[row + halo] = value
        return carry

    lax.fori_loop(first, last, body, 0)


def tile_sum(value):
    total = None
    for x in range(0, value.shape[0], 8):
        for z in range(0, value.shape[1], 128):
            part = value[x : x + 8, z : z + 128]
            total = part if total is None else total + part
    return total


def column_copies(whole, columns, sem, inward):
    copies = []
    for index in range(columns.shape[0]):
        pair = (whole.at[:, pl.ds(index * 128, 128)], columns.at[index])
        source, target = pair if inward else pair[::-1]
        copies.append(pltpu.make_async_copy(source, target, sem.at[index]))
    return copies


def column_places(grid):
    nx, nz, bx, by, bz = grid
    for s in range(nx * nz):
        for column in range(bz // 128):
            z = (s % nz) * bz + column * 128
            yield s, column, pl.ds((s // nz) * bx, bx), pl.ds(z, 128)


def assemble_kernel(grid, blocks_ref, own_ref, low_ref, high_ref, columns_ref, sem):
    nx, nz, bx, by, bz = grid
    copies = column_copies(blocks_ref, columns_ref, sem, True)
    for copy in copies:
        copy.start()
    for copy in copies:
        copy.wait()
    for s, column, xs, zs in column_places(grid):
        for y in range(by):
            value = columns_ref[column, pl.ds(s * bx * by + y, bx, stride=by), :]
            own_ref[y, xs, zs] = value
            if y < DEPTH:
                low_ref[y, xs, zs] = value
            if y >= by - DEPTH:
                high_ref[y - (by - DEPTH), xs, zs] = value


def first_kernel(
    grid,
    bounds_ref, own_ref, low_ref, high_ref, kappa_ref,
    d0_out, c1_out, d1_out, c2_out, d2_out, diagonal_out, moments_ref,
    c0_ref, d0_ref, c1_ref, d1_ref, c2_ref, d2_ref, diagonal_ref, columns_ref,
    in_sem, out_sem, columns_sem,
):
    nx, nz, bx, by, bz = grid
    kappa_copies = column_copies(kappa_ref, columns_ref, columns_sem, True)
    for copy in kappa_copies:
        copy.start()
    arrivals = [
        pltpu.make_async_copy(low_ref, c0_ref.at[pl.ds(0, DEPTH)], in_sem.at[0]),
        pltpu.make_async_copy(own_ref, c0_ref.at[pl.ds(DEPTH, by)], in_sem.at[1]),
        pltpu.make_async_copy(high_ref, c0_ref.at[pl.ds(DEPTH + by, DEPTH)], in_sem.at[2]),
    ]
    for copy in arrivals:
        copy.start()
    ext = by + 2 * KAPPA_HALO

    def diagonal_row(y, carry):
        for s, column, xs, zs in column_places(grid):
            value = columns_ref[column, pl.ds(s * bx * ext + y, bx, stride=ext), :]
            diagonal_ref[y, xs, zs] = 6.0 + value
        return carry

    for copy in kappa_copies:
        copy.wait()
    lax.fori_loop(0, ext, diagonal_row, 0)
    c0 = Field(c0_ref, 9)
    d0 = Field(d0_ref, 8)
    c1 = Field(c1_ref, 7)
    d1 = Field(d1_ref, 6)
    c2 = Field(c2_ref, 5)
    d2 = Field(d2_ref, 4)
    diagonal = Field(diagonal_ref, KAPPA_HALO)
    departures = []

    def depart(field, halo, out):
        copy = pltpu.make_async_copy(field.rows(by, halo), out, out_sem.at[len(departures)])
        copy.start()
        departures.append(copy)

    depart(diagonal, 3, diagonal_out)
    for copy in arrivals:
        copy.wait()
    steps = functools.partial(apply_steps, bounds_ref, by)
    steps(d0, c0, diagonal)
    depart(d0, 0, d0_out)
    steps(c1, d0, diagonal, c0)
    depart(c1, 0, c1_out)
    steps(d1, c1, diagonal)
    depart(d1, 0, d1_out)
    steps(c2, d1, diagonal, c1)
    depart(c2, 3, c2_out)
    steps(d2, c2, diagonal)
    depart(d2, 4, d2_out)

    def moment_row(row, sums):
        a, b, c, d = c0.row(row), c1.row(row), c2.row(row), d2.row(row)
        pairs = ((a, a), (a, b), (b, b), (b, c), (c, c), (d, d))
        return tuple(total + tile_sum(u * v) for total, (u, v) in zip(sums, pairs))

    zero = jnp.zeros((8, 128), jnp.float32)
    sums = lax.fori_loop(0, by, moment_row, (zero,) * 6)
    for index, total in enumerate(sums):
        moments_ref[index] = total
    for copy in departures:
        copy.wait()


def second_kernel(
    grid, inverse_count, parts,
    bounds_ref, weights_ref, moments_ref,
    c0_in, d0_in, c1_in, d1_in, c2_in, d2_in, diagonal_in,
    out_ref,
    c0_ref, d0_ref, c1_ref, d1_ref, c2_ref, d2_ref, diagonal_ref,
    c3_ref, d3_ref, c4_ref, columns_ref, in_sem, out_sem,
):
    nx, nz, bx, by, bz = grid
    pairs = (
        (diagonal_in, diagonal_ref), (c2_in, c2_ref), (d2_in, d2_ref), (c0_in, c0_ref),
        (d0_in, d0_ref), (c1_in, c1_ref), (d1_in, d1_ref),
    )
    copies = [
        pltpu.make_async_copy(source, target, in_sem.at[index])
        for index, (source, target) in enumerate(pairs)
    ]
    for copy in copies:
        copy.start()
    raw = []
    for k in range(6):
        total = moments_ref[k]
        for part in range(1, parts):
            total = total + moments_ref[part * 6 + k]
        total = jnp.sum(jnp.sum(total, axis=0, keepdims=True), axis=1, keepdims=True)
        raw.append(jnp.broadcast_to(total * inverse_count, (8, 128)))
    moments = tuple(raw[:5]) + (raw[5] - SHIFT * raw[4],)
    weights = [weights_ref[k] for k in range(5)]
    value, pullback = jax.vjp(lambda m: loss_of_moments(m, weights), moments)
    (slopes,) = pullback(jnp.full((8, 128), 2.0, jnp.float32))
    slopes = [slope[0, 0] for slope in slopes]

    for copy in copies[:3]:
        copy.wait()
    c0, d0, c1, d1 = (Field(ref, 0) for ref in (c0_ref, d0_ref, c1_ref, d1_ref))
    c2 = Field(c2_ref, 3)
    d2 = Field(d2_ref, 4)
    c3 = Field(c3_ref, 3)
    d3 = Field(d3_ref, 2)
    c4 = Field(c4_ref, 1)
    diagonal = Field(diagonal_ref, 3)
    steps = functools.partial(apply_steps, bounds_ref, by)
    steps(c3, d2, diagonal, c2)
    steps(d3, c3, diagonal)
    steps(c4, d3, diagonal, c3)
    for copy in copies[3:]:
        copy.wait()

    def out_row(row, carry):
        d4 = stencil_row(c4.ref, row + 1, diagonal.row(row))
        cs = [field.row(row) for field in (c0, c1, c2, c3, c4)]
        ds = [field.row(row) for field in (d0, d1, d2, d3)] + [d4]
        total = None
        for i in range(5):
            inner = None
            for j in range(5 - i):
                term = slopes[i + j + 1] * ds[j]
                inner = term if inner is None else inner + term
            term = cs[i] * inner
            total = term if total is None else total + term
        for s, column, xs, zs in column_places(grid):
            part = total[xs.start : xs.start + bx, zs.start : zs.start + 128]
            columns_ref[column, pl.ds(s * bx * by + row, bx, stride=by), :] = part
        return carry

    lax.fori_loop(0, by, out_row, 0)
    copies = column_copies(out_ref, columns_ref, out_sem, False)
    for copy in copies:
        copy.start()
    for copy in copies:
        copy.wait()


def vmem():
    return pl.BlockSpec(memory_space=pltpu.VMEM)


def smem():
    return pl.BlockSpec(memory_space=pltpu.SMEM)


def anywhere():
    return pl.BlockSpec(memory_space=pl.ANY)


def f32(*shape):
    return jax.ShapeDtypeStruct(shape, jnp.float32)


def body(probes, kappa2, cotangents):
    nx, ny, nz = (lax.axis_size(axis) for axis in ("gx", "gy", "gz"))
    count, bx, by, bz = probes.shape
    group = nx * nz
    assert group % count == 0
    copies = group // count
    X, Z = nx * bx, nz * bz
    grid = (nx, nz, bx, by, bz)
    gy = lax.axis_index("gy")
    mine = (lax.axis_index("gx") * nz + lax.axis_index("gz")) % count
    up = [(i, i + 1) for i in range(ny - 1)]
    down = [(target, source) for source, target in up]

    def scratch(rows):
        return pltpu.VMEM((rows, X, Z), jnp.float32)

    def columns_of(rows):
        return pltpu.VMEM((bz // 128, rows, 128), jnp.float32)

    low = lax.ppermute(kappa2[:, by - KAPPA_HALO :], "gy", up)
    high = lax.ppermute(kappa2[:, :KAPPA_HALO], "gy", down)
    kappa = jnp.concatenate([low, kappa2, high], axis=1)
    kappa = lax.all_gather(kappa, ("gx", "gz"), axis=0, tiled=False)
    kappa = kappa.reshape(group * bx * (by + 2 * KAPPA_HALO), bz)

    blocks = jnp.concatenate([probes] * copies, axis=0) if copies > 1 else probes
    blocks = lax.all_to_all(blocks, ("gx", "gz"), 0, 0, tiled=True)
    own, first, last = pl.pallas_call(
        functools.partial(assemble_kernel, grid),
        out_shape=(f32(by, X, Z), f32(DEPTH, X, Z), f32(DEPTH, X, Z)),
        in_specs=[anywhere()],
        out_specs=(vmem(),) * 3,
        scratch_shapes=[columns_of(group * bx * by), pltpu.SemaphoreType.DMA((bz // 128,))],
        compiler_params=pltpu.CompilerParams(vmem_limit_bytes=24 * MIB),
        name="assemble",
    )(blocks.reshape(group * bx * by, bz))
    low = lax.ppermute(last, "gy", up)
    high = lax.ppermute(first, "gy", down)

    bounds = jnp.stack(
        [jnp.where(gy == 0, 0, -DEPTH), jnp.where(gy == ny - 1, by, by + DEPTH)]
    ).astype(jnp.int32)

    d0, c1, d1, c2, d2, diagonal, moments = pl.pallas_call(
        functools.partial(first_kernel, grid),
        out_shape=(
            f32(by, X, Z), f32(by, X, Z), f32(by, X, Z), f32(by + 6, X, Z), f32(by + 8, X, Z),
            f32(by + 6, X, Z), f32(6, 8, 128),
        ),
        in_specs=[smem()] + [anywhere()] * 4,
        out_specs=(anywhere(),) * 6 + (vmem(),),
        scratch_shapes=[scratch(by + 2 * halo) for halo in (9, 8, 7, 6, 5, 4, KAPPA_HALO)]
        + [
            columns_of(group * bx * (by + 2 * KAPPA_HALO)),
            pltpu.SemaphoreType.DMA((3,)),
            pltpu.SemaphoreType.DMA((6,)),
            pltpu.SemaphoreType.DMA((bz // 128,)),
        ],
        compiler_params=pltpu.CompilerParams(vmem_limit_bytes=48 * MIB),
        name="first_steps",
    )(bounds, own, low, high, kappa)

    shares = [moments]
    for step in range(1, ny):
        shares.append(lax.ppermute(moments, "gy", [(i, (i + step) % ny) for i in range(ny)]))
    moments = jnp.concatenate(shares, axis=0)

    weights = lax.dynamic_slice_in_dim(cotangents, mine, 1, axis=1)[:, 0]
    inverse_count = 1.0 / (X * by * ny * Z)
    out = pl.pallas_call(
        functools.partial(second_kernel, grid, inverse_count, ny),
        out_shape=f32(group * bx * by, bz),
        in_specs=[smem(), smem(), vmem()] + [anywhere()] * 7,
        out_specs=anywhere(),
        scratch_shapes=[
            scratch(rows)
            for rows in (by, by, by, by, by + 6, by + 8, by + 6, by + 6, by + 4, by + 2)
        ]
        + [
            columns_of(group * bx * by),
            pltpu.SemaphoreType.DMA((7,)),
            pltpu.SemaphoreType.DMA((bz // 128,)),
        ],
        compiler_params=pltpu.CompilerParams(vmem_limit_bytes=48 * MIB),
        name="last_steps",
    )(bounds, weights, moments, own, d0, c1, d1, c2, d2, diagonal)

    out = lax.all_to_all(out.reshape(group, bx, by, bz), ("gx", "gz"), 0, 0, tiled=True)
    return jnp.sum(out[:count], axis=0)


def solution(mesh):
    return jax.shard_map(
        body,
        mesh=mesh,
        in_specs=(P(None, "gx", "gy", "gz"), P("gx", "gy", "gz"), P()),
        out_specs=P("gx", "gy", "gz"),
        check_vma=False,
    )
```

time: 757 us -> 133 us (0.18); the launches traced: 744 us -> 133 us
  blocking collectives: 368 us -> 37.7 us
  starting transfers between devices: 125 us -> 17.5 us
  local copies, waits for them, and re-layouts: 84.7 us -> 7.12 us
  other arithmetic: 74.6 us -> 2.43 us
  waiting for transfers between devices: 90.4 us -> 25 us
  Pallas kernels: 0 us -> 29.7 us
  between operations: 1.52 us -> 13.5 us
    psum x9 -> x0, blocking collectives: 368 us -> none  [the longest x2 83.8 us: orthogonalize(): lax.psum(local_sum(basis, image), ('gx', 'gy', 'gz')) * inverse_count]
    ppermute x54 -> x7, starting transfers between devices: 125 us -> 17.5 us  [the longest x3 6.46 us: body(): lax.ppermute(moments, 'gy', [(i, (i + step) % ny) for i in range(ny)])]
    ppermute x54 -> x7, waiting for transfers between devices: 90.4 us -> 25 us  [the longest x1 12 us: body(): low = lax.ppermute(last, 'gy', up)]
    reduce_sum x11 -> x1, other arithmetic: 49.5 us -> 0.73 us  [body(): return jnp.sum(out[:count], axis=0)]
    slice x36 -> x1, local copies, waits for them, and re-layouts: 45.9 us -> 0.97 us  [body(): low = lax.ppermute(kappa2[:, by - KAPPA_HALO:], 'gy', up)]
    all_to_all x0 -> x2, blocking collectives: none -> 37.7 us  [the longest x1 20.8 us: body(): blocks = lax.all_to_all(blocks, ('gx', 'gz'), 0, 0, tiled=True)]
    ppermute x18 -> x0, local copies, waits for them, and re-layouts: 35.6 us -> none  [the longest x9 17.8 us: with_halo(): lax.ppermute(lax.slice_in_dim(block, 0, width, axis=dim), axis, backward)]
    pallas_call x0 -> x3, Pallas kernels: none -> 29.7 us  [the longest x1 17.5 us: body(): pl.pallas_call(functools.partial(first_kernel, grid), out_shape=(f32(by,...]
  transfers between devices with their start and end apart: 54 -> 8, of which waited for: 31 -> 7; matrix products, arithmetic and copies ran while one was open for 4% -> 0% of each run, Pallas kernels for 0% -> 1%
where the time goes in v1:
time: 133 us
  blocking collectives  37.7 us (28%)
  Pallas kernels  29.7 us (22%)
  waiting for transfers between devices  25 us (19%)
  starting transfers between devices  17.5 us (13%)
  between operations  13.5 us (10%)
  local copies, waits for them, and re-layouts  7.12 us (5%)
  other arithmetic  2.43 us (2%)
    all_to_all x1, blocking collectives, body(): blocks = lax.all_to_all(blocks, ('gx', 'gz'), 0, 0, tiled=True)  20.8 us
    pallas_call x1, Pallas kernels, body(): pl.pallas_call(functools.partial(first_kernel, grid), out_shape=(f32(by,...  17.5 us
    all_to_all x1, blocking collectives, body(): lax.all_to_all(out.reshape(group, bx, by, bz), ('gx', 'gz'), 0, 0, tiled=...  16.9 us
    ppermute x1, waiting for transfers between devices, body(): low = lax.ppermute(last, 'gy', up)  12 us
    pallas_call x1, Pallas kernels, body(): pl.pallas_call(functools.partial(second_kernel, grid, inverse_count, ny),...  11 us
    ppermute x3, starting transfers between devices, body(): lax.ppermute(moments, 'gy', [(i, (i + step) % ny) for i in range(ny)])  6.46 us
    unnamed x16, local copies, waits for them, and re-layouts  5.97 us
    ppermute x3, waiting for transfers between devices, body(): lax.ppermute(moments, 'gy', [(i, (i + step) % ny) for i in range(ny)])  5.14 us
  transfers between devices with their start and end apart: 8, of which 7 were waited for; matrix products, arithmetic and copies ran while one was open for 0% of the time, Pallas kernels for 1%

profile of v1, /device:TPU:0, one launch (start us, length us, event | category | flops | bytes accessed | tf_op | source)
XLA Modules:
  0.0 133.0 jit_solution(3262087378867942785)
XLA Ops:
  6.5 1.0 fusion
  7.5 4.9 %collective-permute-start.2 = (f32[8,8,256]{2,1,0:T(8,128)S(1)}, f32[8,8,256]{2,1,0:T(8,128)S(1)}, u32[]{:S(2)}, u32[]{:S(2)}) collective-permute-start(f32[8,8,256]{2,1,0:T(8,128)S(1)} %get-tuple-element.25), channel_id=1, source_target_pairs={{0,2},{2,4},{4,6},{1,3},{3,5},{5,7},{8,10},{10,12},{12,14},{9,11},... | collective-permute-start | bytes 196616 | tf_op jit(solution)/shard_map/ppermute | solution.py:322
  12.5 1.3 collective-permute-start.3
  14.3 4.3 %collective-permute-done.3 = f32[8,8,256]{2,1,0:T(8,128)S(1)} collective-permute-done((f32[8,8,256]{2,1,0:T(8,128)S(1)}, f32[8,8,256]{2,1,0:T(8,128)S(1)}, u32[]{:S(2)}, u32[]{:S(2)}) %collective-permute-start.3) | collective-permute-done | bytes 65568 | tf_op jit(solution)/shard_map/ppermute | solution.py:323
  18.6 1.6 %pad_maximum_fusion = f32[8,32,256]{2,1,0:T(8,128)} fusion(f32[8,8,256]{2,1,0:T(8,128)S(1)} %collective-permute-done.3, f32[8,16,256]{2,1,0:T(8,128)} %param.4, f32[8,8,256]{2,1,0:T(8,128)S(1)} %collective-permute-done.2), kind=kLoop, calls=%fused_computation | loop fusion | flops 131072 | bytes 524288 | tf_op jit(solution)/shard_map/concatenate | solution.py:324
  20.3 20.8 %all_to_all.10 = f32[8,8,16,256]{3,2,1,0:T(8,128)S(1)} all-to-all(f32[8,8,16,256]{3,2,1,0:T(8,128)S(1)} %copy-done.7), channel_id=1, replica_groups=mesh['gx'=4,'gy'=4,'gz'=2] {'gx','gz'}, dimensions={0} | all-to-all | bytes 2097152 | tf_op jit(solution)/shard_map/all_to_all | solution.py:329
  41.1 1.3 assemble.1
  42.3 3.5 %collective-permute-start = (f32[9,32,512]{2,1,0:T(8,128)}, f32[9,32,512]{2,1,0:T(8,128)S(1)}, u32[]{:S(2)}, u32[]{:S(2)}) collective-permute-start(f32[9,32,512]{2,1,0:T(8,128)} %get-tuple-element.16), channel_id=1, source_target_pairs={{0,2},{2,4},{4,6},{1,3},{3,5},{5,7},{8,10},{10,12},{12,14},{9,11},... | collective-permute-start | bytes 1769480 | tf_op jit(solution)/shard_map/ppermute | solution.py:339
  45.9 1.3 collective-permute-start.1
  47.2 12.0 %collective-permute-done.low_ref = f32[9,32,512]{2,1,0:T(8,128)S(1)} collective-permute-done((f32[9,32,512]{2,1,0:T(8,128)}, f32[9,32,512]{2,1,0:T(8,128)S(1)}, u32[]{:S(2)}, u32[]{:S(2)}) %collective-permute-start) | collective-permute-done | bytes 589856 | tf_op jit(solution)/shard_map/ppermute | solution.py:339
  59.2 0.8 copy-done.3
  60.0 3.0 %collective-permute-done.1.high_ref = f32[9,32,512]{2,1,0:T(8,128)S(1)} collective-permute-done((f32[9,32,512]{2,1,0:T(8,128)S(1)}, f32[9,32,512]{2,1,0:T(8,128)S(1)}, u32[]{:S(2)}, u32[]{:S(2)}) %collective-permute-start.1) | collective-permute-done | bytes 589856 | tf_op jit(solution)/shard_map/ppermute | solution.py:340
  63.1 0.8 copy-done.5
  63.9 1.1 copy-done.4
  64.9 1.1 copy-done.6
  66.0 17.5 %first_steps.1 = (f32[16,32,512]{2,1,0:T(8,128)S(1)}, f32[16,32,512]{2,1,0:T(8,128)S(1)}, f32[16,32,512]{2,1,0:T(8,128)S(1)}, f32[22,32,512]{2,1,0:T(8,128)}, f3...) custom-call(s32[2]{0:T(128)S(1)} %pad_add_fusion.bounds_ref, ...), custom_call_target="tpu_custom_call" | custom-call | tf_op jit(solution)/shard_map/first_steps/pallas_call | solution.py:346
  83.5 1.0 copy-done.1
  84.8 5.9 %collective-permute-start.5 = (f32[6,8,128]{2,1,0:T(8,128)S(1)}, f32[6,8,128]{2,1,0:T(8,128)S(1)}, u32[]{:S(2)}, u32[]{:S(2)}) collective-permute-start(f32[6,8,128]{2,1,0:T(8,128)S(1)} %get-tuple-element.18), channel_id=1, source_target_pairs={{0,4},{2,6},{4,0},{6,2},{1,5},{3,7},{5,1},{7,3},{8,12},{10,14},{12... | collective-permute-start | bytes 73736 | tf_op jit(solution)/shard_map/ppermute | solution.py:367
  91.3 1.5 %collective-permute-done.5 = f32[6,8,128]{2,1,0:T(8,128)S(1)} collective-permute-done((f32[6,8,128]{2,1,0:T(8,128)S(1)}, f32[6,8,128]{2,1,0:T(8,128)S(1)}, u32[]{:S(2)}, u32[]{:S(2)}) %collective-permute-start.5) | collective-permute-done | bytes 24608 | tf_op jit(solution)/shard_map/ppermute | solution.py:367
  92.7 3.6 %collective-permute-done.4 = f32[6,8,128]{2,1,0:T(8,128)S(1)} collective-permute-done((f32[6,8,128]{2,1,0:T(8,128)S(1)}, f32[6,8,128]{2,1,0:T(8,128)S(1)}, u32[]{:S(2)}, u32[]{:S(2)}) %collective-permute-start.4) | collective-permute-done | bytes 24608 | tf_op jit(solution)/shard_map/ppermute | solution.py:367
  96.3 1.2 copy-done.2
  97.5 11.0 %last_steps.1 = f32[1024,256]{1,0:T(8,128)S(1)} custom-call(s32[2]{0:T(128)S(1)} %pad_add_fusion.bounds_ref, f32[5]{0:T(128)S(1)} %dynamic-slice_reduce_fusion.weights_ref, f32[24,8,128]{2,1,0:T(8,128)S(1)} %pad_maximum_fusion.1.moments_ref, f32[16,32,512]{2,1,0:T(8,128)S(1)} %get-tuple-element.15.own_ref.c0_in, f32[16,32,512]{2,1,0:T(8,128)S(1)} %get-tuple-element.19.d0_in, ...), custom_call_target="tpu_custom_call" | custom-call | tf_op jit(solution)/shard_map/last_steps/pallas_call | solution.py:372
  108.5 16.9 %all_to_all.11 = f32[8,8,16,256]{3,2,1,0:T(8,128)S(1)} all-to-all(f32[8,8,16,256]{3,2,1,0:T(8,128)S(1)} %bitcast.5), channel_id=1, replica_groups=mesh['gx'=4,'gy'=4,'gz'=2] {'gx','gz'}, dimensions={0} | all-to-all | bytes 2097152 | tf_op jit(solution)/shard_map/all_to_all | solution.py:390
  125.4 0.7 reduce_sum.9
  (20 shorter events, 1.5 us)
Async XLA Ops:
  6.5 84.4 %copy-start = (f32[5,8]{1,0:T(8,128)S(1)}, f32[5,8]{1,0:T(8,128)}, u32[]{:S(2)}) copy-start(f32[5,8]{1,0:T(8,128)} %param.5) | copy-start | bytes 484
  6.5 13.7 %copy-start.7 = (f32[8,8,16,256]{3,2,1,0:T(8,128)S(1)}, f32[8,8,16,256]{3,2,1,0:T(8,128)}, u32[]{:S(2)}) copy-start(f32[8,8,16,256]{3,2,1,0:T(8,128)} %param.3) | copy-start | bytes 3145732
  6.5 57.3 %all-gather.3.cloned.1.call-start = ((), (), s32[]{:S(2)}) async-start(), calls=%async_computation.2 | async-start | bytes 2359296 | tf_op jit(solution)/shard_map/all_gather | solution.py:325
  7.5 6.8 %collective-permute-start.2 = (f32[8,8,256]{2,1,0:T(8,128)S(1)}, f32[8,8,256]{2,1,0:T(8,128)S(1)}, u32[]{:S(2)}, u32[]{:S(2)}) collective-permute-start(f32[8,8,256]{2,1,0:T(8,128)S(1)} %get-tuple-element.25), channel_id=1, source_target_pairs={{0,2},{2,4},{4,6},{1,3},{3,5},{5,7},{8,10},{10,12},{12,14},{9,11},... | collective-permute-start | bytes 196616 | tf_op jit(solution)/shard_map/ppermute | solution.py:322
  12.5 6.2 %collective-permute-start.3 = (f32[8,8,256]{2,1,0:T(8,128)S(1)}, f32[8,8,256]{2,1,0:T(8,128)S(1)}, u32[]{:S(2)}, u32[]{:S(2)}) collective-permute-start(f32[8,8,256]{2,1,0:T(8,128)S(1)} %get-tuple-element.26), channel_id=1, source_target_pairs={{2,0},{4,2},{6,4},{3,1},{5,3},{7,5},{10,8},{12,10},{14,12},{11,9},... | collective-permute-start | bytes 196616 | tf_op jit(solution)/shard_map/ppermute | solution.py:323
  42.3 16.9 %collective-permute-start = (f32[9,32,512]{2,1,0:T(8,128)}, f32[9,32,512]{2,1,0:T(8,128)S(1)}, u32[]{:S(2)}, u32[]{:S(2)}) collective-permute-start(f32[9,32,512]{2,1,0:T(8,128)} %get-tuple-element.16), channel_id=1, source_target_pairs={{0,2},{2,4},{4,6},{1,3},{3,5},{5,7},{8,10},{10,12},{12,14},{9,11},... | collective-permute-start | bytes 1769480 | tf_op jit(solution)/shard_map/ppermute | solution.py:339
  45.9 17.2 %collective-permute-start.1 = (f32[9,32,512]{2,1,0:T(8,128)S(1)}, f32[9,32,512]{2,1,0:T(8,128)S(1)}, u32[]{:S(2)}, u32[]{:S(2)}) collective-permute-start(f32[9,32,512]{2,1,0:T(8,128)S(1)} %get-tuple-element.17), channel_id=1, source_target_pairs={{2,0},{4,2},{6,4},{3,1},{5,3},{7,5},{10,8},{12,10},{14,12},{11,9},... | collective-permute-start | bytes 1769480 | tf_op jit(solution)/shard_map/ppermute | solution.py:340
  59.2 0.8 copy-start.3
  63.1 0.8 copy-start.5
  63.9 1.1 copy-start.4
  64.9 1.1 copy-start.6
  83.5 1.0 copy-start.1
  84.5 6.8 %collective-permute-start.6 = (f32[6,8,128]{2,1,0:T(8,128)S(1)}, f32[6,8,128]{2,1,0:T(8,128)S(1)}, u32[]{:S(2)}, u32[]{:S(2)}) collective-permute-start(f32[6,8,128]{2,1,0:T(8,128)S(1)} %get-tuple-element.18), channel_id=1, source_target_pairs={{0,6},{2,0},{4,2},{6,4},{1,7},{3,1},{5,3},{7,5},{8,14},{10,8},{12,... | collective-permute-start | bytes 73736 | tf_op jit(solution)/shard_map/ppermute | solution.py:367
  84.8 8.0 %collective-permute-start.5 = (f32[6,8,128]{2,1,0:T(8,128)S(1)}, f32[6,8,128]{2,1,0:T(8,128)S(1)}, u32[]{:S(2)}, u32[]{:S(2)}) collective-permute-start(f32[6,8,128]{2,1,0:T(8,128)S(1)} %get-tuple-element.18), channel_id=1, source_target_pairs={{0,4},{2,6},{4,0},{6,2},{1,5},{3,7},{5,1},{7,3},{8,12},{10,14},{12... | collective-permute-start | bytes 73736 | tf_op jit(solution)/shard_map/ppermute | solution.py:367
  90.7 5.6 %collective-permute-start.4 = (f32[6,8,128]{2,1,0:T(8,128)S(1)}, f32[6,8,128]{2,1,0:T(8,128)S(1)}, u32[]{:S(2)}, u32[]{:S(2)}) collective-permute-start(f32[6,8,128]{2,1,0:T(8,128)S(1)} %get-tuple-element.18), channel_id=1, source_target_pairs={{0,2},{2,4},{4,6},{6,0},{1,3},{3,5},{5,7},{7,1},{8,10},{10,12},{12... | collective-permute-start | bytes 73736 | tf_op jit(solution)/shard_map/ppermute | solution.py:367
  96.3 1.2 copy-start.2
Sparse Core Ops, SparseCore 0:
  20.4 33.6 all-gather.2

commit v2 on v1

v2 whole, which is shorter than its diff:
```python
import functools

import jax
import jax.numpy as jnp
from jax import lax
from jax.experimental import pallas as pl
from jax.experimental.pallas import tpu as pltpu
from jax.sharding import PartitionSpec as P

EPSILON = 1e-06
SHIFT = 64.0
HALO = 5
DIAGONAL_HALO = 4
PAD = 8
MIB = 1024 * 1024


def loss_of_moments(moments, weights):
    m0, m1, m2, m3, m4, m5 = moments
    norm = m0 + EPSILON
    alpha1 = (m1 + SHIFT * m0) / norm
    e1 = SHIFT - alpha1
    rest1 = jnp.maximum(m2 + 2.0 * e1 * m1 + e1 * e1 * m0, 0.0)
    beta1_square = rest1 / norm + EPSILON
    beta1 = jnp.sqrt(beta1_square)
    scale = 1.0 / (norm * beta1_square)
    alpha2 = scale * (m3 + 2.0 * e1 * m2 + e1 * e1 * m1 + SHIFT * rest1) - (m1 + e1 * m0) / norm
    e2 = SHIFT - alpha2
    f1 = e1 + e2
    f0 = e1 * e2 - beta1_square
    g = f1 * f1 + 2.0 * f0
    rest2 = jnp.maximum(m4 + 2.0 * f1 * m3 + g * m2 + 2.0 * f1 * f0 * m1 + f0 * f0 * m0, 0.0)
    beta2_square = scale * rest2 + EPSILON
    beta2 = jnp.sqrt(beta2_square)
    image2 = m5 + 2.0 * f1 * m4 + g * m3 + 2.0 * f1 * f0 * m2 + f0 * f0 * m1
    cross = m3 + f1 * m2 + f0 * m1 + e1 * (m2 + f1 * m1 + f0 * m0)
    alpha3 = scale * ((image2 + SHIFT * rest2) / beta2_square - cross)
    return (
        weights[0] * alpha1
        + weights[1] * alpha2
        + weights[2] * alpha3
        + weights[3] * beta1
        + weights[4] * beta2
    )


class Field:
    def __init__(self, ref, halo):
        self.ref = ref
        self.halo = halo
        self.columns, self.rows, self.pitch, _ = ref.shape
        self.cells = self.pitch - PAD
        self.flat = ref.reshape(self.columns * self.rows * self.pitch, 128)

    def at(self, column, row, x):
        moving, fixed = row
        start = (column * self.rows + fixed + self.halo) * self.pitch + x
        return pl.ds(moving * self.pitch + start, 8)

    def load(self, column, row, x):
        return self.flat[self.at(column, row, x), :]

    def store(self, column, row, x, value):
        self.flat[self.at(column, row, x), :] = value

    def part(self, first, count):
        return self.ref.at[:, pl.ds(first + self.halo, count), pl.ds(0, self.cells), :]

    def clear_pads(self):
        zero = jnp.zeros((8, 128), jnp.float32)

        def body(row, carry):
            for column in range(self.columns):
                self.store(column, (row, -self.halo), self.cells, zero)
            return carry

        lax.fori_loop(0, self.rows, body, 0)

    def clear_row(self, row):
        zero = jnp.zeros((8, 128), jnp.float32)
        for column in range(self.columns):
            for x in range(0, self.cells, 8):
                self.store(column, (0, row), x, zero)


def lane_masks():
    lane = lax.broadcasted_iota(jnp.int32, (8, 128), 1)
    return lane == 0, lane == 127


def stencil_tiles(source, diagonal, row, x, masks):
    columns = range(source.columns)
    moving, fixed = row
    centre = [source.load(c, row, x) for c in columns]
    after = [pltpu.roll(value, 1, 1) for value in centre]
    before = [pltpu.roll(value, 127, 1) for value in centre]
    results = []
    for c in columns:
        low = after[c - 1] if c else 0.0
        high = before[c + 1] if c + 1 < source.columns else 0.0
        total = jnp.where(masks[0], low, after[c]) + jnp.where(masks[1], high, before[c])
        total = total + (source.load(c, row, x - 1) + source.load(c, row, x + 1))
        total = total + (source.load(c, (moving, fixed - 1), x) + source.load(c, (moving, fixed + 1), x))
        results.append(diagonal.load(c, row, x) * centre[c] - total)
    return results


def apply_rows(target, source, diagonal, first, count, minus=None, unroll=2):
    masks = lane_masks()

    def body(step, carry):
        for offset in range(unroll):
            row = (step * unroll, first + offset)
            for x in range(0, source.cells, 8):
                values = stencil_tiles(source, diagonal, row, x, masks)
                for c, value in enumerate(values):
                    if minus is not None:
                        value = value - SHIFT * minus.load(c, row, x)
                    target.store(c, row, x, value)
        return carry

    assert count % unroll == 0
    lax.fori_loop(0, count // unroll, body, 0)


def clear_outside(ends_ref, own, field):
    @pl.when(ends_ref[0] == 1)
    def _():
        field.clear_row(-1)

    @pl.when(ends_ref[1] == 1)
    def _():
        field.clear_row(own)


def apply_steps(ends_ref, own, target, source, diagonal, halo, minus=None):
    apply_rows(target, source, diagonal, -halo, own + 2 * halo, minus)
    if halo:
        clear_outside(ends_ref, own, target)


def column_copies(whole, columns, sem, inward):
    copies = []
    for index in range(columns.shape[0]):
        pair = (whole.at[:, pl.ds(index * 128, 128)], columns.at[index])
        source, target = pair if inward else pair[::-1]
        copies.append(pltpu.make_async_copy(source, target, sem.at[index]))
    return copies


def start_all(pairs, sem):
    copies = []
    for index, (source, target) in enumerate(pairs):
        copy = pltpu.make_async_copy(source, target, sem.at[index])
        copy.start()
        copies.append(copy)
    return copies


def places(grid):
    nx, nz, bx, by, bz = grid
    per = bz // 128
    for s in range(nx * nz):
        for column in range(per):
            yield (s // nz) * bx, (s % nz) * per + column, s, column


def assemble_kernel(
    grid, blocks_ref, kappa_ref,
    own_ref, diagonal_ref, up_ref, down_ref,
    block_columns, kappa_columns, block_sem, kappa_sem,
):
    nx, nz, bx, by, bz = grid
    copies = column_copies(blocks_ref, block_columns, block_sem, True)
    copies += column_copies(kappa_ref, kappa_columns, kappa_sem, True)
    for copy in copies:
        copy.start()
    for copy in copies:
        copy.wait()
    for x, z, s, column in places(grid):
        xs = pl.ds(x, bx)
        for y in range(by):
            rows = pl.ds(s * bx * by + y, bx, stride=by)
            value = block_columns[column, rows, :]
            own_ref[z, y, xs, :] = value
            if y < HALO:
                down_ref[z, y, xs, :] = value
            if y >= by - HALO:
                up_ref[z, y - (by - HALO), xs, :] = value
            value = 6.0 + kappa_columns[column, rows, :]
            diagonal_ref[z, y, xs, :] = value
            if y < DIAGONAL_HALO:
                down_ref[z, HALO + y, xs, :] = value
            if y >= by - DIAGONAL_HALO:
                up_ref[z, HALO + y - (by - DIAGONAL_HALO), xs, :] = value


def halo_pairs(field, own, low_ref, high_ref, start, halo):
    rows = pl.ds(start, halo)
    return [
        (low_ref.at[:, rows], field.part(-halo, halo)),
        (high_ref.at[:, rows], field.part(own, halo)),
    ]


def first_kernel(
    grid,
    ends_ref, own_in, diagonal_in, low_in, high_in,
    d0_out, c1_out, d1_out, c2_out, up_out, down_out,
    c0_ref, d0_ref, c1_ref, d1_ref, c2_ref, diagonal_ref, in_sem, out_sem,
):
    nx, nz, bx, by, bz = grid
    c0 = Field(c0_ref, 5)
    d0 = Field(d0_ref, 4)
    c1 = Field(c1_ref, 3)
    d1 = Field(d1_ref, 2)
    c2 = Field(c2_ref, 1)
    diagonal = Field(diagonal_ref, DIAGONAL_HALO)
    arrivals = start_all(
        [(own_in, c0.part(0, by)), (diagonal_in, diagonal.part(0, by))]
        + halo_pairs(c0, by, low_in, high_in, 0, HALO)
        + halo_pairs(diagonal, by, low_in, high_in, HALO, DIAGONAL_HALO),
        in_sem,
    )
    for field in (c0, d0, c1, d1, c2):
        field.clear_pads()
    departures = []

    def depart(source, out):
        copy = pltpu.make_async_copy(source, out, out_sem.at[len(departures)])
        copy.start()
        departures.append(copy)

    for copy in arrivals:
        copy.wait()
    steps = functools.partial(apply_steps, ends_ref, by)
    steps(d0, c0, diagonal, 4)
    depart(d0.part(0, by), d0_out)
    steps(c1, d0, diagonal, 3, c0)
    depart(c1.part(0, by), c1_out)
    steps(d1, c1, diagonal, 2)
    depart(d1.part(0, by), d1_out)
    steps(c2, d1, diagonal, 1, c1)
    depart(c2.part(by - HALO, HALO), up_out)
    depart(c2.part(0, HALO), down_out)
    depart(c2.part(-1, by + 2), c2_out)
    for copy in departures:
        copy.wait()


def middle_kernel(
    grid,
    c0_in, c1_in, c2_in, diagonal_in,
    d2_out, moments_ref,
    c0_ref, c1_ref, c2_ref, d2_ref, diagonal_ref, in_sem, out_sem,
):
    nx, nz, bx, by, bz = grid
    c0 = Field(c0_ref, 0)
    c1 = Field(c1_ref, 0)
    c2 = Field(c2_ref, 1)
    d2 = Field(d2_ref, 0)
    diagonal = Field(diagonal_ref, 0)
    copies = start_all(
        [
            (c2_in, c2.part(-1, by + 2)), (diagonal_in, diagonal.part(0, by)),
            (c0_in, c0.part(0, by)), (c1_in, c1.part(0, by)),
        ],
        in_sem,
    )
    c2.clear_pads()
    for copy in copies[:2]:
        copy.wait()
    apply_rows(d2, c2, diagonal, 0, by)
    out = pltpu.make_async_copy(d2.part(0, by), d2_out, out_sem.at[0])
    out.start()
    for copy in copies[2:]:
        copy.wait()

    def moment_row(step, sums):
        row = (step, 0)
        for x in range(0, c0.cells, 8):
            for c in range(c0.columns):
                a, b, e, d = (field.load(c, row, x) for field in (c0, c1, c2, d2))
                pairs = ((a, a), (a, b), (b, b), (b, e), (e, e), (d, d))
                sums = tuple(total + u * v for total, (u, v) in zip(sums, pairs))
        return sums

    zero = jnp.zeros((8, 128), jnp.float32)
    sums = lax.fori_loop(0, by, moment_row, (zero,) * 6)
    for index, total in enumerate(sums):
        moments_ref[index] = total
    out.wait()


def moment_slopes(inverse_count, parts, weights_ref, moments_ref):
    raw = []
    for k in range(6):
        total = moments_ref[k]
        for part in range(1, parts):
            total = total + moments_ref[part * 6 + k]
        total = jnp.sum(jnp.sum(total, axis=0, keepdims=True), axis=1, keepdims=True)
        raw.append(jnp.broadcast_to(total * inverse_count, (8, 128)))
    moments = tuple(raw[:5]) + (raw[5] - SHIFT * raw[4],)
    weights = [weights_ref[k] for k in range(5)]
    value, pullback = jax.vjp(lambda m: loss_of_moments(m, weights), moments)
    (slopes,) = pullback(jnp.full((8, 128), 2.0, jnp.float32))
    return [slope[0, 0] for slope in slopes]


def last_kernel(
    grid, inverse_count, parts,
    ends_ref, weights_ref, moments_ref,
    c0_in, d0_in, c1_in, d1_in, c2_in, d2_in, diagonal_in, low1_in, high1_in, low2_in, high2_in,
    out_ref,
    c0_ref, d0_ref, c1_ref, d1_ref, c2_ref, d2_ref, diagonal_ref, c3_ref, d3_ref, c4_ref,
    columns_ref, in_sem, out_sem,
):
    nx, nz, bx, by, bz = grid
    c0, d0, c1, d1 = (Field(ref, 0) for ref in (c0_ref, d0_ref, c1_ref, d1_ref))
    c2 = Field(c2_ref, HALO)
    d2 = Field(d2_ref, 4)
    c3 = Field(c3_ref, 3)
    d3 = Field(d3_ref, 2)
    c4 = Field(c4_ref, 1)
    diagonal = Field(diagonal_ref, DIAGONAL_HALO)
    copies = start_all(
        [(diagonal_in, diagonal.part(0, by)), (c2_in.at[:, pl.ds(1, by)], c2.part(0, by))]
        + halo_pairs(diagonal, by, low1_in, high1_in, HALO, DIAGONAL_HALO)
        + halo_pairs(c2, by, low2_in, high2_in, 0, HALO)
        + [
            (d2_in, d2.part(0, by)), (c0_in, c0.part(0, by)), (d0_in, d0.part(0, by)),
            (c1_in, c1.part(0, by)), (d1_in, d1.part(0, by)),
        ],
        in_sem,
    )
    for field in (c2, d2, c3, d3, c4):
        field.clear_pads()
    slopes = moment_slopes(inverse_count, parts, weights_ref, moments_ref)
    for copy in copies[:6]:
        copy.wait()
    apply_rows(d2, c2, diagonal, -4, 4)
    apply_rows(d2, c2, diagonal, by, 4)
    clear_outside(ends_ref, by, d2)
    copies[6].wait()
    steps = functools.partial(apply_steps, ends_ref, by)
    steps(c3, d2, diagonal, 3, c2)
    steps(d3, c3, diagonal, 2)
    steps(c4, d3, diagonal, 1, c3)
    for copy in copies[7:]:
        copy.wait()
    masks = lane_masks()
    place = {(x, z): (s, column) for x, z, s, column in places(grid)}

    def out_row(step, carry):
        row = (step, 0)
        for x in range(0, c4.cells, 8):
            last = stencil_tiles(c4, diagonal, row, x, masks)
            for z in range(c4.columns):
                cs = [field.load(z, row, x) for field in (c0, c1, c2, c3, c4)]
                ds = [field.load(z, row, x) for field in (d0, d1, d2, d3)] + [last[z]]
                total = None
                for i in range(5):
                    inner = None
                    for j in range(5 - i):
                        term = slopes[i + j + 1] * ds[j]
                        inner = term if inner is None else inner + term
                    term = cs[i] * inner
                    total = term if total is None else total + term
                s, column = place[x, z]
                columns_ref[column, pl.ds(s * bx * by + step, bx, stride=by), :] = total
        return carry

    lax.fori_loop(0, by, out_row, 0)
    copies = column_copies(out_ref, columns_ref, out_sem, False)
    for copy in copies:
        copy.start()
    for copy in copies:
        copy.wait()


def vmem():
    return pl.BlockSpec(memory_space=pltpu.VMEM)


def smem():
    return pl.BlockSpec(memory_space=pltpu.SMEM)


def anywhere():
    return pl.BlockSpec(memory_space=pl.ANY)


def f32(*shape):
    return jax.ShapeDtypeStruct(shape, jnp.float32)


def params():
    return pltpu.CompilerParams(vmem_limit_bytes=60 * MIB)


def body(probes, kappa2, cotangents):
    nx, ny, nz = (lax.axis_size(axis) for axis in ("gx", "gy", "gz"))
    count, bx, by, bz = probes.shape
    group = nx * nz
    assert group % count == 0 and bx == 8 and by % 2 == 0 and by >= HALO and bz % 128 == 0
    copies = group // count
    X = nx * bx
    columns = nz * bz // 128
    per = bz // 128
    grid = (nx, nz, bx, by, bz)
    gy = lax.axis_index("gy")
    mine = (lax.axis_index("gx") * nz + lax.axis_index("gz")) % count
    up = [(i, i + 1) for i in range(ny - 1)]
    down = [(target, source) for source, target in up]

    def rows_of(rows):
        return f32(columns, rows, X, 128)

    def scratch(rows):
        return pltpu.VMEM((columns, rows, X + PAD, 128), jnp.float32)

    def block_scratch():
        return pltpu.VMEM((per, group * bx * by, 128), jnp.float32)

    dma = pltpu.SemaphoreType.DMA

    kappa = lax.all_gather(kappa2, ("gx", "gz"), axis=0, tiled=False)
    blocks = jnp.concatenate([probes] * copies, axis=0) if copies > 1 else probes
    blocks = lax.all_to_all(blocks, ("gx", "gz"), 0, 0, tiled=True)
    c0, diagonal, up_edge, down_edge = pl.pallas_call(
        functools.partial(assemble_kernel, grid),
        out_shape=(
            rows_of(by), rows_of(by), rows_of(HALO + DIAGONAL_HALO), rows_of(HALO + DIAGONAL_HALO)
        ),
        in_specs=[anywhere(), anywhere()],
        out_specs=(vmem(),) * 4,
        scratch_shapes=[block_scratch(), block_scratch(), dma((per,)), dma((per,))],
        compiler_params=params(),
        name="assemble",
    )(blocks.reshape(group * bx * by, bz), kappa.reshape(group * bx * by, bz))
    low1 = lax.ppermute(up_edge, "gy", up)
    high1 = lax.ppermute(down_edge, "gy", down)

    ends = jnp.stack([gy == 0, gy == ny - 1]).astype(jnp.int32)
    d0, c1, d1, c2, up_edge, down_edge = pl.pallas_call(
        functools.partial(first_kernel, grid),
        out_shape=(rows_of(by),) * 3 + (rows_of(by + 2), rows_of(HALO), rows_of(HALO)),
        in_specs=[smem()] + [anywhere()] * 4,
        out_specs=(anywhere(),) * 6,
        scratch_shapes=[scratch(by + 2 * halo) for halo in (5, 4, 3, 2, 1, DIAGONAL_HALO)]
        + [dma((6,)), dma((6,))],
        compiler_params=params(),
        name="first_steps",
    )(ends, c0, diagonal, low1, high1)
    low2 = lax.ppermute(up_edge, "gy", up)
    high2 = lax.ppermute(down_edge, "gy", down)

    d2, moments = pl.pallas_call(
        functools.partial(middle_kernel, grid),
        out_shape=(rows_of(by), f32(6, 8, 128)),
        in_specs=[anywhere()] * 4,
        out_specs=(anywhere(), vmem()),
        scratch_shapes=[scratch(rows) for rows in (by, by, by + 2, by, by)] + [dma((4,)), dma((1,))],
        compiler_params=params(),
        cost_estimate=pl.CostEstimate(
            flops=40 * by * X * columns * 128, bytes_accessed=24 * by * X * columns * 128,
            transcendentals=0,
        ),
        name="middle_step",
    )(c0, c1, c2, diagonal)
    shares = [moments]
    for step in range(1, ny):
        shares.append(lax.ppermute(moments, "gy", [(i, (i + step) % ny) for i in range(ny)]))
    moments = jnp.concatenate(shares, axis=0)

    weights = lax.dynamic_slice_in_dim(cotangents, mine, 1, axis=1)[:, 0]
    inverse_count = 1.0 / (X * by * ny * columns * 128)
    out = pl.pallas_call(
        functools.partial(last_kernel, grid, inverse_count, ny),
        out_shape=f32(group * bx * by, bz),
        in_specs=[smem(), smem(), vmem()] + [anywhere()] * 11,
        out_specs=anywhere(),
        scratch_shapes=[
            scratch(by + rows) for rows in (0, 0, 0, 0, 2 * HALO, 8, 2 * DIAGONAL_HALO, 6, 4, 2)
        ]
        + [block_scratch(), dma((11,)), dma((per,))],
        compiler_params=params(),
        name="last_steps",
    )(ends, weights, moments, c0, d0, c1, d1, c2, d2, diagonal, low1, high1, low2, high2)

    out = lax.all_to_all(out.reshape(group, bx, by, bz), ("gx", "gz"), 0, 0, tiled=True)
    return jnp.sum(out[:count], axis=0)


def solution(mesh):
    return jax.shard_map(
        body,
        mesh=mesh,
        in_specs=(P(None, "gx", "gy", "gz"), P("gx", "gy", "gz"), P()),
        out_specs=P("gx", "gy", "gz"),
        check_vma=False,
    )
```

time: 133 us -> 132 us (level)
  waiting for transfers between devices: 25 us -> 30.1 us
  local copies, waits for them, and re-layouts: 7.12 us -> 2.33 us
  starting transfers between devices: 17.5 us -> 15 us
  blocking collectives: 37.7 us -> 39.1 us
    all_gather x1, waiting for transfers between devices: 0.01 us -> 10.3 us  [body(): kappa = lax.all_gather(kappa2, ('gx', 'gz'), axis=0, tiled=False)]
    ppermute x4, waiting for transfers between devices: 19.8 us -> 15.4 us  [the longest x1 11.4 us: body(): low1 = lax.ppermute(up_edge, 'gy', up)]
    unnamed x16 -> x10, local copies, waits for them, and re-layouts: 5.97 us -> 1.63 us
    ppermute x4, starting transfers between devices: 11 us -> 9.38 us  [the longest x1 3.43 us: body(): low1 = lax.ppermute(up_edge, 'gy', up)]
    concatenate x1 -> x0, other arithmetic: 1.61 us -> none  [body(): kappa = jnp.concatenate([low, kappa2, high], axis=1)]
    ppermute x3, waiting for transfers between devices: 5.14 us -> 3.66 us  [body(): lax.ppermute(moments, 'gy', [(i, (i + step) % ny) for i in range(ny)])]
    concatenate x1, other arithmetic: 0.01 us -> 1.38 us  [body(): moments = jnp.concatenate(shares, axis=0)]
    pallas_call x3 -> x4, Pallas kernels: 29.7 us -> 28.8 us  [the longest x1 11 us: body(): pl.pallas_call(functools.partial(last_kernel, grid, inverse_count, ny), o...]
  transfers between devices with their start and end apart: 8 -> 8, of which waited for: 7 -> 5; matrix products, arithmetic and copies ran while one was open for 0% -> 2% of each run, Pallas kernels for 1% -> 3%
where the time goes in v2:
time: 132 us; the launch traced here: 131 us
  blocking collectives  39.1 us (30%)
  waiting for transfers between devices  30.1 us (23%)
  Pallas kernels  28.8 us (22%)
  starting transfers between devices  15 us (11%)
  between operations  13.5 us (10%)
  other arithmetic  2.7 us (2%)
  local copies, waits for them, and re-layouts  2.33 us (2%)
    all_to_all x1, blocking collectives, body(): blocks = lax.all_to_all(blocks, ('gx', 'gz'), 0, 0, tiled=True)  21.1 us
    all_to_all x1, blocking collectives, body(): lax.all_to_all(out.reshape(group, bx, by, bz), ('gx', 'gz'), 0, 0, tiled=...  17.9 us
    ppermute x1, waiting for transfers between devices, body(): low1 = lax.ppermute(up_edge, 'gy', up)  11.4 us
    pallas_call x1, Pallas kernels, body(): pl.pallas_call(functools.partial(last_kernel, grid, inverse_count, ny), o...  11 us
    all_gather x1, waiting for transfers between devices, body(): kappa = lax.all_gather(kappa2, ('gx', 'gz'), axis=0, tiled=False)  10.3 us
    pallas_call x1, Pallas kernels, body(): pl.pallas_call(functools.partial(first_kernel, grid), out_shape=(rows_of(...  9.86 us
    ppermute x3, starting transfers between devices, body(): lax.ppermute(moments, 'gy', [(i, (i + step) % ny) for i in range(ny)])  5.63 us
    pallas_call x1, Pallas kernels, body(): pl.pallas_call(functools.partial(middle_kernel, grid), out_shape=(rows_of...  4.33 us
  transfers between devices with their start and end apart: 8, of which 5 were waited for; matrix products, arithmetic and copies ran while one was open for 2% of the time, Pallas kernels for 3%

profile of v2, /device:TPU:0, one launch (start us, length us, event | category | flops | bytes accessed | tf_op | source)
XLA Modules:
  0.0 131.5 jit_solution(16977222656549047277)
XLA Ops:
  6.5 0.7 all-gather.3.cloned.1.call-update
  7.3 21.1 %all_to_all.10 = f32[8,8,16,256]{3,2,1,0:T(8,128)} all-to-all(f32[8,8,16,256]{3,2,1,0:T(8,128)} %param.3), channel_id=1, replica_groups=mesh['gx'=4,'gy'=4,'gz'=2] {'gx','gz'}, dimensions={0} | all-to-all | bytes 2097152 | tf_op jit(solution)/shard_map/all_to_all | solution.py:429
  28.4 10.3 %all-gather.3.cloned.1.call-done = f32[64,16,256]{2,1,0:T(8,128)} async-done(((f32[8,16,256]{2,1,0:T(8,128)}), f32[64,16,256]{2,1,0:T(8,128)}) %all-gather.3.cloned.1.call-update) | async-done | bytes 1048592 | tf_op jit(solution)/shard_map/all_gather | solution.py:427
  38.7 3.7 %assemble.1 = (f32[4,16,32,128]{3,2,1,0:T(8,128)}, f32[4,16,32,128]{3,2,1,0:T(8,128)}, f32[4,9,32,128]{3,2,1,0:T(8,128)}, f32[4,9,32,128]{3,2,1,0:T(8,128)}) custom-call(f32[1024,256]{1,0:T(8,128)} %bitcast.5, f32[1024,256]{1,0:T(8,128)} %bitcast.7), custom_call_target="tpu_custom_call" | custom-call | tf_op jit(solution)/shard_map/assemble/pallas_call | solution.py:430
  42.3 3.4 %collective-permute-start = (f32[4,9,32,128]{3,2,1,0:T(8,128)}, f32[4,9,32,128]{3,2,1,0:T(8,128)S(1)}, u32[]{:S(2)}, u32[]{:S(2)}) collective-permute-start(f32[4,9,32,128]{3,2,1,0:T(8,128)} %get-tuple-element.19), channel_id=1, source_target_pairs={{0,2},{2,4},{4,6},{1,3},{3,5},{5,7},{8,10},{10,12},{12,14},{9,11},... | collective-permute-start | bytes 1769480 | tf_op jit(solution)/shard_map/ppermute | solution.py:441
  45.8 1.3 collective-permute-start.1
  47.6 11.4 %collective-permute-done.low_in.low1_in = f32[4,9,32,128]{3,2,1,0:T(8,128)S(1)} collective-permute-done((f32[4,9,32,128]{3,2,1,0:T(8,128)}, f32[4,9,32,128]{3,2,1,0:T(8,128)S(1)}, u32[]{:S(2)}, u32[]{:S(2)}) %collective-permute-start) | collective-permute-done | bytes 589856 | tf_op jit(solution)/shard_map/ppermute | solution.py:441
  59.0 4.0 %collective-permute-done.1.high_in.high1_in = f32[4,9,32,128]{3,2,1,0:T(8,128)S(1)} collective-permute-done((f32[4,9,32,128]{3,2,1,0:T(8,128)}, f32[4,9,32,128]{3,2,1,0:T(8,128)S(1)}, u32[]{:S(2)}, u32[]{:S(2)}) %collective-permute-start.1) | collective-permute-done | bytes 589856 | tf_op jit(solution)/shard_map/ppermute | solution.py:442
  63.1 0.8 copy-done.2
  63.9 9.9 %first_steps.1 = (f32[4,16,32,128]{3,2,1,0:T(8,128)}, f32[4,16,32,128]{3,2,1,0:T(8,128)}, f32[4,16,32,128]{3,2,1,0:T(8,128)}, f32[4,18,32,128]{3,2,1,0:T(8,128)}...) custom-call(s32[2]{0:T(128)} %add_convert_fusion.ends_ref, f32[4,16,32,128]{3,2,1,0:T(8,128)} %get-tuple-element.17.own_in.c0_in, ...), custom_call_target="tpu_custom_call" | custom-call | tf_op jit(solution)/shard_map/first_steps/pallas_call | solution.py:445
  73.8 3.4 %collective-permute-start.5 = (f32[4,5,32,128]{3,2,1,0:T(8,128)}, f32[4,5,32,128]{3,2,1,0:T(8,128)S(1)}, u32[]{:S(2)}, u32[]{:S(2)}) collective-permute-start(f32[4,5,32,128]{3,2,1,0:T(8,128)} %get-tuple-element.27), channel_id=1, source_target_pairs={{0,2},{2,4},{4,6},{1,3},{3,5},{5,7},{8,10},{10,12},{12,14},{9,11},... | collective-permute-start | bytes 983048 | tf_op jit(solution)/shard_map/ppermute | solution.py:455
  77.1 1.3 collective-permute-start.6
  78.4 4.3 %middle_step.1 = (f32[4,16,32,128]{3,2,1,0:T(8,128)}, f32[6,8,128]{2,1,0:T(8,128)}) custom-call(f32[4,16,32,128]{3,2,1,0:T(8,128)} %get-tuple-element.17.own_in.c0_in, f32[4,16,32,128]{3,2,1,0:T(8,128)} %get-tuple-element.21.c1_in, f32[4,18,32,128]{3,2,1,0:T(8,128)} %get-tuple-element.22.c2_in, f32[4,16,32,128]{3,2,1,0:T(8,128)} %get-tuple-element.18.diagonal_in), custom_call_target="tpu_custom_call" | custom-call | flops 10485760 | bytes 6291456 | tf_op jit(solution)/shard_map/middle_step/pallas_call | solution.py:458
  82.8 3.1 %collective-permute-start.4 = (f32[6,8,128]{2,1,0:T(8,128)}, f32[6,8,128]{2,1,0:T(8,128)S(1)}, u32[]{:S(2)}, u32[]{:S(2)}) collective-permute-start(f32[6,8,128]{2,1,0:T(8,128)} %get-tuple-element.23), channel_id=1, source_target_pairs={{0,6},{2,0},{4,2},{6,4},{1,7},{3,1},{5,3},{7,5},{8,14},{10,8},{12,... | collective-permute-start | bytes 73736 | tf_op jit(solution)/shard_map/ppermute | solution.py:473
  85.9 1.1 collective-permute-start.3
  86.9 1.5 %collective-permute-start.2 = (f32[6,8,128]{2,1,0:T(8,128)}, f32[6,8,128]{2,1,0:T(8,128)S(1)}, u32[]{:S(2)}, u32[]{:S(2)}) collective-permute-start(f32[6,8,128]{2,1,0:T(8,128)} %get-tuple-element.23), channel_id=1, source_target_pairs={{0,2},{2,4},{4,6},{6,0},{1,3},{3,5},{5,7},{7,1},{8,10},{10,12},{12... | collective-permute-start | bytes 73736 | tf_op jit(solution)/shard_map/ppermute | solution.py:473
  88.4 0.7 dynamic-slice_reduce_fusion.weights_ref
  89.1 1.7 %collective-permute-done.3 = f32[6,8,128]{2,1,0:T(8,128)S(1)} collective-permute-done((f32[6,8,128]{2,1,0:T(8,128)}, f32[6,8,128]{2,1,0:T(8,128)S(1)}, u32[]{:S(2)}, u32[]{:S(2)}) %collective-permute-start.3) | collective-permute-done | bytes 24608 | tf_op jit(solution)/shard_map/ppermute | solution.py:473
  90.8 2.0 %collective-permute-done.2 = f32[6,8,128]{2,1,0:T(8,128)S(1)} collective-permute-done((f32[6,8,128]{2,1,0:T(8,128)}, f32[6,8,128]{2,1,0:T(8,128)S(1)}, u32[]{:S(2)}, u32[]{:S(2)}) %collective-permute-start.2) | collective-permute-done | bytes 24608 | tf_op jit(solution)/shard_map/ppermute | solution.py:473
  92.8 1.4 %pad_maximum_fusion.moments_ref = f32[24,8,128]{2,1,0:T(8,128)} fusion(f32[6,8,128]{2,1,0:T(8,128)S(1)} %collective-permute-done.4, f32[6,8,128]{2,1,0:T(8,128)S(1)} %collective-permute-done.3, f32[6,8,128]{2,1,0:T(8,128)S(1)} %collective-permute-done.2, f32[6,8,128]{2,1,0:T(8,128)} %get-tuple-element.23), kind=kLoop, calls=%fused_computation | loop fusion | flops 73728 | bytes 196608 | tf_op jit(solution)/shard_map/concatenate | solution.py:474
  94.2 0.7 copy-done.3
  95.0 11.0 %last_steps.1 = f32[1024,256]{1,0:T(8,128)} custom-call(s32[2]{0:T(128)} %add_convert_fusion.ends_ref, f32[5]{0:T(128)} %dynamic-slice_reduce_fusion.weights_ref, f32[24,8,128]{2,1,0:T(8,128)} %pad_maximum_fusion.moments_ref, f32[4,16,32,128]{3,2,1,0:T(8,128)} %get-tuple-element.17.own_in.c0_in, f32[4,16,32,128]{3,2,1,0:T(8,128)} %get-tuple-element.24.d0_in, ...), custom_call_target="tpu_custom_call" | custom-call | tf_op jit(solution)/shard_map/last_steps/pallas_call | solution.py:478
  106.0 17.9 %all_to_all.11 = f32[8,8,16,256]{3,2,1,0:T(8,128)S(1)} all-to-all(f32[8,8,16,256]{3,2,1,0:T(8,128)} %bitcast.6), channel_id=1, replica_groups=mesh['gx'=4,'gy'=4,'gz'=2] {'gx','gz'}, dimensions={0} | all-to-all | bytes 2097152 | tf_op jit(solution)/shard_map/all_to_all | solution.py:491
  123.9 0.7 reduce_sum.9
  (13 shorter events, 0.7 us)
Async XLA Ops:
  6.5 81.9 %copy-start = (f32[5,8]{1,0:T(8,128)S(1)}, f32[5,8]{1,0:T(8,128)}, u32[]{:S(2)}) copy-start(f32[5,8]{1,0:T(8,128)} %param.5) | copy-start | bytes 484
  6.5 32.1 %all-gather.3.cloned.1.call-start = ((), (), s32[]{:S(2)}) async-start(), calls=%async_computation.2 | async-start | bytes 1179648 | tf_op jit(solution)/shard_map/all_gather | solution.py:427
  42.3 16.7 %collective-permute-start = (f32[4,9,32,128]{3,2,1,0:T(8,128)}, f32[4,9,32,128]{3,2,1,0:T(8,128)S(1)}, u32[]{:S(2)}, u32[]{:S(2)}) collective-permute-start(f32[4,9,32,128]{3,2,1,0:T(8,128)} %get-tuple-element.19), channel_id=1, source_target_pairs={{0,2},{2,4},{4,6},{1,3},{3,5},{5,7},{8,10},{10,12},{12,14},{9,11},... | collective-permute-start | bytes 1769480 | tf_op jit(solution)/shard_map/ppermute | solution.py:441
  45.8 17.3 %collective-permute-start.1 = (f32[4,9,32,128]{3,2,1,0:T(8,128)}, f32[4,9,32,128]{3,2,1,0:T(8,128)S(1)}, u32[]{:S(2)}, u32[]{:S(2)}) collective-permute-start(f32[4,9,32,128]{3,2,1,0:T(8,128)} %get-tuple-element.20), channel_id=1, source_target_pairs={{2,0},{4,2},{6,4},{3,1},{5,3},{7,5},{10,8},{12,10},{14,12},{11,9},... | collective-permute-start | bytes 1769480 | tf_op jit(solution)/shard_map/ppermute | solution.py:442
  59.0 4.0 %copy-start.1 = (f32[4,9,32,128]{3,2,1,0:T(8,128)}, f32[4,9,32,128]{3,2,1,0:T(8,128)S(1)}, u32[]{:S(2)}) copy-start(f32[4,9,32,128]{3,2,1,0:T(8,128)S(1)} %collective-permute-done.low_in.low1_in) | copy-start | bytes 1769476
  63.1 0.8 copy-start.2
  73.8 20.4 %collective-permute-start.5 = (f32[4,5,32,128]{3,2,1,0:T(8,128)}, f32[4,5,32,128]{3,2,1,0:T(8,128)S(1)}, u32[]{:S(2)}, u32[]{:S(2)}) collective-permute-start(f32[4,5,32,128]{3,2,1,0:T(8,128)} %get-tuple-element.27), channel_id=1, source_target_pairs={{0,2},{2,4},{4,6},{1,3},{3,5},{5,7},{8,10},{10,12},{12,14},{9,11},... | collective-permute-start | bytes 983048 | tf_op jit(solution)/shard_map/ppermute | solution.py:455
  77.1 17.0 %collective-permute-start.6 = (f32[4,5,32,128]{3,2,1,0:T(8,128)}, f32[4,5,32,128]{3,2,1,0:T(8,128)S(1)}, u32[]{:S(2)}, u32[]{:S(2)}) collective-permute-start(f32[4,5,32,128]{3,2,1,0:T(8,128)} %get-tuple-element.28), channel_id=1, source_target_pairs={{2,0},{4,2},{6,4},{3,1},{5,3},{7,5},{10,8},{12,10},{14,12},{11,9},... | collective-permute-start | bytes 983048 | tf_op jit(solution)/shard_map/ppermute | solution.py:456
  82.8 6.3 %collective-permute-start.4 = (f32[6,8,128]{2,1,0:T(8,128)}, f32[6,8,128]{2,1,0:T(8,128)S(1)}, u32[]{:S(2)}, u32[]{:S(2)}) collective-permute-start(f32[6,8,128]{2,1,0:T(8,128)} %get-tuple-element.23), channel_id=1, source_target_pairs={{0,6},{2,0},{4,2},{6,4},{1,7},{3,1},{5,3},{7,5},{8,14},{10,8},{12,... | collective-permute-start | bytes 73736 | tf_op jit(solution)/shard_map/ppermute | solution.py:473
  85.9 4.9 %collective-permute-start.3 = (f32[6,8,128]{2,1,0:T(8,128)}, f32[6,8,128]{2,1,0:T(8,128)S(1)}, u32[]{:S(2)}, u32[]{:S(2)}) collective-permute-start(f32[6,8,128]{2,1,0:T(8,128)} %get-tuple-element.23), channel_id=1, source_target_pairs={{0,4},{2,6},{4,0},{6,2},{1,5},{3,7},{5,1},{7,3},{8,12},{10,14},{12... | collective-permute-start | bytes 73736 | tf_op jit(solution)/shard_map/ppermute | solution.py:473
  86.9 5.8 %collective-permute-start.2 = (f32[6,8,128]{2,1,0:T(8,128)}, f32[6,8,128]{2,1,0:T(8,128)S(1)}, u32[]{:S(2)}, u32[]{:S(2)}) collective-permute-start(f32[6,8,128]{2,1,0:T(8,128)} %get-tuple-element.23), channel_id=1, source_target_pairs={{0,2},{2,4},{4,6},{6,0},{1,3},{3,5},{5,7},{7,1},{8,10},{10,12},{12... | collective-permute-start | bytes 73736 | tf_op jit(solution)/shard_map/ppermute | solution.py:473
  94.2 0.7 copy-start.3
  94.2 0.8 copy-start.4
Sparse Core Ops, SparseCore 0:
  9.2 29.3 all-gather.2

commit v3 on v2

--- a/solution.py
+++ b/solution.py
@@ -109,6 +109,7 @@
     masks = lane_masks()
 
     def body(step, carry):
+        results = []
         for offset in range(unroll):
             row = (step * unroll, first + offset)
             for x in range(0, source.cells, 8):
@@ -116,7 +117,9 @@
                 for c, value in enumerate(values):
                     if minus is not None:
                         value = value - SHIFT * minus.load(c, row, x)
-                    target.store(c, row, x, value)
+                    results.append((c, row, x, value))
+        for result in results:
+            target.store(*result)
         return carry
 
     assert count % unroll == 0
@@ -166,33 +169,30 @@
 
 
 def assemble_kernel(
-    grid, blocks_ref, kappa_ref,
-    own_ref, diagonal_ref, up_ref, down_ref,
-    block_columns, kappa_columns, block_sem, kappa_sem,
+    grid, blocks_ref, own_ref, diagonal_ref, up_ref, down_ref, block_columns, block_sem,
 ):
     nx, nz, bx, by, bz = grid
     copies = column_copies(blocks_ref, block_columns, block_sem, True)
-    copies += column_copies(kappa_ref, kappa_columns, kappa_sem, True)
     for copy in copies:
         copy.start()
     for copy in copies:
         copy.wait()
     for x, z, s, column in places(grid):
         xs = pl.ds(x, bx)
+        start = 2 * s * bx * by
+        rows = [pl.ds(start + y, bx, stride=by) for y in range(by)]
+        probe = [block_columns[column, at, :] for at in rows]
+        rows = [pl.ds(start + bx * by + y, bx, stride=by) for y in range(by)]
+        kappa = [6.0 + block_columns[column, at, :] for at in rows]
         for y in range(by):
-            rows = pl.ds(s * bx * by + y, bx, stride=by)
-            value = block_columns[column, rows, :]
-            own_ref[z, y, xs, :] = value
-            if y < HALO:
-                down_ref[z, y, xs, :] = value
-            if y >= by - HALO:
-                up_ref[z, y - (by - HALO), xs, :] = value
-            value = 6.0 + kappa_columns[column, rows, :]
-            diagonal_ref[z, y, xs, :] = value
-            if y < DIAGONAL_HALO:
-                down_ref[z, HALO + y, xs, :] = value
-            if y >= by - DIAGONAL_HALO:
-                up_ref[z, HALO + y - (by - DIAGONAL_HALO), xs, :] = value
+            own_ref[z, y, xs, :] = probe[y]
+            diagonal_ref[z, y, xs, :] = kappa[y]
+        for y in range(HALO):
+            down_ref[z, y, xs, :] = probe[y]
+            up_ref[z, y, xs, :] = probe[by - HALO + y]
+        for y in range(DIAGONAL_HALO):
+            down_ref[z, HALO + y, xs, :] = kappa[y]
+            up_ref[z, HALO + y, xs, :] = kappa[by - DIAGONAL_HALO + y]
 
 
 def halo_pairs(field, own, low_ref, high_ref, start, halo):
@@ -353,6 +353,7 @@
 
     def out_row(step, carry):
         row = (step, 0)
+        results = []
         for x in range(0, c4.cells, 8):
             last = stencil_tiles(c4, diagonal, row, x, masks)
             for z in range(c4.columns):
@@ -367,7 +368,9 @@
                     term = cs[i] * inner
                     total = term if total is None else total + term
                 s, column = place[x, z]
-                columns_ref[column, pl.ds(s * bx * by + step, bx, stride=by), :] = total
+                results.append((column, s, total))
+        for column, s, total in results:
+            columns_ref[column, pl.ds(s * bx * by + step, bx, stride=by), :] = total
         return carry
 
     lax.fori_loop(0, by, out_row, 0)
@@ -424,20 +427,21 @@
 
     dma = pltpu.SemaphoreType.DMA
 
-    kappa = lax.all_gather(kappa2, ("gx", "gz"), axis=0, tiled=False)
     blocks = jnp.concatenate([probes] * copies, axis=0) if copies > 1 else probes
+    kappa = jnp.broadcast_to(kappa2[None], blocks.shape)
+    blocks = jnp.concatenate([blocks, kappa], axis=1)
     blocks = lax.all_to_all(blocks, ("gx", "gz"), 0, 0, tiled=True)
     c0, diagonal, up_edge, down_edge = pl.pallas_call(
         functools.partial(assemble_kernel, grid),
         out_shape=(
             rows_of(by), rows_of(by), rows_of(HALO + DIAGONAL_HALO), rows_of(HALO + DIAGONAL_HALO)
         ),
-        in_specs=[anywhere(), anywhere()],
+        in_specs=[anywhere()],
         out_specs=(vmem(),) * 4,
-        scratch_shapes=[block_scratch(), block_scratch(), dma((per,)), dma((per,))],
+        scratch_shapes=[pltpu.VMEM((per, 2 * group * bx * by, 128), jnp.float32), dma((per,))],
         compiler_params=params(),
         name="assemble",
-    )(blocks.reshape(group * bx * by, bz), kappa.reshape(group * bx * by, bz))
+    )(blocks.reshape(2 * group * bx * by, bz))
     low1 = lax.ppermute(up_edge, "gy", up)
     high1 = lax.ppermute(down_edge, "gy", down)
 

time: 132 us -> 120 us (0.909)
  between operations: 13.5 us -> 0.11 us
  waiting for transfers between devices: 30.1 us -> 19 us
  blocking collectives: 39.1 us -> 48.7 us
  other arithmetic: 2.7 us -> 4.23 us
    all_gather x1 -> x0, waiting for transfers between devices: 10.3 us -> none  [body(): kappa = lax.all_gather(kappa2, ('gx', 'gz'), axis=0, tiled=False)]
    all_to_all x1, blocking collectives: 21.1 us -> 30.8 us  [body(): blocks = lax.all_to_all(blocks, ('gx', 'gz'), 0, 0, tiled=True)]
    concatenate x0 -> x1, other arithmetic: none -> 1.47 us  [body(): blocks = jnp.concatenate([blocks, kappa], axis=1)]
  transfers between devices with their start and end apart: 8 -> 7, of which waited for: 5 -> 4; matrix products, arithmetic and copies ran while one was open for 2% -> 2% of each run, Pallas kernels for 3% -> 4%
where the time goes in v3:
time: 120 us
  blocking collectives  48.7 us (41%)
  Pallas kernels  29 us (24%)
  waiting for transfers between devices  19 us (16%)
  starting transfers between devices  15.3 us (13%)
  other arithmetic  4.23 us (4%)
  local copies, waits for them, and re-layouts  3.41 us (3%)
    all_to_all x1, blocking collectives, body(): blocks = lax.all_to_all(blocks, ('gx', 'gz'), 0, 0, tiled=True)  30.8 us
    all_to_all x1, blocking collectives, body(): lax.all_to_all(out.reshape(group, bx, by, bz), ('gx', 'gz'), 0, 0, tiled=...  17.9 us
    ppermute x1, waiting for transfers between devices, body(): low1 = lax.ppermute(up_edge, 'gy', up)  11.4 us
    pallas_call x1, Pallas kernels, body(): pl.pallas_call(functools.partial(last_kernel, grid, inverse_count, ny), o...  11.1 us
    pallas_call x1, Pallas kernels, body(): pl.pallas_call(functools.partial(first_kernel, grid), out_shape=(rows_of(...  9.88 us
    ppermute x3, starting transfers between devices, body(): lax.ppermute(moments, 'gy', [(i, (i + step) % ny) for i in range(ny)])  5.72 us
    pallas_call x1, Pallas kernels, body(): pl.pallas_call(functools.partial(middle_kernel, grid), out_shape=(rows_of...  4.35 us
    ppermute x1, waiting for transfers between devices, body(): high1 = lax.ppermute(down_edge, 'gy', down)  4.04 us
  transfers between devices with their start and end apart: 7, of which 4 were waited for; matrix products, arithmetic and copies ran while one was open for 2% of the time, Pallas kernels for 4%

profile of v3, /device:TPU:0, one launch (start us, length us, event | category | flops | bytes accessed | tf_op | source)
XLA Modules:
  0.0 119.7 jit_solution(1228350801763905081)
XLA Ops:
  0.0 1.0 broadcast_in_dim.2
  1.0 1.5 %pad_maximum_fusion = f32[8,16,16,256]{3,2,1,0:T(8,128)S(1)} fusion(f32[8,8,16,256]{3,2,1,0:T(8,128)S(1)} %broadcast_in_dim.2, f32[8,8,16,256]{3,2,1,0:T(8,128)} %param.3), kind=kLoop, calls=%fused_computation | loop fusion | flops 524288 | bytes 4194304 | tf_op jit(solution)/shard_map/concatenate | solution.py:432
  2.5 30.8 %all_to_all.10 = f32[8,16,16,256]{3,2,1,0:T(8,128)} all-to-all(f32[8,16,16,256]{3,2,1,0:T(8,128)S(1)} %pad_maximum_fusion), channel_id=1, replica_groups=mesh['gx'=4,'gy'=4,'gz'=2] {'gx','gz'}, dimensions={0} | all-to-all | bytes 4194304 | tf_op jit(solution)/shard_map/all_to_all | solution.py:433
  33.3 3.6 %assemble.1 = (f32[4,16,32,128]{3,2,1,0:T(8,128)}, f32[4,16,32,128]{3,2,1,0:T(8,128)}, f32[4,9,32,128]{3,2,1,0:T(8,128)}, f32[4,9,32,128]{3,2,1,0:T(8,128)}) custom-call(f32[2048,256]{1,0:T(8,128)} %bitcast.4), custom_call_target="tpu_custom_call" | custom-call | tf_op jit(solution)/shard_map/assemble/pallas_call | solution.py:434
  36.9 3.5 %collective-permute-start = (f32[4,9,32,128]{3,2,1,0:T(8,128)}, f32[4,9,32,128]{3,2,1,0:T(8,128)S(1)}, u32[]{:S(2)}, u32[]{:S(2)}) collective-permute-start(f32[4,9,32,128]{3,2,1,0:T(8,128)} %get-tuple-element.19), channel_id=1, source_target_pairs={{0,2},{2,4},{4,6},{1,3},{3,5},{5,7},{8,10},{10,12},{12,14},{9,11},... | collective-permute-start | bytes 1769480 | tf_op jit(solution)/shard_map/ppermute | solution.py:445
  40.5 1.3 %collective-permute-start.1 = (f32[4,9,32,128]{3,2,1,0:T(8,128)}, f32[4,9,32,128]{3,2,1,0:T(8,128)S(1)}, u32[]{:S(2)}, u32[]{:S(2)}) collective-permute-start(f32[4,9,32,128]{3,2,1,0:T(8,128)} %get-tuple-element.20), channel_id=1, source_target_pairs={{2,0},{4,2},{6,4},{3,1},{5,3},{7,5},{10,8},{12,10},{14,12},{11,9},... | collective-permute-start | bytes 1769480 | tf_op jit(solution)/shard_map/ppermute | solution.py:446
  42.4 11.4 %collective-permute-done.low_in.low1_in = f32[4,9,32,128]{3,2,1,0:T(8,128)S(1)} collective-permute-done((f32[4,9,32,128]{3,2,1,0:T(8,128)}, f32[4,9,32,128]{3,2,1,0:T(8,128)S(1)}, u32[]{:S(2)}, u32[]{:S(2)}) %collective-permute-start) | collective-permute-done | bytes 589856 | tf_op jit(solution)/shard_map/ppermute | solution.py:445
  53.8 4.0 %collective-permute-done.1.high_in.high1_in = f32[4,9,32,128]{3,2,1,0:T(8,128)S(1)} collective-permute-done((f32[4,9,32,128]{3,2,1,0:T(8,128)}, f32[4,9,32,128]{3,2,1,0:T(8,128)S(1)}, u32[]{:S(2)}, u32[]{:S(2)}) %collective-permute-start.1) | collective-permute-done | bytes 589856 | tf_op jit(solution)/shard_map/ppermute | solution.py:446
  57.9 0.8 copy-done.2
  58.7 9.9 %first_steps.1 = (f32[4,16,32,128]{3,2,1,0:T(8,128)}, f32[4,16,32,128]{3,2,1,0:T(8,128)}, f32[4,16,32,128]{3,2,1,0:T(8,128)}, f32[4,18,32,128]{3,2,1,0:T(8,128)}...) custom-call(s32[2]{0:T(128)} %add_convert_fusion.ends_ref, f32[4,16,32,128]{3,2,1,0:T(8,128)} %get-tuple-element.17.own_in.c0_in, ...), custom_call_target="tpu_custom_call" | custom-call | tf_op jit(solution)/shard_map/first_steps/pallas_call | solution.py:449
  68.6 3.5 %collective-permute-start.5 = (f32[4,5,32,128]{3,2,1,0:T(8,128)}, f32[4,5,32,128]{3,2,1,0:T(8,128)S(1)}, u32[]{:S(2)}, u32[]{:S(2)}) collective-permute-start(f32[4,5,32,128]{3,2,1,0:T(8,128)} %get-tuple-element.27), channel_id=1, source_target_pairs={{0,2},{2,4},{4,6},{1,3},{3,5},{5,7},{8,10},{10,12},{12,14},{9,11},... | collective-permute-start | bytes 983048 | tf_op jit(solution)/shard_map/ppermute | solution.py:459
  72.1 1.3 %collective-permute-start.6 = (f32[4,5,32,128]{3,2,1,0:T(8,128)}, f32[4,5,32,128]{3,2,1,0:T(8,128)S(1)}, u32[]{:S(2)}, u32[]{:S(2)}) collective-permute-start(f32[4,5,32,128]{3,2,1,0:T(8,128)} %get-tuple-element.28), channel_id=1, source_target_pairs={{2,0},{4,2},{6,4},{3,1},{5,3},{7,5},{10,8},{12,10},{14,12},{11,9},... | collective-permute-start | bytes 983048 | tf_op jit(solution)/shard_map/ppermute | solution.py:460
  73.4 4.4 %middle_step.1 = (f32[4,16,32,128]{3,2,1,0:T(8,128)}, f32[6,8,128]{2,1,0:T(8,128)}) custom-call(f32[4,16,32,128]{3,2,1,0:T(8,128)} %get-tuple-element.17.own_in.c0_in, f32[4,16,32,128]{3,2,1,0:T(8,128)} %get-tuple-element.21.c1_in, f32[4,18,32,128]{3,2,1,0:T(8,128)} %get-tuple-element.22.c2_in, f32[4,16,32,128]{3,2,1,0:T(8,128)} %get-tuple-element.18.diagonal_in), custom_call_target="tpu_custom_call" | custom-call | flops 10485760 | bytes 6291456 | tf_op jit(solution)/shard_map/middle_step/pallas_call | solution.py:462
  77.7 3.2 %collective-permute-start.4 = (f32[6,8,128]{2,1,0:T(8,128)}, f32[6,8,128]{2,1,0:T(8,128)S(1)}, u32[]{:S(2)}, u32[]{:S(2)}) collective-permute-start(f32[6,8,128]{2,1,0:T(8,128)} %get-tuple-element.23), channel_id=1, source_target_pairs={{0,6},{2,0},{4,2},{6,4},{1,7},{3,1},{5,3},{7,5},{8,14},{10,8},{12,... | collective-permute-start | bytes 73736 | tf_op jit(solution)/shard_map/ppermute | solution.py:477
  80.9 1.0 collective-permute-start.3
  81.9 1.6 %collective-permute-start.2 = (f32[6,8,128]{2,1,0:T(8,128)}, f32[6,8,128]{2,1,0:T(8,128)S(1)}, u32[]{:S(2)}, u32[]{:S(2)}) collective-permute-start(f32[6,8,128]{2,1,0:T(8,128)} %get-tuple-element.23), channel_id=1, source_target_pairs={{0,2},{2,4},{4,6},{6,0},{1,3},{3,5},{5,7},{7,1},{8,10},{10,12},{12... | collective-permute-start | bytes 73736 | tf_op jit(solution)/shard_map/ppermute | solution.py:477
  83.5 0.7 dynamic-slice_reduce_fusion.weights_ref
  84.2 1.6 %collective-permute-done.3 = f32[6,8,128]{2,1,0:T(8,128)S(1)} collective-permute-done((f32[6,8,128]{2,1,0:T(8,128)}, f32[6,8,128]{2,1,0:T(8,128)S(1)}, u32[]{:S(2)}, u32[]{:S(2)}) %collective-permute-start.3) | collective-permute-done | bytes 24608 | tf_op jit(solution)/shard_map/ppermute | solution.py:477
  85.8 1.9 %collective-permute-done.2 = f32[6,8,128]{2,1,0:T(8,128)S(1)} collective-permute-done((f32[6,8,128]{2,1,0:T(8,128)}, f32[6,8,128]{2,1,0:T(8,128)S(1)}, u32[]{:S(2)}, u32[]{:S(2)}) %collective-permute-start.2) | collective-permute-done | bytes 24608 | tf_op jit(solution)/shard_map/ppermute | solution.py:477
  87.7 1.4 %pad_maximum_fusion.1.moments_ref = f32[24,8,128]{2,1,0:T(8,128)} fusion(f32[6,8,128]{2,1,0:T(8,128)S(1)} %collective-permute-done.4, f32[6,8,128]{2,1,0:T(8,128)S(1)} %collective-permute-done.3, f32[6,8,128]{2,1,0:T(8,128)S(1)} %collective-permute-done.2, f32[6,8,128]{2,1,0:T(8,128)} %get-tuple-element.23), kind=kLoop, calls=%fused_computation.1 | loop fusion | flops 73728 | bytes 196608 | tf_op jit(solution)/shard_map/concatenate | solution.py:478
  89.1 0.7 copy-done.3
  89.9 11.1 %last_steps.1 = f32[1024,256]{1,0:T(8,128)} custom-call(s32[2]{0:T(128)} %add_convert_fusion.ends_ref, f32[5]{0:T(128)} %dynamic-slice_reduce_fusion.weights_ref, f32[24,8,128]{2,1,0:T(8,128)} %pad_maximum_fusion.1.moments_ref, f32[4,16,32,128]{3,2,1,0:T(8,128)} %get-tuple-element.17.own_in.c0_in, f32[4,16,32,128]{3,2,1,0:T(8,128)} %get-tuple-element.24.d0_in, ...), custom_call_target="tpu_custom_call" | custom-call | tf_op jit(solution)/shard_map/last_steps/pallas_call | solution.py:482
  101.0 17.9 %all_to_all.11 = f32[8,8,16,256]{3,2,1,0:T(8,128)S(1)} all-to-all(f32[8,8,16,256]{3,2,1,0:T(8,128)} %bitcast.5), channel_id=1, replica_groups=mesh['gx'=4,'gy'=4,'gz'=2] {'gx','gz'}, dimensions={0} | all-to-all | bytes 2097152 | tf_op jit(solution)/shard_map/all_to_all | solution.py:495
  119.0 0.7 reduce_sum.9
  (12 shorter events, 0.8 us)
Async XLA Ops:
  0.0 83.5 %copy-start = (f32[5,8]{1,0:T(8,128)S(1)}, f32[5,8]{1,0:T(8,128)}, u32[]{:S(2)}) copy-start(f32[5,8]{1,0:T(8,128)} %param.5) | copy-start | bytes 484
  36.9 16.9 %collective-permute-start = (f32[4,9,32,128]{3,2,1,0:T(8,128)}, f32[4,9,32,128]{3,2,1,0:T(8,128)S(1)}, u32[]{:S(2)}, u32[]{:S(2)}) collective-permute-start(f32[4,9,32,128]{3,2,1,0:T(8,128)} %get-tuple-element.19), channel_id=1, source_target_pairs={{0,2},{2,4},{4,6},{1,3},{3,5},{5,7},{8,10},{10,12},{12,14},{9,11},... | collective-permute-start | bytes 1769480 | tf_op jit(solution)/shard_map/ppermute | solution.py:445
  40.5 17.4 %collective-permute-start.1 = (f32[4,9,32,128]{3,2,1,0:T(8,128)}, f32[4,9,32,128]{3,2,1,0:T(8,128)S(1)}, u32[]{:S(2)}, u32[]{:S(2)}) collective-permute-start(f32[4,9,32,128]{3,2,1,0:T(8,128)} %get-tuple-element.20), channel_id=1, source_target_pairs={{2,0},{4,2},{6,4},{3,1},{5,3},{7,5},{10,8},{12,10},{14,12},{11,9},... | collective-permute-start | bytes 1769480 | tf_op jit(solution)/shard_map/ppermute | solution.py:446
  53.8 4.0 %copy-start.1 = (f32[4,9,32,128]{3,2,1,0:T(8,128)}, f32[4,9,32,128]{3,2,1,0:T(8,128)S(1)}, u32[]{:S(2)}) copy-start(f32[4,9,32,128]{3,2,1,0:T(8,128)S(1)} %collective-permute-done.low_in.low1_in) | copy-start | bytes 1769476
  57.9 0.8 copy-start.2
  68.6 20.5 %collective-permute-start.5 = (f32[4,5,32,128]{3,2,1,0:T(8,128)}, f32[4,5,32,128]{3,2,1,0:T(8,128)S(1)}, u32[]{:S(2)}, u32[]{:S(2)}) collective-permute-start(f32[4,5,32,128]{3,2,1,0:T(8,128)} %get-tuple-element.27), channel_id=1, source_target_pairs={{0,2},{2,4},{4,6},{1,3},{3,5},{5,7},{8,10},{10,12},{12,14},{9,11},... | collective-permute-start | bytes 983048 | tf_op jit(solution)/shard_map/ppermute | solution.py:459
  72.1 17.0 %collective-permute-start.6 = (f32[4,5,32,128]{3,2,1,0:T(8,128)}, f32[4,5,32,128]{3,2,1,0:T(8,128)S(1)}, u32[]{:S(2)}, u32[]{:S(2)}) collective-permute-start(f32[4,5,32,128]{3,2,1,0:T(8,128)} %get-tuple-element.28), channel_id=1, source_target_pairs={{2,0},{4,2},{6,4},{3,1},{5,3},{7,5},{10,8},{12,10},{14,12},{11,9},... | collective-permute-start | bytes 983048 | tf_op jit(solution)/shard_map/ppermute | solution.py:460
  77.7 6.5 %collective-permute-start.4 = (f32[6,8,128]{2,1,0:T(8,128)}, f32[6,8,128]{2,1,0:T(8,128)S(1)}, u32[]{:S(2)}, u32[]{:S(2)}) collective-permute-start(f32[6,8,128]{2,1,0:T(8,128)} %get-tuple-element.23), channel_id=1, source_target_pairs={{0,6},{2,0},{4,2},{6,4},{1,7},{3,1},{5,3},{7,5},{8,14},{10,8},{12,... | collective-permute-start | bytes 73736 | tf_op jit(solution)/shard_map/ppermute | solution.py:477
  80.9 4.9 %collective-permute-start.3 = (f32[6,8,128]{2,1,0:T(8,128)}, f32[6,8,128]{2,1,0:T(8,128)S(1)}, u32[]{:S(2)}, u32[]{:S(2)}) collective-permute-start(f32[6,8,128]{2,1,0:T(8,128)} %get-tuple-element.23), channel_id=1, source_target_pairs={{0,4},{2,6},{4,0},{6,2},{1,5},{3,7},{5,1},{7,3},{8,12},{10,14},{12... | collective-permute-start | bytes 73736 | tf_op jit(solution)/shard_map/ppermute | solution.py:477
  81.9 5.8 %collective-permute-start.2 = (f32[6,8,128]{2,1,0:T(8,128)}, f32[6,8,128]{2,1,0:T(8,128)S(1)}, u32[]{:S(2)}, u32[]{:S(2)}) collective-permute-start(f32[6,8,128]{2,1,0:T(8,128)} %get-tuple-element.23), channel_id=1, source_target_pairs={{0,2},{2,4},{4,6},{6,0},{1,3},{3,5},{5,7},{7,1},{8,10},{10,12},{12... | collective-permute-start | bytes 73736 | tf_op jit(solution)/shard_map/ppermute | solution.py:477
  89.1 0.7 copy-start.3
  89.1 0.8 copy-start.4

commit v4 on v3

v4 whole, which is shorter than its diff:
```python
import functools

import jax
import jax.numpy as jnp
from jax import lax
from jax.experimental import pallas as pl
from jax.experimental.pallas import tpu as pltpu
from jax.sharding import PartitionSpec as P

EPSILON = 1e-06
SHIFT = 64.0
HALO = 5
DIAGONAL_HALO = 4
PAD = 8
MIB = 1024 * 1024


def loss_of_moments(moments, weights):
    m0, m1, m2, m3, m4, m5 = moments
    norm = m0 + EPSILON
    alpha1 = (m1 + SHIFT * m0) / norm
    e1 = SHIFT - alpha1
    rest1 = jnp.maximum(m2 + 2.0 * e1 * m1 + e1 * e1 * m0, 0.0)
    beta1_square = rest1 / norm + EPSILON
    beta1 = jnp.sqrt(beta1_square)
    scale = 1.0 / (norm * beta1_square)
    alpha2 = scale * (m3 + 2.0 * e1 * m2 + e1 * e1 * m1 + SHIFT * rest1) - (m1 + e1 * m0) / norm
    e2 = SHIFT - alpha2
    f1 = e1 + e2
    f0 = e1 * e2 - beta1_square
    g = f1 * f1 + 2.0 * f0
    rest2 = jnp.maximum(m4 + 2.0 * f1 * m3 + g * m2 + 2.0 * f1 * f0 * m1 + f0 * f0 * m0, 0.0)
    beta2_square = scale * rest2 + EPSILON
    beta2 = jnp.sqrt(beta2_square)
    image2 = m5 + 2.0 * f1 * m4 + g * m3 + 2.0 * f1 * f0 * m2 + f0 * f0 * m1
    cross = m3 + f1 * m2 + f0 * m1 + e1 * (m2 + f1 * m1 + f0 * m0)
    alpha3 = scale * ((image2 + SHIFT * rest2) / beta2_square - cross)
    return (
        weights[0] * alpha1
        + weights[1] * alpha2
        + weights[2] * alpha3
        + weights[3] * beta1
        + weights[4] * beta2
    )


class Field:
    def __init__(self, ref, halo):
        self.ref = ref
        self.halo = halo
        self.columns, self.rows, self.pitch, _ = ref.shape
        self.cells = self.pitch - PAD
        self.flat = ref.reshape(self.columns * self.rows * self.pitch, 128)

    def at(self, column, row, x):
        moving, fixed = row
        start = (column * self.rows + fixed + self.halo) * self.pitch + x
        return pl.ds(moving * self.pitch + start, 8)

    def load(self, column, row, x):
        return self.flat[self.at(column, row, x), :]

    def store(self, column, row, x, value):
        self.flat[self.at(column, row, x), :] = value

    def part(self, first, count):
        return self.ref.at[:, pl.ds(first + self.halo, count), pl.ds(0, self.cells), :]

    def clear_pads(self):
        zero = jnp.zeros((8, 128), jnp.float32)

        def body(row, carry):
            for column in range(self.columns):
                self.store(column, (row, -self.halo), self.cells, zero)
            return carry

        lax.fori_loop(0, self.rows, body, 0)

    def clear_row(self, row):
        zero = jnp.zeros((8, 128), jnp.float32)
        for column in range(self.columns):
            for x in range(0, self.cells, 8):
                self.store(column, (0, row), x, zero)


def lane_masks():
    lane = lax.broadcasted_iota(jnp.int32, (8, 128), 1)
    return lane == 0, lane == 127


def stencil_tiles(source, diagonal, row, x, masks):
    columns = range(source.columns)
    moving, fixed = row
    centre = [source.load(c, row, x) for c in columns]
    after = [pltpu.roll(value, 1, 1) for value in centre]
    before = [pltpu.roll(value, 127, 1) for value in centre]
    results = []
    for c in columns:
        low = after[c - 1] if c else 0.0
        high = before[c + 1] if c + 1 < source.columns else 0.0
        total = jnp.where(masks[0], low, after[c]) + jnp.where(masks[1], high, before[c])
        total = total + (source.load(c, row, x - 1) + source.load(c, row, x + 1))
        total = total + (source.load(c, (moving, fixed - 1), x) + source.load(c, (moving, fixed + 1), x))
        results.append(diagonal.load(c, row, x) * centre[c] - total)
    return results


def apply_rows(target, source, diagonal, first, count, minus=None, unroll=2):
    masks = lane_masks()

    def body(step, carry):
        results = []
        for offset in range(unroll):
            row = (step * unroll, first + offset)
            for x in range(0, source.cells, 8):
                values = stencil_tiles(source, diagonal, row, x, masks)
                for c, value in enumerate(values):
                    if minus is not None:
                        value = value - SHIFT * minus.load(c, row, x)
                    results.append((c, row, x, value))
        for result in results:
            target.store(*result)
        return carry

    assert count % unroll == 0
    lax.fori_loop(0, count // unroll, body, 0)


def clear_outside(ends_ref, own, field):
    @pl.when(ends_ref[0] == 1)
    def _():
        field.clear_row(-1)

    @pl.when(ends_ref[1] == 1)
    def _():
        field.clear_row(own)


def apply_steps(ends_ref, own, target, source, diagonal, halo, minus=None):
    apply_rows(target, source, diagonal, -halo, own + 2 * halo, minus)
    if halo:
        clear_outside(ends_ref, own, target)


def places(grid):
    nx, nz, bx, by, bz = grid
    per = bz // 128
    for s in range(nx * nz):
        for column in range(per):
            yield s, column, (s // nz) * bx, (s % nz) * per + column


def pack_kernel(grid, count, probes_ref, kappa_ref, out_ref, sem):
    nx, nz, bx, by, bz = grid
    per = bz // 128
    rows = bx * by
    copies = []
    for s in range(nx * nz):
        parts = [
            probes_ref.at[pl.ds((s % count) * rows, rows), pl.ds(column * 128, 128)]
            for column in range(per)
        ]
        parts.append(kappa_ref.at[:, pl.ds((s // nz) % 2 * 128, 128)])
        for index, part in enumerate(parts):
            copies.append(pltpu.make_async_copy(part, out_ref.at[s, index], sem.at[s, index]))
    for copy in copies:
        copy.start()
    for copy in copies:
        copy.wait()


def probe_kernel(grid, blocks_ref, own_ref, up_ref, down_ref, half_ref):
    nx, nz, bx, by, bz = grid
    per = bz // 128
    own = Field(own_ref, HALO)
    own.clear_pads()
    for s, column, x, z in places(grid):
        values = [blocks_ref[s, column, pl.ds(y, bx, stride=by), :] for y in range(by)]
        for y in range(by):
            own.store(z, (0, y), x, values[y])
        for y in range(HALO):
            down_ref[z, y, pl.ds(x, bx), :] = values[y]
            up_ref[z, y, pl.ds(x, bx), :] = values[by - HALO + y]
    for s in range(nx * nz):
        half_ref[s] = blocks_ref[s, per]


def diagonal_kernel(grid, core_ref, half_ref, other_ref, own_ref, up_ref, down_ref):
    nx, nz, bx, by, bz = grid
    own = Field(own_ref, DIAGONAL_HALO)
    first = core_ref[0] == 0
    for s, column, x, z in places(grid):
        values = []
        for y in range(by):
            rows = pl.ds(y, bx, stride=by)
            mine, other = half_ref[s, rows, :], other_ref[s, rows, :]
            pair = (mine, other) if column == 0 else (other, mine)
            values.append(6.0 + jnp.where(first, *pair))
        for y in range(by):
            own.store(z, (0, y), x, values[y])
        for y in range(DIAGONAL_HALO):
            down_ref[z, y, pl.ds(x, bx), :] = values[y]
            up_ref[z, y, pl.ds(x, bx), :] = values[by - DIAGONAL_HALO + y]


def fill_halo(field, own, low_ref, high_ref):
    for c in range(field.columns):
        for y in range(field.halo):
            for x in range(0, field.cells, 8):
                field.store(c, (0, y - field.halo), x, low_ref[c, y, pl.ds(x, 8), :])
                field.store(c, (0, own + y), x, high_ref[c, y, pl.ds(x, 8), :])


def first_kernel(
    own,
    ends_ref, c0_in, diagonal_in, low_ref, high_ref, low_diagonal_ref, high_diagonal_ref,
    c0_ref, diagonal_ref, d0_ref, c1_ref, d1_ref, c2_ref, d2_ref, up_ref, down_ref, moments_ref,
):
    c0 = Field(c0_ref, HALO)
    diagonal = Field(diagonal_ref, DIAGONAL_HALO)
    d0 = Field(d0_ref, 4)
    c1 = Field(c1_ref, 3)
    d1 = Field(d1_ref, 2)
    c2 = Field(c2_ref, HALO)
    d2 = Field(d2_ref, 4)
    for field in (d0, c1, d1, c2, d2):
        field.clear_pads()
    fill_halo(c0, own, low_ref, high_ref)
    fill_halo(diagonal, own, low_diagonal_ref, high_diagonal_ref)
    steps = functools.partial(apply_steps, ends_ref, own)
    steps(d0, c0, diagonal, 4)
    steps(c1, d0, diagonal, 3, c0)
    steps(d1, c1, diagonal, 2)
    steps(c2, d1, diagonal, 1, c1)
    for c in range(c2.columns):
        for y in range(HALO):
            for x in range(0, c2.cells, 8):
                down_ref[c, y, pl.ds(x, 8), :] = c2.load(c, (0, y), x)
                up_ref[c, y, pl.ds(x, 8), :] = c2.load(c, (0, own - HALO + y), x)
    steps(d2, c2, diagonal, 0)

    def moment_row(step, sums):
        row = (step, 0)
        for x in range(0, c0.cells, 8):
            for c in range(c0.columns):
                a, b, e, d = (field.load(c, row, x) for field in (c0, c1, c2, d2))
                pairs = ((a, a), (a, b), (b, b), (b, e), (e, e), (d, d))
                sums = tuple(total + u * v for total, (u, v) in zip(sums, pairs))
        return sums

    zero = jnp.zeros((8, 128), jnp.float32)
    sums = lax.fori_loop(0, own, moment_row, (zero,) * 6)
    for index, total in enumerate(sums):
        for part in range(moments_ref.shape[0]):
            moments_ref[part, index] = total


def moment_slopes(inverse_count, probe, weights_ref, moments_ref):
    raw = []
    for k in range(6):
        total = moments_ref[0, k]
        for part in range(1, moments_ref.shape[0]):
            total = total + moments_ref[part, k]
        total = jnp.sum(jnp.sum(total, axis=0, keepdims=True), axis=1, keepdims=True)
        raw.append(jnp.broadcast_to(total * inverse_count, (8, 128)))
    moments = tuple(raw[:5]) + (raw[5] - SHIFT * raw[4],)
    weights = [weights_ref[k, probe] for k in range(5)]
    value, pullback = jax.vjp(lambda m: loss_of_moments(m, weights), moments)
    (slopes,) = pullback(jnp.full((8, 128), 2.0, jnp.float32))
    return [slope[0, 0] for slope in slopes]


def last_kernel(
    grid, inverse_count,
    ends_ref, weights_ref, moments_ref, c0_ref, diagonal_ref, d0_ref, c1_ref, d1_ref,
    c2_in, d2_in, low_ref, high_ref,
    c2_ref, d2_ref, out_ref, c3_ref, d3_ref, c4_ref,
):
    nx, nz, bx, by, bz = grid
    c0 = Field(c0_ref, HALO)
    diagonal = Field(diagonal_ref, DIAGONAL_HALO)
    d0 = Field(d0_ref, 4)
    c1 = Field(c1_ref, 3)
    d1 = Field(d1_ref, 2)
    c2 = Field(c2_ref, HALO)
    d2 = Field(d2_ref, 4)
    c3 = Field(c3_ref, 3)
    d3 = Field(d3_ref, 2)
    c4 = Field(c4_ref, 1)
    for field in (c3, d3, c4):
        field.clear_pads()
    slopes = moment_slopes(inverse_count, ends_ref[2], weights_ref, moments_ref)
    fill_halo(c2, by, low_ref, high_ref)
    apply_rows(d2, c2, diagonal, -4, 4)
    apply_rows(d2, c2, diagonal, by, 4)
    clear_outside(ends_ref, by, d2)
    steps = functools.partial(apply_steps, ends_ref, by)
    steps(c3, d2, diagonal, 3, c2)
    steps(d3, c3, diagonal, 2)
    steps(c4, d3, diagonal, 1, c3)
    masks = lane_masks()
    place = {(x, z): (s, column) for s, column, x, z in places(grid)}

    def out_row(step, carry):
        row = (step, 0)
        results = []
        for x in range(0, c4.cells, 8):
            last = stencil_tiles(c4, diagonal, row, x, masks)
            for z in range(c4.columns):
                cs = [field.load(z, row, x) for field in (c0, c1, c2, c3, c4)]
                ds = [field.load(z, row, x) for field in (d0, d1, d2, d3)] + [last[z]]
                total = None
                for i in range(5):
                    inner = None
                    for j in range(5 - i):
                        term = slopes[i + j + 1] * ds[j]
                        inner = term if inner is None else inner + term
                    term = cs[i] * inner
                    total = term if total is None else total + term
                results.append(place[x, z] + (total,))
        for s, column, total in results:
            out_ref[s, column, pl.ds(step, bx, stride=by), :] = total
        return carry

    lax.fori_loop(0, by, out_row, 0)


def sum_kernel(grid, count, parts_ref, out_ref):
    nx, nz, bx, by, bz = grid
    for column in range(bz // 128):
        for x in range(bx):
            total = None
            for p in range(count):
                part = parts_ref[p, column, pl.ds(x * by, by), :]
                total = part if total is None else total + part
            out_ref[x, :, pl.ds(column * 128, 128)] = total


def vmem():
    return pl.BlockSpec(memory_space=pltpu.VMEM)


def smem():
    return pl.BlockSpec(memory_space=pltpu.SMEM)


def anywhere():
    return pl.BlockSpec(memory_space=pl.ANY)


def f32(*shape):
    return jax.ShapeDtypeStruct(shape, jnp.float32)


def params():
    return pltpu.CompilerParams(vmem_limit_bytes=32 * MIB)


def body(probes, kappa2, cotangents):
    nx, ny, nz = (lax.axis_size(axis) for axis in ("gx", "gy", "gz"))
    count, bx, by, bz = probes.shape
    group = nx * nz
    assert group % count == 0 and nx % 2 == 0 and bx == 8 and bz == 256
    assert by % 8 == 0 and by >= HALO
    X = nx * bx
    columns = nz * bz // 128
    per = bz // 128
    rows = bx * by
    grid = (nx, nz, bx, by, bz)
    gx, gy = lax.axis_index("gx"), lax.axis_index("gy")
    mine = (gx * nz + lax.axis_index("gz")) % count
    up = [(i, i + 1) for i in range(ny - 1)]
    down = [(target, source) for source, target in up]
    sibling = [(i, i ^ 1) for i in range(nx)]

    def edge(halo):
        return f32(columns, halo, X, 128)

    def padded(halo):
        return (columns, by + 2 * halo, X + PAD, 128)

    blocks = pl.pallas_call(
        functools.partial(pack_kernel, grid, count),
        out_shape=f32(group, per + 1, rows, 128),
        in_specs=[anywhere(), anywhere()],
        out_specs=vmem(),
        scratch_shapes=[pltpu.SemaphoreType.DMA((group, per + 1))],
        compiler_params=params(),
        name="pack",
    )(probes.reshape(count * rows, bz), kappa2.reshape(rows, bz))
    blocks = lax.all_to_all(blocks, ("gx", "gz"), 0, 0, tiled=True)
    c0, up_edge, down_edge, half = pl.pallas_call(
        functools.partial(probe_kernel, grid),
        out_shape=(f32(*padded(HALO)), edge(HALO), edge(HALO), f32(group, rows, 128)),
        in_specs=[vmem()],
        out_specs=(vmem(),) * 4,
        compiler_params=params(),
        name="probe_rows",
    )(blocks)
    low1 = lax.ppermute(up_edge, "gy", up)
    high1 = lax.ppermute(down_edge, "gy", down)
    other = lax.ppermute(half, "gx", sibling)
    diagonal, up_edge, down_edge = pl.pallas_call(
        functools.partial(diagonal_kernel, grid),
        out_shape=(f32(*padded(DIAGONAL_HALO)), edge(DIAGONAL_HALO), edge(DIAGONAL_HALO)),
        in_specs=[smem(), vmem(), vmem()],
        out_specs=(vmem(),) * 3,
        compiler_params=params(),
        name="diagonal_rows",
    )((gx % 2).astype(jnp.int32).reshape(1), half, other)
    low_diagonal = lax.ppermute(up_edge, "gy", up)
    high_diagonal = lax.ppermute(down_edge, "gy", down)

    ends = jnp.stack([gy == 0, gy == ny - 1, mine]).astype(jnp.int32)
    c0, diagonal, d0, c1, d1, c2, d2, up_edge, down_edge, moments = pl.pallas_call(
        functools.partial(first_kernel, by),
        out_shape=tuple(f32(*padded(h)) for h in (HALO, DIAGONAL_HALO, 4, 3, 2, HALO, 4))
        + (edge(HALO), edge(HALO), f32(ny, 6, 8, 128)),
        in_specs=[smem()] + [vmem()] * 6,
        out_specs=(vmem(),) * 10,
        input_output_aliases={1: 0, 2: 1},
        compiler_params=params(),
        name="first_steps",
    )(ends, c0, diagonal, low1, high1, low_diagonal, high_diagonal)
    low2 = lax.ppermute(up_edge, "gy", up)
    high2 = lax.ppermute(down_edge, "gy", down)
    moments = lax.all_to_all(moments, "gy", 0, 0, tiled=True)

    inverse_count = 1.0 / (X * by * ny * columns * 128)
    _, _, out = pl.pallas_call(
        functools.partial(last_kernel, grid, inverse_count),
        out_shape=(f32(*padded(HALO)), f32(*padded(4)), f32(group, per, rows, 128)),
        in_specs=[smem(), smem()] + [vmem()] * 10,
        out_specs=(vmem(),) * 3,
        scratch_shapes=[pltpu.VMEM(padded(h), jnp.float32) for h in (3, 2, 1)],
        input_output_aliases={8: 0, 9: 1},
        compiler_params=params(),
        name="last_steps",
    )(ends, cotangents, moments, c0, diagonal, d0, c1, d1, c2, d2, low2, high2)

    out = lax.all_to_all(out, ("gx", "gz"), 0, 0, tiled=True)
    return pl.pallas_call(
        functools.partial(sum_kernel, grid, count),
        out_shape=f32(bx, by, bz),
        in_specs=[vmem()],
        out_specs=vmem(),
        compiler_params=params(),
        name="sum_probes",
    )(out)


def solution(mesh):
    return jax.shard_map(
        body,
        mesh=mesh,
        in_specs=(P(None, "gx", "gy", "gz"), P("gx", "gy", "gz"), P()),
        out_specs=P("gx", "gy", "gz"),
        check_vma=False,
    )
```

time: 120 us -> 106 us (0.88)
  waiting for transfers between devices: 19 us -> 8.22 us
  Pallas kernels: 29 us -> 21.8 us
  blocking collectives: 48.7 us -> 54 us
  other arithmetic: 4.23 us -> 0.08 us
  local copies, waits for them, and re-layouts: 3.41 us -> 4.99 us
    ppermute x1, waiting for transfers between devices: 11.4 us -> 0.01 us  [body(): low1 = lax.ppermute(up_edge, 'gy', up)]
    all_to_all x1 -> x2, blocking collectives: 17.9 us -> 29 us  [the longest x1 17.4 us: body(): out = lax.all_to_all(out, ('gx', 'gz'), 0, 0, tiled=True)]
    pallas_call x4 -> x6, Pallas kernels: 29 us -> 21.8 us  [the longest x1 9.65 us: body(): pl.pallas_call(functools.partial(first_kernel, by), out_shape=tuple((f32(...]
    all_to_all x1, blocking collectives: 30.8 us -> 25 us  [body(): blocks = lax.all_to_all(blocks, ('gx', 'gz'), 0, 0, tiled=True)]
    unnamed x10, local copies, waits for them, and re-layouts: 1.65 us -> 4.99 us
    concatenate x2 -> x0, other arithmetic: 2.85 us -> none  [the longest x1 1.47 us: body(): blocks = jnp.concatenate([blocks, kappa], axis=1)]
    ppermute x3, waiting for transfers between devices: 3.54 us -> 6.26 us  [the longest x1 4.02 us: body(): high_diagonal = lax.ppermute(down_edge, 'gy', down)]
    ppermute x1, waiting for transfers between devices: 4.04 us -> 1.96 us  [body(): high1 = lax.ppermute(down_edge, 'gy', down)]
  transfers between devices with their start and end apart: 7 -> 7, of which waited for: 4 -> 3; matrix products, arithmetic and copies ran while one was open for 2% -> 0% of each run, Pallas kernels for 4% -> 1%
where the time goes in v4:
time: 106 us; the launch traced here: 105 us
  blocking collectives  54 us (51%)
  Pallas kernels  21.8 us (21%)
  starting transfers between devices  16.3 us (15%)
  waiting for transfers between devices  8.22 us (8%)
  local copies, waits for them, and re-layouts  4.99 us (5%)
    all_to_all x1, blocking collectives, body(): blocks = lax.all_to_all(blocks, ('gx', 'gz'), 0, 0, tiled=True)  25 us
    all_to_all x1, blocking collectives, body(): out = lax.all_to_all(out, ('gx', 'gz'), 0, 0, tiled=True)  17.4 us
    all_to_all x1, blocking collectives, body(): moments = lax.all_to_all(moments, 'gy', 0, 0, tiled=True)  11.6 us
    pallas_call x1, Pallas kernels, body(): pl.pallas_call(functools.partial(first_kernel, by), out_shape=tuple((f32(...  9.65 us
    pallas_call x1, Pallas kernels, body(): pl.pallas_call(functools.partial(last_kernel, grid, inverse_count), out_s...  8.54 us
    unnamed x10, local copies, waits for them, and re-layouts  4.99 us
    ppermute x1, starting transfers between devices, body(): low_diagonal = lax.ppermute(up_edge, 'gy', up)  4.55 us
    ppermute x1, waiting for transfers between devices, body(): high_diagonal = lax.ppermute(down_edge, 'gy', down)  4.02 us
  transfers between devices with their start and end apart: 7, of which 3 were waited for; matrix products, arithmetic and copies ran while one was open for 0% of the time, Pallas kernels for 1%

profile of v4, /device:TPU:0, one launch (start us, length us, event | category | flops | bytes accessed | tf_op | source)
XLA Modules:
  0.0 105.5 jit_solution(13661410144585373282)
XLA Ops:
  0.0 1.2 %copy-done.2 = f32[8,8,16,256]{3,2,1,0:T(8,128)S(1)} copy-done((f32[8,8,16,256]{3,2,1,0:T(8,128)S(1)}, f32[8,8,16,256]{3,2,1,0:T(8,128)}, u32[]{:S(2)}) %copy-start.2) | copy-done | bytes 1048600
  1.2 0.9 copy-done.3
  2.1 0.4 pack.1
  2.5 25.0 %all_to_all.15.blocks_ref = f32[8,3,128,128]{3,2,1,0:T(8,128)S(1)} all-to-all(f32[8,3,128,128]{3,2,1,0:T(8,128)S(1)} %pack.1), channel_id=1, replica_groups=mesh['gx'=4,'gy'=4,'gz'=2] {'gx','gz'}, dimensions={0} | all-to-all | bytes 3145728 | tf_op jit(solution)/shard_map/all_to_all | solution.py:391
  27.6 1.3 %probe_rows.1 = (f32[4,26,40,128]{3,2,1,0:T(8,128)S(1)}, f32[4,5,32,128]{3,2,1,0:T(8,128)}, f32[4,5,32,128]{3,2,1,0:T(8,128)}, f32[8,128,128]{2,1,0:T(8,128)S(1)}) custom-call(f32[8,3,128,128]{3,2,1,0:T(8,128)S(1)} %all_to_all.15.blocks_ref), custom_call_target="tpu_custom_call" | custom-call | tf_op jit(solution)/shard_map/probe_rows/pallas_call | solution.py:392
  28.9 0.4 collective-permute-start
  29.3 3.5 %collective-permute-start.1 = (f32[4,5,32,128]{3,2,1,0:T(8,128)}, f32[4,5,32,128]{3,2,1,0:T(8,128)S(1)}, u32[]{:S(2)}, u32[]{:S(2)}) collective-permute-start(f32[4,5,32,128]{3,2,1,0:T(8,128)} %get-tuple-element.26), channel_id=1, source_target_pairs={{0,2},{2,4},{4,6},{1,3},{3,5},{5,7},{8,10},{10,12},{12,14},{9,11},... | collective-permute-start | bytes 983048 | tf_op jit(solution)/shard_map/ppermute | solution.py:400
  32.8 1.3 %collective-permute-start.2 = (f32[4,5,32,128]{3,2,1,0:T(8,128)}, f32[4,5,32,128]{3,2,1,0:T(8,128)}, u32[]{:S(2)}, u32[]{:S(2)}) collective-permute-start(f32[4,5,32,128]{3,2,1,0:T(8,128)} %get-tuple-element.27), channel_id=1, source_target_pairs={{2,0},{4,2},{6,4},{3,1},{5,3},{7,5},{10,8},{12,10},{14,12},{11,9},... | collective-permute-start | bytes 983048 | tf_op jit(solution)/shard_map/ppermute | solution.py:401
  34.1 1.1 %diagonal_rows.1 = (f32[4,24,40,128]{3,2,1,0:T(8,128)S(1)}, f32[4,4,32,128]{3,2,1,0:T(8,128)}, f32[4,4,32,128]{3,2,1,0:T(8,128)}) custom-call(s32[1]{0:T(128)} %bitcast.5.core_ref, f32[8,128,128]{2,1,0:T(8,128)S(1)} %get-tuple-element.24.half_ref, f32[8,128,128]{2,1,0:T(8,128)S(1)} %collective-permute-done.other_ref), custom_call_target="tpu_custom_call" | custom-call | tf_op jit(solution)/shard_map/diagonal_rows/pallas_call | solution.py:403
  35.2 1.3 %copy-done = f32[4,24,40,128]{3,2,1,0:T(8,128)} copy-done((f32[4,24,40,128]{3,2,1,0:T(8,128)}, f32[4,24,40,128]{3,2,1,0:T(8,128)S(1)}, u32[]{:S(2)}) %copy-start) | copy-done | bytes 1966104
  36.6 4.6 %collective-permute-start.3 = (f32[4,4,32,128]{3,2,1,0:T(8,128)}, f32[4,4,32,128]{3,2,1,0:T(8,128)S(1)}, u32[]{:S(2)}, u32[]{:S(2)}) collective-permute-start(f32[4,4,32,128]{3,2,1,0:T(8,128)} %get-tuple-element.28), channel_id=1, source_target_pairs={{0,2},{2,4},{4,6},{1,3},{3,5},{5,7},{8,10},{10,12},{12,14},{9,11},... | collective-permute-start | bytes 786440 | tf_op jit(solution)/shard_map/ppermute | solution.py:411
  41.1 1.3 %collective-permute-start.4 = (f32[4,4,32,128]{3,2,1,0:T(8,128)}, f32[4,4,32,128]{3,2,1,0:T(8,128)S(1)}, u32[]{:S(2)}, u32[]{:S(2)}) collective-permute-start(f32[4,4,32,128]{3,2,1,0:T(8,128)} %get-tuple-element.29), channel_id=1, source_target_pairs={{2,0},{4,2},{6,4},{3,1},{5,3},{7,5},{10,8},{12,10},{14,12},{11,9},... | collective-permute-start | bytes 786440 | tf_op jit(solution)/shard_map/ppermute | solution.py:412
  42.4 0.1 pad_add_fusion.ends_ref
  42.5 2.0 %collective-permute-done.2.high_ref = f32[4,5,32,128]{3,2,1,0:T(8,128)} collective-permute-done((f32[4,5,32,128]{3,2,1,0:T(8,128)}, f32[4,5,32,128]{3,2,1,0:T(8,128)}, u32[]{:S(2)}, u32[]{:S(2)}) %collective-permute-start.2) | collective-permute-done | bytes 327712 | tf_op jit(solution)/shard_map/ppermute | solution.py:401
  44.5 2.2 %collective-permute-done.3.low_diagonal_ref = f32[4,4,32,128]{3,2,1,0:T(8,128)S(1)} collective-permute-done((f32[4,4,32,128]{3,2,1,0:T(8,128)}, f32[4,4,32,128]{3,2,1,0:T(8,128)S(1)}, u32[]{:S(2)}, u32[]{:S(2)}) %collective-permute-start.3) | collective-permute-done | bytes 262176 | tf_op jit(solution)/shard_map/ppermute | solution.py:411
  46.7 4.0 %collective-permute-done.4.high_diagonal_ref = f32[4,4,32,128]{3,2,1,0:T(8,128)S(1)} collective-permute-done((f32[4,4,32,128]{3,2,1,0:T(8,128)}, f32[4,4,32,128]{3,2,1,0:T(8,128)S(1)}, u32[]{:S(2)}, u32[]{:S(2)}) %collective-permute-start.4) | collective-permute-done | bytes 262176 | tf_op jit(solution)/shard_map/ppermute | solution.py:412
  50.7 1.5 %copy-done.1 = f32[4,24,40,128]{3,2,1,0:T(8,128)S(1)} copy-done((f32[4,24,40,128]{3,2,1,0:T(8,128)S(1)}, f32[4,24,40,128]{3,2,1,0:T(8,128)}, u32[]{:S(2)}) %copy-start.1) | copy-done | bytes 1966104
  52.3 9.6 %first_steps.1 = (f32[4,26,40,128]{3,2,1,0:T(8,128)S(1)}, f32[4,24,40,128]{3,2,1,0:T(8,128)S(1)}, f32[4,24,40,128]{3,2,1,0:T(8,128)S(1)}, f32[4,22,40,128]{3,2,1...) custom-call(s32[3]{0:T(128)S(1)} %pad_add_fusion.ends_ref, ...), custom_call_target="tpu_custom_call", output_to_operand_aliasing={{0}: (1, {}), {1}: (2, {})} | custom-call | tf_op jit(solution)/shard_map/first_steps/pallas_call | solution.py:415
  61.9 4.0 %collective-permute-start.5 = (f32[4,5,32,128]{3,2,1,0:T(8,128)S(1)}, f32[4,5,32,128]{3,2,1,0:T(8,128)S(1)}, u32[]{:S(2)}, u32[]{:S(2)}) collective-permute-start(f32[4,5,32,128]{3,2,1,0:T(8,128)S(1)} %get-tuple-element.38), channel_id=1, source_target_pairs={{0,2},{2,4},{4,6},{1,3},{3,5},{5,7},{8,10},{10,12},{12,14},{9,11},... | collective-permute-start | bytes 983048 | tf_op jit(solution)/shard_map/ppermute | solution.py:425
  65.9 1.3 %collective-permute-start.6 = (f32[4,5,32,128]{3,2,1,0:T(8,128)S(1)}, f32[4,5,32,128]{3,2,1,0:T(8,128)S(1)}, u32[]{:S(2)}, u32[]{:S(2)}) collective-permute-start(f32[4,5,32,128]{3,2,1,0:T(8,128)S(1)} %get-tuple-element.39), channel_id=1, source_target_pairs={{2,0},{4,2},{6,4},{3,1},{5,3},{7,5},{10,8},{12,10},{14,12},{11,9},... | collective-permute-start | bytes 983048 | tf_op jit(solution)/shard_map/ppermute | solution.py:426
  67.2 11.6 %all_to_all.16.moments_ref = f32[4,6,8,128]{3,2,1,0:T(8,128)S(1)} all-to-all(f32[4,6,8,128]{3,2,1,0:T(8,128)S(1)} %get-tuple-element.30), channel_id=1, replica_groups=mesh['gx'=4,'gy'=4,'gz'=2] {'gy'}, dimensions={0} | all-to-all | bytes 196608 | tf_op jit(solution)/shard_map/all_to_all | solution.py:427
  78.8 8.5 %last_steps.1 = (f32[4,26,40,128]{3,2,1,0:T(8,128)S(1)}, f32[4,24,40,128]{3,2,1,0:T(8,128)S(1)}, f32[8,2,128,128]{3,2,1,0:T(8,128)S(1)}) custom-call(s32[3]{0:T(128)S(1)} %pad_add_fusion.ends_ref, f32[5,8]{1,0:T(8,128)S(1)} %copy-done.4, f32[4,6,8,128]{3,2,1,0:T(8,128)S(1)} %all_to_all.16.moments_ref, ...), custom_call_target="tpu_custom_call", output_to_operand_aliasing={{0}: (8, {}), {1}: (9, {})} | custom-call | tf_op jit(solution)/shard_map/last_steps/pallas_call | solution.py:430
  87.4 17.4 %all_to_all.17.parts_ref = f32[8,2,128,128]{3,2,1,0:T(8,128)S(1)} all-to-all(f32[8,2,128,128]{3,2,1,0:T(8,128)S(1)} %get-tuple-element.40), channel_id=1, replica_groups=mesh['gx'=4,'gy'=4,'gz'=2] {'gx','gz'}, dimensions={0} | all-to-all | bytes 2097152 | tf_op jit(solution)/shard_map/all_to_all | solution.py:441
  104.8 0.7 sum_probes.1
  (10 shorter events, 0.0 us)
Async XLA Ops:
  0.0 1.2 %copy-start.2 = (f32[8,8,16,256]{3,2,1,0:T(8,128)S(1)}, f32[8,8,16,256]{3,2,1,0:T(8,128)}, u32[]{:S(2)}) copy-start(f32[8,8,16,256]{3,2,1,0:T(8,128)} %param.3) | copy-start | bytes 3145732
  1.2 0.9 copy-start.3
  28.9 5.2 %collective-permute-start = (f32[8,128,128]{2,1,0:T(8,128)S(1)}, f32[8,128,128]{2,1,0:T(8,128)S(1)}, u32[]{:S(2)}, u32[]{:S(2)}) collective-permute-start(f32[8,128,128]{2,1,0:T(8,128)S(1)} %get-tuple-element.24.half_ref), channel_id=1, source_target_pairs={{0,8},{8,0},{16,24},{24,16},{1,9},{9,1},{17,25},{25,17},{2,10},{10... | collective-permute-start | bytes 1572872 | tf_op jit(solution)/shard_map/ppermute | solution.py:402
  29.3 13.2 %collective-permute-start.1 = (f32[4,5,32,128]{3,2,1,0:T(8,128)}, f32[4,5,32,128]{3,2,1,0:T(8,128)S(1)}, u32[]{:S(2)}, u32[]{:S(2)}) collective-permute-start(f32[4,5,32,128]{3,2,1,0:T(8,128)} %get-tuple-element.26), channel_id=1, source_target_pairs={{0,2},{2,4},{4,6},{1,3},{3,5},{5,7},{8,10},{10,12},{12,14},{9,11},... | collective-permute-start | bytes 983048 | tf_op jit(solution)/shard_map/ppermute | solution.py:400
  32.8 11.7 %collective-permute-start.2 = (f32[4,5,32,128]{3,2,1,0:T(8,128)}, f32[4,5,32,128]{3,2,1,0:T(8,128)}, u32[]{:S(2)}, u32[]{:S(2)}) collective-permute-start(f32[4,5,32,128]{3,2,1,0:T(8,128)} %get-tuple-element.27), channel_id=1, source_target_pairs={{2,0},{4,2},{6,4},{3,1},{5,3},{7,5},{10,8},{12,10},{14,12},{11,9},... | collective-permute-start | bytes 983048 | tf_op jit(solution)/shard_map/ppermute | solution.py:401
  35.2 1.3 %copy-start = (f32[4,24,40,128]{3,2,1,0:T(8,128)}, f32[4,24,40,128]{3,2,1,0:T(8,128)S(1)}, u32[]{:S(2)}) copy-start(f32[4,24,40,128]{3,2,1,0:T(8,128)S(1)} %get-tuple-element.25.diagonal_in) | copy-start | bytes 5898244
  36.6 10.2 %collective-permute-start.3 = (f32[4,4,32,128]{3,2,1,0:T(8,128)}, f32[4,4,32,128]{3,2,1,0:T(8,128)S(1)}, u32[]{:S(2)}, u32[]{:S(2)}) collective-permute-start(f32[4,4,32,128]{3,2,1,0:T(8,128)} %get-tuple-element.28), channel_id=1, source_target_pairs={{0,2},{2,4},{4,6},{1,3},{3,5},{5,7},{8,10},{10,12},{12,14},{9,11},... | collective-permute-start | bytes 786440 | tf_op jit(solution)/shard_map/ppermute | solution.py:411
  41.1 9.6 %collective-permute-start.4 = (f32[4,4,32,128]{3,2,1,0:T(8,128)}, f32[4,4,32,128]{3,2,1,0:T(8,128)S(1)}, u32[]{:S(2)}, u32[]{:S(2)}) collective-permute-start(f32[4,4,32,128]{3,2,1,0:T(8,128)} %get-tuple-element.29), channel_id=1, source_target_pairs={{2,0},{4,2},{6,4},{3,1},{5,3},{7,5},{10,8},{12,10},{14,12},{11,9},... | collective-permute-start | bytes 786440 | tf_op jit(solution)/shard_map/ppermute | solution.py:412
  50.7 1.5 %copy-start.1 = (f32[4,24,40,128]{3,2,1,0:T(8,128)S(1)}, f32[4,24,40,128]{3,2,1,0:T(8,128)}, u32[]{:S(2)}) copy-start(f32[4,24,40,128]{3,2,1,0:T(8,128)} %copy-done) | copy-start | bytes 5898244
  52.3 26.5 %copy-start.4 = (f32[5,8]{1,0:T(8,128)S(1)}, f32[5,8]{1,0:T(8,128)}, u32[]{:S(2)}) copy-start(f32[5,8]{1,0:T(8,128)} %weights_ref.1) | copy-start | bytes 484
  61.9 16.9 %collective-permute-start.5 = (f32[4,5,32,128]{3,2,1,0:T(8,128)S(1)}, f32[4,5,32,128]{3,2,1,0:T(8,128)S(1)}, u32[]{:S(2)}, u32[]{:S(2)}) collective-permute-start(f32[4,5,32,128]{3,2,1,0:T(8,128)S(1)} %get-tuple-element.38), channel_id=1, source_target_pairs={{0,2},{2,4},{4,6},{1,3},{3,5},{5,7},{8,10},{10,12},{12,14},{9,11},... | collective-permute-start | bytes 983048 | tf_op jit(solution)/shard_map/ppermute | solution.py:425
  65.9 12.9 %collective-permute-start.6 = (f32[4,5,32,128]{3,2,1,0:T(8,128)S(1)}, f32[4,5,32,128]{3,2,1,0:T(8,128)S(1)}, u32[]{:S(2)}, u32[]{:S(2)}) collective-permute-start(f32[4,5,32,128]{3,2,1,0:T(8,128)S(1)} %get-tuple-element.39), channel_id=1, source_target_pairs={{2,0},{4,2},{6,4},{3,1},{5,3},{7,5},{10,8},{12,10},{14,12},{11,9},... | collective-permute-start | bytes 983048 | tf_op jit(solution)/shard_map/ppermute | solution.py:426

commit v5 on v4

--- a/solution.py
+++ b/solution.py
@@ -49,29 +49,21 @@
         self.ref = ref
         self.halo = halo
         self.columns, self.rows, self.pitch, _ = ref.shape
-        self.cells = self.pitch - PAD
-        self.flat = ref.reshape(self.columns * self.rows * self.pitch, 128)
-
-    def at(self, column, row, x):
-        moving, fixed = row
-        start = (column * self.rows + fixed + self.halo) * self.pitch + x
-        return pl.ds(moving * self.pitch + start, 8)
+        self.cells = self.pitch - 2 * PAD
 
     def load(self, column, row, x):
-        return self.flat[self.at(column, row, x), :]
+        return self.ref[column, row + self.halo, pl.ds(PAD + x, 8), :]
 
     def store(self, column, row, x, value):
-        self.flat[self.at(column, row, x), :] = value
-
-    def part(self, first, count):
-        return self.ref.at[:, pl.ds(first + self.halo, count), pl.ds(0, self.cells), :]
+        self.ref[column, row + self.halo, pl.ds(PAD + x, 8), :] = value
 
     def clear_pads(self):
         zero = jnp.zeros((8, 128), jnp.float32)
 
-        def body(row, carry):
+        def body(at, carry):
             for column in range(self.columns):
-                self.store(column, (row, -self.halo), self.cells, zero)
+                self.ref[column, at, pl.ds(0, PAD), :] = zero
+                self.ref[column, at, pl.ds(PAD + self.cells, PAD), :] = zero
             return carry
 
         lax.fori_loop(0, self.rows, body, 0)
@@ -80,7 +72,7 @@
         zero = jnp.zeros((8, 128), jnp.float32)
         for column in range(self.columns):
             for x in range(0, self.cells, 8):
-                self.store(column, (0, row), x, zero)
+                self.store(column, row, x, zero)
 
 
 def lane_masks():
@@ -90,7 +82,6 @@
 
 def stencil_tiles(source, diagonal, row, x, masks):
     columns = range(source.columns)
-    moving, fixed = row
     centre = [source.load(c, row, x) for c in columns]
     after = [pltpu.roll(value, 1, 1) for value in centre]
     before = [pltpu.roll(value, 127, 1) for value in centre]
@@ -100,7 +91,7 @@
         high = before[c + 1] if c + 1 < source.columns else 0.0
         total = jnp.where(masks[0], low, after[c]) + jnp.where(masks[1], high, before[c])
         total = total + (source.load(c, row, x - 1) + source.load(c, row, x + 1))
-        total = total + (source.load(c, (moving, fixed - 1), x) + source.load(c, (moving, fixed + 1), x))
+        total = total + (source.load(c, row - 1, x) + source.load(c, row + 1, x))
         results.append(diagonal.load(c, row, x) * centre[c] - total)
     return results
 
@@ -111,7 +102,7 @@
     def body(step, carry):
         results = []
         for offset in range(unroll):
-            row = (step * unroll, first + offset)
+            row = step * unroll + (first + offset)
             for x in range(0, source.cells, 8):
                 values = stencil_tiles(source, diagonal, row, x, masks)
                 for c, value in enumerate(values):
@@ -177,7 +168,7 @@
     for s, column, x, z in places(grid):
         values = [blocks_ref[s, column, pl.ds(y, bx, stride=by), :] for y in range(by)]
         for y in range(by):
-            own.store(z, (0, y), x, values[y])
+            own.store(z, y, x, values[y])
         for y in range(HALO):
             down_ref[z, y, pl.ds(x, bx), :] = values[y]
             up_ref[z, y, pl.ds(x, bx), :] = values[by - HALO + y]
@@ -197,7 +188,7 @@
             pair = (mine, other) if column == 0 else (other, mine)
             values.append(6.0 + jnp.where(first, *pair))
         for y in range(by):
-            own.store(z, (0, y), x, values[y])
+            own.store(z, y, x, values[y])
         for y in range(DIAGONAL_HALO):
             down_ref[z, y, pl.ds(x, bx), :] = values[y]
             up_ref[z, y, pl.ds(x, bx), :] = values[by - DIAGONAL_HALO + y]
@@ -207,14 +198,14 @@
     for c in range(field.columns):
         for y in range(field.halo):
             for x in range(0, field.cells, 8):
-                field.store(c, (0, y - field.halo), x, low_ref[c, y, pl.ds(x, 8), :])
-                field.store(c, (0, own + y), x, high_ref[c, y, pl.ds(x, 8), :])
+                field.store(c, y - field.halo, x, low_ref[c, y, pl.ds(x, 8), :])
+                field.store(c, own + y, x, high_ref[c, y, pl.ds(x, 8), :])
 
 
 def first_kernel(
     own,
     ends_ref, c0_in, diagonal_in, low_ref, high_ref, low_diagonal_ref, high_diagonal_ref,
-    c0_ref, diagonal_ref, d0_ref, c1_ref, d1_ref, c2_ref, d2_ref, up_ref, down_ref, moments_ref,
+    c0_ref, diagonal_ref, d0_ref, c1_ref, d1_ref, c2_ref, up_ref, down_ref,
 ):
     c0 = Field(c0_ref, HALO)
     diagonal = Field(diagonal_ref, DIAGONAL_HALO)
@@ -222,8 +213,7 @@
     c1 = Field(c1_ref, 3)
     d1 = Field(d1_ref, 2)
     c2 = Field(c2_ref, HALO)
-    d2 = Field(d2_ref, 4)
-    for field in (d0, c1, d1, c2, d2):
+    for field in (d0, c1, d1, c2):
         field.clear_pads()
     fill_halo(c0, own, low_ref, high_ref)
     fill_halo(diagonal, own, low_diagonal_ref, high_diagonal_ref)
@@ -235,12 +225,20 @@
     for c in range(c2.columns):
         for y in range(HALO):
             for x in range(0, c2.cells, 8):
-                down_ref[c, y, pl.ds(x, 8), :] = c2.load(c, (0, y), x)
-                up_ref[c, y, pl.ds(x, 8), :] = c2.load(c, (0, own - HALO + y), x)
-    steps(d2, c2, diagonal, 0)
-
-    def moment_row(step, sums):
-        row = (step, 0)
+                down_ref[c, y, pl.ds(x, 8), :] = c2.load(c, y, x)
+                up_ref[c, y, pl.ds(x, 8), :] = c2.load(c, own - HALO + y, x)
+
+
+def middle_kernel(own, c0_ref, c1_ref, c2_ref, diagonal_ref, d2_ref, moments_ref):
+    c0 = Field(c0_ref, HALO)
+    diagonal = Field(diagonal_ref, DIAGONAL_HALO)
+    c1 = Field(c1_ref, 3)
+    c2 = Field(c2_ref, HALO)
+    d2 = Field(d2_ref, 4)
+    d2.clear_pads()
+    apply_rows(d2, c2, diagonal, 0, own)
+
+    def moment_row(row, sums):
         for x in range(0, c0.cells, 8):
             for c in range(c0.columns):
                 a, b, e, d = (field.load(c, row, x) for field in (c0, c1, c2, d2))
@@ -250,19 +248,18 @@
 
     zero = jnp.zeros((8, 128), jnp.float32)
     sums = lax.fori_loop(0, own, moment_row, (zero,) * 6)
-    for index, total in enumerate(sums):
-        for part in range(moments_ref.shape[0]):
-            moments_ref[part, index] = total
+    sums = [jnp.sum(total, axis=0, keepdims=True) for total in sums]
+    sums = jnp.concatenate(sums + [zero[:2]], axis=0)
+    for part in range(moments_ref.shape[0]):
+        moments_ref[part] = sums
 
 
 def moment_slopes(inverse_count, probe, weights_ref, moments_ref):
-    raw = []
-    for k in range(6):
-        total = moments_ref[0, k]
-        for part in range(1, moments_ref.shape[0]):
-            total = total + moments_ref[part, k]
-        total = jnp.sum(jnp.sum(total, axis=0, keepdims=True), axis=1, keepdims=True)
-        raw.append(jnp.broadcast_to(total * inverse_count, (8, 128)))
+    total = moments_ref[0]
+    for part in range(1, moments_ref.shape[0]):
+        total = total + moments_ref[part]
+    total = jnp.sum(total, axis=1, keepdims=True) * inverse_count
+    raw = [jnp.broadcast_to(total[k : k + 1], (8, 128)) for k in range(6)]
     moments = tuple(raw[:5]) + (raw[5] - SHIFT * raw[4],)
     weights = [weights_ref[k, probe] for k in range(5)]
     value, pullback = jax.vjp(lambda m: loss_of_moments(m, weights), moments)
@@ -302,7 +299,7 @@
     place = {(x, z): (s, column) for s, column, x, z in places(grid)}
 
     def out_row(step, carry):
-        row = (step, 0)
+        row = step
         results = []
         for x in range(0, c4.cells, 8):
             last = stencil_tiles(c4, diagonal, row, x, masks)
@@ -344,8 +341,16 @@
     return pl.BlockSpec(memory_space=pltpu.SMEM)
 
 
-def anywhere():
-    return pl.BlockSpec(memory_space=pl.ANY)
+def hbm():
+    return pl.BlockSpec(memory_space=pltpu.HBM)
+
+
+def here(value):
+    return pltpu.with_memory_space_constraint(value, pltpu.VMEM)
+
+
+def there(value):
+    return pltpu.with_memory_space_constraint(value, pltpu.HBM)
 
 
 def f32(*shape):
@@ -353,7 +358,7 @@
 
 
 def params():
-    return pltpu.CompilerParams(vmem_limit_bytes=32 * MIB)
+    return pltpu.CompilerParams(vmem_limit_bytes=24 * MIB)
 
 
 def body(probes, kappa2, cotangents):
@@ -377,21 +382,24 @@
         return f32(columns, halo, X, 128)
 
     def padded(halo):
-        return (columns, by + 2 * halo, X + PAD, 128)
+        return (columns, by + 2 * halo, X + 2 * PAD, 128)
+
+    def vector(halo):
+        return pltpu.VMEM(padded(halo), jnp.float32)
 
     blocks = pl.pallas_call(
         functools.partial(pack_kernel, grid, count),
         out_shape=f32(group, per + 1, rows, 128),
-        in_specs=[anywhere(), anywhere()],
+        in_specs=[hbm(), hbm()],
         out_specs=vmem(),
         scratch_shapes=[pltpu.SemaphoreType.DMA((group, per + 1))],
         compiler_params=params(),
         name="pack",
-    )(probes.reshape(count * rows, bz), kappa2.reshape(rows, bz))
+    )(there(probes.reshape(count * rows, bz)), there(kappa2.reshape(rows, bz)))
     blocks = lax.all_to_all(blocks, ("gx", "gz"), 0, 0, tiled=True)
     c0, up_edge, down_edge, half = pl.pallas_call(
         functools.partial(probe_kernel, grid),
-        out_shape=(f32(*padded(HALO)), edge(HALO), edge(HALO), f32(group, rows, 128)),
+        out_shape=(vector(HALO), edge(HALO), edge(HALO), f32(group, rows, 128)),
         in_specs=[vmem()],
         out_specs=(vmem(),) * 4,
         compiler_params=params(),
@@ -402,7 +410,7 @@
     other = lax.ppermute(half, "gx", sibling)
     diagonal, up_edge, down_edge = pl.pallas_call(
         functools.partial(diagonal_kernel, grid),
-        out_shape=(f32(*padded(DIAGONAL_HALO)), edge(DIAGONAL_HALO), edge(DIAGONAL_HALO)),
+        out_shape=(vector(DIAGONAL_HALO), edge(DIAGONAL_HALO), edge(DIAGONAL_HALO)),
         in_specs=[smem(), vmem(), vmem()],
         out_specs=(vmem(),) * 3,
         compiler_params=params(),
@@ -412,31 +420,45 @@
     high_diagonal = lax.ppermute(down_edge, "gy", down)
 
     ends = jnp.stack([gy == 0, gy == ny - 1, mine]).astype(jnp.int32)
-    c0, diagonal, d0, c1, d1, c2, d2, up_edge, down_edge, moments = pl.pallas_call(
+    c0, diagonal, d0, c1, d1, c2, up_edge, down_edge = pl.pallas_call(
         functools.partial(first_kernel, by),
-        out_shape=tuple(f32(*padded(h)) for h in (HALO, DIAGONAL_HALO, 4, 3, 2, HALO, 4))
-        + (edge(HALO), edge(HALO), f32(ny, 6, 8, 128)),
+        out_shape=tuple(vector(h) for h in (HALO, DIAGONAL_HALO, 4, 3, 2, HALO))
+        + (edge(HALO), edge(HALO)),
         in_specs=[smem()] + [vmem()] * 6,
-        out_specs=(vmem(),) * 10,
+        out_specs=(vmem(),) * 8,
         input_output_aliases={1: 0, 2: 1},
         compiler_params=params(),
         name="first_steps",
-    )(ends, c0, diagonal, low1, high1, low_diagonal, high_diagonal)
+    )(ends, here(c0), here(diagonal), low1, high1, low_diagonal, high_diagonal)
     low2 = lax.ppermute(up_edge, "gy", up)
     high2 = lax.ppermute(down_edge, "gy", down)
+    cells = by * X * columns * 128
+    d2, moments = pl.pallas_call(
+        functools.partial(middle_kernel, by),
+        out_shape=(vector(4), f32(ny, 8, 128)),
+        in_specs=[vmem()] * 4,
+        out_specs=(vmem(),) * 2,
+        compiler_params=params(),
+        cost_estimate=pl.CostEstimate(
+            flops=40 * cells, bytes_accessed=24 * cells, transcendentals=0
+        ),
+        name="middle_step",
+    )(here(c0), here(c1), here(c2), here(diagonal))
     moments = lax.all_to_all(moments, "gy", 0, 0, tiled=True)
 
     inverse_count = 1.0 / (X * by * ny * columns * 128)
     _, _, out = pl.pallas_call(
         functools.partial(last_kernel, grid, inverse_count),
-        out_shape=(f32(*padded(HALO)), f32(*padded(4)), f32(group, per, rows, 128)),
+        out_shape=(vector(HALO), vector(4), f32(group, per, rows, 128)),
         in_specs=[smem(), smem()] + [vmem()] * 10,
         out_specs=(vmem(),) * 3,
-        scratch_shapes=[pltpu.VMEM(padded(h), jnp.float32) for h in (3, 2, 1)],
+        scratch_shapes=[vector(h) for h in (3, 2, 1)],
         input_output_aliases={8: 0, 9: 1},
         compiler_params=params(),
         name="last_steps",
-    )(ends, cotangents, moments, c0, diagonal, d0, c1, d1, c2, d2, low2, high2)
+    )(
+        ends, cotangents, moments, *(here(x) for x in (c0, diagonal, d0, c1, d1, c2, d2)), low2, high2
+    )
 
     out = lax.all_to_all(out, ("gx", "gz"), 0, 0, tiled=True)
     return pl.pallas_call(

time: 106 us -> 105 us (level)
  Pallas kernels: 21.8 us -> 23.8 us
  local copies, waits for them, and re-layouts: 4.99 us -> 3.1 us
  blocking collectives: 54 us -> 52.5 us
    unnamed x10 -> x6, local copies, waits for them, and re-layouts: 4.99 us -> 3.1 us
    pallas_call x1, Pallas kernels: 0.4 us -> 1.6 us  [body(): pl.pallas_call(functools.partial(pack_kernel, grid, count), out_shape=f32...]
    ppermute x1, waiting for transfers between devices: 2.23 us -> 3.36 us  [body(): low_diagonal = lax.ppermute(up_edge, 'gy', up)]
    ppermute x1, waiting for transfers between devices: 1.96 us -> 0.83 us  [body(): high1 = lax.ppermute(down_edge, 'gy', down)]
    all_to_all x1, blocking collectives: 11.6 us -> 10.5 us  [body(): moments = lax.all_to_all(moments, 'gy', 0, 0, tiled=True)]
    pallas_call x3 -> x4, Pallas kernels: 12.1 us -> 13.1 us  [the longest x1 7.9 us: body(): pl.pallas_call(functools.partial(first_kernel, by), out_shape=tuple((vect...]
  transfers between devices with their start and end apart: 7 -> 7, of which waited for: 3 -> 3; matrix products, arithmetic and copies ran while one was open for 0% -> 0% of each run, Pallas kernels for 1% -> 4%
where the time goes in v5:
time: 105 us; the launch traced here: 104 us
  blocking collectives  52.5 us (50%)
  Pallas kernels  23.8 us (23%)
  starting transfers between devices  16.3 us (16%)
  waiting for transfers between devices  8.22 us (8%)
  local copies, waits for them, and re-layouts  3.1 us (3%)
    all_to_all x1, blocking collectives, body(): blocks = lax.all_to_all(blocks, ('gx', 'gz'), 0, 0, tiled=True)  25 us
    all_to_all x1, blocking collectives, body(): out = lax.all_to_all(out, ('gx', 'gz'), 0, 0, tiled=True)  17 us
    all_to_all x1, blocking collectives, body(): moments = lax.all_to_all(moments, 'gy', 0, 0, tiled=True)  10.5 us
    pallas_call x1, Pallas kernels, body(): pl.pallas_call(functools.partial(last_kernel, grid, inverse_count), out_s...  8.37 us
    pallas_call x1, Pallas kernels, body(): pl.pallas_call(functools.partial(first_kernel, by), out_shape=tuple((vect...  7.9 us
    ppermute x1, starting transfers between devices, body(): low_diagonal = lax.ppermute(up_edge, 'gy', up)  4.55 us
    ppermute x1, waiting for transfers between devices, body(): high_diagonal = lax.ppermute(down_edge, 'gy', down)  4.02 us
    ppermute x1, starting transfers between devices, body(): low2 = lax.ppermute(up_edge, 'gy', up)  4.01 us
  transfers between devices with their start and end apart: 7, of which 3 were waited for; matrix products, arithmetic and copies ran while one was open for 0% of the time, Pallas kernels for 4%

profile of v5, /device:TPU:0, one launch (start us, length us, event | category | flops | bytes accessed | tf_op | source)
XLA Modules:
  0.0 104.2 jit_solution(10397784909289661825)
XLA Ops:
  0.0 1.6 %pack.1 = f32[8,3,128,128]{3,2,1,0:T(8,128)S(1)} custom-call(f32[1024,256]{1,0:T(8,128)} %bitcast.6, f32[128,256]{1,0:T(8,128)} %bitcast.7), custom_call_target="tpu_custom_call" | custom-call | tf_op jit(solution)/shard_map/pack/pallas_call | solution.py:390
  1.6 25.0 %all_to_all.15.blocks_ref = f32[8,3,128,128]{3,2,1,0:T(8,128)S(1)} all-to-all(f32[8,3,128,128]{3,2,1,0:T(8,128)S(1)} %pack.1), channel_id=1, replica_groups=mesh['gx'=4,'gy'=4,'gz'=2] {'gx','gz'}, dimensions={0} | all-to-all | bytes 3145728 | tf_op jit(solution)/shard_map/all_to_all | solution.py:399
  26.7 1.3 %probe_rows.1 = (f32[4,26,48,128]{3,2,1,0:T(8,128)S(1)}, f32[4,5,32,128]{3,2,1,0:T(8,128)}, f32[4,5,32,128]{3,2,1,0:T(8,128)}, f32[8,128,128]{2,1,0:T(8,128)S(1)}) custom-call(f32[8,3,128,128]{3,2,1,0:T(8,128)S(1)} %all_to_all.15.blocks_ref), custom_call_target="tpu_custom_call" | custom-call | tf_op jit(solution)/shard_map/probe_rows/pallas_call | solution.py:400
  28.0 0.4 collective-permute-start
  28.4 3.5 %collective-permute-start.1 = (f32[4,5,32,128]{3,2,1,0:T(8,128)}, f32[4,5,32,128]{3,2,1,0:T(8,128)S(1)}, u32[]{:S(2)}, u32[]{:S(2)}) collective-permute-start(f32[4,5,32,128]{3,2,1,0:T(8,128)} %get-tuple-element.26), channel_id=1, source_target_pairs={{0,2},{2,4},{4,6},{1,3},{3,5},{5,7},{8,10},{10,12},{12,14},{9,11},... | collective-permute-start | bytes 983048 | tf_op jit(solution)/shard_map/ppermute | solution.py:408
  31.9 1.3 %collective-permute-start.2 = (f32[4,5,32,128]{3,2,1,0:T(8,128)}, f32[4,5,32,128]{3,2,1,0:T(8,128)}, u32[]{:S(2)}, u32[]{:S(2)}) collective-permute-start(f32[4,5,32,128]{3,2,1,0:T(8,128)} %get-tuple-element.27), channel_id=1, source_target_pairs={{2,0},{4,2},{6,4},{3,1},{5,3},{7,5},{10,8},{12,10},{14,12},{11,9},... | collective-permute-start | bytes 983048 | tf_op jit(solution)/shard_map/ppermute | solution.py:409
  33.2 2.1 %diagonal_rows.1 = (f32[4,24,48,128]{3,2,1,0:T(8,128)S(1)}, f32[4,4,32,128]{3,2,1,0:T(8,128)}, f32[4,4,32,128]{3,2,1,0:T(8,128)}) custom-call(s32[1]{0:T(128)} %bitcast.5.core_ref, f32[8,128,128]{2,1,0:T(8,128)S(1)} %get-tuple-element.24.half_ref, f32[8,128,128]{2,1,0:T(8,128)} %collective-permute-done.other_ref), custom_call_target="tpu_custom_call" | custom-call | tf_op jit(solution)/shard_map/diagonal_rows/pallas_call | solution.py:411
  35.3 1.4 %copy-done = f32[4,24,48,128]{3,2,1,0:T(8,128)} copy-done((f32[4,24,48,128]{3,2,1,0:T(8,128)}, f32[4,24,48,128]{3,2,1,0:T(8,128)S(1)}, u32[]{:S(2)}) %copy-start) | copy-done | bytes 2359320
  36.8 4.6 %collective-permute-start.3 = (f32[4,4,32,128]{3,2,1,0:T(8,128)}, f32[4,4,32,128]{3,2,1,0:T(8,128)S(1)}, u32[]{:S(2)}, u32[]{:S(2)}) collective-permute-start(f32[4,4,32,128]{3,2,1,0:T(8,128)} %get-tuple-element.28), channel_id=1, source_target_pairs={{0,2},{2,4},{4,6},{1,3},{3,5},{5,7},{8,10},{10,12},{12,14},{9,11},... | collective-permute-start | bytes 786440 | tf_op jit(solution)/shard_map/ppermute | solution.py:419
  41.3 1.3 %collective-permute-start.4 = (f32[4,4,32,128]{3,2,1,0:T(8,128)}, f32[4,4,32,128]{3,2,1,0:T(8,128)S(1)}, u32[]{:S(2)}, u32[]{:S(2)}) collective-permute-start(f32[4,4,32,128]{3,2,1,0:T(8,128)} %get-tuple-element.29), channel_id=1, source_target_pairs={{2,0},{4,2},{6,4},{3,1},{5,3},{7,5},{10,8},{12,10},{14,12},{11,9},... | collective-permute-start | bytes 786440 | tf_op jit(solution)/shard_map/ppermute | solution.py:420
  42.6 0.1 pad_add_fusion.ends_ref
  42.7 0.8 collective-permute-done.2.high_ref
  43.6 3.4 %collective-permute-done.3.low_diagonal_ref = f32[4,4,32,128]{3,2,1,0:T(8,128)S(1)} collective-permute-done((f32[4,4,32,128]{3,2,1,0:T(8,128)}, f32[4,4,32,128]{3,2,1,0:T(8,128)S(1)}, u32[]{:S(2)}, u32[]{:S(2)}) %collective-permute-start.3) | collective-permute-done | bytes 262176 | tf_op jit(solution)/shard_map/ppermute | solution.py:419
  46.9 4.0 %collective-permute-done.4.high_diagonal_ref = f32[4,4,32,128]{3,2,1,0:T(8,128)S(1)} collective-permute-done((f32[4,4,32,128]{3,2,1,0:T(8,128)}, f32[4,4,32,128]{3,2,1,0:T(8,128)S(1)}, u32[]{:S(2)}, u32[]{:S(2)}) %collective-permute-start.4) | collective-permute-done | bytes 262176 | tf_op jit(solution)/shard_map/ppermute | solution.py:420
  50.9 1.7 %copy-done.1 = f32[4,24,48,128]{3,2,1,0:T(8,128)S(1)} copy-done((f32[4,24,48,128]{3,2,1,0:T(8,128)S(1)}, f32[4,24,48,128]{3,2,1,0:T(8,128)}, u32[]{:S(2)}) %copy-start.1) | copy-done | bytes 2359320
  52.6 7.9 %first_steps.1 = (f32[4,26,48,128]{3,2,1,0:T(8,128)S(1)}, f32[4,24,48,128]{3,2,1,0:T(8,128)S(1)}, f32[4,24,48,128]{3,2,1,0:T(8,128)S(1)}, f32[4,22,48,128]{3,2,1...) custom-call(s32[3]{0:T(128)S(1)} %pad_add_fusion.ends_ref, ...), custom_call_target="tpu_custom_call", output_to_operand_aliasing={{0}: (1, {}), {1}: (2, {})} | custom-call | tf_op jit(solution)/shard_map/first_steps/pallas_call | solution.py:423
  60.5 4.0 %collective-permute-start.5 = (f32[4,5,32,128]{3,2,1,0:T(8,128)S(1)}, f32[4,5,32,128]{3,2,1,0:T(8,128)S(1)}, u32[]{:S(2)}, u32[]{:S(2)}) collective-permute-start(f32[4,5,32,128]{3,2,1,0:T(8,128)S(1)} %get-tuple-element.38), channel_id=1, source_target_pairs={{0,2},{2,4},{4,6},{1,3},{3,5},{5,7},{8,10},{10,12},{12,14},{9,11},... | collective-permute-start | bytes 983048 | tf_op jit(solution)/shard_map/ppermute | solution.py:433
  64.5 1.3 %collective-permute-start.6 = (f32[4,5,32,128]{3,2,1,0:T(8,128)S(1)}, f32[4,5,32,128]{3,2,1,0:T(8,128)S(1)}, u32[]{:S(2)}, u32[]{:S(2)}) collective-permute-start(f32[4,5,32,128]{3,2,1,0:T(8,128)S(1)} %get-tuple-element.39), channel_id=1, source_target_pairs={{2,0},{4,2},{6,4},{3,1},{5,3},{7,5},{10,8},{12,10},{14,12},{11,9},... | collective-permute-start | bytes 983048 | tf_op jit(solution)/shard_map/ppermute | solution.py:434
  65.8 0.0 copy-start.2
  65.8 1.7 %middle_step.1 = (f32[4,24,48,128]{3,2,1,0:T(8,128)S(1)}, f32[4,8,128]{2,1,0:T(8,128)S(1)}) custom-call(f32[4,26,48,128]{3,2,1,0:T(8,128)S(1)} %get-tuple-element.30.c0_ref, f32[4,22,48,128]{3,2,1,0:T(8,128)S(1)} %get-tuple-element.31.c1_ref, f32[4,26,48,128]{3,2,1,0:T(8,128)S(1)} %get-tuple-element.32.c2_ref.c2_in, ...), custom_call_target="tpu_custom_call" | custom-call | flops 10485760 | bytes 6291456 | tf_op jit(solution)/shard_map/middle_step/pallas_call | solution.py:436
  67.6 10.5 %all_to_all.16.moments_ref = f32[4,8,128]{2,1,0:T(8,128)S(1)} all-to-all(f32[4,8,128]{2,1,0:T(8,128)S(1)} %get-tuple-element.34), channel_id=1, replica_groups=mesh['gx'=4,'gy'=4,'gz'=2] {'gy'}, dimensions={0} | all-to-all | bytes 32768 | tf_op jit(solution)/shard_map/all_to_all | solution.py:447
  78.1 8.4 %last_steps.1 = (f32[4,26,48,128]{3,2,1,0:T(8,128)S(1)}, f32[4,24,48,128]{3,2,1,0:T(8,128)S(1)}, f32[8,2,128,128]{3,2,1,0:T(8,128)S(1)}) custom-call(s32[3]{0:T(128)S(1)} %pad_add_fusion.ends_ref, f32[5,8]{1,0:T(8,128)S(1)} %copy-done.2, f32[4,8,128]{2,1,0:T(8,128)S(1)} %all_to_all.16.moments_ref, ...), custom_call_target="tpu_custom_call", output_to_operand_aliasing={{0}: (8, {}), {1}: (9, {})} | custom-call | tf_op jit(solution)/shard_map/last_steps/pallas_call | solution.py:450
  86.5 17.0 %all_to_all.17.parts_ref = f32[8,2,128,128]{3,2,1,0:T(8,128)S(1)} all-to-all(f32[8,2,128,128]{3,2,1,0:T(8,128)S(1)} %get-tuple-element.40), channel_id=1, replica_groups=mesh['gx'=4,'gy'=4,'gz'=2] {'gx','gz'}, dimensions={0} | all-to-all | bytes 2097152 | tf_op jit(solution)/shard_map/all_to_all | solution.py:463
  103.5 0.7 sum_probes.1
  (7 shorter events, 0.0 us)
Async XLA Ops:
  28.0 5.2 %collective-permute-start = (f32[8,128,128]{2,1,0:T(8,128)S(1)}, f32[8,128,128]{2,1,0:T(8,128)}, u32[]{:S(2)}, u32[]{:S(2)}) collective-permute-start(f32[8,128,128]{2,1,0:T(8,128)S(1)} %get-tuple-element.24.half_ref), channel_id=1, source_target_pairs={{0,8},{8,0},{16,24},{24,16},{1,9},{9,1},{17,25},{25,17},{2,10},{10... | collective-permute-start | bytes 1572872 | tf_op jit(solution)/shard_map/ppermute | solution.py:410
  28.4 14.4 %collective-permute-start.1 = (f32[4,5,32,128]{3,2,1,0:T(8,128)}, f32[4,5,32,128]{3,2,1,0:T(8,128)S(1)}, u32[]{:S(2)}, u32[]{:S(2)}) collective-permute-start(f32[4,5,32,128]{3,2,1,0:T(8,128)} %get-tuple-element.26), channel_id=1, source_target_pairs={{0,2},{2,4},{4,6},{1,3},{3,5},{5,7},{8,10},{10,12},{12,14},{9,11},... | collective-permute-start | bytes 983048 | tf_op jit(solution)/shard_map/ppermute | solution.py:408
  31.9 11.7 %collective-permute-start.2 = (f32[4,5,32,128]{3,2,1,0:T(8,128)}, f32[4,5,32,128]{3,2,1,0:T(8,128)}, u32[]{:S(2)}, u32[]{:S(2)}) collective-permute-start(f32[4,5,32,128]{3,2,1,0:T(8,128)} %get-tuple-element.27), channel_id=1, source_target_pairs={{2,0},{4,2},{6,4},{3,1},{5,3},{7,5},{10,8},{12,10},{14,12},{11,9},... | collective-permute-start | bytes 983048 | tf_op jit(solution)/shard_map/ppermute | solution.py:409
  35.3 1.4 %copy-start = (f32[4,24,48,128]{3,2,1,0:T(8,128)}, f32[4,24,48,128]{3,2,1,0:T(8,128)S(1)}, u32[]{:S(2)}) copy-start(f32[4,24,48,128]{3,2,1,0:T(8,128)S(1)} %get-tuple-element.25.diagonal_in) | copy-start | bytes 7077892
  36.8 10.2 %collective-permute-start.3 = (f32[4,4,32,128]{3,2,1,0:T(8,128)}, f32[4,4,32,128]{3,2,1,0:T(8,128)S(1)}, u32[]{:S(2)}, u32[]{:S(2)}) collective-permute-start(f32[4,4,32,128]{3,2,1,0:T(8,128)} %get-tuple-element.28), channel_id=1, source_target_pairs={{0,2},{2,4},{4,6},{1,3},{3,5},{5,7},{8,10},{10,12},{12,14},{9,11},... | collective-permute-start | bytes 786440 | tf_op jit(solution)/shard_map/ppermute | solution.py:419
  41.3 9.6 %collective-permute-start.4 = (f32[4,4,32,128]{3,2,1,0:T(8,128)}, f32[4,4,32,128]{3,2,1,0:T(8,128)S(1)}, u32[]{:S(2)}, u32[]{:S(2)}) collective-permute-start(f32[4,4,32,128]{3,2,1,0:T(8,128)} %get-tuple-element.29), channel_id=1, source_target_pairs={{2,0},{4,2},{6,4},{3,1},{5,3},{7,5},{10,8},{12,10},{14,12},{11,9},... | collective-permute-start | bytes 786440 | tf_op jit(solution)/shard_map/ppermute | solution.py:420
  50.9 1.7 %copy-start.1 = (f32[4,24,48,128]{3,2,1,0:T(8,128)S(1)}, f32[4,24,48,128]{3,2,1,0:T(8,128)}, u32[]{:S(2)}) copy-start(f32[4,24,48,128]{3,2,1,0:T(8,128)} %copy-done) | copy-start | bytes 7077892
  60.5 17.6 %collective-permute-start.5 = (f32[4,5,32,128]{3,2,1,0:T(8,128)S(1)}, f32[4,5,32,128]{3,2,1,0:T(8,128)S(1)}, u32[]{:S(2)}, u32[]{:S(2)}) collective-permute-start(f32[4,5,32,128]{3,2,1,0:T(8,128)S(1)} %get-tuple-element.38), channel_id=1, source_target_pairs={{0,2},{2,4},{4,6},{1,3},{3,5},{5,7},{8,10},{10,12},{12,14},{9,11},... | collective-permute-start | bytes 983048 | tf_op jit(solution)/shard_map/ppermute | solution.py:433
  64.5 13.5 %collective-permute-start.6 = (f32[4,5,32,128]{3,2,1,0:T(8,128)S(1)}, f32[4,5,32,128]{3,2,1,0:T(8,128)S(1)}, u32[]{:S(2)}, u32[]{:S(2)}) collective-permute-start(f32[4,5,32,128]{3,2,1,0:T(8,128)S(1)} %get-tuple-element.39), channel_id=1, source_target_pairs={{2,0},{4,2},{6,4},{3,1},{5,3},{7,5},{10,8},{12,10},{14,12},{11,9},... | collective-permute-start | bytes 983048 | tf_op jit(solution)/shard_map/ppermute | solution.py:434
  65.8 12.2 %copy-start.2 = (f32[5,8]{1,0:T(8,128)S(1)}, f32[5,8]{1,0:T(8,128)}, u32[]{:S(2)}) copy-start(f32[5,8]{1,0:T(8,128)} %weights_ref.1) | copy-start | bytes 484

commit v6 on v5

--- a/solution.py
+++ b/solution.py
@@ -80,41 +80,55 @@
     return lane == 0, lane == 127
 
 
-def stencil_tiles(source, diagonal, row, x, masks):
+def stencil_block(source, diagonal, row, rows, x, masks):
     columns = range(source.columns)
-    centre = [source.load(c, row, x) for c in columns]
-    after = [pltpu.roll(value, 1, 1) for value in centre]
-    before = [pltpu.roll(value, 127, 1) for value in centre]
+    centre = {(r, c): source.load(c, row + r, x) for r in range(-1, rows + 1) for c in columns}
     results = []
-    for c in columns:
-        low = after[c - 1] if c else 0.0
-        high = before[c + 1] if c + 1 < source.columns else 0.0
-        total = jnp.where(masks[0], low, after[c]) + jnp.where(masks[1], high, before[c])
-        total = total + (source.load(c, row, x - 1) + source.load(c, row, x + 1))
-        total = total + (source.load(c, row - 1, x) + source.load(c, row + 1, x))
-        results.append(diagonal.load(c, row, x) * centre[c] - total)
+    for r in range(rows):
+        after = [pltpu.roll(centre[r, c], 1, 1) for c in columns]
+        before = [pltpu.roll(centre[r, c], 127, 1) for c in columns]
+        for c in columns:
+            low = after[c - 1] if c else 0.0
+            high = before[c + 1] if c + 1 < source.columns else 0.0
+            total = jnp.where(masks[0], low, after[c]) + jnp.where(masks[1], high, before[c])
+            total = total + (source.load(c, row + r, x - 1) + source.load(c, row + r, x + 1))
+            total = total + (centre[r - 1, c] + centre[r + 1, c])
+            value = diagonal.load(c, row + r, x) * centre[r, c] - total
+            results.append((c, row + r, value))
     return results
 
 
-def apply_rows(target, source, diagonal, first, count, minus=None, unroll=2):
+def apply_block(target, source, diagonal, row, rows, minus, masks):
+    for x in range(0, source.cells, 8):
+        results = stencil_block(source, diagonal, row, rows, x, masks)
+        if minus is not None:
+            results = [(c, r, value - SHIFT * minus.load(c, r, x)) for c, r, value in results]
+        for c, r, value in results:
+            target.store(c, r, x, value)
+
+
+def apply_rows(target, source, diagonal, first, count, minus=None, block=4):
     masks = lane_masks()
 
     def body(step, carry):
-        results = []
-        for offset in range(unroll):
-            row = step * unroll + (first + offset)
-            for x in range(0, source.cells, 8):
-                values = stencil_tiles(source, diagonal, row, x, masks)
-                for c, value in enumerate(values):
-                    if minus is not None:
-                        value = value - SHIFT * minus.load(c, row, x)
-                    results.append((c, row, x, value))
-        for result in results:
-            target.store(*result)
+        apply_block(target, source, diagonal, step * block + first, block, minus, masks)
         return carry
 
-    assert count % unroll == 0
-    lax.fori_loop(0, count // unroll, body, 0)
+    lax.fori_loop(0, count // block, body, 0)
+    if count % block:
+        start = first + count - count % block
+        apply_block(target, source, diagonal, start, count % block, minus, masks)
+
+
+def apply_strips(target, source, diagonal, own, halo, minus=None):
+    masks = lane_masks()
+
+    def body(step, carry):
+        row = step * (own - HALO + 2 * halo) - halo
+        apply_block(target, source, diagonal, row, HALO, minus, masks)
+        return carry
+
+    lax.fori_loop(0, 2, body, 0)
 
 
 def clear_outside(ends_ref, own, field):
@@ -202,9 +216,25 @@
                 field.store(c, own + y, x, high_ref[c, y, pl.ds(x, 8), :])
 
 
+def inner_kernel(own, c0_ref, diagonal_ref, d0_ref, c1_ref, d1_ref, c2_ref):
+    c0 = Field(c0_ref, HALO)
+    diagonal = Field(diagonal_ref, DIAGONAL_HALO)
+    d0 = Field(d0_ref, 4)
+    c1 = Field(c1_ref, 3)
+    d1 = Field(d1_ref, 2)
+    c2 = Field(c2_ref, HALO)
+    for field in (d0, c1, d1, c2):
+        field.clear_pads()
+    apply_rows(d0, c0, diagonal, 1, own - 2)
+    apply_rows(c1, d0, diagonal, 2, own - 4, c0)
+    apply_rows(d1, c1, diagonal, 3, own - 6)
+    apply_rows(c2, d1, diagonal, 4, own - 8, c1)
+
+
 def first_kernel(
     own,
-    ends_ref, c0_in, diagonal_in, low_ref, high_ref, low_diagonal_ref, high_diagonal_ref,
+    ends_ref, c0_in, diagonal_in, d0_in, c1_in, d1_in, c2_in,
+    low_ref, high_ref, low_diagonal_ref, high_diagonal_ref,
     c0_ref, diagonal_ref, d0_ref, c1_ref, d1_ref, c2_ref, up_ref, down_ref,
 ):
     c0 = Field(c0_ref, HALO)
@@ -213,15 +243,16 @@
     c1 = Field(c1_ref, 3)
     d1 = Field(d1_ref, 2)
     c2 = Field(c2_ref, HALO)
-    for field in (d0, c1, d1, c2):
-        field.clear_pads()
     fill_halo(c0, own, low_ref, high_ref)
     fill_halo(diagonal, own, low_diagonal_ref, high_diagonal_ref)
-    steps = functools.partial(apply_steps, ends_ref, own)
-    steps(d0, c0, diagonal, 4)
-    steps(c1, d0, diagonal, 3, c0)
-    steps(d1, c1, diagonal, 2)
-    steps(c2, d1, diagonal, 1, c1)
+    apply_strips(d0, c0, diagonal, own, 4)
+    clear_outside(ends_ref, own, d0)
+    apply_strips(c1, d0, diagonal, own, 3, c0)
+    clear_outside(ends_ref, own, c1)
+    apply_strips(d1, c1, diagonal, own, 2)
+    clear_outside(ends_ref, own, d1)
+    apply_strips(c2, d1, diagonal, own, 1, c1)
+    clear_outside(ends_ref, own, c2)
     for c in range(c2.columns):
         for y in range(HALO):
             for x in range(0, c2.cells, 8):
@@ -249,15 +280,13 @@
     zero = jnp.zeros((8, 128), jnp.float32)
     sums = lax.fori_loop(0, own, moment_row, (zero,) * 6)
     sums = [jnp.sum(total, axis=0, keepdims=True) for total in sums]
-    sums = jnp.concatenate(sums + [zero[:2]], axis=0)
-    for part in range(moments_ref.shape[0]):
-        moments_ref[part] = sums
-
-
-def moment_slopes(inverse_count, probe, weights_ref, moments_ref):
-    total = moments_ref[0]
-    for part in range(1, moments_ref.shape[0]):
-        total = total + moments_ref[part]
+    moments_ref[...] = jnp.concatenate(sums + [zero[:2]], axis=0)
+
+
+def moment_slopes(inverse_count, probe, weights_ref, moment_refs):
+    total = moment_refs[0][...]
+    for ref in moment_refs[1:]:
+        total = total + ref[...]
     total = jnp.sum(total, axis=1, keepdims=True) * inverse_count
     raw = [jnp.broadcast_to(total[k : k + 1], (8, 128)) for k in range(6)]
     moments = tuple(raw[:5]) + (raw[5] - SHIFT * raw[4],)
@@ -267,13 +296,36 @@
     return [slope[0, 0] for slope in slopes]
 
 
+def third_kernel(
+    own,
+    ends_ref, diagonal_ref, c2_in, d2_in, low_ref, high_ref,
+    c2_ref, d2_ref, c3_ref, d3_ref, c4_ref,
+):
+    diagonal = Field(diagonal_ref, DIAGONAL_HALO)
+    c2 = Field(c2_ref, HALO)
+    d2 = Field(d2_ref, 4)
+    c3 = Field(c3_ref, 3)
+    d3 = Field(d3_ref, 2)
+    c4 = Field(c4_ref, 1)
+    for field in (c3, d3, c4):
+        field.clear_pads()
+    fill_halo(c2, own, low_ref, high_ref)
+    apply_rows(d2, c2, diagonal, -4, 4)
+    apply_rows(d2, c2, diagonal, own, 4)
+    clear_outside(ends_ref, own, d2)
+    steps = functools.partial(apply_steps, ends_ref, own)
+    steps(c3, d2, diagonal, 3, c2)
+    steps(d3, c3, diagonal, 2)
+    steps(c4, d3, diagonal, 1, c3)
+
+
 def last_kernel(
     grid, inverse_count,
-    ends_ref, weights_ref, moments_ref, c0_ref, diagonal_ref, d0_ref, c1_ref, d1_ref,
-    c2_in, d2_in, low_ref, high_ref,
-    c2_ref, d2_ref, out_ref, c3_ref, d3_ref, c4_ref,
+    ends_ref, weights_ref, c0_ref, diagonal_ref, d0_ref, c1_ref, d1_ref,
+    c2_ref, d2_ref, c3_ref, d3_ref, c4_ref, *rest,
 ):
     nx, nz, bx, by, bz = grid
+    moment_refs, out_ref = rest[:-1], rest[-1]
     c0 = Field(c0_ref, HALO)
     diagonal = Field(diagonal_ref, DIAGONAL_HALO)
     d0 = Field(d0_ref, 4)
@@ -284,28 +336,18 @@
     c3 = Field(c3_ref, 3)
     d3 = Field(d3_ref, 2)
     c4 = Field(c4_ref, 1)
-    for field in (c3, d3, c4):
-        field.clear_pads()
-    slopes = moment_slopes(inverse_count, ends_ref[2], weights_ref, moments_ref)
-    fill_halo(c2, by, low_ref, high_ref)
-    apply_rows(d2, c2, diagonal, -4, 4)
-    apply_rows(d2, c2, diagonal, by, 4)
-    clear_outside(ends_ref, by, d2)
-    steps = functools.partial(apply_steps, ends_ref, by)
-    steps(c3, d2, diagonal, 3, c2)
-    steps(d3, c3, diagonal, 2)
-    steps(c4, d3, diagonal, 1, c3)
+    slopes = moment_slopes(inverse_count, ends_ref[2], weights_ref, moment_refs)
     masks = lane_masks()
     place = {(x, z): (s, column) for s, column, x, z in places(grid)}
-
-    def out_row(step, carry):
-        row = step
-        results = []
+    block = 2
+
+    def out_rows(step, carry):
+        row = step * block
         for x in range(0, c4.cells, 8):
-            last = stencil_tiles(c4, diagonal, row, x, masks)
-            for z in range(c4.columns):
-                cs = [field.load(z, row, x) for field in (c0, c1, c2, c3, c4)]
-                ds = [field.load(z, row, x) for field in (d0, d1, d2, d3)] + [last[z]]
+            results = []
+            for z, at, d4 in stencil_block(c4, diagonal, row, block, x, masks):
+                cs = [field.load(z, at, x) for field in (c0, c1, c2, c3, c4)]
+                ds = [field.load(z, at, x) for field in (d0, d1, d2, d3)] + [d4]
                 total = None
                 for i in range(5):
                     inner = None
@@ -314,12 +356,12 @@
                         inner = term if inner is None else inner + term
                     term = cs[i] * inner
                     total = term if total is None else total + term
-                results.append(place[x, z] + (total,))
-        for s, column, total in results:
-            out_ref[s, column, pl.ds(step, bx, stride=by), :] = total
+                results.append(place[x, z] + (at, total))
+            for s, column, at, total in results:
+                out_ref[s, column, pl.ds(at, bx, stride=by), :] = total
         return carry
 
-    lax.fori_loop(0, by, out_row, 0)
+    lax.fori_loop(0, by // block, out_rows, 0)
 
 
 def sum_kernel(grid, count, parts_ref, out_ref):
@@ -358,7 +400,7 @@
 
 
 def params():
-    return pltpu.CompilerParams(vmem_limit_bytes=24 * MIB)
+    return pltpu.CompilerParams(vmem_limit_bytes=12 * MIB)
 
 
 def body(probes, kappa2, cotangents):
@@ -419,46 +461,69 @@
     low_diagonal = lax.ppermute(up_edge, "gy", up)
     high_diagonal = lax.ppermute(down_edge, "gy", down)
 
+    cells = by * X * columns * 128
+
+    def cost(operations):
+        return pl.CostEstimate(
+            flops=operations * cells, bytes_accessed=16 * cells, transcendentals=0
+        )
+
+    inner = pl.pallas_call(
+        functools.partial(inner_kernel, by),
+        out_shape=tuple(vector(h) for h in (4, 3, 2, HALO)),
+        in_specs=[vmem()] * 2,
+        out_specs=(vmem(),) * 4,
+        compiler_params=params(),
+        cost_estimate=cost(32),
+        name="inner_steps",
+    )(here(c0), here(diagonal))
     ends = jnp.stack([gy == 0, gy == ny - 1, mine]).astype(jnp.int32)
+    vectors = [here(value) for value in (c0, diagonal) + tuple(inner)]
     c0, diagonal, d0, c1, d1, c2, up_edge, down_edge = pl.pallas_call(
         functools.partial(first_kernel, by),
         out_shape=tuple(vector(h) for h in (HALO, DIAGONAL_HALO, 4, 3, 2, HALO))
         + (edge(HALO), edge(HALO)),
-        in_specs=[smem()] + [vmem()] * 6,
+        in_specs=[smem()] + [vmem()] * 10,
         out_specs=(vmem(),) * 8,
-        input_output_aliases={1: 0, 2: 1},
+        input_output_aliases={i + 1: i for i in range(6)},
         compiler_params=params(),
         name="first_steps",
-    )(ends, here(c0), here(diagonal), low1, high1, low_diagonal, high_diagonal)
+    )(ends, *vectors, low1, high1, low_diagonal, high_diagonal)
     low2 = lax.ppermute(up_edge, "gy", up)
     high2 = lax.ppermute(down_edge, "gy", down)
-    cells = by * X * columns * 128
     d2, moments = pl.pallas_call(
         functools.partial(middle_kernel, by),
-        out_shape=(vector(4), f32(ny, 8, 128)),
+        out_shape=(vector(4), f32(8, 128)),
         in_specs=[vmem()] * 4,
         out_specs=(vmem(),) * 2,
         compiler_params=params(),
-        cost_estimate=pl.CostEstimate(
-            flops=40 * cells, bytes_accessed=24 * cells, transcendentals=0
-        ),
+        cost_estimate=cost(24),
         name="middle_step",
     )(here(c0), here(c1), here(c2), here(diagonal))
-    moments = lax.all_to_all(moments, "gy", 0, 0, tiled=True)
-
-    inverse_count = 1.0 / (X * by * ny * columns * 128)
-    _, _, out = pl.pallas_call(
+    shares = [moments]
+    for step in range(1, ny):
+        shares.append(lax.ppermute(moments, "gy", [(i, (i + step) % ny) for i in range(ny)]))
+
+    c2, d2, c3, d3, c4 = pl.pallas_call(
+        functools.partial(third_kernel, by),
+        out_shape=tuple(vector(h) for h in (HALO, 4, 3, 2, 1)),
+        in_specs=[smem()] + [vmem()] * 5,
+        out_specs=(vmem(),) * 5,
+        input_output_aliases={2: 0, 3: 1},
+        compiler_params=params(),
+        cost_estimate=cost(40),
+        name="third_steps",
+    )(ends, here(diagonal), here(c2), here(d2), low2, high2)
+    inverse_count = 1.0 / (ny * cells)
+    vectors = [here(value) for value in (c0, diagonal, d0, c1, d1, c2, d2, c3, d3, c4)]
+    out = pl.pallas_call(
         functools.partial(last_kernel, grid, inverse_count),
-        out_shape=(vector(HALO), vector(4), f32(group, per, rows, 128)),
-        in_specs=[smem(), smem()] + [vmem()] * 10,
-        out_specs=(vmem(),) * 3,
-        scratch_shapes=[vector(h) for h in (3, 2, 1)],
-        input_output_aliases={8: 0, 9: 1},
-        compiler_params=params(),
-        name="last_steps",
-    )(
-        ends, cotangents, moments, *(here(x) for x in (c0, diagonal, d0, c1, d1, c2, d2)), low2, high2
-    )
+        out_shape=f32(group, per, rows, 128),
+        in_specs=[smem(), smem()] + [vmem()] * (10 + ny),
+        out_specs=vmem(),
+        compiler_params=params(),
+        name="last_step",
+    )(ends, cotangents, *vectors, *shares)
 
     out = lax.all_to_all(out, ("gx", "gz"), 0, 0, tiled=True)
     return pl.pallas_call(

time: 105 us -> 93.6 us (0.89)
  blocking collectives: 52.5 us -> 42.5 us
  starting transfers between devices: 16.3 us -> 21.6 us
  Pallas kernels: 23.8 us -> 20.2 us
  waiting for transfers between devices: 8.22 us -> 5.39 us
    all_to_all x1 -> x0, blocking collectives: 10.5 us -> none  [body(): moments = lax.all_to_all(moments, 'gy', 0, 0, tiled=True)]
    pallas_call x0 -> x2, Pallas kernels: none -> 7.63 us  [the longest x1 4.65 us: body(): pl.pallas_call(functools.partial(third_kernel, by), out_shape=tuple((vect...]
    ppermute x0 -> x3, starting transfers between devices: none -> 5.85 us  [body(): lax.ppermute(moments, 'gy', [(i, (i + step) % ny) for i in range(ny)])]
    pallas_call x1, Pallas kernels: 8.37 us -> 2.92 us  [body(): pl.pallas_call(functools.partial(last_kernel, grid, inverse_count), out_s...]
    pallas_call x1, Pallas kernels: 7.9 us -> 3.31 us  [body(): pl.pallas_call(functools.partial(first_kernel, by), out_shape=tuple((vect...]
    ppermute x1, waiting for transfers between devices: 3.36 us -> 0.01 us  [body(): low_diagonal = lax.ppermute(up_edge, 'gy', up)]
    ppermute x1, waiting for transfers between devices: 0.01 us -> 1.34 us  [body(): high2 = lax.ppermute(down_edge, 'gy', down)]
    ppermute x1, starting transfers between devices: 4.01 us -> 2.76 us  [body(): low2 = lax.ppermute(up_edge, 'gy', up)]
  transfers between devices with their start and end apart: 7 -> 10, of which waited for: 3 -> 2; matrix products, arithmetic and copies ran while one was open for 0% -> 0% of each run, Pallas kernels for 4% -> 11%
where the time goes in v6:
time: 93.6 us; the launch traced here: 93.2 us
  blocking collectives  42.5 us (45%)
  starting transfers between devices  21.6 us (23%)
  Pallas kernels  20.2 us (22%)
  waiting for transfers between devices  5.39 us (6%)
  local copies, waits for them, and re-layouts  3.21 us (3%)
    all_to_all x1, blocking collectives, body(): blocks = lax.all_to_all(blocks, ('gx', 'gz'), 0, 0, tiled=True)  25 us
    all_to_all x1, blocking collectives, body(): out = lax.all_to_all(out, ('gx', 'gz'), 0, 0, tiled=True)  17.4 us
    ppermute x3, starting transfers between devices, body(): lax.ppermute(moments, 'gy', [(i, (i + step) % ny) for i in range(ny)])  5.85 us
    pallas_call x1, Pallas kernels, body(): pl.pallas_call(functools.partial(third_kernel, by), out_shape=tuple((vect...  4.65 us
    ppermute x1, starting transfers between devices, body(): low_diagonal = lax.ppermute(up_edge, 'gy', up)  4.55 us
    ppermute x1, starting transfers between devices, body(): low1 = lax.ppermute(up_edge, 'gy', up)  4.23 us
    ppermute x1, waiting for transfers between devices, body(): high_diagonal = lax.ppermute(down_edge, 'gy', down)  4.03 us
    pallas_call x1, Pallas kernels, body(): pl.pallas_call(functools.partial(first_kernel, by), out_shape=tuple((vect...  3.31 us
  transfers between devices with their start and end apart: 10, of which 2 were waited for; matrix products, arithmetic and copies ran while one was open for 0% of the time, Pallas kernels for 11%

profile of v6, /device:TPU:0, one launch (start us, length us, event | category | flops | bytes accessed | tf_op | source)
XLA Modules:
  0.0 93.2 jit_solution(16670302795966541902)
XLA Ops:
  0.0 1.6 %pack.1 = f32[8,3,128,128]{3,2,1,0:T(8,128)S(1)} custom-call(f32[1024,256]{1,0:T(8,128)} %bitcast.6, f32[128,256]{1,0:T(8,128)} %bitcast.7), custom_call_target="tpu_custom_call" | custom-call | tf_op jit(solution)/shard_map/pack/pallas_call | solution.py:432
  1.6 25.0 %all_to_all.10.blocks_ref = f32[8,3,128,128]{3,2,1,0:T(8,128)S(1)} all-to-all(f32[8,3,128,128]{3,2,1,0:T(8,128)S(1)} %pack.1), channel_id=1, replica_groups=mesh['gx'=4,'gy'=4,'gz'=2] {'gx','gz'}, dimensions={0} | all-to-all | bytes 3145728 | tf_op jit(solution)/shard_map/all_to_all | solution.py:441
  26.7 1.3 %probe_rows.1 = (f32[4,26,48,128]{3,2,1,0:T(8,128)S(1)}, f32[4,5,32,128]{3,2,1,0:T(8,128)}, f32[4,5,32,128]{3,2,1,0:T(8,128)}, f32[8,128,128]{2,1,0:T(8,128)S(1)}) custom-call(f32[8,3,128,128]{3,2,1,0:T(8,128)S(1)} %all_to_all.10.blocks_ref), custom_call_target="tpu_custom_call" | custom-call | tf_op jit(solution)/shard_map/probe_rows/pallas_call | solution.py:442
  28.0 1.5 %copy-done = f32[4,26,48,128]{3,2,1,0:T(8,128)} copy-done((f32[4,26,48,128]{3,2,1,0:T(8,128)}, f32[4,26,48,128]{3,2,1,0:T(8,128)S(1)}, u32[]{:S(2)}) %copy-start) | copy-done | bytes 2555928
  29.8 4.2 %collective-permute-start.1 = (f32[4,5,32,128]{3,2,1,0:T(8,128)}, f32[4,5,32,128]{3,2,1,0:T(8,128)}, u32[]{:S(2)}, u32[]{:S(2)}) collective-permute-start(f32[4,5,32,128]{3,2,1,0:T(8,128)} %get-tuple-element.38), channel_id=1, source_target_pairs={{0,2},{2,4},{4,6},{1,3},{3,5},{5,7},{8,10},{10,12},{12,14},{9,11},... | collective-permute-start | bytes 983048 | tf_op jit(solution)/shard_map/ppermute | solution.py:450
  34.1 1.3 %collective-permute-start.2 = (f32[4,5,32,128]{3,2,1,0:T(8,128)}, f32[4,5,32,128]{3,2,1,0:T(8,128)}, u32[]{:S(2)}, u32[]{:S(2)}) collective-permute-start(f32[4,5,32,128]{3,2,1,0:T(8,128)} %get-tuple-element.39), channel_id=1, source_target_pairs={{2,0},{4,2},{6,4},{3,1},{5,3},{7,5},{10,8},{12,10},{14,12},{11,9},... | collective-permute-start | bytes 983048 | tf_op jit(solution)/shard_map/ppermute | solution.py:451
  35.4 1.1 %diagonal_rows.1 = (f32[4,24,48,128]{3,2,1,0:T(8,128)S(1)}, f32[4,4,32,128]{3,2,1,0:T(8,128)}, f32[4,4,32,128]{3,2,1,0:T(8,128)}) custom-call(s32[1]{0:T(128)} %bitcast.5.core_ref, f32[8,128,128]{2,1,0:T(8,128)S(1)} %get-tuple-element.32.half_ref, f32[8,128,128]{2,1,0:T(8,128)S(1)} %collective-permute-done.other_ref), custom_call_target="tpu_custom_call" | custom-call | tf_op jit(solution)/shard_map/diagonal_rows/pallas_call | solution.py:453
  36.5 4.6 %collective-permute-start.3 = (f32[4,4,32,128]{3,2,1,0:T(8,128)}, f32[4,4,32,128]{3,2,1,0:T(8,128)S(1)}, u32[]{:S(2)}, u32[]{:S(2)}) collective-permute-start(f32[4,4,32,128]{3,2,1,0:T(8,128)} %get-tuple-element.40), channel_id=1, source_target_pairs={{0,2},{2,4},{4,6},{1,3},{3,5},{5,7},{8,10},{10,12},{12,14},{9,11},... | collective-permute-start | bytes 786440 | tf_op jit(solution)/shard_map/ppermute | solution.py:461
  41.1 1.3 %collective-permute-start.4 = (f32[4,4,32,128]{3,2,1,0:T(8,128)}, f32[4,4,32,128]{3,2,1,0:T(8,128)S(1)}, u32[]{:S(2)}, u32[]{:S(2)}) collective-permute-start(f32[4,4,32,128]{3,2,1,0:T(8,128)} %get-tuple-element.41), channel_id=1, source_target_pairs={{2,0},{4,2},{6,4},{3,1},{5,3},{7,5},{10,8},{12,10},{14,12},{11,9},... | collective-permute-start | bytes 786440 | tf_op jit(solution)/shard_map/ppermute | solution.py:462
  42.5 1.7 %copy-done.1 = f32[4,26,48,128]{3,2,1,0:T(8,128)S(1)} copy-done((f32[4,26,48,128]{3,2,1,0:T(8,128)S(1)}, f32[4,26,48,128]{3,2,1,0:T(8,128)}, u32[]{:S(2)}) %copy-start.1) | copy-done | bytes 2555928
  44.2 3.0 %inner_steps.1 = (f32[4,24,48,128]{3,2,1,0:T(8,128)S(1)}, f32[4,22,48,128]{3,2,1,0:T(8,128)S(1)}, f32[4,20,48,128]{3,2,1,0:T(8,128)S(1)}, f32[4,26,48,128]{3,2,1,0:T(8,128)S(1)}) custom-call(f32[4,26,48,128]{3,2,1,0:T(8,128)S(1)} %copy-done.1, f32[4,24,48,128]{3,2,1,0:T(8,128)S(1)} %get-tuple-element.33.diagonal_ref.diagonal_in), custom_call_target="tpu_custom_call" | custom-call | flops 8388608 | bytes 4194304 | tf_op jit(solution)/shard_map/inner_steps/pallas_call | solution.py:471
  47.2 4.0 %collective-permute-done.4.high_diagonal_ref = f32[4,4,32,128]{3,2,1,0:T(8,128)S(1)} collective-permute-done((f32[4,4,32,128]{3,2,1,0:T(8,128)}, f32[4,4,32,128]{3,2,1,0:T(8,128)S(1)}, u32[]{:S(2)}, u32[]{:S(2)}) %collective-permute-start.4) | collective-permute-done | bytes 262176 | tf_op jit(solution)/shard_map/ppermute | solution.py:462
  51.3 3.3 %first_steps.1 = (f32[4,26,48,128]{3,2,1,0:T(8,128)S(1)}, f32[4,24,48,128]{3,2,1,0:T(8,128)S(1)}, f32[4,24,48,128]{3,2,1,0:T(8,128)S(1)}, f32[4,22,48,128]{3,2,1...) custom-call(s32[3]{0:T(128)S(1)} %pad_add_fusion.ends_ref, ...), custom_call_target="tpu_custom_call", output_to_operand_aliasing={{0}: (1, {}), {1}: (2, {}), {2}: (3, {}), {3}: (4, {}), {4}... | custom-call | tf_op jit(solution)/shard_map/first_steps/pallas_call | solution.py:482
  54.6 2.8 %collective-permute-start.5 = (f32[4,5,32,128]{3,2,1,0:T(8,128)S(1)}, f32[4,5,32,128]{3,2,1,0:T(8,128)S(1)}, u32[]{:S(2)}, u32[]{:S(2)}) collective-permute-start(f32[4,5,32,128]{3,2,1,0:T(8,128)S(1)} %get-tuple-element.49), channel_id=1, source_target_pairs={{0,2},{2,4},{4,6},{1,3},{3,5},{5,7},{8,10},{10,12},{12,14},{9,11},... | collective-permute-start | bytes 983048 | tf_op jit(solution)/shard_map/ppermute | solution.py:492
  57.3 1.3 %collective-permute-start.6 = (f32[4,5,32,128]{3,2,1,0:T(8,128)S(1)}, f32[4,5,32,128]{3,2,1,0:T(8,128)S(1)}, u32[]{:S(2)}, u32[]{:S(2)}) collective-permute-start(f32[4,5,32,128]{3,2,1,0:T(8,128)S(1)} %get-tuple-element.50), channel_id=1, source_target_pairs={{2,0},{4,2},{6,4},{3,1},{5,3},{7,5},{10,8},{12,10},{14,12},{11,9},... | collective-permute-start | bytes 983048 | tf_op jit(solution)/shard_map/ppermute | solution.py:493
  58.6 1.6 %middle_step.1 = (f32[4,24,48,128]{3,2,1,0:T(8,128)S(1)}, f32[8,128]{1,0:T(8,128)S(1)}) custom-call(f32[4,26,48,128]{3,2,1,0:T(8,128)S(1)} %get-tuple-element.42.c0_ref, f32[4,22,48,128]{3,2,1,0:T(8,128)S(1)} %get-tuple-element.45.c1_ref, f32[4,26,48,128]{3,2,1,0:T(8,128)S(1)} %get-tuple-element.47.c2_ref.c2_in, ...), custom_call_target="tpu_custom_call" | custom-call | flops 6291456 | bytes 4194304 | tf_op jit(solution)/shard_map/middle_step/pallas_call | solution.py:494
  60.2 3.3 %collective-permute-start.9 = (f32[8,128]{1,0:T(8,128)S(1)}, f32[8,128]{1,0:T(8,128)S(1)}, u32[]{:S(2)}, u32[]{:S(2)}) collective-permute-start(f32[8,128]{1,0:T(8,128)S(1)} %get-tuple-element.56.rest_0_), channel_id=1, source_target_pairs={{0,6},{2,0},{4,2},{6,4},{1,7},{3,1},{5,3},{7,5},{8,14},{10,8},{12,... | collective-permute-start | bytes 12296 | tf_op jit(solution)/shard_map/ppermute | solution.py:505
  63.5 0.9 collective-permute-start.8
  64.4 1.7 %collective-permute-start.7 = (f32[8,128]{1,0:T(8,128)S(1)}, f32[8,128]{1,0:T(8,128)S(1)}, u32[]{:S(2)}, u32[]{:S(2)}) collective-permute-start(f32[8,128]{1,0:T(8,128)S(1)} %get-tuple-element.56.rest_0_), channel_id=1, source_target_pairs={{0,2},{2,4},{4,6},{6,0},{1,3},{3,5},{5,7},{7,1},{8,10},{10,12},{12... | collective-permute-start | bytes 12296 | tf_op jit(solution)/shard_map/ppermute | solution.py:505
  66.1 1.3 %collective-permute-done.6.high_ref = f32[4,5,32,128]{3,2,1,0:T(8,128)S(1)} collective-permute-done((f32[4,5,32,128]{3,2,1,0:T(8,128)S(1)}, f32[4,5,32,128]{3,2,1,0:T(8,128)S(1)}, u32[]{:S(2)}, u32[]{:S(2)}) %collective-permute-start.6) | collective-permute-done | bytes 327712 | tf_op jit(solution)/shard_map/ppermute | solution.py:493
  67.4 4.6 %third_steps.1 = (f32[4,26,48,128]{3,2,1,0:T(8,128)S(1)}, f32[4,24,48,128]{3,2,1,0:T(8,128)S(1)}, f32[4,22,48,128]{3,2,1,0:T(8,128)S(1)}, f32[4,20,48,128]{3,2,1,0:T(8,128)S(1)}, f32[4,18,48,128]{3,2,1,0:T(8,128)S(1)}) custom-call(s32[3]{0:T(128)S(1)} %pad_add_fusion.ends_ref, ...), custom_call_target="tpu_custom_call", output_to_operand_aliasing={{0}: (2, {}), {1}: (3, {})} | custom-call | flops 10485760 | bytes 4194304 | tf_op jit(solution)/shard_map/third_steps/pallas_call | solution.py:507
  72.1 2.9 %last_step.1 = f32[8,2,128,128]{3,2,1,0:T(8,128)S(1)} custom-call(s32[3]{0:T(128)S(1)} %pad_add_fusion.ends_ref, f32[5,8]{1,0:T(8,128)S(1)} %copy-done.4, f32[4,26,48,128]{3,2,1,0:T(8,128)S(1)} %copy-done.3, f32[4,24,48,128]{3,2,1,0:T(8,128)S(1)} %get-tuple-element.43.diagonal_ref, f32[4,24,48,128]{3,2,1,0:T(8,128)S(1)} %get-tuple-element.44.d0_ref, ...), custom_call_target="tpu_custom_call" | custom-call | tf_op jit(solution)/shard_map/last_step/pallas_call | solution.py:519
  75.0 17.4 %all_to_all.11.parts_ref = f32[8,2,128,128]{3,2,1,0:T(8,128)S(1)} all-to-all(f32[8,2,128,128]{3,2,1,0:T(8,128)S(1)} %last_step.1), channel_id=1, replica_groups=mesh['gx'=4,'gy'=4,'gz'=2] {'gx','gz'}, dimensions={0} | all-to-all | bytes 2097152 | tf_op jit(solution)/shard_map/all_to_all | solution.py:528
  92.5 0.7 sum_probes.1
  (18 shorter events, 0.5 us)
Async XLA Ops:
  28.0 1.5 %copy-start = (f32[4,26,48,128]{3,2,1,0:T(8,128)}, f32[4,26,48,128]{3,2,1,0:T(8,128)S(1)}, u32[]{:S(2)}) copy-start(f32[4,26,48,128]{3,2,1,0:T(8,128)S(1)} %get-tuple-element.31.c0_ref.c0_in) | copy-start | bytes 7667716
  29.5 5.9 %collective-permute-start = (f32[8,128,128]{2,1,0:T(8,128)S(1)}, f32[8,128,128]{2,1,0:T(8,128)S(1)}, u32[]{:S(2)}, u32[]{:S(2)}) collective-permute-start(f32[8,128,128]{2,1,0:T(8,128)S(1)} %get-tuple-element.32.half_ref), channel_id=1, source_target_pairs={{0,8},{8,0},{16,24},{24,16},{1,9},{9,1},{17,25},{25,17},{2,10},{10... | collective-permute-start | bytes 1572872 | tf_op jit(solution)/shard_map/ppermute | solution.py:452
  29.8 17.4 %collective-permute-start.1 = (f32[4,5,32,128]{3,2,1,0:T(8,128)}, f32[4,5,32,128]{3,2,1,0:T(8,128)}, u32[]{:S(2)}, u32[]{:S(2)}) collective-permute-start(f32[4,5,32,128]{3,2,1,0:T(8,128)} %get-tuple-element.38), channel_id=1, source_target_pairs={{0,2},{2,4},{4,6},{1,3},{3,5},{5,7},{8,10},{10,12},{12,14},{9,11},... | collective-permute-start | bytes 983048 | tf_op jit(solution)/shard_map/ppermute | solution.py:450
  34.1 13.1 %collective-permute-start.2 = (f32[4,5,32,128]{3,2,1,0:T(8,128)}, f32[4,5,32,128]{3,2,1,0:T(8,128)}, u32[]{:S(2)}, u32[]{:S(2)}) collective-permute-start(f32[4,5,32,128]{3,2,1,0:T(8,128)} %get-tuple-element.39), channel_id=1, source_target_pairs={{2,0},{4,2},{6,4},{3,1},{5,3},{7,5},{10,8},{12,10},{14,12},{11,9},... | collective-permute-start | bytes 983048 | tf_op jit(solution)/shard_map/ppermute | solution.py:451
  36.5 10.7 %collective-permute-start.3 = (f32[4,4,32,128]{3,2,1,0:T(8,128)}, f32[4,4,32,128]{3,2,1,0:T(8,128)S(1)}, u32[]{:S(2)}, u32[]{:S(2)}) collective-permute-start(f32[4,4,32,128]{3,2,1,0:T(8,128)} %get-tuple-element.40), channel_id=1, source_target_pairs={{0,2},{2,4},{4,6},{1,3},{3,5},{5,7},{8,10},{10,12},{12,14},{9,11},... | collective-permute-start | bytes 786440 | tf_op jit(solution)/shard_map/ppermute | solution.py:461
  41.1 10.2 %collective-permute-start.4 = (f32[4,4,32,128]{3,2,1,0:T(8,128)}, f32[4,4,32,128]{3,2,1,0:T(8,128)S(1)}, u32[]{:S(2)}, u32[]{:S(2)}) collective-permute-start(f32[4,4,32,128]{3,2,1,0:T(8,128)} %get-tuple-element.41), channel_id=1, source_target_pairs={{2,0},{4,2},{6,4},{3,1},{5,3},{7,5},{10,8},{12,10},{14,12},{11,9},... | collective-permute-start | bytes 786440 | tf_op jit(solution)/shard_map/ppermute | solution.py:462
  42.5 1.7 %copy-start.1 = (f32[4,26,48,128]{3,2,1,0:T(8,128)S(1)}, f32[4,26,48,128]{3,2,1,0:T(8,128)}, u32[]{:S(2)}) copy-start(f32[4,26,48,128]{3,2,1,0:T(8,128)} %copy-done) | copy-start | bytes 7667716
  54.6 5.6 %copy-start.2 = (f32[4,26,48,128]{3,2,1,0:T(8,128)}, f32[4,26,48,128]{3,2,1,0:T(8,128)S(1)}, u32[]{:S(2)}) copy-start(f32[4,26,48,128]{3,2,1,0:T(8,128)S(1)} %get-tuple-element.42.c0_ref) | copy-start | bytes 7667716
  54.6 11.5 %collective-permute-start.5 = (f32[4,5,32,128]{3,2,1,0:T(8,128)S(1)}, f32[4,5,32,128]{3,2,1,0:T(8,128)S(1)}, u32[]{:S(2)}, u32[]{:S(2)}) collective-permute-start(f32[4,5,32,128]{3,2,1,0:T(8,128)S(1)} %get-tuple-element.49), channel_id=1, source_target_pairs={{0,2},{2,4},{4,6},{1,3},{3,5},{5,7},{8,10},{10,12},{12,14},{9,11},... | collective-permute-start | bytes 983048 | tf_op jit(solution)/shard_map/ppermute | solution.py:492
  57.3 10.1 %collective-permute-start.6 = (f32[4,5,32,128]{3,2,1,0:T(8,128)S(1)}, f32[4,5,32,128]{3,2,1,0:T(8,128)S(1)}, u32[]{:S(2)}, u32[]{:S(2)}) collective-permute-start(f32[4,5,32,128]{3,2,1,0:T(8,128)S(1)} %get-tuple-element.50), channel_id=1, source_target_pairs={{2,0},{4,2},{6,4},{3,1},{5,3},{7,5},{10,8},{12,10},{14,12},{11,9},... | collective-permute-start | bytes 983048 | tf_op jit(solution)/shard_map/ppermute | solution.py:493
  60.2 11.9 %collective-permute-start.9 = (f32[8,128]{1,0:T(8,128)S(1)}, f32[8,128]{1,0:T(8,128)S(1)}, u32[]{:S(2)}, u32[]{:S(2)}) collective-permute-start(f32[8,128]{1,0:T(8,128)S(1)} %get-tuple-element.56.rest_0_), channel_id=1, source_target_pairs={{0,6},{2,0},{4,2},{6,4},{1,7},{3,1},{5,3},{7,5},{8,14},{10,8},{12,... | collective-permute-start | bytes 12296 | tf_op jit(solution)/shard_map/ppermute | solution.py:505
  63.5 8.6 %collective-permute-start.8 = (f32[8,128]{1,0:T(8,128)S(1)}, f32[8,128]{1,0:T(8,128)S(1)}, u32[]{:S(2)}, u32[]{:S(2)}) collective-permute-start(f32[8,128]{1,0:T(8,128)S(1)} %get-tuple-element.56.rest_0_), channel_id=1, source_target_pairs={{0,4},{2,6},{4,0},{6,2},{1,5},{3,7},{5,1},{7,3},{8,12},{10,14},{12... | collective-permute-start | bytes 12296 | tf_op jit(solution)/shard_map/ppermute | solution.py:505
  64.4 7.7 %collective-permute-start.7 = (f32[8,128]{1,0:T(8,128)S(1)}, f32[8,128]{1,0:T(8,128)S(1)}, u32[]{:S(2)}, u32[]{:S(2)}) collective-permute-start(f32[8,128]{1,0:T(8,128)S(1)} %get-tuple-element.56.rest_0_), channel_id=1, source_target_pairs={{0,2},{2,4},{4,6},{6,0},{1,3},{3,5},{5,7},{7,1},{8,10},{10,12},{12... | collective-permute-start | bytes 12296 | tf_op jit(solution)/shard_map/ppermute | solution.py:505
  67.4 4.7 %copy-start.3 = (f32[4,26,48,128]{3,2,1,0:T(8,128)S(1)}, f32[4,26,48,128]{3,2,1,0:T(8,128)}, u32[]{:S(2)}) copy-start(f32[4,26,48,128]{3,2,1,0:T(8,128)} %copy-done.2) | copy-start | bytes 7667716
  67.4 4.7 %copy-start.4 = (f32[5,8]{1,0:T(8,128)S(1)}, f32[5,8]{1,0:T(8,128)}, u32[]{:S(2)}) copy-start(f32[5,8]{1,0:T(8,128)} %weights_ref.1) | copy-start | bytes 484

commit v7 on v6

--- a/solution.py
+++ b/solution.py
@@ -174,26 +174,28 @@
         copy.wait()
 
 
-def probe_kernel(grid, blocks_ref, own_ref, up_ref, down_ref, half_ref):
+def half_kernel(blocks_ref, half_ref):
+    half_ref[...] = blocks_ref[:, blocks_ref.shape[1] - 1]
+
+
+def edge_kernel(grid, blocks_ref, up_ref, down_ref):
     nx, nz, bx, by, bz = grid
-    per = bz // 128
-    own = Field(own_ref, HALO)
-    own.clear_pads()
     for s, column, x, z in places(grid):
-        values = [blocks_ref[s, column, pl.ds(y, bx, stride=by), :] for y in range(by)]
-        for y in range(by):
-            own.store(z, y, x, values[y])
+        rows = list(range(HALO)) + list(range(by - HALO, by))
+        values = [blocks_ref[s, column, pl.ds(y, bx, stride=by), :] for y in rows]
         for y in range(HALO):
             down_ref[z, y, pl.ds(x, bx), :] = values[y]
-            up_ref[z, y, pl.ds(x, bx), :] = values[by - HALO + y]
-    for s in range(nx * nz):
-        half_ref[s] = blocks_ref[s, per]
-
-
-def diagonal_kernel(grid, core_ref, half_ref, other_ref, own_ref, up_ref, down_ref):
+            up_ref[z, y, pl.ds(x, bx), :] = values[HALO + y]
+
+
+def diagonal_kernel(
+    grid, core_ref, half_ref, other_ref, up_in, down_in, own_ref, up_ref, down_ref
+):
     nx, nz, bx, by, bz = grid
     own = Field(own_ref, DIAGONAL_HALO)
     first = core_ref[0] == 0
+    up_ref[:, pl.ds(0, HALO)] = up_in[...]
+    down_ref[:, pl.ds(0, HALO)] = down_in[...]
     for s, column, x, z in places(grid):
         values = []
         for y in range(by):
@@ -204,27 +206,32 @@
         for y in range(by):
             own.store(z, y, x, values[y])
         for y in range(DIAGONAL_HALO):
-            down_ref[z, y, pl.ds(x, bx), :] = values[y]
-            up_ref[z, y, pl.ds(x, bx), :] = values[by - DIAGONAL_HALO + y]
-
-
-def fill_halo(field, own, low_ref, high_ref):
+            down_ref[z, HALO + y, pl.ds(x, bx), :] = values[y]
+            up_ref[z, HALO + y, pl.ds(x, bx), :] = values[by - DIAGONAL_HALO + y]
+
+
+def fill_halo(field, own, low_ref, high_ref, start=0):
     for c in range(field.columns):
         for y in range(field.halo):
             for x in range(0, field.cells, 8):
-                field.store(c, y - field.halo, x, low_ref[c, y, pl.ds(x, 8), :])
-                field.store(c, own + y, x, high_ref[c, y, pl.ds(x, 8), :])
-
-
-def inner_kernel(own, c0_ref, diagonal_ref, d0_ref, c1_ref, d1_ref, c2_ref):
+                field.store(c, y - field.halo, x, low_ref[c, start + y, pl.ds(x, 8), :])
+                field.store(c, own + y, x, high_ref[c, start + y, pl.ds(x, 8), :])
+
+
+def inner_kernel(grid, blocks_ref, diagonal_ref, c0_ref, d0_ref, c1_ref, d1_ref, c2_ref):
+    nx, nz, bx, own, bz = grid
     c0 = Field(c0_ref, HALO)
     diagonal = Field(diagonal_ref, DIAGONAL_HALO)
     d0 = Field(d0_ref, 4)
     c1 = Field(c1_ref, 3)
     d1 = Field(d1_ref, 2)
     c2 = Field(c2_ref, HALO)
-    for field in (d0, c1, d1, c2):
+    for field in (c0, d0, c1, d1, c2):
         field.clear_pads()
+    for s, column, x, z in places(grid):
+        values = [blocks_ref[s, column, pl.ds(y, bx, stride=own), :] for y in range(own)]
+        for y in range(own):
+            c0.store(z, y, x, values[y])
     apply_rows(d0, c0, diagonal, 1, own - 2)
     apply_rows(c1, d0, diagonal, 2, own - 4, c0)
     apply_rows(d1, c1, diagonal, 3, own - 6)
@@ -234,7 +241,7 @@
 def first_kernel(
     own,
     ends_ref, c0_in, diagonal_in, d0_in, c1_in, d1_in, c2_in,
-    low_ref, high_ref, low_diagonal_ref, high_diagonal_ref,
+    low_ref, high_ref,
     c0_ref, diagonal_ref, d0_ref, c1_ref, d1_ref, c2_ref, up_ref, down_ref,
 ):
     c0 = Field(c0_ref, HALO)
@@ -244,7 +251,7 @@
     d1 = Field(d1_ref, 2)
     c2 = Field(c2_ref, HALO)
     fill_halo(c0, own, low_ref, high_ref)
-    fill_halo(diagonal, own, low_diagonal_ref, high_diagonal_ref)
+    fill_halo(diagonal, own, low_ref, high_ref, HALO)
     apply_strips(d0, c0, diagonal, own, 4)
     clear_outside(ends_ref, own, d0)
     apply_strips(c1, d0, diagonal, own, 3, c0)
@@ -439,27 +446,34 @@
         name="pack",
     )(there(probes.reshape(count * rows, bz)), there(kappa2.reshape(rows, bz)))
     blocks = lax.all_to_all(blocks, ("gx", "gz"), 0, 0, tiled=True)
-    c0, up_edge, down_edge, half = pl.pallas_call(
-        functools.partial(probe_kernel, grid),
-        out_shape=(vector(HALO), edge(HALO), edge(HALO), f32(group, rows, 128)),
+    half = pl.pallas_call(
+        half_kernel,
+        out_shape=f32(group, rows, 128),
         in_specs=[vmem()],
-        out_specs=(vmem(),) * 4,
-        compiler_params=params(),
-        name="probe_rows",
-    )(blocks)
+        out_specs=vmem(),
+        compiler_params=params(),
+        name="half",
+    )(here(blocks))
+    other = lax.ppermute(half, "gx", sibling)
+    message = edge(HALO + DIAGONAL_HALO)
+    up_edge, down_edge = pl.pallas_call(
+        functools.partial(edge_kernel, grid),
+        out_shape=(edge(HALO), edge(HALO)),
+        in_specs=[vmem()],
+        out_specs=(vmem(),) * 2,
+        compiler_params=params(),
+        name="probe_edges",
+    )(here(blocks))
+    diagonal, up_edge, down_edge = pl.pallas_call(
+        functools.partial(diagonal_kernel, grid),
+        out_shape=(vector(DIAGONAL_HALO), message, message),
+        in_specs=[smem()] + [vmem()] * 4,
+        out_specs=(vmem(),) * 3,
+        compiler_params=params(),
+        name="diagonal_rows",
+    )((gx % 2).astype(jnp.int32).reshape(1), half, other, up_edge, down_edge)
     low1 = lax.ppermute(up_edge, "gy", up)
     high1 = lax.ppermute(down_edge, "gy", down)
-    other = lax.ppermute(half, "gx", sibling)
-    diagonal, up_edge, down_edge = pl.pallas_call(
-        functools.partial(diagonal_kernel, grid),
-        out_shape=(vector(DIAGONAL_HALO), edge(DIAGONAL_HALO), edge(DIAGONAL_HALO)),
-        in_specs=[smem(), vmem(), vmem()],
-        out_specs=(vmem(),) * 3,
-        compiler_params=params(),
-        name="diagonal_rows",
-    )((gx % 2).astype(jnp.int32).reshape(1), half, other)
-    low_diagonal = lax.ppermute(up_edge, "gy", up)
-    high_diagonal = lax.ppermute(down_edge, "gy", down)
 
     cells = by * X * columns * 128
 
@@ -469,26 +483,26 @@
         )
 
     inner = pl.pallas_call(
-        functools.partial(inner_kernel, by),
-        out_shape=tuple(vector(h) for h in (4, 3, 2, HALO)),
+        functools.partial(inner_kernel, grid),
+        out_shape=tuple(vector(h) for h in (HALO, 4, 3, 2, HALO)),
         in_specs=[vmem()] * 2,
-        out_specs=(vmem(),) * 4,
+        out_specs=(vmem(),) * 5,
         compiler_params=params(),
         cost_estimate=cost(32),
         name="inner_steps",
-    )(here(c0), here(diagonal))
+    )(here(blocks), here(diagonal))
     ends = jnp.stack([gy == 0, gy == ny - 1, mine]).astype(jnp.int32)
-    vectors = [here(value) for value in (c0, diagonal) + tuple(inner)]
+    vectors = [here(value) for value in (inner[0], diagonal) + tuple(inner[1:])]
     c0, diagonal, d0, c1, d1, c2, up_edge, down_edge = pl.pallas_call(
         functools.partial(first_kernel, by),
         out_shape=tuple(vector(h) for h in (HALO, DIAGONAL_HALO, 4, 3, 2, HALO))
         + (edge(HALO), edge(HALO)),
-        in_specs=[smem()] + [vmem()] * 10,
+        in_specs=[smem()] + [vmem()] * 8,
         out_specs=(vmem(),) * 8,
         input_output_aliases={i + 1: i for i in range(6)},
         compiler_params=params(),
         name="first_steps",
-    )(ends, *vectors, low1, high1, low_diagonal, high_diagonal)
+    )(ends, *vectors, low1, high1)
     low2 = lax.ppermute(up_edge, "gy", up)
     high2 = lax.ppermute(down_edge, "gy", down)
     d2, moments = pl.pallas_call(

time: 93.6 us -> 93.4 us (level)
  waiting for transfers between devices: 5.39 us -> 14.5 us
  starting transfers between devices: 21.6 us -> 15.7 us
  local copies, waits for them, and re-layouts: 3.21 us -> 1.42 us
    ppermute x1, waiting for transfers between devices: 0.01 us -> 7.07 us  [body(): low1 = lax.ppermute(up_edge, 'gy', up)]
    ppermute x2 -> x0, starting transfers between devices: 5.84 us -> none  [the longest x1 4.55 us: body(): low_diagonal = lax.ppermute(up_edge, 'gy', up)]
    ppermute x1, waiting for transfers between devices: 0.01 us -> 4.04 us  [body(): high1 = lax.ppermute(down_edge, 'gy', down)]
    ppermute x2 -> x0, waiting for transfers between devices: 4.03 us -> none  [the longest x1 4.03 us: body(): high_diagonal = lax.ppermute(down_edge, 'gy', down)]
    unnamed x10 -> x6, local copies, waits for them, and re-layouts: 3.21 us -> 1.42 us
    ppermute x1, waiting for transfers between devices: 0.01 us -> 1.33 us  [body(): other = lax.ppermute(half, 'gx', sibling)]
    pallas_call x2 -> x3, Pallas kernels: 4.32 us -> 3.72 us  [the longest x1 3.48 us: body(): pl.pallas_call(functools.partial(inner_kernel, grid), out_shape=tuple((ve...]
  transfers between devices with their start and end apart: 10 -> 8, of which waited for: 2 -> 4; matrix products, arithmetic and copies ran while one was open for 0% -> 0% of each run, Pallas kernels for 11% -> 11%
where the time goes in v7:
time: 93.4 us; the launch traced here: 93.1 us
  blocking collectives  41.9 us (45%)
  Pallas kernels  19.3 us (21%)
  starting transfers between devices  15.7 us (17%)
  waiting for transfers between devices  14.5 us (16%)
  local copies, waits for them, and re-layouts  1.42 us (2%)
    all_to_all x1, blocking collectives, body(): blocks = lax.all_to_all(blocks, ('gx', 'gz'), 0, 0, tiled=True)  25 us
    all_to_all x1, blocking collectives, body(): out = lax.all_to_all(out, ('gx', 'gz'), 0, 0, tiled=True)  16.9 us
    ppermute x1, waiting for transfers between devices, body(): low1 = lax.ppermute(up_edge, 'gy', up)  7.07 us
    ppermute x3, starting transfers between devices, body(): lax.ppermute(moments, 'gy', [(i, (i + step) % ny) for i in range(ny)])  5.72 us
    pallas_call x1, Pallas kernels, body(): pl.pallas_call(functools.partial(third_kernel, by), out_shape=tuple((vect...  4.68 us
    ppermute x1, waiting for transfers between devices, body(): high1 = lax.ppermute(down_edge, 'gy', down)  4.04 us
    ppermute x1, starting transfers between devices, body(): low1 = lax.ppermute(up_edge, 'gy', up)  3.52 us
    pallas_call x1, Pallas kernels, body(): pl.pallas_call(functools.partial(inner_kernel, grid), out_shape=tuple((ve...  3.48 us
  transfers between devices with their start and end apart: 8, of which 4 were waited for; matrix products, arithmetic and copies ran while one was open for 0% of the time, Pallas kernels for 11%

profile of v7, /device:TPU:0, one launch (start us, length us, event | category | flops | bytes accessed | tf_op | source)
XLA Modules:
  0.0 93.1 jit_solution(17863101377942212495)
XLA Ops:
  0.0 1.6 %pack.1 = f32[8,3,128,128]{3,2,1,0:T(8,128)S(1)} custom-call(f32[1024,256]{1,0:T(8,128)} %bitcast.6, f32[128,256]{1,0:T(8,128)} %bitcast.7), custom_call_target="tpu_custom_call" | custom-call | tf_op jit(solution)/shard_map/pack/pallas_call | solution.py:439
  1.6 25.0 %all_to_all.10.blocks_ref = f32[8,3,128,128]{3,2,1,0:T(8,128)S(1)} all-to-all(f32[8,3,128,128]{3,2,1,0:T(8,128)S(1)} %pack.1), channel_id=1, replica_groups=mesh['gx'=4,'gy'=4,'gz'=2] {'gx','gz'}, dimensions={0} | all-to-all | bytes 3145728 | tf_op jit(solution)/shard_map/all_to_all | solution.py:448
  26.7 0.4 collective-permute-start
  27.1 0.2 probe_edges.1
  27.3 1.3 %collective-permute-done.other_ref = f32[8,128,128]{2,1,0:T(8,128)S(1)} collective-permute-done((f32[8,128,128]{2,1,0:T(8,128)S(1)}, f32[8,128,128]{2,1,0:T(8,128)S(1)}, u32[]{:S(2)}, u32[]{:S(2)}) %collective-permute-start) | collective-permute-done | bytes 524320 | tf_op jit(solution)/shard_map/ppermute | solution.py:457
  28.7 1.4 %diagonal_rows.1 = (f32[4,24,48,128]{3,2,1,0:T(8,128)S(1)}, f32[4,9,32,128]{3,2,1,0:T(8,128)}, f32[4,9,32,128]{3,2,1,0:T(8,128)}) custom-call(s32[1]{0:T(128)} %bitcast.5.core_ref, f32[8,128,128]{2,1,0:T(8,128)S(1)} %half.1.half_ref, f32[8,128,128]{2,1,0:T(8,128)S(1)} %collective-permute-done.other_ref, f32[4,5,32,128]{3,2,1,0:T(8,128)S(1)} %get-tuple-element.30.up_in, ...), custom_call_target="tpu_custom_call" | custom-call | tf_op jit(solution)/shard_map/diagonal_rows/pallas_call | solution.py:467
  30.1 3.5 %collective-permute-start.1 = (f32[4,9,32,128]{3,2,1,0:T(8,128)}, f32[4,9,32,128]{3,2,1,0:T(8,128)S(1)}, u32[]{:S(2)}, u32[]{:S(2)}) collective-permute-start(f32[4,9,32,128]{3,2,1,0:T(8,128)} %get-tuple-element.38), channel_id=1, source_target_pairs={{0,2},{2,4},{4,6},{1,3},{3,5},{5,7},{8,10},{10,12},{12,14},{9,11},... | collective-permute-start | bytes 1769480 | tf_op jit(solution)/shard_map/ppermute | solution.py:475
  33.6 1.3 %collective-permute-start.2 = (f32[4,9,32,128]{3,2,1,0:T(8,128)}, f32[4,9,32,128]{3,2,1,0:T(8,128)S(1)}, u32[]{:S(2)}, u32[]{:S(2)}) collective-permute-start(f32[4,9,32,128]{3,2,1,0:T(8,128)} %get-tuple-element.39), channel_id=1, source_target_pairs={{2,0},{4,2},{6,4},{3,1},{5,3},{7,5},{10,8},{12,10},{14,12},{11,9},... | collective-permute-start | bytes 1769480 | tf_op jit(solution)/shard_map/ppermute | solution.py:476
  35.0 1.4 %copy-done.1 = f32[8,3,128,128]{3,2,1,0:T(8,128)S(1)} copy-done((f32[8,3,128,128]{3,2,1,0:T(8,128)S(1)}, f32[8,3,128,128]{3,2,1,0:T(8,128)}, u32[]{:S(2)}) %copy-start.1) | copy-done | bytes 1572888
  36.4 3.5 %inner_steps.1 = (f32[4,26,48,128]{3,2,1,0:T(8,128)S(1)}, f32[4,24,48,128]{3,2,1,0:T(8,128)S(1)}, f32[4,22,48,128]{3,2,1,0:T(8,128)S(1)}, f32[4,20,48,128]{3,2,1,0:T(8,128)S(1)}, f32[4,26,48,128]{3,2,1,0:T(8,128)S(1)}) custom-call(f32[8,3,128,128]{3,2,1,0:T(8,128)S(1)} %copy-done.1, f32[4,24,48,128]{3,2,1,0:T(8,128)S(1)} %get-tuple-element.32.diagonal_ref.diagonal_in), custom_call_target="tpu_custom_call" | custom-call | flops 8388608 | bytes 4194304 | tf_op jit(solution)/shard_map/inner_steps/pallas_call | solution.py:485
  39.9 7.1 %collective-permute-done.1.low_ref = f32[4,9,32,128]{3,2,1,0:T(8,128)S(1)} collective-permute-done((f32[4,9,32,128]{3,2,1,0:T(8,128)}, f32[4,9,32,128]{3,2,1,0:T(8,128)S(1)}, u32[]{:S(2)}, u32[]{:S(2)}) %collective-permute-start.1) | collective-permute-done | bytes 589856 | tf_op jit(solution)/shard_map/ppermute | solution.py:475
  47.0 4.0 %collective-permute-done.2.high_ref = f32[4,9,32,128]{3,2,1,0:T(8,128)S(1)} collective-permute-done((f32[4,9,32,128]{3,2,1,0:T(8,128)}, f32[4,9,32,128]{3,2,1,0:T(8,128)S(1)}, u32[]{:S(2)}, u32[]{:S(2)}) %collective-permute-start.2) | collective-permute-done | bytes 589856 | tf_op jit(solution)/shard_map/ppermute | solution.py:476
  51.0 2.8 %first_steps.1 = (f32[4,26,48,128]{3,2,1,0:T(8,128)S(1)}, f32[4,24,48,128]{3,2,1,0:T(8,128)S(1)}, f32[4,24,48,128]{3,2,1,0:T(8,128)S(1)}, f32[4,22,48,128]{3,2,1...) custom-call(s32[3]{0:T(128)S(1)} %pad_add_fusion.ends_ref, ...), custom_call_target="tpu_custom_call", output_to_operand_aliasing={{0}: (1, {}), {1}: (2, {}), {2}: (3, {}), {3}: (4, {}), {4}... | custom-call | tf_op jit(solution)/shard_map/first_steps/pallas_call | solution.py:496
  53.8 3.5 %collective-permute-start.3 = (f32[4,5,32,128]{3,2,1,0:T(8,128)S(1)}, f32[4,5,32,128]{3,2,1,0:T(8,128)S(1)}, u32[]{:S(2)}, u32[]{:S(2)}) collective-permute-start(f32[4,5,32,128]{3,2,1,0:T(8,128)S(1)} %get-tuple-element.47), channel_id=1, source_target_pairs={{0,2},{2,4},{4,6},{1,3},{3,5},{5,7},{8,10},{10,12},{12,14},{9,11},... | collective-permute-start | bytes 983048 | tf_op jit(solution)/shard_map/ppermute | solution.py:506
  57.3 1.3 %collective-permute-start.4 = (f32[4,5,32,128]{3,2,1,0:T(8,128)S(1)}, f32[4,5,32,128]{3,2,1,0:T(8,128)S(1)}, u32[]{:S(2)}, u32[]{:S(2)}) collective-permute-start(f32[4,5,32,128]{3,2,1,0:T(8,128)S(1)} %get-tuple-element.48), channel_id=1, source_target_pairs={{2,0},{4,2},{6,4},{3,1},{5,3},{7,5},{10,8},{12,10},{14,12},{11,9},... | collective-permute-start | bytes 983048 | tf_op jit(solution)/shard_map/ppermute | solution.py:507
  58.6 1.5 %middle_step.1 = (f32[4,24,48,128]{3,2,1,0:T(8,128)S(1)}, f32[8,128]{1,0:T(8,128)S(1)}) custom-call(f32[4,26,48,128]{3,2,1,0:T(8,128)S(1)} %get-tuple-element.40.c0_ref, f32[4,22,48,128]{3,2,1,0:T(8,128)S(1)} %get-tuple-element.43.c1_ref, f32[4,26,48,128]{3,2,1,0:T(8,128)S(1)} %get-tuple-element.45.c2_ref.c2_in, ...), custom_call_target="tpu_custom_call" | custom-call | flops 6291456 | bytes 4194304 | tf_op jit(solution)/shard_map/middle_step/pallas_call | solution.py:508
  60.1 3.2 %collective-permute-start.7 = (f32[8,128]{1,0:T(8,128)S(1)}, f32[8,128]{1,0:T(8,128)S(1)}, u32[]{:S(2)}, u32[]{:S(2)}) collective-permute-start(f32[8,128]{1,0:T(8,128)S(1)} %get-tuple-element.54.rest_0_), channel_id=1, source_target_pairs={{0,6},{2,0},{4,2},{6,4},{1,7},{3,1},{5,3},{7,5},{8,14},{10,8},{12,... | collective-permute-start | bytes 12296 | tf_op jit(solution)/shard_map/ppermute | solution.py:519
  63.3 1.0 %collective-permute-start.6 = (f32[8,128]{1,0:T(8,128)S(1)}, f32[8,128]{1,0:T(8,128)S(1)}, u32[]{:S(2)}, u32[]{:S(2)}) collective-permute-start(f32[8,128]{1,0:T(8,128)S(1)} %get-tuple-element.54.rest_0_), channel_id=1, source_target_pairs={{0,4},{2,6},{4,0},{6,2},{1,5},{3,7},{5,1},{7,3},{8,12},{10,14},{12... | collective-permute-start | bytes 12296 | tf_op jit(solution)/shard_map/ppermute | solution.py:519
  64.3 1.6 %collective-permute-start.5 = (f32[8,128]{1,0:T(8,128)S(1)}, f32[8,128]{1,0:T(8,128)S(1)}, u32[]{:S(2)}, u32[]{:S(2)}) collective-permute-start(f32[8,128]{1,0:T(8,128)S(1)} %get-tuple-element.54.rest_0_), channel_id=1, source_target_pairs={{0,2},{2,4},{4,6},{6,0},{1,3},{3,5},{5,7},{7,1},{8,10},{10,12},{12... | collective-permute-start | bytes 12296 | tf_op jit(solution)/shard_map/ppermute | solution.py:519
  65.8 2.0 %collective-permute-done.4.high_ref = f32[4,5,32,128]{3,2,1,0:T(8,128)S(1)} collective-permute-done((f32[4,5,32,128]{3,2,1,0:T(8,128)S(1)}, f32[4,5,32,128]{3,2,1,0:T(8,128)S(1)}, u32[]{:S(2)}, u32[]{:S(2)}) %collective-permute-start.4) | collective-permute-done | bytes 327712 | tf_op jit(solution)/shard_map/ppermute | solution.py:507
  67.9 4.7 %third_steps.1 = (f32[4,26,48,128]{3,2,1,0:T(8,128)S(1)}, f32[4,24,48,128]{3,2,1,0:T(8,128)S(1)}, f32[4,22,48,128]{3,2,1,0:T(8,128)S(1)}, f32[4,20,48,128]{3,2,1,0:T(8,128)S(1)}, f32[4,18,48,128]{3,2,1,0:T(8,128)S(1)}) custom-call(s32[3]{0:T(128)S(1)} %pad_add_fusion.ends_ref, ...), custom_call_target="tpu_custom_call", output_to_operand_aliasing={{0}: (2, {}), {1}: (3, {})} | custom-call | flops 10485760 | bytes 4194304 | tf_op jit(solution)/shard_map/third_steps/pallas_call | solution.py:521
  72.6 2.9 %last_step.1 = f32[8,2,128,128]{3,2,1,0:T(8,128)S(1)} custom-call(s32[3]{0:T(128)S(1)} %pad_add_fusion.ends_ref, f32[5,8]{1,0:T(8,128)S(1)} %copy-done.2, f32[4,26,48,128]{3,2,1,0:T(8,128)S(1)} %get-tuple-element.40.c0_ref, f32[4,24,48,128]{3,2,1,0:T(8,128)S(1)} %get-tuple-element.41.diagonal_ref, f32[4,24,48,128]{3,2,1,0:T(8,128)S(1)} %get-tuple-element.42.d0_ref, ...), custom_call_target="tpu_custom_call" | custom-call | tf_op jit(solution)/shard_map/last_step/pallas_call | solution.py:533
  75.5 16.9 %all_to_all.11.parts_ref = f32[8,2,128,128]{3,2,1,0:T(8,128)S(1)} all-to-all(f32[8,2,128,128]{3,2,1,0:T(8,128)S(1)} %last_step.1), channel_id=1, replica_groups=mesh['gx'=4,'gy'=4,'gz'=2] {'gx','gz'}, dimensions={0} | all-to-all | bytes 2097152 | tf_op jit(solution)/shard_map/all_to_all | solution.py:542
  92.4 0.7 sum_probes.1
  (11 shorter events, 0.1 us)
Async XLA Ops:
  26.7 2.0 %copy-start = (f32[8,3,128,128]{3,2,1,0:T(8,128)}, f32[8,3,128,128]{3,2,1,0:T(8,128)S(1)}, u32[]{:S(2)}) copy-start(f32[8,3,128,128]{3,2,1,0:T(8,128)S(1)} %all_to_all.10.blocks_ref) | copy-start | bytes 4718596
  26.7 2.0 %collective-permute-start = (f32[8,128,128]{2,1,0:T(8,128)S(1)}, f32[8,128,128]{2,1,0:T(8,128)S(1)}, u32[]{:S(2)}, u32[]{:S(2)}) collective-permute-start(f32[8,128,128]{2,1,0:T(8,128)S(1)} %half.1.half_ref), channel_id=1, source_target_pairs={{0,8},{8,0},{16,24},{24,16},{1,9},{9,1},{17,25},{25,17},{2,10},{10... | collective-permute-start | bytes 1572872 | tf_op jit(solution)/shard_map/ppermute | solution.py:457
  30.1 16.9 %collective-permute-start.1 = (f32[4,9,32,128]{3,2,1,0:T(8,128)}, f32[4,9,32,128]{3,2,1,0:T(8,128)S(1)}, u32[]{:S(2)}, u32[]{:S(2)}) collective-permute-start(f32[4,9,32,128]{3,2,1,0:T(8,128)} %get-tuple-element.38), channel_id=1, source_target_pairs={{0,2},{2,4},{4,6},{1,3},{3,5},{5,7},{8,10},{10,12},{12,14},{9,11},... | collective-permute-start | bytes 1769480 | tf_op jit(solution)/shard_map/ppermute | solution.py:475
  33.6 17.4 %collective-permute-start.2 = (f32[4,9,32,128]{3,2,1,0:T(8,128)}, f32[4,9,32,128]{3,2,1,0:T(8,128)S(1)}, u32[]{:S(2)}, u32[]{:S(2)}) collective-permute-start(f32[4,9,32,128]{3,2,1,0:T(8,128)} %get-tuple-element.39), channel_id=1, source_target_pairs={{2,0},{4,2},{6,4},{3,1},{5,3},{7,5},{10,8},{12,10},{14,12},{11,9},... | collective-permute-start | bytes 1769480 | tf_op jit(solution)/shard_map/ppermute | solution.py:476
  35.0 1.4 %copy-start.1 = (f32[8,3,128,128]{3,2,1,0:T(8,128)S(1)}, f32[8,3,128,128]{3,2,1,0:T(8,128)}, u32[]{:S(2)}) copy-start(f32[8,3,128,128]{3,2,1,0:T(8,128)} %copy-done) | copy-start | bytes 4718596
  53.8 12.0 %collective-permute-start.3 = (f32[4,5,32,128]{3,2,1,0:T(8,128)S(1)}, f32[4,5,32,128]{3,2,1,0:T(8,128)S(1)}, u32[]{:S(2)}, u32[]{:S(2)}) collective-permute-start(f32[4,5,32,128]{3,2,1,0:T(8,128)S(1)} %get-tuple-element.47), channel_id=1, source_target_pairs={{0,2},{2,4},{4,6},{1,3},{3,5},{5,7},{8,10},{10,12},{12,14},{9,11},... | collective-permute-start | bytes 983048 | tf_op jit(solution)/shard_map/ppermute | solution.py:506
  57.3 10.6 %collective-permute-start.4 = (f32[4,5,32,128]{3,2,1,0:T(8,128)S(1)}, f32[4,5,32,128]{3,2,1,0:T(8,128)S(1)}, u32[]{:S(2)}, u32[]{:S(2)}) collective-permute-start(f32[4,5,32,128]{3,2,1,0:T(8,128)S(1)} %get-tuple-element.48), channel_id=1, source_target_pairs={{2,0},{4,2},{6,4},{3,1},{5,3},{7,5},{10,8},{12,10},{14,12},{11,9},... | collective-permute-start | bytes 983048 | tf_op jit(solution)/shard_map/ppermute | solution.py:507
  60.1 12.4 %collective-permute-start.7 = (f32[8,128]{1,0:T(8,128)S(1)}, f32[8,128]{1,0:T(8,128)S(1)}, u32[]{:S(2)}, u32[]{:S(2)}) collective-permute-start(f32[8,128]{1,0:T(8,128)S(1)} %get-tuple-element.54.rest_0_), channel_id=1, source_target_pairs={{0,6},{2,0},{4,2},{6,4},{1,7},{3,1},{5,3},{7,5},{8,14},{10,8},{12,... | collective-permute-start | bytes 12296 | tf_op jit(solution)/shard_map/ppermute | solution.py:519
  63.3 9.3 %collective-permute-start.6 = (f32[8,128]{1,0:T(8,128)S(1)}, f32[8,128]{1,0:T(8,128)S(1)}, u32[]{:S(2)}, u32[]{:S(2)}) collective-permute-start(f32[8,128]{1,0:T(8,128)S(1)} %get-tuple-element.54.rest_0_), channel_id=1, source_target_pairs={{0,4},{2,6},{4,0},{6,2},{1,5},{3,7},{5,1},{7,3},{8,12},{10,14},{12... | collective-permute-start | bytes 12296 | tf_op jit(solution)/shard_map/ppermute | solution.py:519
  64.3 8.3 %collective-permute-start.5 = (f32[8,128]{1,0:T(8,128)S(1)}, f32[8,128]{1,0:T(8,128)S(1)}, u32[]{:S(2)}, u32[]{:S(2)}) collective-permute-start(f32[8,128]{1,0:T(8,128)S(1)} %get-tuple-element.54.rest_0_), channel_id=1, source_target_pairs={{0,2},{2,4},{4,6},{6,0},{1,3},{3,5},{5,7},{7,1},{8,10},{10,12},{12... | collective-permute-start | bytes 12296 | tf_op jit(solution)/shard_map/ppermute | solution.py:519
  67.9 4.7 %copy-start.2 = (f32[5,8]{1,0:T(8,128)S(1)}, f32[5,8]{1,0:T(8,128)}, u32[]{:S(2)}) copy-start(f32[5,8]{1,0:T(8,128)} %weights_ref.1) | copy-start | bytes 484

commit v8 on v7

--- a/solution.py
+++ b/solution.py
@@ -120,15 +120,16 @@
         apply_block(target, source, diagonal, start, count % block, minus, masks)
 
 
-def apply_strips(target, source, diagonal, own, halo, minus=None):
+def apply_strips(ends_ref, own, target, source, diagonal, halo, size, minus=None):
     masks = lane_masks()
 
     def body(step, carry):
-        row = step * (own - HALO + 2 * halo) - halo
-        apply_block(target, source, diagonal, row, HALO, minus, masks)
+        row = step * (own - size + 2 * halo) - halo
+        apply_block(target, source, diagonal, row, size, minus, masks)
         return carry
 
     lax.fori_loop(0, 2, body, 0)
+    clear_outside(ends_ref, own, target)
 
 
 def clear_outside(ends_ref, own, field):
@@ -139,12 +140,6 @@
     @pl.when(ends_ref[1] == 1)
     def _():
         field.clear_row(own)
-
-
-def apply_steps(ends_ref, own, target, source, diagonal, halo, minus=None):
-    apply_rows(target, source, diagonal, -halo, own + 2 * halo, minus)
-    if halo:
-        clear_outside(ends_ref, own, target)
 
 
 def places(grid):
@@ -252,14 +247,11 @@
     c2 = Field(c2_ref, HALO)
     fill_halo(c0, own, low_ref, high_ref)
     fill_halo(diagonal, own, low_ref, high_ref, HALO)
-    apply_strips(d0, c0, diagonal, own, 4)
-    clear_outside(ends_ref, own, d0)
-    apply_strips(c1, d0, diagonal, own, 3, c0)
-    clear_outside(ends_ref, own, c1)
-    apply_strips(d1, c1, diagonal, own, 2)
-    clear_outside(ends_ref, own, d1)
-    apply_strips(c2, d1, diagonal, own, 1, c1)
-    clear_outside(ends_ref, own, c2)
+    strips = functools.partial(apply_strips, ends_ref, own)
+    strips(d0, c0, diagonal, 4, HALO)
+    strips(c1, d0, diagonal, 3, HALO, c0)
+    strips(d1, c1, diagonal, 2, HALO)
+    strips(c2, d1, diagonal, 1, HALO, c1)
     for c in range(c2.columns):
         for y in range(HALO):
             for x in range(0, c2.cells, 8):
@@ -303,9 +295,23 @@
     return [slope[0, 0] for slope in slopes]
 
 
+def second_inner_kernel(own, diagonal_ref, c2_ref, d2_ref, c3_ref, d3_ref, c4_ref):
+    diagonal = Field(diagonal_ref, DIAGONAL_HALO)
+    c2 = Field(c2_ref, HALO)
+    d2 = Field(d2_ref, 4)
+    c3 = Field(c3_ref, 3)
+    d3 = Field(d3_ref, 2)
+    c4 = Field(c4_ref, 1)
+    for field in (c3, d3, c4):
+        field.clear_pads()
+    apply_rows(c3, d2, diagonal, 1, own - 2, c2)
+    apply_rows(d3, c3, diagonal, 2, own - 4)
+    apply_rows(c4, d3, diagonal, 3, own - 6, c3)
+
+
 def third_kernel(
     own,
-    ends_ref, diagonal_ref, c2_in, d2_in, low_ref, high_ref,
+    ends_ref, diagonal_ref, c2_in, d2_in, c3_in, d3_in, c4_in, low_ref, high_ref,
     c2_ref, d2_ref, c3_ref, d3_ref, c4_ref,
 ):
     diagonal = Field(diagonal_ref, DIAGONAL_HALO)
@@ -314,24 +320,21 @@
     c3 = Field(c3_ref, 3)
     d3 = Field(d3_ref, 2)
     c4 = Field(c4_ref, 1)
-    for field in (c3, d3, c4):
-        field.clear_pads()
     fill_halo(c2, own, low_ref, high_ref)
-    apply_rows(d2, c2, diagonal, -4, 4)
-    apply_rows(d2, c2, diagonal, own, 4)
-    clear_outside(ends_ref, own, d2)
-    steps = functools.partial(apply_steps, ends_ref, own)
-    steps(c3, d2, diagonal, 3, c2)
-    steps(d3, c3, diagonal, 2)
-    steps(c4, d3, diagonal, 1, c3)
+    strips = functools.partial(apply_strips, ends_ref, own)
+    strips(d2, c2, diagonal, 4, 4)
+    strips(c3, d2, diagonal, 3, 4, c2)
+    strips(d3, c3, diagonal, 2, 4)
+    strips(c4, d3, diagonal, 1, 4, c3)
 
 
 def last_kernel(
-    grid, inverse_count,
+    grid, inverse_count, flip,
     ends_ref, weights_ref, c0_ref, diagonal_ref, d0_ref, c1_ref, d1_ref,
     c2_ref, d2_ref, c3_ref, d3_ref, c4_ref, *rest,
 ):
     nx, nz, bx, by, bz = grid
+    per = bz // 128
     moment_refs, out_ref = rest[:-1], rest[-1]
     c0 = Field(c0_ref, HALO)
     diagonal = Field(diagonal_ref, DIAGONAL_HALO)
@@ -345,12 +348,12 @@
     c4 = Field(c4_ref, 1)
     slopes = moment_slopes(inverse_count, ends_ref[2], weights_ref, moment_refs)
     masks = lane_masks()
-    place = {(x, z): (s, column) for s, column, x, z in places(grid)}
     block = 2
 
-    def out_rows(step, carry):
+    def out_rows(core, step, carry):
         row = step * block
-        for x in range(0, c4.cells, 8):
+        for chip in range(nx // 2):
+            x = (2 * chip + core) * bx
             results = []
             for z, at, d4 in stencil_block(c4, diagonal, row, block, x, masks):
                 cs = [field.load(z, at, x) for field in (c0, c1, c2, c3, c4)]
@@ -363,20 +366,28 @@
                         inner = term if inner is None else inner + term
                     term = cs[i] * inner
                     total = term if total is None else total + term
-                results.append(place[x, z] + (at, total))
-            for s, column, at, total in results:
-                out_ref[s, column, pl.ds(at, bx, stride=by), :] = total
+                results.append((chip * nz + z // per, z % per, at, total))
+            for place, column, at, total in results:
+                out_ref[place, column, pl.ds(at, bx, stride=by), :] = total
         return carry
 
-    lax.fori_loop(0, by // block, out_rows, 0)
-
-
-def sum_kernel(grid, count, parts_ref, out_ref):
+    for core in range(2):
+
+        @pl.when(ends_ref[3] == (1 - core if flip else core))
+        def _():
+            lax.fori_loop(0, by // block, functools.partial(out_rows, core), 0)
+
+
+def add_kernel(kept_ref, got_ref, out_ref):
+    out_ref[...] = kept_ref[...] + got_ref[...]
+
+
+def sum_kernel(grid, parts_ref, out_ref):
     nx, nz, bx, by, bz = grid
     for column in range(bz // 128):
         for x in range(bx):
             total = None
-            for p in range(count):
+            for p in range(parts_ref.shape[0]):
                 part = parts_ref[p, column, pl.ds(x * by, by), :]
                 total = part if total is None else total + part
             out_ref[x, :, pl.ds(column * 128, 128)] = total
@@ -411,7 +422,7 @@
 
 
 def body(probes, kappa2, cotangents):
-    nx, ny, nz = (lax.axis_size(axis) for axis in ("gx", "gy", "gz"))
+    nx, ny, nz = (lax.axis_size(axis) for axis in (("chip", "core"), "gy", "gz"))
     count, bx, by, bz = probes.shape
     group = nx * nz
     assert group % count == 0 and nx % 2 == 0 and bx == 8 and bz == 256
@@ -421,11 +432,12 @@
     per = bz // 128
     rows = bx * by
     grid = (nx, nz, bx, by, bz)
-    gx, gy = lax.axis_index("gx"), lax.axis_index("gy")
-    mine = (gx * nz + lax.axis_index("gz")) % count
+    core, gy = lax.axis_index("core"), lax.axis_index("gy")
+    place = (lax.axis_index("chip") * 2 + core) * nz + lax.axis_index("gz")
+    mine = place % count
     up = [(i, i + 1) for i in range(ny - 1)]
     down = [(target, source) for source, target in up]
-    sibling = [(i, i ^ 1) for i in range(nx)]
+    swap = [(0, 1), (1, 0)]
 
     def edge(halo):
         return f32(columns, halo, X, 128)
@@ -445,7 +457,7 @@
         compiler_params=params(),
         name="pack",
     )(there(probes.reshape(count * rows, bz)), there(kappa2.reshape(rows, bz)))
-    blocks = lax.all_to_all(blocks, ("gx", "gz"), 0, 0, tiled=True)
+    blocks = lax.all_to_all(blocks, ("chip", "core", "gz"), 0, 0, tiled=True)
     half = pl.pallas_call(
         half_kernel,
         out_shape=f32(group, rows, 128),
@@ -454,7 +466,7 @@
         compiler_params=params(),
         name="half",
     )(here(blocks))
-    other = lax.ppermute(half, "gx", sibling)
+    other = lax.ppermute(half, "core", swap)
     message = edge(HALO + DIAGONAL_HALO)
     up_edge, down_edge = pl.pallas_call(
         functools.partial(edge_kernel, grid),
@@ -471,7 +483,7 @@
         out_specs=(vmem(),) * 3,
         compiler_params=params(),
         name="diagonal_rows",
-    )((gx % 2).astype(jnp.int32).reshape(1), half, other, up_edge, down_edge)
+    )(core.astype(jnp.int32).reshape(1), half, other, up_edge, down_edge)
     low1 = lax.ppermute(up_edge, "gy", up)
     high1 = lax.ppermute(down_edge, "gy", down)
 
@@ -491,7 +503,7 @@
         cost_estimate=cost(32),
         name="inner_steps",
     )(here(blocks), here(diagonal))
-    ends = jnp.stack([gy == 0, gy == ny - 1, mine]).astype(jnp.int32)
+    ends = jnp.stack([gy == 0, gy == ny - 1, mine, core]).astype(jnp.int32)
     vectors = [here(value) for value in (inner[0], diagonal) + tuple(inner[1:])]
     c0, diagonal, d0, c1, d1, c2, up_edge, down_edge = pl.pallas_call(
         functools.partial(first_kernel, by),
@@ -518,43 +530,72 @@
     for step in range(1, ny):
         shares.append(lax.ppermute(moments, "gy", [(i, (i + step) % ny) for i in range(ny)]))
 
+    c3, d3, c4 = pl.pallas_call(
+        functools.partial(second_inner_kernel, by),
+        out_shape=tuple(vector(h) for h in (3, 2, 1)),
+        in_specs=[vmem()] * 3,
+        out_specs=(vmem(),) * 3,
+        compiler_params=params(),
+        cost_estimate=cost(30),
+        name="second_inner_steps",
+    )(here(diagonal), here(c2), here(d2))
+    vectors = [here(value) for value in (diagonal, c2, d2, c3, d3, c4)]
     c2, d2, c3, d3, c4 = pl.pallas_call(
         functools.partial(third_kernel, by),
         out_shape=tuple(vector(h) for h in (HALO, 4, 3, 2, 1)),
-        in_specs=[smem()] + [vmem()] * 5,
+        in_specs=[smem()] + [vmem()] * 8,
         out_specs=(vmem(),) * 5,
-        input_output_aliases={2: 0, 3: 1},
-        compiler_params=params(),
-        cost_estimate=cost(40),
+        input_output_aliases={i + 2: i for i in range(5)},
+        compiler_params=params(),
+        cost_estimate=cost(20),
         name="third_steps",
-    )(ends, here(diagonal), here(c2), here(d2), low2, high2)
+    )(ends, *vectors, low2, high2)
     inverse_count = 1.0 / (ny * cells)
     vectors = [here(value) for value in (c0, diagonal, d0, c1, d1, c2, d2, c3, d3, c4)]
-    out = pl.pallas_call(
-        functools.partial(last_kernel, grid, inverse_count),
-        out_shape=f32(group, per, rows, 128),
-        in_specs=[smem(), smem()] + [vmem()] * (10 + ny),
+    if group > count:
+        cotangents = jnp.where(place < count, cotangents, 0.0)
+    blocks = f32(group // 2, per, rows, 128)
+
+    def last_step(flip):
+        return pl.pallas_call(
+            functools.partial(last_kernel, grid, inverse_count, flip),
+            out_shape=blocks,
+            in_specs=[smem(), smem()] + [vmem()] * (10 + ny),
+            out_specs=vmem(),
+            compiler_params=params(),
+            cost_estimate=cost(20),
+            name="last_step_given" if flip else "last_step_kept",
+        )(ends, cotangents, *vectors, *shares)
+
+    got = lax.ppermute(last_step(True), "core", swap)
+    parts = pl.pallas_call(
+        add_kernel,
+        out_shape=blocks,
+        in_specs=[vmem()] * 2,
         out_specs=vmem(),
         compiler_params=params(),
-        name="last_step",
-    )(ends, cotangents, *vectors, *shares)
-
-    out = lax.all_to_all(out, ("gx", "gz"), 0, 0, tiled=True)
+        name="add_cores",
+    )(last_step(False), got)
+    parts = lax.all_to_all(parts, ("chip", "gz"), 0, 0, tiled=True)
     return pl.pallas_call(
-        functools.partial(sum_kernel, grid, count),
+        functools.partial(sum_kernel, grid),
         out_shape=f32(bx, by, bz),
         in_specs=[vmem()],
         out_specs=vmem(),
         compiler_params=params(),
-        name="sum_probes",
-    )(out)
+        name="sum_chips",
+    )(parts)
 
 
 def solution(mesh):
+    nx, ny, nz = (mesh.shape[axis] for axis in ("gx", "gy", "gz"))
+    devices = mesh.devices.reshape(nx // 2, 2, ny, nz)
+    split = jax.sharding.Mesh(devices, ("chip", "core", "gy", "gz"))
+    gx = ("chip", "core")
     return jax.shard_map(
         body,
-        mesh=mesh,
-        in_specs=(P(None, "gx", "gy", "gz"), P("gx", "gy", "gz"), P()),
-        out_specs=P("gx", "gy", "gz"),
+        mesh=split,
+        in_specs=(P(None, gx, "gy", "gz"), P(gx, "gy", "gz"), P()),
+        out_specs=P(gx, "gy", "gz"),
         check_vma=False,
     )

time: 93.4 us -> 88.9 us (0.952)
  blocking collectives: 41.9 us -> 36.9 us
  waiting for transfers between devices: 14.5 us -> 12.4 us
  Pallas kernels: 19.3 us -> 20.9 us
  starting transfers between devices: 15.7 us -> 16.7 us
    all_to_all x2, blocking collectives: 41.9 us -> 36.9 us  [the longest x1 25 us: body(): blocks = lax.all_to_all(blocks, ('chip', 'core', 'gz'), 0, 0, tiled=True)]
    pallas_call x2 -> x5, Pallas kernels: 3.61 us -> 7.24 us  [the longest x2 4.12 us: last_step(): pl.pallas_call(functools.partial(last_kernel, grid, inverse_count, flip),...]
    pallas_call x1, Pallas kernels: 4.68 us -> 2.45 us  [body(): pl.pallas_call(functools.partial(third_kernel, by), out_shape=tuple((vect...]
    ppermute x1, waiting for transfers between devices: 2.02 us -> 0.01 us  [body(): high2 = lax.ppermute(down_edge, 'gy', down)]
  transfers between devices with their start and end apart: 8 -> 9, of which waited for: 4 -> 3; matrix products, arithmetic and copies ran while one was open for 0% -> 0% of each run, Pallas kernels for 11% -> 14%
where the time goes in v8:
time: 88.9 us; the launch traced here: 88.6 us
  blocking collectives  36.9 us (42%)
  Pallas kernels  20.9 us (24%)
  starting transfers between devices  16.7 us (19%)
  waiting for transfers between devices  12.4 us (14%)
  local copies, waits for them, and re-layouts  1.42 us (2%)
    all_to_all x1, blocking collectives, body(): blocks = lax.all_to_all(blocks, ('chip', 'core', 'gz'), 0, 0, tiled=True)  25 us
    all_to_all x1, blocking collectives, body(): parts = lax.all_to_all(parts, ('chip', 'gz'), 0, 0, tiled=True)  11.8 us
    ppermute x1, waiting for transfers between devices, body(): low1 = lax.ppermute(up_edge, 'gy', up)  7.04 us
    ppermute x3, starting transfers between devices, body(): lax.ppermute(moments, 'gy', [(i, (i + step) % ny) for i in range(ny)])  6.62 us
    pallas_call x2, Pallas kernels, last_step(): pl.pallas_call(functools.partial(last_kernel, grid, inverse_count, flip),...  4.12 us
    ppermute x1, waiting for transfers between devices, body(): high1 = lax.ppermute(down_edge, 'gy', down)  4.04 us
    ppermute x1, starting transfers between devices, body(): low1 = lax.ppermute(up_edge, 'gy', up)  3.52 us
    pallas_call x1, Pallas kernels, body(): pl.pallas_call(functools.partial(inner_kernel, grid), out_shape=tuple((ve...  3.5 us
  transfers between devices with their start and end apart: 9, of which 3 were waited for; matrix products, arithmetic and copies ran while one was open for 0% of the time, Pallas kernels for 14%

profile of v8, /device:TPU:0, one launch (start us, length us, event | category | flops | bytes accessed | tf_op | source)
XLA Modules:
  0.0 88.6 jit_solution(9899712531429779193)
XLA Ops:
  0.0 1.6 %pack.1 = f32[8,3,128,128]{3,2,1,0:T(8,128)S(1)} custom-call(f32[1024,256]{1,0:T(8,128)} %bitcast.6, f32[128,256]{1,0:T(8,128)} %bitcast.7), custom_call_target="tpu_custom_call" | custom-call | tf_op jit(solution)/shard_map/pack/pallas_call | solution.py:451
  1.6 25.0 %all_to_all.10.blocks_ref = f32[8,3,128,128]{3,2,1,0:T(8,128)S(1)} all-to-all(f32[8,3,128,128]{3,2,1,0:T(8,128)S(1)} %pack.1), channel_id=1, replica_groups=mesh['chip'=2,'core'=2,'gy'=4,'gz'=2] {'chip','core','gz'}, dimensions={0} | all-to-all | bytes 3145728 | tf_op jit(solution)/shard_map/all_to_all | solution.py:460
  26.7 0.4 collective-permute-start
  27.3 1.3 %collective-permute-done.other_ref = f32[8,128,128]{2,1,0:T(8,128)S(1)} collective-permute-done((f32[8,128,128]{2,1,0:T(8,128)S(1)}, f32[8,128,128]{2,1,0:T(8,128)S(1)}, u32[]{:S(2)}, u32[]{:S(2)}) %collective-permute-start) | collective-permute-done | bytes 524320 | tf_op jit(solution)/shard_map/ppermute | solution.py:469
  28.7 1.4 %diagonal_rows.1 = (f32[4,24,48,128]{3,2,1,0:T(8,128)S(1)}, f32[4,9,32,128]{3,2,1,0:T(8,128)}, f32[4,9,32,128]{3,2,1,0:T(8,128)}) custom-call(s32[1]{0:T(128)} %bitcast.3.core_ref, f32[8,128,128]{2,1,0:T(8,128)S(1)} %half.1.half_ref, f32[8,128,128]{2,1,0:T(8,128)S(1)} %collective-permute-done.other_ref, f32[4,5,32,128]{3,2,1,0:T(8,128)S(1)} %get-tuple-element.33.up_in, ...), custom_call_target="tpu_custom_call" | custom-call | tf_op jit(solution)/shard_map/diagonal_rows/pallas_call | solution.py:479
  30.1 3.5 %collective-permute-start.1 = (f32[4,9,32,128]{3,2,1,0:T(8,128)}, f32[4,9,32,128]{3,2,1,0:T(8,128)S(1)}, u32[]{:S(2)}, u32[]{:S(2)}) collective-permute-start(f32[4,9,32,128]{3,2,1,0:T(8,128)} %get-tuple-element.41), channel_id=1, source_target_pairs={{0,2},{2,4},{4,6},{1,3},{3,5},{5,7},{8,10},{10,12},{12,14},{9,11},... | collective-permute-start | bytes 1769480 | tf_op jit(solution)/shard_map/ppermute | solution.py:487
  33.6 1.3 %collective-permute-start.2 = (f32[4,9,32,128]{3,2,1,0:T(8,128)}, f32[4,9,32,128]{3,2,1,0:T(8,128)S(1)}, u32[]{:S(2)}, u32[]{:S(2)}) collective-permute-start(f32[4,9,32,128]{3,2,1,0:T(8,128)} %get-tuple-element.42), channel_id=1, source_target_pairs={{2,0},{4,2},{6,4},{3,1},{5,3},{7,5},{10,8},{12,10},{14,12},{11,9},... | collective-permute-start | bytes 1769480 | tf_op jit(solution)/shard_map/ppermute | solution.py:488
  35.0 1.4 %copy-done.1 = f32[8,3,128,128]{3,2,1,0:T(8,128)S(1)} copy-done((f32[8,3,128,128]{3,2,1,0:T(8,128)S(1)}, f32[8,3,128,128]{3,2,1,0:T(8,128)}, u32[]{:S(2)}) %copy-start.1) | copy-done | bytes 1572888
  36.4 3.5 %inner_steps.1 = (f32[4,26,48,128]{3,2,1,0:T(8,128)S(1)}, f32[4,24,48,128]{3,2,1,0:T(8,128)S(1)}, f32[4,22,48,128]{3,2,1,0:T(8,128)S(1)}, f32[4,20,48,128]{3,2,1,0:T(8,128)S(1)}, f32[4,26,48,128]{3,2,1,0:T(8,128)S(1)}) custom-call(f32[8,3,128,128]{3,2,1,0:T(8,128)S(1)} %copy-done.1, f32[4,24,48,128]{3,2,1,0:T(8,128)S(1)} %get-tuple-element.35.diagonal_ref.diagonal_in), custom_call_target="tpu_custom_call" | custom-call | flops 8388608 | bytes 4194304 | tf_op jit(solution)/shard_map/inner_steps/pallas_call | solution.py:497
  39.9 7.0 %collective-permute-done.1.low_ref = f32[4,9,32,128]{3,2,1,0:T(8,128)S(1)} collective-permute-done((f32[4,9,32,128]{3,2,1,0:T(8,128)}, f32[4,9,32,128]{3,2,1,0:T(8,128)S(1)}, u32[]{:S(2)}, u32[]{:S(2)}) %collective-permute-start.1) | collective-permute-done | bytes 589856 | tf_op jit(solution)/shard_map/ppermute | solution.py:487
  47.0 4.0 %collective-permute-done.2.high_ref = f32[4,9,32,128]{3,2,1,0:T(8,128)S(1)} collective-permute-done((f32[4,9,32,128]{3,2,1,0:T(8,128)}, f32[4,9,32,128]{3,2,1,0:T(8,128)S(1)}, u32[]{:S(2)}, u32[]{:S(2)}) %collective-permute-start.2) | collective-permute-done | bytes 589856 | tf_op jit(solution)/shard_map/ppermute | solution.py:488
  51.0 2.8 %first_steps.1 = (f32[4,26,48,128]{3,2,1,0:T(8,128)S(1)}, f32[4,24,48,128]{3,2,1,0:T(8,128)S(1)}, f32[4,24,48,128]{3,2,1,0:T(8,128)S(1)}, f32[4,22,48,128]{3,2,1...) custom-call(s32[4]{0:T(128)S(1)} %pad_add_fusion.ends_ref, ...), custom_call_target="tpu_custom_call", output_to_operand_aliasing={{0}: (1, {}), {1}: (2, {}), {2}: (3, {}), {3}: (4, {}), {4}... | custom-call | tf_op jit(solution)/shard_map/first_steps/pallas_call | solution.py:508
  53.8 3.5 %collective-permute-start.3 = (f32[4,5,32,128]{3,2,1,0:T(8,128)S(1)}, f32[4,5,32,128]{3,2,1,0:T(8,128)S(1)}, u32[]{:S(2)}, u32[]{:S(2)}) collective-permute-start(f32[4,5,32,128]{3,2,1,0:T(8,128)S(1)} %get-tuple-element.53), channel_id=1, source_target_pairs={{0,2},{2,4},{4,6},{1,3},{3,5},{5,7},{8,10},{10,12},{12,14},{9,11},... | collective-permute-start | bytes 983048 | tf_op jit(solution)/shard_map/ppermute | solution.py:518
  57.3 1.3 %collective-permute-start.4 = (f32[4,5,32,128]{3,2,1,0:T(8,128)S(1)}, f32[4,5,32,128]{3,2,1,0:T(8,128)S(1)}, u32[]{:S(2)}, u32[]{:S(2)}) collective-permute-start(f32[4,5,32,128]{3,2,1,0:T(8,128)S(1)} %get-tuple-element.54), channel_id=1, source_target_pairs={{2,0},{4,2},{6,4},{3,1},{5,3},{7,5},{10,8},{12,10},{14,12},{11,9},... | collective-permute-start | bytes 983048 | tf_op jit(solution)/shard_map/ppermute | solution.py:519
  58.6 1.6 %middle_step.1 = (f32[4,24,48,128]{3,2,1,0:T(8,128)S(1)}, f32[8,128]{1,0:T(8,128)S(1)}) custom-call(f32[4,26,48,128]{3,2,1,0:T(8,128)S(1)} %get-tuple-element.43.c0_ref, f32[4,22,48,128]{3,2,1,0:T(8,128)S(1)} %get-tuple-element.46.c1_ref, f32[4,26,48,128]{3,2,1,0:T(8,128)S(1)} %get-tuple-element.48.c2_ref.c2_in, ...), custom_call_target="tpu_custom_call" | custom-call | flops 6291456 | bytes 4194304 | tf_op jit(solution)/shard_map/middle_step/pallas_call | solution.py:520
  60.2 2.7 %collective-permute-start.5 = (f32[8,128]{1,0:T(8,128)S(1)}, f32[8,128]{1,0:T(8,128)S(1)}, u32[]{:S(2)}, u32[]{:S(2)}) collective-permute-start(f32[8,128]{1,0:T(8,128)S(1)} %get-tuple-element.60.rest_0_), channel_id=1, source_target_pairs={{0,2},{2,4},{4,6},{6,0},{1,3},{3,5},{5,7},{7,1},{8,10},{10,12},{12... | collective-permute-start | bytes 12296 | tf_op jit(solution)/shard_map/ppermute | solution.py:531
  62.9 1.1 %collective-permute-start.6 = (f32[8,128]{1,0:T(8,128)S(1)}, f32[8,128]{1,0:T(8,128)S(1)}, u32[]{:S(2)}, u32[]{:S(2)}) collective-permute-start(f32[8,128]{1,0:T(8,128)S(1)} %get-tuple-element.60.rest_0_), channel_id=1, source_target_pairs={{0,4},{2,6},{4,0},{6,2},{1,5},{3,7},{5,1},{7,3},{8,12},{10,14},{12... | collective-permute-start | bytes 12296 | tf_op jit(solution)/shard_map/ppermute | solution.py:531
  64.0 2.8 %collective-permute-start.7 = (f32[8,128]{1,0:T(8,128)S(1)}, f32[8,128]{1,0:T(8,128)S(1)}, u32[]{:S(2)}, u32[]{:S(2)}) collective-permute-start(f32[8,128]{1,0:T(8,128)S(1)} %get-tuple-element.60.rest_0_), channel_id=1, source_target_pairs={{0,6},{2,0},{4,2},{6,4},{1,7},{3,1},{5,3},{7,5},{8,14},{10,8},{12,... | collective-permute-start | bytes 12296 | tf_op jit(solution)/shard_map/ppermute | solution.py:531
  66.8 2.4 %second_inner_steps.1 = (f32[4,22,48,128]{3,2,1,0:T(8,128)S(1)}, f32[4,20,48,128]{3,2,1,0:T(8,128)S(1)}, f32[4,18,48,128]{3,2,1,0:T(8,128)S(1)}) custom-call(f32[4,24,48,128]{3,2,1,0:T(8,128)S(1)} %get-tuple-element.44.diagonal_ref, f32[4,26,48,128]{3,2,1,0:T(8,128)S(1)} %get-tuple-element.48.c2_ref.c2_in, f32[4,24,48,128]{3,2,1,0:T(8,128)S(1)} %get-tuple-element.49.d2_ref.d2_in), custom_call_target="tpu_custom_call" | custom-call | flops 7864320 | bytes 4194304 | tf_op jit(solution)/shard_map/second_inner_steps/pallas_call | solution.py:533
  69.3 2.5 %third_steps.1 = (f32[4,26,48,128]{3,2,1,0:T(8,128)S(1)}, f32[4,24,48,128]{3,2,1,0:T(8,128)S(1)}, f32[4,22,48,128]{3,2,1,0:T(8,128)S(1)}, f32[4,20,48,128]{3,2,1,0:T(8,128)S(1)}, f32[4,18,48,128]{3,2,1,0:T(8,128)S(1)}) custom-call(s32[4]{0:T(128)S(1)} %pad_add_fusion.ends_ref, ...), custom_call_target="tpu_custom_call", output_to_operand_aliasing={{0}: (2, {}), {1}: (3, {}), {2}: (4, {}), {3}: (5, {}), {4}... | custom-call | flops 5242880 | bytes 4194304 | tf_op jit(solution)/shard_map/third_steps/pallas_call | solution.py:543
  71.8 2.1 %last_step_given.1 = f32[4,2,128,128]{3,2,1,0:T(8,128)S(1)} custom-call(s32[4]{0:T(128)S(1)} %pad_add_fusion.ends_ref, f32[5,8]{1,0:T(8,128)S(1)} %copy-done.2, f32[4,26,48,128]{3,2,1,0:T(8,128)S(1)} %get-tuple-element.43.c0_ref, f32[4,24,48,128]{3,2,1,0:T(8,128)S(1)} %get-tuple-element.44.diagonal_ref, f32[4,24,48,128]{3,2,1,0:T(8,128)S(1)} %get-tuple-element.45.d0_ref, ...), custom_call_target="tpu_custom_call" | custom-call | flops 5242880 | bytes 4194304 | tf_op jit(solution)/shard_map/last_step_given/pallas_call | solution.py:560
  73.9 2.1 %last_step_kept.1.kept_ref = f32[4,2,128,128]{3,2,1,0:T(8,128)S(1)} custom-call(s32[4]{0:T(128)S(1)} %pad_add_fusion.ends_ref, f32[5,8]{1,0:T(8,128)S(1)} %copy-done.2, f32[4,26,48,128]{3,2,1,0:T(8,128)S(1)} %get-tuple-element.43.c0_ref, f32[4,24,48,128]{3,2,1,0:T(8,128)S(1)} %get-tuple-element.44.diagonal_ref, ...), custom_call_target="tpu_custom_call" | custom-call | flops 5242880 | bytes 4194304 | tf_op jit(solution)/shard_map/last_step_kept/pallas_call | solution.py:560
  76.1 11.8 %all_to_all.11.parts_ref = f32[4,2,128,128]{3,2,1,0:T(8,128)S(1)} all-to-all(f32[4,2,128,128]{3,2,1,0:T(8,128)S(1)} %add_cores.1), channel_id=1, replica_groups=mesh['chip'=2,'core'=2,'gy'=4,'gz'=2] {'chip','gz'}, dimensions={0} | all-to-all | bytes 1048576 | tf_op jit(solution)/shard_map/all_to_all | solution.py:579
  87.9 0.7 sum_chips.1
  (16 shorter events, 0.5 us)
Async XLA Ops:
  26.7 2.0 %copy-start = (f32[8,3,128,128]{3,2,1,0:T(8,128)}, f32[8,3,128,128]{3,2,1,0:T(8,128)S(1)}, u32[]{:S(2)}) copy-start(f32[8,3,128,128]{3,2,1,0:T(8,128)S(1)} %all_to_all.10.blocks_ref) | copy-start | bytes 4718596
  26.7 2.0 %collective-permute-start = (f32[8,128,128]{2,1,0:T(8,128)S(1)}, f32[8,128,128]{2,1,0:T(8,128)S(1)}, u32[]{:S(2)}, u32[]{:S(2)}) collective-permute-start(f32[8,128,128]{2,1,0:T(8,128)S(1)} %half.1.half_ref), channel_id=1, source_target_pairs={{0,8},{8,0},{1,9},{9,1},{2,10},{10,2},{3,11},{11,3},{4,12},{12,4},... | collective-permute-start | bytes 1572872 | tf_op jit(solution)/shard_map/ppermute | solution.py:469
  30.1 16.9 %collective-permute-start.1 = (f32[4,9,32,128]{3,2,1,0:T(8,128)}, f32[4,9,32,128]{3,2,1,0:T(8,128)S(1)}, u32[]{:S(2)}, u32[]{:S(2)}) collective-permute-start(f32[4,9,32,128]{3,2,1,0:T(8,128)} %get-tuple-element.41), channel_id=1, source_target_pairs={{0,2},{2,4},{4,6},{1,3},{3,5},{5,7},{8,10},{10,12},{12,14},{9,11},... | collective-permute-start | bytes 1769480 | tf_op jit(solution)/shard_map/ppermute | solution.py:487
  33.6 17.4 %collective-permute-start.2 = (f32[4,9,32,128]{3,2,1,0:T(8,128)}, f32[4,9,32,128]{3,2,1,0:T(8,128)S(1)}, u32[]{:S(2)}, u32[]{:S(2)}) collective-permute-start(f32[4,9,32,128]{3,2,1,0:T(8,128)} %get-tuple-element.42), channel_id=1, source_target_pairs={{2,0},{4,2},{6,4},{3,1},{5,3},{7,5},{10,8},{12,10},{14,12},{11,9},... | collective-permute-start | bytes 1769480 | tf_op jit(solution)/shard_map/ppermute | solution.py:488
  35.0 1.4 %copy-start.1 = (f32[8,3,128,128]{3,2,1,0:T(8,128)S(1)}, f32[8,3,128,128]{3,2,1,0:T(8,128)}, u32[]{:S(2)}) copy-start(f32[8,3,128,128]{3,2,1,0:T(8,128)} %copy-done) | copy-start | bytes 4718596
  53.8 15.4 %collective-permute-start.3 = (f32[4,5,32,128]{3,2,1,0:T(8,128)S(1)}, f32[4,5,32,128]{3,2,1,0:T(8,128)S(1)}, u32[]{:S(2)}, u32[]{:S(2)}) collective-permute-start(f32[4,5,32,128]{3,2,1,0:T(8,128)S(1)} %get-tuple-element.53), channel_id=1, source_target_pairs={{0,2},{2,4},{4,6},{1,3},{3,5},{5,7},{8,10},{10,12},{12,14},{9,11},... | collective-permute-start | bytes 983048 | tf_op jit(solution)/shard_map/ppermute | solution.py:518
  57.3 11.9 %collective-permute-start.4 = (f32[4,5,32,128]{3,2,1,0:T(8,128)S(1)}, f32[4,5,32,128]{3,2,1,0:T(8,128)S(1)}, u32[]{:S(2)}, u32[]{:S(2)}) collective-permute-start(f32[4,5,32,128]{3,2,1,0:T(8,128)S(1)} %get-tuple-element.54), channel_id=1, source_target_pairs={{2,0},{4,2},{6,4},{3,1},{5,3},{7,5},{10,8},{12,10},{14,12},{11,9},... | collective-permute-start | bytes 983048 | tf_op jit(solution)/shard_map/ppermute | solution.py:519
  60.2 11.5 %collective-permute-start.5 = (f32[8,128]{1,0:T(8,128)S(1)}, f32[8,128]{1,0:T(8,128)S(1)}, u32[]{:S(2)}, u32[]{:S(2)}) collective-permute-start(f32[8,128]{1,0:T(8,128)S(1)} %get-tuple-element.60.rest_0_), channel_id=1, source_target_pairs={{0,2},{2,4},{4,6},{6,0},{1,3},{3,5},{5,7},{7,1},{8,10},{10,12},{12... | collective-permute-start | bytes 12296 | tf_op jit(solution)/shard_map/ppermute | solution.py:531
  62.9 8.8 %collective-permute-start.6 = (f32[8,128]{1,0:T(8,128)S(1)}, f32[8,128]{1,0:T(8,128)S(1)}, u32[]{:S(2)}, u32[]{:S(2)}) collective-permute-start(f32[8,128]{1,0:T(8,128)S(1)} %get-tuple-element.60.rest_0_), channel_id=1, source_target_pairs={{0,4},{2,6},{4,0},{6,2},{1,5},{3,7},{5,1},{7,3},{8,12},{10,14},{12... | collective-permute-start | bytes 12296 | tf_op jit(solution)/shard_map/ppermute | solution.py:531
  64.0 7.8 %collective-permute-start.7 = (f32[8,128]{1,0:T(8,128)S(1)}, f32[8,128]{1,0:T(8,128)S(1)}, u32[]{:S(2)}, u32[]{:S(2)}) collective-permute-start(f32[8,128]{1,0:T(8,128)S(1)} %get-tuple-element.60.rest_0_), channel_id=1, source_target_pairs={{0,6},{2,0},{4,2},{6,4},{1,7},{3,1},{5,3},{7,5},{8,14},{10,8},{12,... | collective-permute-start | bytes 12296 | tf_op jit(solution)/shard_map/ppermute | solution.py:531
  69.2 2.5 %copy-start.2 = (f32[5,8]{1,0:T(8,128)S(1)}, f32[5,8]{1,0:T(8,128)}, u32[]{:S(2)}) copy-start(f32[5,8]{1,0:T(8,128)} %weights_ref.3) | copy-start | bytes 484
  73.8 2.2 %collective-permute-start.8 = (f32[4,2,128,128]{3,2,1,0:T(8,128)S(1)}, f32[4,2,128,128]{3,2,1,0:T(8,128)S(1)}, u32[]{:S(2)}, u32[]{:S(2)}) collective-permute-start(f32[4,2,128,128]{3,2,1,0:T(8,128)S(1)} %last_step_given.1), channel_id=1, source_target_pairs={{0,8},{8,0},{1,9},{9,1},{2,10},{10,2},{3,11},{11,3},{4,12},{12,4},... | collective-permute-start | bytes 1572872 | tf_op jit(solution)/shard_map/ppermute | solution.py:570

commit v9 on v8

--- a/solution.py
+++ b/solution.py
@@ -120,7 +120,7 @@
         apply_block(target, source, diagonal, start, count % block, minus, masks)
 
 
-def apply_strips(ends_ref, own, target, source, diagonal, halo, size, minus=None):
+def apply_strips(spot_ref, own, target, source, diagonal, halo, size, minus=None):
     masks = lane_masks()
 
     def body(step, carry):
@@ -129,92 +129,121 @@
         return carry
 
     lax.fori_loop(0, 2, body, 0)
-    clear_outside(ends_ref, own, target)
-
-
-def clear_outside(ends_ref, own, field):
-    @pl.when(ends_ref[0] == 1)
+    clear_outside(spot_ref, own, target)
+
+
+def clear_outside(spot_ref, own, field):
+    @pl.when(spot_ref[0] == 1)
     def _():
         field.clear_row(-1)
 
-    @pl.when(ends_ref[1] == 1)
+    @pl.when(spot_ref[1] == 1)
     def _():
         field.clear_row(own)
 
 
-def places(grid):
-    nx, nz, bx, by, bz = grid
-    per = bz // 128
-    for s in range(nx * nz):
-        for column in range(per):
-            yield s, column, (s // nz) * bx, (s % nz) * per + column
-
-
-def pack_kernel(grid, count, probes_ref, kappa_ref, out_ref, sem):
-    nx, nz, bx, by, bz = grid
-    per = bz // 128
-    rows = bx * by
+def split_chip(grid, chip):
+    nz = grid[1]
+    return lax.div(chip, nz), lax.rem(chip, nz)
+
+
+def pack_kappa_kernel(kappa_ref, out_ref, sem):
     copies = []
-    for s in range(nx * nz):
-        parts = [
-            probes_ref.at[pl.ds((s % count) * rows, rows), pl.ds(column * 128, 128)]
-            for column in range(per)
-        ]
-        parts.append(kappa_ref.at[:, pl.ds((s // nz) % 2 * 128, 128)])
-        for index, part in enumerate(parts):
-            copies.append(pltpu.make_async_copy(part, out_ref.at[s, index], sem.at[s, index]))
+    for column in range(out_ref.shape[0]):
+        part = kappa_ref.at[:, pl.ds(column * 128, 128)]
+        copies.append(pltpu.make_async_copy(part, out_ref.at[column], sem.at[column]))
     for copy in copies:
         copy.start()
     for copy in copies:
         copy.wait()
 
 
-def half_kernel(blocks_ref, half_ref):
-    half_ref[...] = blocks_ref[:, blocks_ref.shape[1] - 1]
-
-
-def edge_kernel(grid, blocks_ref, up_ref, down_ref):
+def pack_probes_kernel(grid, count, spot_ref, probes_ref, *rest):
     nx, nz, bx, by, bz = grid
-    for s, column, x, z in places(grid):
-        rows = list(range(HALO)) + list(range(by - HALO, by))
-        values = [blocks_ref[s, column, pl.ds(y, bx, stride=by), :] for y in rows]
-        for y in range(HALO):
-            down_ref[z, y, pl.ds(x, bx), :] = values[y]
-            up_ref[z, y, pl.ds(x, bx), :] = values[HALO + y]
-
-
-def diagonal_kernel(
-    grid, core_ref, half_ref, other_ref, up_in, down_in, own_ref, up_ref, down_ref
-):
+    rows = bx * by
+    outs, sem = rest[:-1], rest[-1]
+    copies = []
+    for k, out in enumerate(outs):
+        x, z = split_chip(grid, spot_ref[4] ^ k)
+        for core in range(2):
+            start = pl.multiple_of(lax.rem((2 * x + core) * nz + z, count) * rows, rows)
+            for column in range(bz // 128):
+                part = probes_ref.at[pl.ds(start, rows), pl.ds(column * 128, 128)]
+                copies.append(
+                    pltpu.make_async_copy(part, out.at[core, column], sem.at[k, core, column])
+                )
+    for copy in copies:
+        copy.start()
+    for copy in copies:
+        copy.wait()
+
+
+def stack_kernel(*refs):
+    for k, ref in enumerate(refs[:-1]):
+        refs[-1][k] = ref[...]
+
+
+def sort_probes_kernel(spot_ref, *refs):
+    parts, mine_ref, give_ref = refs[:-2], refs[-2], refs[-1]
+    core = spot_ref[3]
+    for k, part in enumerate(parts):
+        mine_ref[k] = part[core]
+        give_ref[k] = part[1 - core]
+
+
+def block_rows(grid, spot_ref, mine_ref, other_ref, rows):
     nx, nz, bx, by, bz = grid
+    per = bz // 128
+    core = spot_ref[3]
+    for k in range(nx // 2 * nz):
+        x, z = split_chip(grid, spot_ref[4] ^ k)
+        for ref, side in ((mine_ref, core), (other_ref, 1 - core)):
+            for column in range(per):
+                values = [ref[k, column, pl.ds(y, bx, stride=by), :] for y in rows]
+                yield (2 * x + side) * bx, z * per + column, values
+
+
+def store_own(field, x, z, values):
+    for y, value in enumerate(values):
+        at = pl.ds(pl.multiple_of(PAD + x, 8), 8)
+        field.ref[z, y + field.halo, at, :] = value
+
+
+def store_edges(up_ref, down_ref, x, z, first, last):
+    at = pl.ds(pl.multiple_of(x, 8), 8)
+    for y, value in enumerate(first):
+        down_ref[z, y, at, :] = value
+    for y, value in enumerate(last):
+        up_ref[z, y, at, :] = value
+
+
+def edge_kernel(grid, spot_ref, mine_ref, other_ref, up_ref, down_ref):
+    by = grid[3]
+    rows = list(range(HALO)) + list(range(by - HALO, by))
+    for x, z, values in block_rows(grid, spot_ref, mine_ref, other_ref, rows):
+        store_edges(up_ref, down_ref, x, z, values[:HALO], values[HALO:])
+
+
+def diagonal_kernel(grid, spot_ref, mine_ref, other_ref, own_ref, up_ref, down_ref):
     own = Field(own_ref, DIAGONAL_HALO)
-    first = core_ref[0] == 0
-    up_ref[:, pl.ds(0, HALO)] = up_in[...]
-    down_ref[:, pl.ds(0, HALO)] = down_in[...]
-    for s, column, x, z in places(grid):
-        values = []
-        for y in range(by):
-            rows = pl.ds(y, bx, stride=by)
-            mine, other = half_ref[s, rows, :], other_ref[s, rows, :]
-            pair = (mine, other) if column == 0 else (other, mine)
-            values.append(6.0 + jnp.where(first, *pair))
-        for y in range(by):
-            own.store(z, y, x, values[y])
-        for y in range(DIAGONAL_HALO):
-            down_ref[z, HALO + y, pl.ds(x, bx), :] = values[y]
-            up_ref[z, HALO + y, pl.ds(x, bx), :] = values[by - DIAGONAL_HALO + y]
-
-
-def fill_halo(field, own, low_ref, high_ref, start=0):
+    for x, z, values in block_rows(grid, spot_ref, mine_ref, other_ref, range(grid[3])):
+        values = [6.0 + value for value in values]
+        store_own(own, x, z, values)
+        store_edges(up_ref, down_ref, x, z, values[:DIAGONAL_HALO], values[-DIAGONAL_HALO:])
+
+
+def fill_halo(field, own, low_ref, high_ref):
     for c in range(field.columns):
         for y in range(field.halo):
             for x in range(0, field.cells, 8):
-                field.store(c, y - field.halo, x, low_ref[c, start + y, pl.ds(x, 8), :])
-                field.store(c, own + y, x, high_ref[c, start + y, pl.ds(x, 8), :])
-
-
-def inner_kernel(grid, blocks_ref, diagonal_ref, c0_ref, d0_ref, c1_ref, d1_ref, c2_ref):
-    nx, nz, bx, own, bz = grid
+                field.store(c, y - field.halo, x, low_ref[c, y, pl.ds(x, 8), :])
+                field.store(c, own + y, x, high_ref[c, y, pl.ds(x, 8), :])
+
+
+def inner_kernel(
+    grid, spot_ref, mine_ref, other_ref, diagonal_ref, c0_ref, d0_ref, c1_ref, d1_ref, c2_ref
+):
+    own = grid[3]
     c0 = Field(c0_ref, HALO)
     diagonal = Field(diagonal_ref, DIAGONAL_HALO)
     d0 = Field(d0_ref, 4)
@@ -223,10 +252,8 @@
     c2 = Field(c2_ref, HALO)
     for field in (c0, d0, c1, d1, c2):
         field.clear_pads()
-    for s, column, x, z in places(grid):
-        values = [blocks_ref[s, column, pl.ds(y, bx, stride=own), :] for y in range(own)]
-        for y in range(own):
-            c0.store(z, y, x, values[y])
+    for x, z, values in block_rows(grid, spot_ref, mine_ref, other_ref, range(own)):
+        store_own(c0, x, z, values)
     apply_rows(d0, c0, diagonal, 1, own - 2)
     apply_rows(c1, d0, diagonal, 2, own - 4, c0)
     apply_rows(d1, c1, diagonal, 3, own - 6)
@@ -235,8 +262,8 @@
 
 def first_kernel(
     own,
-    ends_ref, c0_in, diagonal_in, d0_in, c1_in, d1_in, c2_in,
-    low_ref, high_ref,
+    spot_ref, c0_in, diagonal_in, d0_in, c1_in, d1_in, c2_in,
+    low_ref, high_ref, low_diagonal_ref, high_diagonal_ref,
     c0_ref, diagonal_ref, d0_ref, c1_ref, d1_ref, c2_ref, up_ref, down_ref,
 ):
     c0 = Field(c0_ref, HALO)
@@ -246,8 +273,8 @@
     d1 = Field(d1_ref, 2)
     c2 = Field(c2_ref, HALO)
     fill_halo(c0, own, low_ref, high_ref)
-    fill_halo(diagonal, own, low_ref, high_ref, HALO)
-    strips = functools.partial(apply_strips, ends_ref, own)
+    fill_halo(diagonal, own, low_diagonal_ref, high_diagonal_ref)
+    strips = functools.partial(apply_strips, spot_ref, own)
     strips(d0, c0, diagonal, 4, HALO)
     strips(c1, d0, diagonal, 3, HALO, c0)
     strips(d1, c1, diagonal, 2, HALO)
@@ -311,7 +338,7 @@
 
 def third_kernel(
     own,
-    ends_ref, diagonal_ref, c2_in, d2_in, c3_in, d3_in, c4_in, low_ref, high_ref,
+    spot_ref, diagonal_ref, c2_in, d2_in, c3_in, d3_in, c4_in, low_ref, high_ref,
     c2_ref, d2_ref, c3_ref, d3_ref, c4_ref,
 ):
     diagonal = Field(diagonal_ref, DIAGONAL_HALO)
@@ -321,7 +348,7 @@
     d3 = Field(d3_ref, 2)
     c4 = Field(c4_ref, 1)
     fill_halo(c2, own, low_ref, high_ref)
-    strips = functools.partial(apply_strips, ends_ref, own)
+    strips = functools.partial(apply_strips, spot_ref, own)
     strips(d2, c2, diagonal, 4, 4)
     strips(c3, d2, diagonal, 3, 4, c2)
     strips(d3, c3, diagonal, 2, 4)
@@ -330,7 +357,7 @@
 
 def last_kernel(
     grid, inverse_count, flip,
-    ends_ref, weights_ref, c0_ref, diagonal_ref, d0_ref, c1_ref, d1_ref,
+    spot_ref, weights_ref, c0_ref, diagonal_ref, d0_ref, c1_ref, d1_ref,
     c2_ref, d2_ref, c3_ref, d3_ref, c4_ref, *rest,
 ):
     nx, nz, bx, by, bz = grid
@@ -346,7 +373,7 @@
     c3 = Field(c3_ref, 3)
     d3 = Field(d3_ref, 2)
     c4 = Field(c4_ref, 1)
-    slopes = moment_slopes(inverse_count, ends_ref[2], weights_ref, moment_refs)
+    slopes = moment_slopes(inverse_count, spot_ref[2], weights_ref, moment_refs)
     masks = lane_masks()
     block = 2
 
@@ -373,22 +400,25 @@
 
     for core in range(2):
 
-        @pl.when(ends_ref[3] == (1 - core if flip else core))
+        @pl.when(spot_ref[3] == (1 - core if flip else core))
         def _():
             lax.fori_loop(0, by // block, functools.partial(out_rows, core), 0)
 
 
-def add_kernel(kept_ref, got_ref, out_ref):
-    out_ref[...] = kept_ref[...] + got_ref[...]
-
-
-def sum_kernel(grid, parts_ref, out_ref):
+def add_kernel(spot_ref, kept_ref, got_ref, *outs):
+    for k, out in enumerate(outs):
+        chip = spot_ref[4] ^ k
+        out[...] = kept_ref[chip] + got_ref[chip]
+
+
+def sum_kernel(grid, *refs):
     nx, nz, bx, by, bz = grid
+    parts, out_ref = refs[:-1], refs[-1]
     for column in range(bz // 128):
         for x in range(bx):
             total = None
-            for p in range(parts_ref.shape[0]):
-                part = parts_ref[p, column, pl.ds(x * by, by), :]
+            for ref in parts:
+                part = ref[column, pl.ds(x * by, by), :]
                 total = part if total is None else total + part
             out_ref[x, :, pl.ds(column * 128, 128)] = total
 
@@ -448,42 +478,60 @@
     def vector(halo):
         return pltpu.VMEM(padded(halo), jnp.float32)
 
-    blocks = pl.pallas_call(
-        functools.partial(pack_kernel, grid, count),
-        out_shape=f32(group, per + 1, rows, 128),
-        in_specs=[hbm(), hbm()],
-        out_specs=vmem(),
-        scratch_shapes=[pltpu.SemaphoreType.DMA((group, per + 1))],
-        compiler_params=params(),
-        name="pack",
-    )(there(probes.reshape(count * rows, bz)), there(kappa2.reshape(rows, bz)))
-    blocks = lax.all_to_all(blocks, ("chip", "core", "gz"), 0, 0, tiled=True)
-    half = pl.pallas_call(
-        half_kernel,
-        out_shape=f32(group, rows, 128),
-        in_specs=[vmem()],
-        out_specs=vmem(),
-        compiler_params=params(),
-        name="half",
-    )(here(blocks))
-    other = lax.ppermute(half, "core", swap)
-    message = edge(HALO + DIAGONAL_HALO)
-    up_edge, down_edge = pl.pallas_call(
-        functools.partial(edge_kernel, grid),
-        out_shape=(edge(HALO), edge(HALO)),
-        in_specs=[vmem()],
-        out_specs=(vmem(),) * 2,
-        compiler_params=params(),
-        name="probe_edges",
-    )(here(blocks))
-    diagonal, up_edge, down_edge = pl.pallas_call(
-        functools.partial(diagonal_kernel, grid),
-        out_shape=(vector(DIAGONAL_HALO), message, message),
-        in_specs=[smem()] + [vmem()] * 4,
-        out_specs=(vmem(),) * 3,
-        compiler_params=params(),
-        name="diagonal_rows",
-    )(core.astype(jnp.int32).reshape(1), half, other, up_edge, down_edge)
+    chips = nx // 2 * nz
+    assert chips & (chips - 1) == 0
+    chip = lax.axis_index("chip") * nz + lax.axis_index("gz")
+    spot = jnp.stack([gy == 0, gy == ny - 1, mine, core, chip]).astype(jnp.int32)
+
+    def to_chip(value, k):
+        pairs = [(i, i ^ k) for i in range(chips)]
+        return lax.ppermute(value, ("chip", "gz"), pairs)
+
+    def plain(kernel, name, out_shape, specs, *operands, **options):
+        return pl.pallas_call(
+            kernel,
+            out_shape=out_shape,
+            in_specs=specs,
+            out_specs=(vmem(),) * len(out_shape) if isinstance(out_shape, tuple) else vmem(),
+            compiler_params=params(),
+            name=name,
+            **options,
+        )(*operands)
+
+    dma = pltpu.SemaphoreType.DMA
+    block = f32(per, rows, 128)
+    stacked = f32(chips, per, rows, 128)
+    kappa = plain(
+        pack_kappa_kernel, "pack_kappa", block, [hbm()], there(kappa2.reshape(rows, bz)),
+        scratch_shapes=[dma((per,))],
+    )
+    kappas = [kappa] + [to_chip(kappa, k) for k in range(1, chips)]
+    packed = plain(
+        functools.partial(pack_probes_kernel, grid, count), "pack_probes",
+        (f32(2, per, rows, 128),) * chips, [smem(), hbm()],
+        spot, there(probes.reshape(count * rows, bz)), scratch_shapes=[dma((chips, 2, per))],
+    )
+    probes = [packed[0]] + [to_chip(packed[k], k) for k in range(1, chips)]
+
+    kappa = plain(stack_kernel, "stack_kappa", stacked, [vmem()] * chips, *kappas)
+    other = lax.ppermute(kappa, "core", swap)
+    diagonal, up_edge, down_edge = plain(
+        functools.partial(diagonal_kernel, grid), "diagonal_rows",
+        (vector(DIAGONAL_HALO), edge(DIAGONAL_HALO), edge(DIAGONAL_HALO)),
+        [smem(), vmem(), vmem()], spot, kappa, other,
+    )
+    low_diagonal = lax.ppermute(up_edge, "gy", up)
+    high_diagonal = lax.ppermute(down_edge, "gy", down)
+
+    probe, give = plain(
+        sort_probes_kernel, "sort_probes", (stacked, stacked),
+        [smem()] + [vmem()] * chips, spot, *probes,
+    )
+    other = lax.ppermute(give, "core", swap)
+    up_edge, down_edge = plain(
+        functools.partial(edge_kernel, grid), "probe_edges", (edge(HALO), edge(HALO)),
+        [smem(), vmem(), vmem()], spot, probe, other,
+    )
     low1 = lax.ppermute(up_edge, "gy", up)
     high1 = lax.ppermute(down_edge, "gy", down)
 
@@ -497,24 +545,23 @@
     inner = pl.pallas_call(
         functools.partial(inner_kernel, grid),
         out_shape=tuple(vector(h) for h in (HALO, 4, 3, 2, HALO)),
-        in_specs=[vmem()] * 2,
+        in_specs=[smem()] + [vmem()] * 3,
         out_specs=(vmem(),) * 5,
         compiler_params=params(),
         cost_estimate=cost(32),
         name="inner_steps",
-    )(here(blocks), here(diagonal))
-    ends = jnp.stack([gy == 0, gy == ny - 1, mine, core]).astype(jnp.int32)
+    )(spot, probe, other, here(diagonal))
     vectors = [here(value) for value in (inner[0], diagonal) + tuple(inner[1:])]
     c0, diagonal, d0, c1, d1, c2, up_edge, down_edge = pl.pallas_call(
         functools.partial(first_kernel, by),
         out_shape=tuple(vector(h) for h in (HALO, DIAGONAL_HALO, 4, 3, 2, HALO))
         + (edge(HALO), edge(HALO)),
-        in_specs=[smem()] + [vmem()] * 8,
+        in_specs=[smem()] + [vmem()] * 10,
         out_specs=(vmem(),) * 8,
         input_output_aliases={i + 1: i for i in range(6)},
         compiler_params=params(),
         name="first_steps",
-    )(ends, *vectors, low1, high1)
+    )(spot, *vectors, low1, high1, low_diagonal, high_diagonal)
     low2 = lax.ppermute(up_edge, "gy", up)
     high2 = lax.ppermute(down_edge, "gy", down)
     d2, moments = pl.pallas_call(
@@ -549,42 +596,32 @@
         compiler_params=params(),
         cost_estimate=cost(20),
         name="third_steps",
-    )(ends, *vectors, low2, high2)
+    )(spot, *vectors, low2, high2)
     inverse_count = 1.0 / (ny * cells)
     vectors = [here(value) for value in (c0, diagonal, d0, c1, d1, c2, d2, c3, d3, c4)]
     if group > count:
         cotangents = jnp.where(place < count, cotangents, 0.0)
-    blocks = f32(group // 2, per, rows, 128)
 
     def last_step(flip):
         return pl.pallas_call(
             functools.partial(last_kernel, grid, inverse_count, flip),
-            out_shape=blocks,
+            out_shape=stacked,
             in_specs=[smem(), smem()] + [vmem()] * (10 + ny),
             out_specs=vmem(),
             compiler_params=params(),
             cost_estimate=cost(20),
             name="last_step_given" if flip else "last_step_kept",
-        )(ends, cotangents, *vectors, *shares)
+        )(spot, cotangents, *vectors, *shares)
 
     got = lax.ppermute(last_step(True), "core", swap)
-    parts = pl.pallas_call(
-        add_kernel,
-        out_shape=blocks,
-        in_specs=[vmem()] * 2,
-        out_specs=vmem(),
-        compiler_params=params(),
-        name="add_cores",
-    )(last_step(False), got)
-    parts = lax.all_to_all(parts, ("chip", "gz"), 0, 0, tiled=True)
-    return pl.pallas_call(
-        functools.partial(sum_kernel, grid),
-        out_shape=f32(bx, by, bz),
-        in_specs=[vmem()],
-        out_specs=vmem(),
-        compiler_params=params(),
-        name="sum_chips",
-    )(parts)
+    parts = plain(
+        add_kernel, "add_cores", (block,) * chips, [smem(), vmem(), vmem()],
+        spot, last_step(False), got,
+    )
+    parts = [parts[0]] + [to_chip(parts[k], k) for k in range(chips - 1, 0, -1)]
+    return plain(
+        functools.partial(sum_kernel, grid), "sum_chips", f32(bx, by, bz), [vmem()] * chips, *parts
+    )
 
 
 def solution(mesh):

time: 88.9 us -> 81.7 us (0.919)
  blocking collectives: 36.9 us -> 0 us
  starting transfers between devices: 16.7 us -> 37.7 us
  waiting for transfers between devices: 12.4 us -> 20.1 us
  Pallas kernels: 20.9 us -> 23.2 us
  local copies, waits for them, and re-layouts: 1.42 us -> 0.09 us
    all_to_all x2 -> x0, blocking collectives: 36.9 us -> none  [the longest x1 25 us: body(): blocks = lax.all_to_all(blocks, ('chip', 'core', 'gz'), 0, 0, tiled=True)]
    ppermute x1 -> x13, starting transfers between devices: 0.43 us -> 21.3 us  [the longest x9 15.3 us: to_chip(): return lax.ppermute(value, ('chip', 'gz'), pairs)]
    ppermute x1 -> x13, waiting for transfers between devices: 1.33 us -> 20 us  [the longest x9 14.7 us: to_chip(): return lax.ppermute(value, ('chip', 'gz'), pairs)]
    ppermute x1, waiting for transfers between devices: 7.04 us -> 0.01 us  [body(): low1 = lax.ppermute(up_edge, 'gy', up)]
    ppermute x1, waiting for transfers between devices: 4.04 us -> 0.01 us  [body(): high1 = lax.ppermute(down_edge, 'gy', down)]
    pallas_call x6 -> x8, Pallas kernels: 3.98 us -> 6.42 us  [plain(): pl.pallas_call(kernel, out_shape=out_shape, in_specs=specs, out_specs=(vm...]
    unnamed x6 -> x2, local copies, waits for them, and re-layouts: 1.42 us -> 0.01 us
  transfers between devices with their start and end apart: 9 -> 21, of which waited for: 3 -> 8; matrix products, arithmetic and copies ran while one was open for 0% -> 0% of each run, Pallas kernels for 14% -> 19%
where the time goes in v9:
time: 81.7 us; the launch traced here: 81.3 us
  starting transfers between devices  37.7 us (46%)
  Pallas kernels  23.2 us (28%)
  waiting for transfers between devices  20.1 us (25%)
    ppermute x9, starting transfers between devices, to_chip(): return lax.ppermute(value, ('chip', 'gz'), pairs)  15.3 us
    ppermute x9, waiting for transfers between devices, to_chip(): return lax.ppermute(value, ('chip', 'gz'), pairs)  14.7 us
    ppermute x3, starting transfers between devices, body(): lax.ppermute(moments, 'gy', [(i, (i + step) % ny) for i in range(ny)])  6.62 us
    pallas_call x8, Pallas kernels, plain(): pl.pallas_call(kernel, out_shape=out_shape, in_specs=specs, out_specs=(vm...  6.42 us
    ppermute x1, starting transfers between devices, body(): low_diagonal = lax.ppermute(up_edge, 'gy', up)  4.56 us
    ppermute x1, waiting for transfers between devices, body(): high_diagonal = lax.ppermute(down_edge, 'gy', down)  4.13 us
    pallas_call x2, Pallas kernels, last_step(): pl.pallas_call(functools.partial(last_kernel, grid, inverse_count, flip),...  4.06 us
    pallas_call x1, Pallas kernels, body(): pl.pallas_call(functools.partial(inner_kernel, grid), out_shape=tuple((ve...  3.91 us
  transfers between devices with their start and end apart: 21, of which 8 were waited for; matrix products, arithmetic and copies ran while one was open for 0% of the time, Pallas kernels for 19%

profile of v9, /device:TPU:0, one launch (start us, length us, event | category | flops | bytes accessed | tf_op | source)
XLA Modules:
  0.0 81.3 jit_solution(15536690479931743700)
XLA Ops:
  0.1 1.9 %pack_probes.1 = (f32[2,2,128,128]{3,2,1,0:T(8,128)S(1)}, f32[2,2,128,128]{3,2,1,0:T(8,128)S(1)}, f32[2,2,128,128]{3,2,1,0:T(8,128)S(1)}, f32[2,2,128,128]{3,2,1,0:T(8,128)S(1)}) custom-call(s32[5]{0:T(128)S(1)} %stack.31.spot_ref, f32[1024,256]{1,0:T(8,128)} %bitcast.7), custom_call_target="tpu_custom_call" | custom-call | tf_op jit(solution)/shard_map/pack_probes/pallas_call | solution.py:491
  2.0 3.0 %collective-permute-start = (f32[2,2,128,128]{3,2,1,0:T(8,128)S(1)}, f32[2,2,128,128]{3,2,1,0:T(8,128)S(1)}, u32[]{:S(2)}, u32[]{:S(2)}) collective-permute-start(f32[2,2,128,128]{3,2,1,0:T(8,128)S(1)} %get-tuple-element.44), channel_id=1, source_target_pairs={{0,1},{1,0},{16,17},{17,16},{2,3},{3,2},{18,19},{19,18},{4,5},{5,4... | collective-permute-start | bytes 786440 | tf_op jit(solution)/shard_map/ppermute | solution.py:488
  5.1 1.5 %collective-permute-start.1 = (f32[2,2,128,128]{3,2,1,0:T(8,128)S(1)}, f32[2,2,128,128]{3,2,1,0:T(8,128)S(1)}, u32[]{:S(2)}, u32[]{:S(2)}) collective-permute-start(f32[2,2,128,128]{3,2,1,0:T(8,128)S(1)} %get-tuple-element.45), channel_id=1, source_target_pairs={{0,16},{1,17},{16,0},{17,1},{2,18},{3,19},{18,2},{19,3},{4,20},{5,... | collective-permute-start | bytes 786440 | tf_op jit(solution)/shard_map/ppermute | solution.py:488
  7.5 2.0 %collective-permute-start.4 = (f32[2,128,128]{2,1,0:T(8,128)S(1)}, f32[2,128,128]{2,1,0:T(8,128)S(1)}, u32[]{:S(2)}, u32[]{:S(2)}) collective-permute-start(f32[2,128,128]{2,1,0:T(8,128)S(1)} %pack_kappa.1.refs_0_), channel_id=1, source_target_pairs={{0,1},{1,0},{16,17},{17,16},{2,3},{3,2},{18,19},{19,18},{4,5},{5,4... | collective-permute-start | bytes 393224 | tf_op jit(solution)/shard_map/ppermute | solution.py:488
  9.5 1.5 %collective-permute-start.5 = (f32[2,128,128]{2,1,0:T(8,128)S(1)}, f32[2,128,128]{2,1,0:T(8,128)S(1)}, u32[]{:S(2)}, u32[]{:S(2)}) collective-permute-start(f32[2,128,128]{2,1,0:T(8,128)S(1)} %pack_kappa.1.refs_0_), channel_id=1, source_target_pairs={{0,16},{1,17},{16,0},{17,1},{2,18},{3,19},{18,2},{19,3},{4,20},{5,... | collective-permute-start | bytes 393224 | tf_op jit(solution)/shard_map/ppermute | solution.py:488
  11.0 1.9 %collective-permute-done.refs_1_ = f32[2,2,128,128]{3,2,1,0:T(8,128)S(1)} collective-permute-done((f32[2,2,128,128]{3,2,1,0:T(8,128)S(1)}, f32[2,2,128,128]{3,2,1,0:T(8,128)S(1)}, u32[]{:S(2)}, u32[]{:S(2)}) %collective-permute-start) | collective-permute-done | bytes 262176 | tf_op jit(solution)/shard_map/ppermute | solution.py:488
  12.9 3.7 %collective-permute-start.6 = (f32[2,128,128]{2,1,0:T(8,128)S(1)}, f32[2,128,128]{2,1,0:T(8,128)S(1)}, u32[]{:S(2)}, u32[]{:S(2)}) collective-permute-start(f32[2,128,128]{2,1,0:T(8,128)S(1)} %pack_kappa.1.refs_0_), channel_id=1, source_target_pairs={{0,17},{1,16},{16,1},{17,0},{2,19},{3,18},{18,3},{19,2},{4,21},{5,... | collective-permute-start | bytes 393224 | tf_op jit(solution)/shard_map/ppermute | solution.py:488
  16.6 2.8 %collective-permute-done.2.refs_3_ = f32[2,2,128,128]{3,2,1,0:T(8,128)S(1)} collective-permute-done((f32[2,2,128,128]{3,2,1,0:T(8,128)S(1)}, f32[2,2,128,128]{3,2,1,0:T(8,128)S(1)}, u32[]{:S(2)}, u32[]{:S(2)}) %collective-permute-start.2) | collective-permute-done | bytes 262176 | tf_op jit(solution)/shard_map/ppermute | solution.py:488
  20.1 2.6 %collective-permute-done.5.refs_2_ = f32[2,128,128]{2,1,0:T(8,128)S(1)} collective-permute-done((f32[2,128,128]{2,1,0:T(8,128)S(1)}, f32[2,128,128]{2,1,0:T(8,128)S(1)}, u32[]{:S(2)}, u32[]{:S(2)}) %collective-permute-start.5) | collective-permute-done | bytes 131104 | tf_op jit(solution)/shard_map/ppermute | solution.py:488
  24.8 3.6 %collective-permute-start.8 = (f32[4,5,32,128]{3,2,1,0:T(8,128)S(1)}, f32[4,5,32,128]{3,2,1,0:T(8,128)S(1)}, u32[]{:S(2)}, u32[]{:S(2)}) collective-permute-start(f32[4,5,32,128]{3,2,1,0:T(8,128)S(1)} %get-tuple-element.55), channel_id=1, source_target_pairs={{0,2},{2,4},{4,6},{1,3},{3,5},{5,7},{8,10},{10,12},{12,14},{9,11},... | collective-permute-start | bytes 983048 | tf_op jit(solution)/shard_map/ppermute | solution.py:535
  30.7 4.6 %collective-permute-start.10 = (f32[4,4,32,128]{3,2,1,0:T(8,128)S(1)}, f32[4,4,32,128]{3,2,1,0:T(8,128)S(1)}, u32[]{:S(2)}, u32[]{:S(2)}) collective-permute-start(f32[4,4,32,128]{3,2,1,0:T(8,128)S(1)} %get-tuple-element.57), channel_id=1, source_target_pairs={{0,2},{2,4},{4,6},{1,3},{3,5},{5,7},{8,10},{10,12},{12,14},{9,11},... | collective-permute-start | bytes 786440 | tf_op jit(solution)/shard_map/ppermute | solution.py:523
  36.6 3.9 %inner_steps.1 = (f32[4,26,48,128]{3,2,1,0:T(8,128)S(1)}, f32[4,24,48,128]{3,2,1,0:T(8,128)S(1)}, f32[4,22,48,128]{3,2,1,0:T(8,128)S(1)}, f32[4,20,48,128]{3,2,1,0:T(8,128)S(1)}, f32[4,26,48,128]{3,2,1,0:T(8,128)S(1)}) custom-call(s32[5]{0:T(128)S(1)} %stack.31.spot_ref, f32[4,2,128,128]{3,2,1,0:T(8,128)S(1)} %get-tuple-element.47.mine_ref, ...), custom_call_target="tpu_custom_call" | custom-call | flops 8388608 | bytes 4194304 | tf_op jit(solution)/shard_map/inner_steps/pallas_call | solution.py:545
  41.6 4.1 %collective-permute-done.11.high_diagonal_ref = f32[4,4,32,128]{3,2,1,0:T(8,128)S(1)} collective-permute-done((f32[4,4,32,128]{3,2,1,0:T(8,128)S(1)}, f32[4,4,32,128]{3,2,1,0:T(8,128)S(1)}, u32[]{:S(2)}, u32[]{:S(2)}) %collective-permute-start.11) | collective-permute-done | bytes 262176 | tf_op jit(solution)/shard_map/ppermute | solution.py:524
  45.8 2.6 %first_steps.1 = (f32[4,26,48,128]{3,2,1,0:T(8,128)S(1)}, f32[4,24,48,128]{3,2,1,0:T(8,128)S(1)}, f32[4,24,48,128]{3,2,1,0:T(8,128)S(1)}, f32[4,22,48,128]{3,2,1...) custom-call(s32[5]{0:T(128)S(1)} %stack.31.spot_ref, ...), custom_call_target="tpu_custom_call", output_to_operand_aliasing={{0}: (1, {}), {1}: (2, {}), {2}: (3, {}), {3}: (4, {}), {4}... | custom-call | tf_op jit(solution)/shard_map/first_steps/pallas_call | solution.py:555
  48.4 3.5 %collective-permute-start.12 = (f32[4,5,32,128]{3,2,1,0:T(8,128)S(1)}, f32[4,5,32,128]{3,2,1,0:T(8,128)S(1)}, u32[]{:S(2)}, u32[]{:S(2)}) collective-permute-start(f32[4,5,32,128]{3,2,1,0:T(8,128)S(1)} %get-tuple-element.69), channel_id=1, source_target_pairs={{0,2},{2,4},{4,6},{1,3},{3,5},{5,7},{8,10},{10,12},{12,14},{9,11},... | collective-permute-start | bytes 983048 | tf_op jit(solution)/shard_map/ppermute | solution.py:565
  54.7 2.7 %collective-permute-start.14 = (f32[8,128]{1,0:T(8,128)S(1)}, f32[8,128]{1,0:T(8,128)S(1)}, u32[]{:S(2)}, u32[]{:S(2)}) collective-permute-start(f32[8,128]{1,0:T(8,128)S(1)} %get-tuple-element.76.rest_0_), channel_id=1, source_target_pairs={{0,2},{2,4},{4,6},{6,0},{1,3},{3,5},{5,7},{7,1},{8,10},{10,12},{12... | collective-permute-start | bytes 12296 | tf_op jit(solution)/shard_map/ppermute | solution.py:578
  58.5 2.8 %collective-permute-start.16 = (f32[8,128]{1,0:T(8,128)S(1)}, f32[8,128]{1,0:T(8,128)S(1)}, u32[]{:S(2)}, u32[]{:S(2)}) collective-permute-start(f32[8,128]{1,0:T(8,128)S(1)} %get-tuple-element.76.rest_0_), channel_id=1, source_target_pairs={{0,6},{2,0},{4,2},{6,4},{1,7},{3,1},{5,3},{7,5},{8,14},{10,8},{12,... | collective-permute-start | bytes 12296 | tf_op jit(solution)/shard_map/ppermute | solution.py:578
  61.3 2.3 %second_inner_steps.1 = (f32[4,22,48,128]{3,2,1,0:T(8,128)S(1)}, f32[4,20,48,128]{3,2,1,0:T(8,128)S(1)}, f32[4,18,48,128]{3,2,1,0:T(8,128)S(1)}) custom-call(f32[4,24,48,128]{3,2,1,0:T(8,128)S(1)} %get-tuple-element.60.diagonal_ref, f32[4,26,48,128]{3,2,1,0:T(8,128)S(1)} %get-tuple-element.64.c2_ref.c2_in, f32[4,24,48,128]{3,2,1,0:T(8,128)S(1)} %get-tuple-element.65.d2_ref.d2_in), custom_call_target="tpu_custom_call" | custom-call | flops 7864320 | bytes 4194304 | tf_op jit(solution)/shard_map/second_inner_steps/pallas_call | solution.py:580
  63.7 2.3 %third_steps.1 = (f32[4,26,48,128]{3,2,1,0:T(8,128)S(1)}, f32[4,24,48,128]{3,2,1,0:T(8,128)S(1)}, f32[4,22,48,128]{3,2,1,0:T(8,128)S(1)}, f32[4,20,48,128]{3,2,1,0:T(8,128)S(1)}, f32[4,18,48,128]{3,2,1,0:T(8,128)S(1)}) custom-call(s32[5]{0:T(128)S(1)} %stack.31.spot_ref, ...), custom_call_target="tpu_custom_call", output_to_operand_aliasing={{0}: (2, {}), {1}: (3, {}), {2}: (4, {}), {3}: (5, {}), {4}... | custom-call | flops 5242880 | bytes 4194304 | tf_op jit(solution)/shard_map/third_steps/pallas_call | solution.py:590
  66.1 2.0 %last_step_given.1 = f32[4,2,128,128]{3,2,1,0:T(8,128)S(1)} custom-call(s32[5]{0:T(128)S(1)} %stack.31.spot_ref, f32[5,8]{1,0:T(8,128)S(1)} %copy-done, f32[4,26,48,128]{3,2,1,0:T(8,128)S(1)} %get-tuple-element.59.c0_ref, f32[4,24,48,128]{3,2,1,0:T(8,128)S(1)} %get-tuple-element.60.diagonal_ref, f32[4,24,48,128]{3,2,1,0:T(8,128)S(1)} %get-tuple-element.61.d0_ref, ...), custom_call_target="tpu_custom_call" | custom-call | flops 5242880 | bytes 4194304 | tf_op jit(solution)/shard_map/last_step_given/pallas_call | solution.py:606
  68.2 2.0 %last_step_kept.1.kept_ref = f32[4,2,128,128]{3,2,1,0:T(8,128)S(1)} custom-call(s32[5]{0:T(128)S(1)} %stack.31.spot_ref, f32[5,8]{1,0:T(8,128)S(1)} %copy-done, f32[4,26,48,128]{3,2,1,0:T(8,128)S(1)} %get-tuple-element.59.c0_ref, f32[4,24,48,128]{3,2,1,0:T(8,128)S(1)} %get-tuple-element.60.diagonal_ref, f32[4,24,48,128]{3,2,1,0:T(8,128)S(1)} %get-tuple-element.61.d0_ref, ...), custom_call_target="tpu_custom_call" | custom-call | flops 5242880 | bytes 4194304 | tf_op jit(solution)/shard_map/last_step_kept/pallas_call | solution.py:606
  70.9 2.5 %collective-permute-start.18 = (f32[2,128,128]{2,1,0:T(8,128)S(1)}, f32[2,128,128]{2,1,0:T(8,128)S(1)}, u32[]{:S(2)}, u32[]{:S(2)}) collective-permute-start(f32[2,128,128]{2,1,0:T(8,128)S(1)} %get-tuple-element.78), channel_id=1, source_target_pairs={{0,17},{1,16},{16,1},{17,0},{2,19},{3,18},{18,3},{19,2},{4,21},{5,... | collective-permute-start | bytes 393224 | tf_op jit(solution)/shard_map/ppermute | solution.py:488
  74.4 3.7 %collective-permute-done.18.refs_1_ = f32[2,128,128]{2,1,0:T(8,128)S(1)} collective-permute-done((f32[2,128,128]{2,1,0:T(8,128)S(1)}, f32[2,128,128]{2,1,0:T(8,128)S(1)}, u32[]{:S(2)}, u32[]{:S(2)}) %collective-permute-start.18) | collective-permute-done | bytes 131104 | tf_op jit(solution)/shard_map/ppermute | solution.py:488
  78.1 2.5 %collective-permute-done.19.refs_2_ = f32[2,128,128]{2,1,0:T(8,128)S(1)} collective-permute-done((f32[2,128,128]{2,1,0:T(8,128)S(1)}, f32[2,128,128]{2,1,0:T(8,128)S(1)}, u32[]{:S(2)}, u32[]{:S(2)}) %collective-permute-start.19) | collective-permute-done | bytes 131104 | tf_op jit(solution)/shard_map/ppermute | solution.py:488
  (36 shorter events, 14.7 us)
Async XLA Ops:
  2.0 10.9 %collective-permute-start = (f32[2,2,128,128]{3,2,1,0:T(8,128)S(1)}, f32[2,2,128,128]{3,2,1,0:T(8,128)S(1)}, u32[]{:S(2)}, u32[]{:S(2)}) collective-permute-start(f32[2,2,128,128]{3,2,1,0:T(8,128)S(1)} %get-tuple-element.44), channel_id=1, source_target_pairs={{0,1},{1,0},{16,17},{17,16},{2,3},{3,2},{18,19},{19,18},{4,5},{5,4... | collective-permute-start | bytes 786440 | tf_op jit(solution)/shard_map/ppermute | solution.py:488
  5.1 11.5 %collective-permute-start.1 = (f32[2,2,128,128]{3,2,1,0:T(8,128)S(1)}, f32[2,2,128,128]{3,2,1,0:T(8,128)S(1)}, u32[]{:S(2)}, u32[]{:S(2)}) collective-permute-start(f32[2,2,128,128]{3,2,1,0:T(8,128)S(1)} %get-tuple-element.45), channel_id=1, source_target_pairs={{0,16},{1,17},{16,0},{17,1},{2,18},{3,19},{18,2},{19,3},{4,20},{5,... | collective-permute-start | bytes 786440 | tf_op jit(solution)/shard_map/ppermute | solution.py:488
  6.5 12.9 %collective-permute-start.2 = (f32[2,2,128,128]{3,2,1,0:T(8,128)S(1)}, f32[2,2,128,128]{3,2,1,0:T(8,128)S(1)}, u32[]{:S(2)}, u32[]{:S(2)}) collective-permute-start(f32[2,2,128,128]{3,2,1,0:T(8,128)S(1)} %get-tuple-element.46), channel_id=1, source_target_pairs={{0,17},{1,16},{16,1},{17,0},{2,19},{3,18},{18,3},{19,2},{4,21},{5,... | collective-permute-start | bytes 786440 | tf_op jit(solution)/shard_map/ppermute | solution.py:488
  7.5 12.6 %collective-permute-start.4 = (f32[2,128,128]{2,1,0:T(8,128)S(1)}, f32[2,128,128]{2,1,0:T(8,128)S(1)}, u32[]{:S(2)}, u32[]{:S(2)}) collective-permute-start(f32[2,128,128]{2,1,0:T(8,128)S(1)} %pack_kappa.1.refs_0_), channel_id=1, source_target_pairs={{0,1},{1,0},{16,17},{17,16},{2,3},{3,2},{18,19},{19,18},{4,5},{5,4... | collective-permute-start | bytes 393224 | tf_op jit(solution)/shard_map/ppermute | solution.py:488
  9.5 13.2 %collective-permute-start.5 = (f32[2,128,128]{2,1,0:T(8,128)S(1)}, f32[2,128,128]{2,1,0:T(8,128)S(1)}, u32[]{:S(2)}, u32[]{:S(2)}) collective-permute-start(f32[2,128,128]{2,1,0:T(8,128)S(1)} %pack_kappa.1.refs_0_), channel_id=1, source_target_pairs={{0,16},{1,17},{16,0},{17,1},{2,18},{3,19},{18,2},{19,3},{4,20},{5,... | collective-permute-start | bytes 393224 | tf_op jit(solution)/shard_map/ppermute | solution.py:488
  12.9 11.0 %collective-permute-start.6 = (f32[2,128,128]{2,1,0:T(8,128)S(1)}, f32[2,128,128]{2,1,0:T(8,128)S(1)}, u32[]{:S(2)}, u32[]{:S(2)}) collective-permute-start(f32[2,128,128]{2,1,0:T(8,128)S(1)} %pack_kappa.1.refs_0_), channel_id=1, source_target_pairs={{0,17},{1,16},{16,1},{17,0},{2,19},{3,18},{18,3},{19,2},{4,21},{5,... | collective-permute-start | bytes 393224 | tf_op jit(solution)/shard_map/ppermute | solution.py:488
  20.0 4.0 %collective-permute-start.3 = (f32[4,2,128,128]{3,2,1,0:T(8,128)S(1)}, f32[4,2,128,128]{3,2,1,0:T(8,128)S(1)}, u32[]{:S(2)}, u32[]{:S(2)}) collective-permute-start(f32[4,2,128,128]{3,2,1,0:T(8,128)S(1)} %get-tuple-element.48), channel_id=1, source_target_pairs={{0,8},{8,0},{1,9},{9,1},{2,10},{10,2},{3,11},{11,3},{4,12},{12,4},... | collective-permute-start | bytes 1572872 | tf_op jit(solution)/shard_map/ppermute | solution.py:530
  23.9 5.8 %collective-permute-start.7 = (f32[4,2,128,128]{3,2,1,0:T(8,128)S(1)}, f32[4,2,128,128]{3,2,1,0:T(8,128)S(1)}, u32[]{:S(2)}, u32[]{:S(2)}) collective-permute-start(f32[4,2,128,128]{3,2,1,0:T(8,128)S(1)} %stack_kappa.1.mine_ref), channel_id=1, source_target_pairs={{0,8},{8,0},{1,9},{9,1},{2,10},{10,2},{3,11},{11,3},{4,12},{12,4},... | collective-permute-start | bytes 1572872 | tf_op jit(solution)/shard_map/ppermute | solution.py:517
  24.8 21.0 %collective-permute-start.8 = (f32[4,5,32,128]{3,2,1,0:T(8,128)S(1)}, f32[4,5,32,128]{3,2,1,0:T(8,128)S(1)}, u32[]{:S(2)}, u32[]{:S(2)}) collective-permute-start(f32[4,5,32,128]{3,2,1,0:T(8,128)S(1)} %get-tuple-element.55), channel_id=1, source_target_pairs={{0,2},{2,4},{4,6},{1,3},{3,5},{5,7},{8,10},{10,12},{12,14},{9,11},... | collective-permute-start | bytes 983048 | tf_op jit(solution)/shard_map/ppermute | solution.py:535
  28.4 17.3 %collective-permute-start.9 = (f32[4,5,32,128]{3,2,1,0:T(8,128)S(1)}, f32[4,5,32,128]{3,2,1,0:T(8,128)S(1)}, u32[]{:S(2)}, u32[]{:S(2)}) collective-permute-start(f32[4,5,32,128]{3,2,1,0:T(8,128)S(1)} %get-tuple-element.56), channel_id=1, source_target_pairs={{2,0},{4,2},{6,4},{3,1},{5,3},{7,5},{10,8},{12,10},{14,12},{11,9},... | collective-permute-start | bytes 983048 | tf_op jit(solution)/shard_map/ppermute | solution.py:536
  30.7 11.0 %collective-permute-start.10 = (f32[4,4,32,128]{3,2,1,0:T(8,128)S(1)}, f32[4,4,32,128]{3,2,1,0:T(8,128)S(1)}, u32[]{:S(2)}, u32[]{:S(2)}) collective-permute-start(f32[4,4,32,128]{3,2,1,0:T(8,128)S(1)} %get-tuple-element.57), channel_id=1, source_target_pairs={{0,2},{2,4},{4,6},{1,3},{3,5},{5,7},{8,10},{10,12},{12,14},{9,11},... | collective-permute-start | bytes 786440 | tf_op jit(solution)/shard_map/ppermute | solution.py:523
  35.3 10.5 %collective-permute-start.11 = (f32[4,4,32,128]{3,2,1,0:T(8,128)S(1)}, f32[4,4,32,128]{3,2,1,0:T(8,128)S(1)}, u32[]{:S(2)}, u32[]{:S(2)}) collective-permute-start(f32[4,4,32,128]{3,2,1,0:T(8,128)S(1)} %get-tuple-element.58), channel_id=1, source_target_pairs={{2,0},{4,2},{6,4},{3,1},{5,3},{7,5},{10,8},{12,10},{14,12},{11,9},... | collective-permute-start | bytes 786440 | tf_op jit(solution)/shard_map/ppermute | solution.py:524
  48.4 15.2 %collective-permute-start.12 = (f32[4,5,32,128]{3,2,1,0:T(8,128)S(1)}, f32[4,5,32,128]{3,2,1,0:T(8,128)S(1)}, u32[]{:S(2)}, u32[]{:S(2)}) collective-permute-start(f32[4,5,32,128]{3,2,1,0:T(8,128)S(1)} %get-tuple-element.69), channel_id=1, source_target_pairs={{0,2},{2,4},{4,6},{1,3},{3,5},{5,7},{8,10},{10,12},{12,14},{9,11},... | collective-permute-start | bytes 983048 | tf_op jit(solution)/shard_map/ppermute | solution.py:565
  51.9 11.7 %collective-permute-start.13 = (f32[4,5,32,128]{3,2,1,0:T(8,128)S(1)}, f32[4,5,32,128]{3,2,1,0:T(8,128)S(1)}, u32[]{:S(2)}, u32[]{:S(2)}) collective-permute-start(f32[4,5,32,128]{3,2,1,0:T(8,128)S(1)} %get-tuple-element.70), channel_id=1, source_target_pairs={{2,0},{4,2},{6,4},{3,1},{5,3},{7,5},{10,8},{12,10},{14,12},{11,9},... | collective-permute-start | bytes 983048 | tf_op jit(solution)/shard_map/ppermute | solution.py:566
  54.7 11.3 %collective-permute-start.14 = (f32[8,128]{1,0:T(8,128)S(1)}, f32[8,128]{1,0:T(8,128)S(1)}, u32[]{:S(2)}, u32[]{:S(2)}) collective-permute-start(f32[8,128]{1,0:T(8,128)S(1)} %get-tuple-element.76.rest_0_), channel_id=1, source_target_pairs={{0,2},{2,4},{4,6},{6,0},{1,3},{3,5},{5,7},{7,1},{8,10},{10,12},{12... | collective-permute-start | bytes 12296 | tf_op jit(solution)/shard_map/ppermute | solution.py:578
  57.4 8.6 %collective-permute-start.15 = (f32[8,128]{1,0:T(8,128)S(1)}, f32[8,128]{1,0:T(8,128)S(1)}, u32[]{:S(2)}, u32[]{:S(2)}) collective-permute-start(f32[8,128]{1,0:T(8,128)S(1)} %get-tuple-element.76.rest_0_), channel_id=1, source_target_pairs={{0,4},{2,6},{4,0},{6,2},{1,5},{3,7},{5,1},{7,3},{8,12},{10,14},{12... | collective-permute-start | bytes 12296 | tf_op jit(solution)/shard_map/ppermute | solution.py:578
  58.5 7.6 %collective-permute-start.16 = (f32[8,128]{1,0:T(8,128)S(1)}, f32[8,128]{1,0:T(8,128)S(1)}, u32[]{:S(2)}, u32[]{:S(2)}) collective-permute-start(f32[8,128]{1,0:T(8,128)S(1)} %get-tuple-element.76.rest_0_), channel_id=1, source_target_pairs={{0,6},{2,0},{4,2},{6,4},{1,7},{3,1},{5,3},{7,5},{8,14},{10,8},{12,... | collective-permute-start | bytes 12296 | tf_op jit(solution)/shard_map/ppermute | solution.py:578
  63.7 2.4 %copy-start = (f32[5,8]{1,0:T(8,128)S(1)}, f32[5,8]{1,0:T(8,128)}, u32[]{:S(2)}) copy-start(f32[5,8]{1,0:T(8,128)} %weights_ref.3) | copy-start | bytes 484
  68.1 2.1 %collective-permute-start.17 = (f32[4,2,128,128]{3,2,1,0:T(8,128)S(1)}, f32[4,2,128,128]{3,2,1,0:T(8,128)S(1)}, u32[]{:S(2)}, u32[]{:S(2)}) collective-permute-start(f32[4,2,128,128]{3,2,1,0:T(8,128)S(1)} %last_step_given.1), channel_id=1, source_target_pairs={{0,8},{8,0},{1,9},{9,1},{2,10},{10,2},{3,11},{11,3},{4,12},{12,4},... | collective-permute-start | bytes 1572872 | tf_op jit(solution)/shard_map/ppermute | solution.py:616
  70.9 7.3 %collective-permute-start.18 = (f32[2,128,128]{2,1,0:T(8,128)S(1)}, f32[2,128,128]{2,1,0:T(8,128)S(1)}, u32[]{:S(2)}, u32[]{:S(2)}) collective-permute-start(f32[2,128,128]{2,1,0:T(8,128)S(1)} %get-tuple-element.78), channel_id=1, source_target_pairs={{0,17},{1,16},{16,1},{17,0},{2,19},{3,18},{18,3},{19,2},{4,21},{5,... | collective-permute-start | bytes 393224 | tf_op jit(solution)/shard_map/ppermute | solution.py:488
  73.4 7.3 %collective-permute-start.19 = (f32[2,128,128]{2,1,0:T(8,128)S(1)}, f32[2,128,128]{2,1,0:T(8,128)S(1)}, u32[]{:S(2)}, u32[]{:S(2)}) collective-permute-start(f32[2,128,128]{2,1,0:T(8,128)S(1)} %get-tuple-element.79), channel_id=1, source_target_pairs={{0,16},{1,17},{16,0},{17,1},{2,18},{3,19},{18,2},{19,3},{4,20},{5,... | collective-permute-start | bytes 393224 | tf_op jit(solution)/shard_map/ppermute | solution.py:488
  73.9 6.7 %collective-permute-start.20 = (f32[2,128,128]{2,1,0:T(8,128)S(1)}, f32[2,128,128]{2,1,0:T(8,128)S(1)}, u32[]{:S(2)}, u32[]{:S(2)}) collective-permute-start(f32[2,128,128]{2,1,0:T(8,128)S(1)} %get-tuple-element.80), channel_id=1, source_target_pairs={{0,1},{1,0},{16,17},{17,16},{2,3},{3,2},{18,19},{19,18},{4,5},{5,4... | collective-permute-start | bytes 393224 | tf_op jit(solution)/shard_map/ppermute | solution.py:488

commit v10 on v9

--- a/solution.py
+++ b/solution.py
@@ -209,35 +209,38 @@
         field.ref[z, y + field.halo, at, :] = value
 
 
-def store_edges(up_ref, down_ref, x, z, first, last):
+def store_edges(spot_ref, even_ref, odd_ref, x, z, first, last):
     at = pl.ds(pl.multiple_of(x, 8), 8)
-    for y, value in enumerate(first):
-        down_ref[z, y, at, :] = value
-    for y, value in enumerate(last):
-        up_ref[z, y, at, :] = value
-
-
-def edge_kernel(grid, spot_ref, mine_ref, other_ref, up_ref, down_ref):
+    odd = spot_ref[5] == 1
+    for y, (below, above) in enumerate(zip(first, last)):
+        even_ref[z, y, at, :] = jnp.where(odd, below, above)
+        odd_ref[z, y, at, :] = jnp.where(odd, above, below)
+
+
+def edge_kernel(grid, spot_ref, mine_ref, other_ref, even_ref, odd_ref):
     by = grid[3]
     rows = list(range(HALO)) + list(range(by - HALO, by))
     for x, z, values in block_rows(grid, spot_ref, mine_ref, other_ref, rows):
-        store_edges(up_ref, down_ref, x, z, values[:HALO], values[HALO:])
-
-
-def diagonal_kernel(grid, spot_ref, mine_ref, other_ref, own_ref, up_ref, down_ref):
+        store_edges(spot_ref, even_ref, odd_ref, x, z, values[:HALO], values[HALO:])
+
+
+def diagonal_kernel(grid, spot_ref, mine_ref, other_ref, own_ref, even_ref, odd_ref):
     own = Field(own_ref, DIAGONAL_HALO)
     for x, z, values in block_rows(grid, spot_ref, mine_ref, other_ref, range(grid[3])):
         values = [6.0 + value for value in values]
         store_own(own, x, z, values)
-        store_edges(up_ref, down_ref, x, z, values[:DIAGONAL_HALO], values[-DIAGONAL_HALO:])
-
-
-def fill_halo(field, own, low_ref, high_ref):
+        first, last = values[:DIAGONAL_HALO], values[-DIAGONAL_HALO:]
+        store_edges(spot_ref, even_ref, odd_ref, x, z, first, last)
+
+
+def fill_halo(spot_ref, field, own, even_ref, odd_ref):
+    odd = spot_ref[5] == 1
     for c in range(field.columns):
         for y in range(field.halo):
             for x in range(0, field.cells, 8):
-                field.store(c, y - field.halo, x, low_ref[c, y, pl.ds(x, 8), :])
-                field.store(c, own + y, x, high_ref[c, y, pl.ds(x, 8), :])
+                even, other = even_ref[c, y, pl.ds(x, 8), :], odd_ref[c, y, pl.ds(x, 8), :]
+                field.store(c, y - field.halo, x, jnp.where(odd, even, other))
+                field.store(c, own + y, x, jnp.where(odd, other, even))
 
 
 def inner_kernel(
@@ -263,8 +266,8 @@
 def first_kernel(
     own,
     spot_ref, c0_in, diagonal_in, d0_in, c1_in, d1_in, c2_in,
-    low_ref, high_ref, low_diagonal_ref, high_diagonal_ref,
-    c0_ref, diagonal_ref, d0_ref, c1_ref, d1_ref, c2_ref, up_ref, down_ref,
+    even_ref, odd_ref, even_diagonal_ref, odd_diagonal_ref,
+    c0_ref, diagonal_ref, d0_ref, c1_ref, d1_ref, c2_ref, even_out, odd_out,
 ):
     c0 = Field(c0_ref, HALO)
     diagonal = Field(diagonal_ref, DIAGONAL_HALO)
@@ -272,18 +275,18 @@
     c1 = Field(c1_ref, 3)
     d1 = Field(d1_ref, 2)
     c2 = Field(c2_ref, HALO)
-    fill_halo(c0, own, low_ref, high_ref)
-    fill_halo(diagonal, own, low_diagonal_ref, high_diagonal_ref)
+    fill_halo(spot_ref, c0, own, even_ref, odd_ref)
+    fill_halo(spot_ref, diagonal, own, even_diagonal_ref, odd_diagonal_ref)
     strips = functools.partial(apply_strips, spot_ref, own)
     strips(d0, c0, diagonal, 4, HALO)
     strips(c1, d0, diagonal, 3, HALO, c0)
     strips(d1, c1, diagonal, 2, HALO)
     strips(c2, d1, diagonal, 1, HALO, c1)
     for c in range(c2.columns):
-        for y in range(HALO):
-            for x in range(0, c2.cells, 8):
-                down_ref[c, y, pl.ds(x, 8), :] = c2.load(c, y, x)
-                up_ref[c, y, pl.ds(x, 8), :] = c2.load(c, own - HALO + y, x)
+        for x in range(0, c2.cells, 8):
+            first = [c2.load(c, y, x) for y in range(HALO)]
+            last = [c2.load(c, own - HALO + y, x) for y in range(HALO)]
+            store_edges(spot_ref, even_out, odd_out, x, c, first, last)
 
 
 def middle_kernel(own, c0_ref, c1_ref, c2_ref, diagonal_ref, d2_ref, moments_ref):
@@ -338,7 +341,7 @@
 
 def third_kernel(
     own,
-    spot_ref, diagonal_ref, c2_in, d2_in, c3_in, d3_in, c4_in, low_ref, high_ref,
+    spot_ref, diagonal_ref, c2_in, d2_in, c3_in, d3_in, c4_in, even_ref, odd_ref,
     c2_ref, d2_ref, c3_ref, d3_ref, c4_ref,
 ):
     diagonal = Field(diagonal_ref, DIAGONAL_HALO)
@@ -347,7 +350,7 @@
     c3 = Field(c3_ref, 3)
     d3 = Field(d3_ref, 2)
     c4 = Field(c4_ref, 1)
-    fill_halo(c2, own, low_ref, high_ref)
+    fill_halo(spot_ref, c2, own, even_ref, odd_ref)
     strips = functools.partial(apply_strips, spot_ref, own)
     strips(d2, c2, diagonal, 4, 4)
     strips(c3, d2, diagonal, 3, 4, c2)
@@ -465,8 +468,9 @@
     core, gy = lax.axis_index("core"), lax.axis_index("gy")
     place = (lax.axis_index("chip") * 2 + core) * nz + lax.axis_index("gz")
     mine = place % count
-    up = [(i, i + 1) for i in range(ny - 1)]
-    down = [(target, source) for source, target in up]
+    assert ny & (ny - 1) == 0
+    even = [(i, i ^ 1) for i in range(ny)]
+    odd = [(i, i + 1 if i % 2 else i - 1) for i in range(1, ny - 1)]
     swap = [(0, 1), (1, 0)]
 
     def edge(halo):
@@ -481,7 +485,7 @@
     chips = nx // 2 * nz
     assert chips & (chips - 1) == 0
     chip = lax.axis_index("chip") * nz + lax.axis_index("gz")
-    spot = jnp.stack([gy == 0, gy == ny - 1, mine, core, chip]).astype(jnp.int32)
+    spot = jnp.stack([gy == 0, gy == ny - 1, mine, core, chip, gy % 2]).astype(jnp.int32)
 
     def to_chip(value, k):
         pairs = [(i, i ^ k) for i in range(chips)]
@@ -515,25 +519,25 @@
 
     kappa = plain(stack_kernel, "stack_kappa", stacked, [vmem()] * chips, *kappas)
     other = lax.ppermute(kappa, "core", swap)
-    diagonal, up_edge, down_edge = plain(
+    diagonal, even_edge, odd_edge = plain(
         functools.partial(diagonal_kernel, grid), "diagonal_rows",
         (vector(DIAGONAL_HALO), edge(DIAGONAL_HALO), edge(DIAGONAL_HALO)),
         [smem(), vmem(), vmem()], spot, kappa, other,
     )
-    low_diagonal = lax.ppermute(up_edge, "gy", up)
-    high_diagonal = lax.ppermute(down_edge, "gy", down)
+    even_diagonal = lax.ppermute(even_edge, "gy", even)
+    odd_diagonal = lax.ppermute(odd_edge, "gy", odd)
 
     probe, give = plain(
         sort_probes_kernel, "sort_probes", (stacked, stacked),
         [smem()] + [vmem()] * chips, spot, *probes,
     )
     other = lax.ppermute(give, "core", swap)
-    up_edge, down_edge = plain(
+    even_edge, odd_edge = plain(
         functools.partial(edge_kernel, grid), "probe_edges", (edge(HALO), edge(HALO)),
         [smem(), vmem(), vmem()], spot, probe, other,
     )
-    low1 = lax.ppermute(up_edge, "gy", up)
-    high1 = lax.ppermute(down_edge, "gy", down)
+    even1 = lax.ppermute(even_edge, "gy", even)
+    odd1 = lax.ppermute(odd_edge, "gy", odd)
 
     cells = by * X * columns * 128
 
@@ -552,7 +556,7 @@
         name="inner_steps",
     )(spot, probe, other, here(diagonal))
     vectors = [here(value) for value in (inner[0], diagonal) + tuple(inner[1:])]
-    c0, diagonal, d0, c1, d1, c2, up_edge, down_edge = pl.pallas_call(
+    c0, diagonal, d0, c1, d1, c2, even_edge, odd_edge = pl.pallas_call(
         functools.partial(first_kernel, by),
         out_shape=tuple(vector(h) for h in (HALO, DIAGONAL_HALO, 4, 3, 2, HALO))
         + (edge(HALO), edge(HALO)),
@@ -561,9 +565,9 @@
         input_output_aliases={i + 1: i for i in range(6)},
         compiler_params=params(),
         name="first_steps",
-    )(spot, *vectors, low1, high1, low_diagonal, high_diagonal)
-    low2 = lax.ppermute(up_edge, "gy", up)
-    high2 = lax.ppermute(down_edge, "gy", down)
+    )(spot, *vectors, even1, odd1, even_diagonal, odd_diagonal)
+    even2 = lax.ppermute(even_edge, "gy", even)
+    odd2 = lax.ppermute(odd_edge, "gy", odd)
     d2, moments = pl.pallas_call(
         functools.partial(middle_kernel, by),
         out_shape=(vector(4), f32(8, 128)),
@@ -575,7 +579,7 @@
     )(here(c0), here(c1), here(c2), here(diagonal))
     shares = [moments]
     for step in range(1, ny):
-        shares.append(lax.ppermute(moments, "gy", [(i, (i + step) % ny) for i in range(ny)]))
+        shares.append(lax.ppermute(moments, "gy", [(i, i ^ step) for i in range(ny)]))
 
     c3, d3, c4 = pl.pallas_call(
         functools.partial(second_inner_kernel, by),
@@ -596,7 +600,7 @@
         compiler_params=params(),
         cost_estimate=cost(20),
         name="third_steps",
-    )(spot, *vectors, low2, high2)
+    )(spot, *vectors, even2, odd2)
     inverse_count = 1.0 / (ny * cells)
     vectors = [here(value) for value in (c0, diagonal, d0, c1, d1, c2, d2, c3, d3, c4)]
     if group > count:

time: 81.7 us -> 76 us (0.930)
  starting transfers between devices: 37.7 us -> 34.1 us
  waiting for transfers between devices: 20.1 us -> 18.1 us
    ppermute x9, starting transfers between devices: 22.2 us -> 18.5 us  [the longest x3 5.49 us: body(): lax.ppermute(moments, 'gy', [(i, i ^ step) for i in range(ny)])]
    ppermute x9, waiting for transfers between devices: 5.33 us -> 3.36 us  [the longest x1 3.34 us: body(): even_diagonal = lax.ppermute(even_edge, 'gy', even)]
  transfers between devices with their start and end apart: 21 -> 21, of which waited for: 8 -> 7; matrix products, arithmetic and copies ran while one was open for 0% -> 0% of each run, Pallas kernels for 19% -> 20%
where the time goes in v10:
time: 76 us; the launch traced here: 75.7 us
  starting transfers between devices  34.1 us (45%)
  Pallas kernels  23.2 us (31%)
  waiting for transfers between devices  18.1 us (24%)
    ppermute x9, starting transfers between devices, to_chip(): return lax.ppermute(value, ('chip', 'gz'), pairs)  15.3 us
    ppermute x9, waiting for transfers between devices, to_chip(): return lax.ppermute(value, ('chip', 'gz'), pairs)  14.7 us
    pallas_call x8, Pallas kernels, plain(): pl.pallas_call(kernel, out_shape=out_shape, in_specs=specs, out_specs=(vm...  6.42 us
    ppermute x3, starting transfers between devices, body(): lax.ppermute(moments, 'gy', [(i, i ^ step) for i in range(ny)])  5.49 us
    ppermute x1, starting transfers between devices, body(): even2 = lax.ppermute(even_edge, 'gy', even)  4.79 us
    ppermute x1, starting transfers between devices, body(): even_diagonal = lax.ppermute(even_edge, 'gy', even)  4.44 us
    pallas_call x2, Pallas kernels, last_step(): pl.pallas_call(functools.partial(last_kernel, grid, inverse_count, flip),...  4.06 us
    pallas_call x1, Pallas kernels, body(): pl.pallas_call(functools.partial(inner_kernel, grid), out_shape=tuple((ve...  3.91 us
  transfers between devices with their start and end apart: 21, of which 7 were waited for; matrix products, arithmetic and copies ran while one was open for 0% of the time, Pallas kernels for 20%

profile of v10, /device:TPU:0, one launch (start us, length us, event | category | flops | bytes accessed | tf_op | source)
XLA Modules:
  0.0 75.7 jit_solution(6095739712378410825)
XLA Ops:
  0.1 1.9 %pack_probes.1 = (f32[2,2,128,128]{3,2,1,0:T(8,128)S(1)}, f32[2,2,128,128]{3,2,1,0:T(8,128)S(1)}, f32[2,2,128,128]{3,2,1,0:T(8,128)S(1)}, f32[2,2,128,128]{3,2,1,0:T(8,128)S(1)}) custom-call(s32[6]{0:T(128)S(1)} %stack.35.spot_ref, f32[1024,256]{1,0:T(8,128)} %bitcast.8), custom_call_target="tpu_custom_call" | custom-call | tf_op jit(solution)/shard_map/pack_probes/pallas_call | solution.py:495
  2.0 3.0 %collective-permute-start = (f32[2,2,128,128]{3,2,1,0:T(8,128)S(1)}, f32[2,2,128,128]{3,2,1,0:T(8,128)S(1)}, u32[]{:S(2)}, u32[]{:S(2)}) collective-permute-start(f32[2,2,128,128]{3,2,1,0:T(8,128)S(1)} %get-tuple-element.44), channel_id=1, source_target_pairs={{0,1},{1,0},{16,17},{17,16},{2,3},{3,2},{18,19},{19,18},{4,5},{5,4... | collective-permute-start | bytes 786440 | tf_op jit(solution)/shard_map/ppermute | solution.py:492
  5.1 1.5 %collective-permute-start.1 = (f32[2,2,128,128]{3,2,1,0:T(8,128)S(1)}, f32[2,2,128,128]{3,2,1,0:T(8,128)S(1)}, u32[]{:S(2)}, u32[]{:S(2)}) collective-permute-start(f32[2,2,128,128]{3,2,1,0:T(8,128)S(1)} %get-tuple-element.45), channel_id=1, source_target_pairs={{0,16},{1,17},{16,0},{17,1},{2,18},{3,19},{18,2},{19,3},{4,20},{5,... | collective-permute-start | bytes 786440 | tf_op jit(solution)/shard_map/ppermute | solution.py:492
  7.5 2.0 %collective-permute-start.4 = (f32[2,128,128]{2,1,0:T(8,128)S(1)}, f32[2,128,128]{2,1,0:T(8,128)S(1)}, u32[]{:S(2)}, u32[]{:S(2)}) collective-permute-start(f32[2,128,128]{2,1,0:T(8,128)S(1)} %pack_kappa.1.refs_0_), channel_id=1, source_target_pairs={{0,1},{1,0},{16,17},{17,16},{2,3},{3,2},{18,19},{19,18},{4,5},{5,4... | collective-permute-start | bytes 393224 | tf_op jit(solution)/shard_map/ppermute | solution.py:492
  9.5 1.5 %collective-permute-start.5 = (f32[2,128,128]{2,1,0:T(8,128)S(1)}, f32[2,128,128]{2,1,0:T(8,128)S(1)}, u32[]{:S(2)}, u32[]{:S(2)}) collective-permute-start(f32[2,128,128]{2,1,0:T(8,128)S(1)} %pack_kappa.1.refs_0_), channel_id=1, source_target_pairs={{0,16},{1,17},{16,0},{17,1},{2,18},{3,19},{18,2},{19,3},{4,20},{5,... | collective-permute-start | bytes 393224 | tf_op jit(solution)/shard_map/ppermute | solution.py:492
  11.0 1.9 %collective-permute-done.refs_1_ = f32[2,2,128,128]{3,2,1,0:T(8,128)S(1)} collective-permute-done((f32[2,2,128,128]{3,2,1,0:T(8,128)S(1)}, f32[2,2,128,128]{3,2,1,0:T(8,128)S(1)}, u32[]{:S(2)}, u32[]{:S(2)}) %collective-permute-start) | collective-permute-done | bytes 262176 | tf_op jit(solution)/shard_map/ppermute | solution.py:492
  12.9 3.7 %collective-permute-start.6 = (f32[2,128,128]{2,1,0:T(8,128)S(1)}, f32[2,128,128]{2,1,0:T(8,128)S(1)}, u32[]{:S(2)}, u32[]{:S(2)}) collective-permute-start(f32[2,128,128]{2,1,0:T(8,128)S(1)} %pack_kappa.1.refs_0_), channel_id=1, source_target_pairs={{0,17},{1,16},{16,1},{17,0},{2,19},{3,18},{18,3},{19,2},{4,21},{5,... | collective-permute-start | bytes 393224 | tf_op jit(solution)/shard_map/ppermute | solution.py:492
  16.6 2.8 %collective-permute-done.2.refs_3_ = f32[2,2,128,128]{3,2,1,0:T(8,128)S(1)} collective-permute-done((f32[2,2,128,128]{3,2,1,0:T(8,128)S(1)}, f32[2,2,128,128]{3,2,1,0:T(8,128)S(1)}, u32[]{:S(2)}, u32[]{:S(2)}) %collective-permute-start.2) | collective-permute-done | bytes 262176 | tf_op jit(solution)/shard_map/ppermute | solution.py:492
  20.1 2.6 %collective-permute-done.5.refs_2_ = f32[2,128,128]{2,1,0:T(8,128)S(1)} collective-permute-done((f32[2,128,128]{2,1,0:T(8,128)S(1)}, f32[2,128,128]{2,1,0:T(8,128)S(1)}, u32[]{:S(2)}, u32[]{:S(2)}) %collective-permute-start.5) | collective-permute-done | bytes 131104 | tf_op jit(solution)/shard_map/ppermute | solution.py:492
  24.8 1.8 %collective-permute-start.8 = (f32[4,5,32,128]{3,2,1,0:T(8,128)S(1)}, f32[4,5,32,128]{3,2,1,0:T(8,128)S(1)}, u32[]{:S(2)}, u32[]{:S(2)}) collective-permute-start(f32[4,5,32,128]{3,2,1,0:T(8,128)S(1)} %get-tuple-element.55), channel_id=1, source_target_pairs={{0,2},{2,0},{4,6},{6,4},{1,3},{3,1},{5,7},{7,5},{8,10},{10,8},{12,... | collective-permute-start | bytes 983048 | tf_op jit(solution)/shard_map/ppermute | solution.py:539
  28.2 4.4 %collective-permute-start.10 = (f32[4,4,32,128]{3,2,1,0:T(8,128)S(1)}, f32[4,4,32,128]{3,2,1,0:T(8,128)S(1)}, u32[]{:S(2)}, u32[]{:S(2)}) collective-permute-start(f32[4,4,32,128]{3,2,1,0:T(8,128)S(1)} %get-tuple-element.57), channel_id=1, source_target_pairs={{0,2},{2,0},{4,6},{6,4},{1,3},{3,1},{5,7},{7,5},{8,10},{10,8},{12,... | collective-permute-start | bytes 786440 | tf_op jit(solution)/shard_map/ppermute | solution.py:527
  33.3 3.9 %inner_steps.1 = (f32[4,26,48,128]{3,2,1,0:T(8,128)S(1)}, f32[4,24,48,128]{3,2,1,0:T(8,128)S(1)}, f32[4,22,48,128]{3,2,1,0:T(8,128)S(1)}, f32[4,20,48,128]{3,2,1,0:T(8,128)S(1)}, f32[4,26,48,128]{3,2,1,0:T(8,128)S(1)}) custom-call(s32[6]{0:T(128)S(1)} %stack.35.spot_ref, f32[4,2,128,128]{3,2,1,0:T(8,128)S(1)} %get-tuple-element.47.mine_ref, ...), custom_call_target="tpu_custom_call" | custom-call | flops 8388608 | bytes 4194304 | tf_op jit(solution)/shard_map/inner_steps/pallas_call | solution.py:549
  37.2 3.3 %collective-permute-done.10.even_diagonal_ref = f32[4,4,32,128]{3,2,1,0:T(8,128)S(1)} collective-permute-done((f32[4,4,32,128]{3,2,1,0:T(8,128)S(1)}, f32[4,4,32,128]{3,2,1,0:T(8,128)S(1)}, u32[]{:S(2)}, u32[]{:S(2)}) %collective-permute-start.10) | collective-permute-done | bytes 262176 | tf_op jit(solution)/shard_map/ppermute | solution.py:527
  40.6 2.7 %first_steps.1 = (f32[4,26,48,128]{3,2,1,0:T(8,128)S(1)}, f32[4,24,48,128]{3,2,1,0:T(8,128)S(1)}, f32[4,24,48,128]{3,2,1,0:T(8,128)S(1)}, f32[4,22,48,128]{3,2,1...) custom-call(s32[6]{0:T(128)S(1)} %stack.35.spot_ref, ...), custom_call_target="tpu_custom_call", output_to_operand_aliasing={{0}: (1, {}), {1}: (2, {}), {2}: (3, {}), {3}: (4, {}), {4}... | custom-call | tf_op jit(solution)/shard_map/first_steps/pallas_call | solution.py:559
  43.2 4.8 %collective-permute-start.12 = (f32[4,5,32,128]{3,2,1,0:T(8,128)S(1)}, f32[4,5,32,128]{3,2,1,0:T(8,128)S(1)}, u32[]{:S(2)}, u32[]{:S(2)}) collective-permute-start(f32[4,5,32,128]{3,2,1,0:T(8,128)S(1)} %get-tuple-element.69), channel_id=1, source_target_pairs={{0,2},{2,0},{4,6},{6,4},{1,3},{3,1},{5,7},{7,5},{8,10},{10,8},{12,... | collective-permute-start | bytes 983048 | tf_op jit(solution)/shard_map/ppermute | solution.py:569
  50.2 3.1 %collective-permute-start.14 = (f32[8,128]{1,0:T(8,128)S(1)}, f32[8,128]{1,0:T(8,128)S(1)}, u32[]{:S(2)}, u32[]{:S(2)}) collective-permute-start(f32[8,128]{1,0:T(8,128)S(1)} %get-tuple-element.76.rest_0_), channel_id=1, source_target_pairs={{0,2},{2,0},{4,6},{6,4},{1,3},{3,1},{5,7},{7,5},{8,10},{10,8},{12,... | collective-permute-start | bytes 12296 | tf_op jit(solution)/shard_map/ppermute | solution.py:582
  53.5 2.2 %collective-permute-start.16 = (f32[8,128]{1,0:T(8,128)S(1)}, f32[8,128]{1,0:T(8,128)S(1)}, u32[]{:S(2)}, u32[]{:S(2)}) collective-permute-start(f32[8,128]{1,0:T(8,128)S(1)} %get-tuple-element.76.rest_0_), channel_id=1, source_target_pairs={{0,6},{2,4},{4,2},{6,0},{1,7},{3,5},{5,3},{7,1},{8,14},{10,12},{12... | collective-permute-start | bytes 12296 | tf_op jit(solution)/shard_map/ppermute | solution.py:582
  55.7 2.3 %second_inner_steps.1 = (f32[4,22,48,128]{3,2,1,0:T(8,128)S(1)}, f32[4,20,48,128]{3,2,1,0:T(8,128)S(1)}, f32[4,18,48,128]{3,2,1,0:T(8,128)S(1)}) custom-call(f32[4,24,48,128]{3,2,1,0:T(8,128)S(1)} %get-tuple-element.60.diagonal_ref, f32[4,26,48,128]{3,2,1,0:T(8,128)S(1)} %get-tuple-element.64.c2_ref.c2_in, f32[4,24,48,128]{3,2,1,0:T(8,128)S(1)} %get-tuple-element.65.d2_ref.d2_in), custom_call_target="tpu_custom_call" | custom-call | flops 7864320 | bytes 4194304 | tf_op jit(solution)/shard_map/second_inner_steps/pallas_call | solution.py:584
  58.1 2.4 %third_steps.1 = (f32[4,26,48,128]{3,2,1,0:T(8,128)S(1)}, f32[4,24,48,128]{3,2,1,0:T(8,128)S(1)}, f32[4,22,48,128]{3,2,1,0:T(8,128)S(1)}, f32[4,20,48,128]{3,2,1,0:T(8,128)S(1)}, f32[4,18,48,128]{3,2,1,0:T(8,128)S(1)}) custom-call(s32[6]{0:T(128)S(1)} %stack.35.spot_ref, ...), custom_call_target="tpu_custom_call", output_to_operand_aliasing={{0}: (2, {}), {1}: (3, {}), {2}: (4, {}), {3}: (5, {}), {4}... | custom-call | flops 5242880 | bytes 4194304 | tf_op jit(solution)/shard_map/third_steps/pallas_call | solution.py:594
  60.5 2.0 %last_step_given.1 = f32[4,2,128,128]{3,2,1,0:T(8,128)S(1)} custom-call(s32[6]{0:T(128)S(1)} %stack.35.spot_ref, f32[5,8]{1,0:T(8,128)S(1)} %copy-done, f32[4,26,48,128]{3,2,1,0:T(8,128)S(1)} %get-tuple-element.59.c0_ref, f32[4,24,48,128]{3,2,1,0:T(8,128)S(1)} %get-tuple-element.60.diagonal_ref, f32[4,24,48,128]{3,2,1,0:T(8,128)S(1)} %get-tuple-element.61.d0_ref, ...), custom_call_target="tpu_custom_call" | custom-call | flops 5242880 | bytes 4194304 | tf_op jit(solution)/shard_map/last_step_given/pallas_call | solution.py:610
  62.6 2.0 %last_step_kept.1.kept_ref = f32[4,2,128,128]{3,2,1,0:T(8,128)S(1)} custom-call(s32[6]{0:T(128)S(1)} %stack.35.spot_ref, f32[5,8]{1,0:T(8,128)S(1)} %copy-done, f32[4,26,48,128]{3,2,1,0:T(8,128)S(1)} %get-tuple-element.59.c0_ref, f32[4,24,48,128]{3,2,1,0:T(8,128)S(1)} %get-tuple-element.60.diagonal_ref, f32[4,24,48,128]{3,2,1,0:T(8,128)S(1)} %get-tuple-element.61.d0_ref, ...), custom_call_target="tpu_custom_call" | custom-call | flops 5242880 | bytes 4194304 | tf_op jit(solution)/shard_map/last_step_kept/pallas_call | solution.py:610
  65.2 2.5 %collective-permute-start.18 = (f32[2,128,128]{2,1,0:T(8,128)S(1)}, f32[2,128,128]{2,1,0:T(8,128)S(1)}, u32[]{:S(2)}, u32[]{:S(2)}) collective-permute-start(f32[2,128,128]{2,1,0:T(8,128)S(1)} %get-tuple-element.78), channel_id=1, source_target_pairs={{0,17},{1,16},{16,1},{17,0},{2,19},{3,18},{18,3},{19,2},{4,21},{5,... | collective-permute-start | bytes 393224 | tf_op jit(solution)/shard_map/ppermute | solution.py:492
  68.8 3.7 %collective-permute-done.18.refs_1_ = f32[2,128,128]{2,1,0:T(8,128)S(1)} collective-permute-done((f32[2,128,128]{2,1,0:T(8,128)S(1)}, f32[2,128,128]{2,1,0:T(8,128)S(1)}, u32[]{:S(2)}, u32[]{:S(2)}) %collective-permute-start.18) | collective-permute-done | bytes 131104 | tf_op jit(solution)/shard_map/ppermute | solution.py:492
  72.5 2.5 %collective-permute-done.19.refs_2_ = f32[2,128,128]{2,1,0:T(8,128)S(1)} collective-permute-done((f32[2,128,128]{2,1,0:T(8,128)S(1)}, f32[2,128,128]{2,1,0:T(8,128)S(1)}, u32[]{:S(2)}, u32[]{:S(2)}) %collective-permute-start.19) | collective-permute-done | bytes 131104 | tf_op jit(solution)/shard_map/ppermute | solution.py:492
  (36 shorter events, 10.8 us)
Async XLA Ops:
  2.0 10.9 %collective-permute-start = (f32[2,2,128,128]{3,2,1,0:T(8,128)S(1)}, f32[2,2,128,128]{3,2,1,0:T(8,128)S(1)}, u32[]{:S(2)}, u32[]{:S(2)}) collective-permute-start(f32[2,2,128,128]{3,2,1,0:T(8,128)S(1)} %get-tuple-element.44), channel_id=1, source_target_pairs={{0,1},{1,0},{16,17},{17,16},{2,3},{3,2},{18,19},{19,18},{4,5},{5,4... | collective-permute-start | bytes 786440 | tf_op jit(solution)/shard_map/ppermute | solution.py:492
  5.1 11.5 %collective-permute-start.1 = (f32[2,2,128,128]{3,2,1,0:T(8,128)S(1)}, f32[2,2,128,128]{3,2,1,0:T(8,128)S(1)}, u32[]{:S(2)}, u32[]{:S(2)}) collective-permute-start(f32[2,2,128,128]{3,2,1,0:T(8,128)S(1)} %get-tuple-element.45), channel_id=1, source_target_pairs={{0,16},{1,17},{16,0},{17,1},{2,18},{3,19},{18,2},{19,3},{4,20},{5,... | collective-permute-start | bytes 786440 | tf_op jit(solution)/shard_map/ppermute | solution.py:492
  6.5 12.9 %collective-permute-start.2 = (f32[2,2,128,128]{3,2,1,0:T(8,128)S(1)}, f32[2,2,128,128]{3,2,1,0:T(8,128)S(1)}, u32[]{:S(2)}, u32[]{:S(2)}) collective-permute-start(f32[2,2,128,128]{3,2,1,0:T(8,128)S(1)} %get-tuple-element.46), channel_id=1, source_target_pairs={{0,17},{1,16},{16,1},{17,0},{2,19},{3,18},{18,3},{19,2},{4,21},{5,... | collective-permute-start | bytes 786440 | tf_op jit(solution)/shard_map/ppermute | solution.py:492
  7.5 12.6 %collective-permute-start.4 = (f32[2,128,128]{2,1,0:T(8,128)S(1)}, f32[2,128,128]{2,1,0:T(8,128)S(1)}, u32[]{:S(2)}, u32[]{:S(2)}) collective-permute-start(f32[2,128,128]{2,1,0:T(8,128)S(1)} %pack_kappa.1.refs_0_), channel_id=1, source_target_pairs={{0,1},{1,0},{16,17},{17,16},{2,3},{3,2},{18,19},{19,18},{4,5},{5,4... | collective-permute-start | bytes 393224 | tf_op jit(solution)/shard_map/ppermute | solution.py:492
  9.5 13.2 %collective-permute-start.5 = (f32[2,128,128]{2,1,0:T(8,128)S(1)}, f32[2,128,128]{2,1,0:T(8,128)S(1)}, u32[]{:S(2)}, u32[]{:S(2)}) collective-permute-start(f32[2,128,128]{2,1,0:T(8,128)S(1)} %pack_kappa.1.refs_0_), channel_id=1, source_target_pairs={{0,16},{1,17},{16,0},{17,1},{2,18},{3,19},{18,2},{19,3},{4,20},{5,... | collective-permute-start | bytes 393224 | tf_op jit(solution)/shard_map/ppermute | solution.py:492
  12.9 11.0 %collective-permute-start.6 = (f32[2,128,128]{2,1,0:T(8,128)S(1)}, f32[2,128,128]{2,1,0:T(8,128)S(1)}, u32[]{:S(2)}, u32[]{:S(2)}) collective-permute-start(f32[2,128,128]{2,1,0:T(8,128)S(1)} %pack_kappa.1.refs_0_), channel_id=1, source_target_pairs={{0,17},{1,16},{16,1},{17,0},{2,19},{3,18},{18,3},{19,2},{4,21},{5,... | collective-permute-start | bytes 393224 | tf_op jit(solution)/shard_map/ppermute | solution.py:492
  20.0 4.0 %collective-permute-start.3 = (f32[4,2,128,128]{3,2,1,0:T(8,128)S(1)}, f32[4,2,128,128]{3,2,1,0:T(8,128)S(1)}, u32[]{:S(2)}, u32[]{:S(2)}) collective-permute-start(f32[4,2,128,128]{3,2,1,0:T(8,128)S(1)} %get-tuple-element.48), channel_id=1, source_target_pairs={{0,8},{8,0},{1,9},{9,1},{2,10},{10,2},{3,11},{11,3},{4,12},{12,4},... | collective-permute-start | bytes 1572872 | tf_op jit(solution)/shard_map/ppermute | solution.py:534
  23.9 3.3 %collective-permute-start.7 = (f32[4,2,128,128]{3,2,1,0:T(8,128)S(1)}, f32[4,2,128,128]{3,2,1,0:T(8,128)S(1)}, u32[]{:S(2)}, u32[]{:S(2)}) collective-permute-start(f32[4,2,128,128]{3,2,1,0:T(8,128)S(1)} %stack_kappa.1.mine_ref), channel_id=1, source_target_pairs={{0,8},{8,0},{1,9},{9,1},{2,10},{10,2},{3,11},{11,3},{4,12},{12,4},... | collective-permute-start | bytes 1572872 | tf_op jit(solution)/shard_map/ppermute | solution.py:521
  24.8 15.8 %collective-permute-start.8 = (f32[4,5,32,128]{3,2,1,0:T(8,128)S(1)}, f32[4,5,32,128]{3,2,1,0:T(8,128)S(1)}, u32[]{:S(2)}, u32[]{:S(2)}) collective-permute-start(f32[4,5,32,128]{3,2,1,0:T(8,128)S(1)} %get-tuple-element.55), channel_id=1, source_target_pairs={{0,2},{2,0},{4,6},{6,4},{1,3},{3,1},{5,7},{7,5},{8,10},{10,8},{12,... | collective-permute-start | bytes 983048 | tf_op jit(solution)/shard_map/ppermute | solution.py:539
  26.6 14.0 %collective-permute-start.9 = (f32[4,5,32,128]{3,2,1,0:T(8,128)S(1)}, f32[4,5,32,128]{3,2,1,0:T(8,128)S(1)}, u32[]{:S(2)}, u32[]{:S(2)}) collective-permute-start(f32[4,5,32,128]{3,2,1,0:T(8,128)S(1)} %get-tuple-element.56), channel_id=1, source_target_pairs={{2,4},{4,2},{3,5},{5,3},{10,12},{12,10},{11,13},{13,11},{18,20},{2... | collective-permute-start | bytes 983048 | tf_op jit(solution)/shard_map/ppermute | solution.py:540
  28.2 12.4 %collective-permute-start.10 = (f32[4,4,32,128]{3,2,1,0:T(8,128)S(1)}, f32[4,4,32,128]{3,2,1,0:T(8,128)S(1)}, u32[]{:S(2)}, u32[]{:S(2)}) collective-permute-start(f32[4,4,32,128]{3,2,1,0:T(8,128)S(1)} %get-tuple-element.57), channel_id=1, source_target_pairs={{0,2},{2,0},{4,6},{6,4},{1,3},{3,1},{5,7},{7,5},{8,10},{10,8},{12,... | collective-permute-start | bytes 786440 | tf_op jit(solution)/shard_map/ppermute | solution.py:527
  32.6 7.9 %collective-permute-start.11 = (f32[4,4,32,128]{3,2,1,0:T(8,128)S(1)}, f32[4,4,32,128]{3,2,1,0:T(8,128)S(1)}, u32[]{:S(2)}, u32[]{:S(2)}) collective-permute-start(f32[4,4,32,128]{3,2,1,0:T(8,128)S(1)} %get-tuple-element.58), channel_id=1, source_target_pairs={{2,4},{4,2},{3,5},{5,3},{10,12},{12,10},{11,13},{13,11},{18,20},{2... | collective-permute-start | bytes 786440 | tf_op jit(solution)/shard_map/ppermute | solution.py:528
  43.2 14.8 %collective-permute-start.12 = (f32[4,5,32,128]{3,2,1,0:T(8,128)S(1)}, f32[4,5,32,128]{3,2,1,0:T(8,128)S(1)}, u32[]{:S(2)}, u32[]{:S(2)}) collective-permute-start(f32[4,5,32,128]{3,2,1,0:T(8,128)S(1)} %get-tuple-element.69), channel_id=1, source_target_pairs={{0,2},{2,0},{4,6},{6,4},{1,3},{3,1},{5,7},{7,5},{8,10},{10,8},{12,... | collective-permute-start | bytes 983048 | tf_op jit(solution)/shard_map/ppermute | solution.py:569
  48.0 10.0 %collective-permute-start.13 = (f32[4,5,32,128]{3,2,1,0:T(8,128)S(1)}, f32[4,5,32,128]{3,2,1,0:T(8,128)S(1)}, u32[]{:S(2)}, u32[]{:S(2)}) collective-permute-start(f32[4,5,32,128]{3,2,1,0:T(8,128)S(1)} %get-tuple-element.70), channel_id=1, source_target_pairs={{2,4},{4,2},{3,5},{5,3},{10,12},{12,10},{11,13},{13,11},{18,20},{2... | collective-permute-start | bytes 983048 | tf_op jit(solution)/shard_map/ppermute | solution.py:570
  50.2 10.2 %collective-permute-start.14 = (f32[8,128]{1,0:T(8,128)S(1)}, f32[8,128]{1,0:T(8,128)S(1)}, u32[]{:S(2)}, u32[]{:S(2)}) collective-permute-start(f32[8,128]{1,0:T(8,128)S(1)} %get-tuple-element.76.rest_0_), channel_id=1, source_target_pairs={{0,2},{2,0},{4,6},{6,4},{1,3},{3,1},{5,7},{7,5},{8,10},{10,8},{12,... | collective-permute-start | bytes 12296 | tf_op jit(solution)/shard_map/ppermute | solution.py:582
  53.3 7.2 %collective-permute-start.15 = (f32[8,128]{1,0:T(8,128)S(1)}, f32[8,128]{1,0:T(8,128)S(1)}, u32[]{:S(2)}, u32[]{:S(2)}) collective-permute-start(f32[8,128]{1,0:T(8,128)S(1)} %get-tuple-element.76.rest_0_), channel_id=1, source_target_pairs={{0,4},{2,6},{4,0},{6,2},{1,5},{3,7},{5,1},{7,3},{8,12},{10,14},{12... | collective-permute-start | bytes 12296 | tf_op jit(solution)/shard_map/ppermute | solution.py:582
  53.5 7.0 %collective-permute-start.16 = (f32[8,128]{1,0:T(8,128)S(1)}, f32[8,128]{1,0:T(8,128)S(1)}, u32[]{:S(2)}, u32[]{:S(2)}) collective-permute-start(f32[8,128]{1,0:T(8,128)S(1)} %get-tuple-element.76.rest_0_), channel_id=1, source_target_pairs={{0,6},{2,4},{4,2},{6,0},{1,7},{3,5},{5,3},{7,1},{8,14},{10,12},{12... | collective-permute-start | bytes 12296 | tf_op jit(solution)/shard_map/ppermute | solution.py:582
  58.0 2.4 %copy-start = (f32[5,8]{1,0:T(8,128)S(1)}, f32[5,8]{1,0:T(8,128)}, u32[]{:S(2)}) copy-start(f32[5,8]{1,0:T(8,128)} %weights_ref.3) | copy-start | bytes 484
  62.5 2.1 %collective-permute-start.17 = (f32[4,2,128,128]{3,2,1,0:T(8,128)S(1)}, f32[4,2,128,128]{3,2,1,0:T(8,128)S(1)}, u32[]{:S(2)}, u32[]{:S(2)}) collective-permute-start(f32[4,2,128,128]{3,2,1,0:T(8,128)S(1)} %last_step_given.1), channel_id=1, source_target_pairs={{0,8},{8,0},{1,9},{9,1},{2,10},{10,2},{3,11},{11,3},{4,12},{12,4},... | collective-permute-start | bytes 1572872 | tf_op jit(solution)/shard_map/ppermute | solution.py:620
  65.2 7.3 %collective-permute-start.18 = (f32[2,128,128]{2,1,0:T(8,128)S(1)}, f32[2,128,128]{2,1,0:T(8,128)S(1)}, u32[]{:S(2)}, u32[]{:S(2)}) collective-permute-start(f32[2,128,128]{2,1,0:T(8,128)S(1)} %get-tuple-element.78), channel_id=1, source_target_pairs={{0,17},{1,16},{16,1},{17,0},{2,19},{3,18},{18,3},{19,2},{4,21},{5,... | collective-permute-start | bytes 393224 | tf_op jit(solution)/shard_map/ppermute | solution.py:492
  67.7 7.3 %collective-permute-start.19 = (f32[2,128,128]{2,1,0:T(8,128)S(1)}, f32[2,128,128]{2,1,0:T(8,128)S(1)}, u32[]{:S(2)}, u32[]{:S(2)}) collective-permute-start(f32[2,128,128]{2,1,0:T(8,128)S(1)} %get-tuple-element.79), channel_id=1, source_target_pairs={{0,16},{1,17},{16,0},{17,1},{2,18},{3,19},{18,2},{19,3},{4,20},{5,... | collective-permute-start | bytes 393224 | tf_op jit(solution)/shard_map/ppermute | solution.py:492
  68.3 6.7 %collective-permute-start.20 = (f32[2,128,128]{2,1,0:T(8,128)S(1)}, f32[2,128,128]{2,1,0:T(8,128)S(1)}, u32[]{:S(2)}, u32[]{:S(2)}) collective-permute-start(f32[2,128,128]{2,1,0:T(8,128)S(1)} %get-tuple-element.80), channel_id=1, source_target_pairs={{0,1},{1,0},{16,17},{17,16},{2,3},{3,2},{18,19},{19,18},{4,5},{5,4... | collective-permute-start | bytes 393224 | tf_op jit(solution)/shard_map/ppermute | solution.py:492

commit v11 on v10

--- a/solution.py
+++ b/solution.py
@@ -158,7 +158,7 @@
         copy.wait()
 
 
-def pack_probes_kernel(grid, count, spot_ref, probes_ref, *rest):
+def pack_probes_kernel(grid, count, spot_ref, after_ref, probes_ref, *rest):
     nx, nz, bx, by, bz = grid
     rows = bx * by
     outs, sem = rest[:-1], rest[-1]
@@ -178,12 +178,12 @@
         copy.wait()
 
 
-def stack_kernel(*refs):
+def stack_kernel(after_ref, *refs):
     for k, ref in enumerate(refs[:-1]):
         refs[-1][k] = ref[...]
 
 
-def sort_probes_kernel(spot_ref, *refs):
+def sort_probes_kernel(spot_ref, after_ref, after_too_ref, *refs):
     parts, mine_ref, give_ref = refs[:-2], refs[-2], refs[-1]
     core = spot_ref[3]
     for k, part in enumerate(parts):
@@ -512,12 +512,15 @@
     kappas = [kappa] + [to_chip(kappa, k) for k in range(1, chips)]
     packed = plain(
         functools.partial(pack_probes_kernel, grid, count), "pack_probes",
-        (f32(2, per, rows, 128),) * chips, [smem(), hbm()],
-        spot, there(probes.reshape(count * rows, bz)), scratch_shapes=[dma((chips, 2, per))],
+        (f32(2, per, rows, 128),) * chips, [smem(), vmem(), hbm()],
+        spot, kappa, there(probes.reshape(count * rows, bz)), scratch_shapes=[dma((chips, 2, per))],
     )
     probes = [packed[0]] + [to_chip(packed[k], k) for k in range(1, chips)]
 
-    kappa = plain(stack_kernel, "stack_kappa", stacked, [vmem()] * chips, *kappas)
+    kappa = plain(
+        stack_kernel, "stack_kappa", stacked,
+        [vmem()] * (chips + 1), packed[0], *kappas,
+    )
     other = lax.ppermute(kappa, "core", swap)
     diagonal, even_edge, odd_edge = plain(
         functools.partial(diagonal_kernel, grid), "diagonal_rows",
@@ -529,7 +532,7 @@
 
     probe, give = plain(
         sort_probes_kernel, "sort_probes", (stacked, stacked),
-        [smem()] + [vmem()] * chips, spot, *probes,
+        [smem()] + [vmem()] * (chips + 2), spot, even_diagonal, odd_diagonal, *probes,
     )
     other = lax.ppermute(give, "core", swap)
     even_edge, odd_edge = plain(

time: 76 us -> 75.7 us (level)
  starting transfers between devices: 34.1 us -> 27.8 us
  waiting for transfers between devices: 18.1 us -> 24.1 us
    ppermute x9, waiting for transfers between devices: 14.7 us -> 18.8 us  [to_chip(): return lax.ppermute(value, ('chip', 'gz'), pairs)]
    ppermute x9, starting transfers between devices: 15.3 us -> 11.7 us  [to_chip(): return lax.ppermute(value, ('chip', 'gz'), pairs)]
    ppermute x1, waiting for transfers between devices: 0.01 us -> 3.42 us  [body(): even1 = lax.ppermute(even_edge, 'gy', even)]
    ppermute x1, waiting for transfers between devices: 3.34 us -> 0.01 us  [body(): even_diagonal = lax.ppermute(even_edge, 'gy', even)]
    ppermute x1, starting transfers between devices: 4.44 us -> 1.8 us  [body(): even_diagonal = lax.ppermute(even_edge, 'gy', even)]
    ppermute x1, waiting for transfers between devices: 0.01 us -> 1.9 us  [body(): other = lax.ppermute(give, 'core', swap)]
  transfers between devices with their start and end apart: 21 -> 21, of which waited for: 7 -> 9; matrix products, arithmetic and copies ran while one was open for 0% -> 0% of each run, Pallas kernels for 20% -> 20%
where the time goes in v11:
time: 75.7 us; the launch traced here: 75.4 us
  starting transfers between devices  27.8 us (37%)
  waiting for transfers between devices  24.1 us (32%)
  Pallas kernels  23.2 us (31%)
    ppermute x9, waiting for transfers between devices, to_chip(): return lax.ppermute(value, ('chip', 'gz'), pairs)  18.8 us
    ppermute x9, starting transfers between devices, to_chip(): return lax.ppermute(value, ('chip', 'gz'), pairs)  11.7 us
    pallas_call x8, Pallas kernels, plain(): pl.pallas_call(kernel, out_shape=out_shape, in_specs=specs, out_specs=(vm...  6.42 us
    ppermute x3, starting transfers between devices, body(): lax.ppermute(moments, 'gy', [(i, i ^ step) for i in range(ny)])  5.49 us
    ppermute x1, starting transfers between devices, body(): even2 = lax.ppermute(even_edge, 'gy', even)  4.81 us
    pallas_call x2, Pallas kernels, last_step(): pl.pallas_call(functools.partial(last_kernel, grid, inverse_count, flip),...  4.06 us
    pallas_call x1, Pallas kernels, body(): pl.pallas_call(functools.partial(inner_kernel, grid), out_shape=tuple((ve...  3.91 us
    ppermute x1, waiting for transfers between devices, body(): even1 = lax.ppermute(even_edge, 'gy', even)  3.42 us
  transfers between devices with their start and end apart: 21, of which 9 were waited for; matrix products, arithmetic and copies ran while one was open for 0% of the time, Pallas kernels for 20%

profile of v11, /device:TPU:0, one launch (start us, length us, event | category | flops | bytes accessed | tf_op | source)
XLA Modules:
  0.0 75.4 jit_solution(4311301095954896860)
XLA Ops:
  0.9 3.0 %collective-permute-start = (f32[2,128,128]{2,1,0:T(8,128)S(1)}, f32[2,128,128]{2,1,0:T(8,128)S(1)}, u32[]{:S(2)}, u32[]{:S(2)}) collective-permute-start(f32[2,128,128]{2,1,0:T(8,128)S(1)} %pack_kappa.1.after_ref.refs_0_), channel_id=1, source_target_pairs={{0,1},{1,0},{16,17},{17,16},{2,3},{3,2},{18,19},{19,18},{4,5},{5,4... | collective-permute-start | bytes 393224 | tf_op jit(solution)/shard_map/ppermute | solution.py:492
  5.6 1.9 %pack_probes.1 = (f32[2,2,128,128]{3,2,1,0:T(8,128)S(1)}, f32[2,2,128,128]{3,2,1,0:T(8,128)S(1)}, f32[2,2,128,128]{3,2,1,0:T(8,128)S(1)}, f32[2,2,128,128]{3,2,1,0:T(8,128)S(1)}) custom-call(s32[6]{0:T(128)S(1)} %stack.35.spot_ref, f32[2,128,128]{2,1,0:T(8,128)S(1)} %pack_kappa.1.after_ref.refs_0_, f32[1024,256]{1,0:T(8,128)} %bitcast.8), custom_call_target="tpu_custom_call" | custom-call | tf_op jit(solution)/shard_map/pack_probes/pallas_call | solution.py:495
  7.5 2.8 %collective-permute-done.1.refs_2_ = f32[2,128,128]{2,1,0:T(8,128)S(1)} collective-permute-done((f32[2,128,128]{2,1,0:T(8,128)S(1)}, f32[2,128,128]{2,1,0:T(8,128)S(1)}, u32[]{:S(2)}, u32[]{:S(2)}) %collective-permute-start.1) | collective-permute-done | bytes 131104 | tf_op jit(solution)/shard_map/ppermute | solution.py:492
  11.6 1.7 %collective-permute-start.6 = (f32[2,2,128,128]{3,2,1,0:T(8,128)S(1)}, f32[2,2,128,128]{3,2,1,0:T(8,128)S(1)}, u32[]{:S(2)}, u32[]{:S(2)}) collective-permute-start(f32[2,2,128,128]{3,2,1,0:T(8,128)S(1)} %get-tuple-element.46), channel_id=1, source_target_pairs={{0,1},{1,0},{16,17},{17,16},{2,3},{3,2},{18,19},{19,18},{4,5},{5,4... | collective-permute-start | bytes 786440 | tf_op jit(solution)/shard_map/ppermute | solution.py:492
  13.3 1.5 %collective-permute-start.7 = (f32[2,2,128,128]{3,2,1,0:T(8,128)S(1)}, f32[2,2,128,128]{3,2,1,0:T(8,128)S(1)}, u32[]{:S(2)}, u32[]{:S(2)}) collective-permute-start(f32[2,2,128,128]{3,2,1,0:T(8,128)S(1)} %get-tuple-element.47), channel_id=1, source_target_pairs={{0,16},{1,17},{16,0},{17,1},{2,18},{3,19},{18,2},{19,3},{4,20},{5,... | collective-permute-start | bytes 786440 | tf_op jit(solution)/shard_map/ppermute | solution.py:492
  16.1 1.8 %collective-permute-start.4 = (f32[4,4,32,128]{3,2,1,0:T(8,128)S(1)}, f32[4,4,32,128]{3,2,1,0:T(8,128)S(1)}, u32[]{:S(2)}, u32[]{:S(2)}) collective-permute-start(f32[4,4,32,128]{3,2,1,0:T(8,128)S(1)} %get-tuple-element.44), channel_id=1, source_target_pairs={{0,2},{2,0},{4,6},{6,4},{1,3},{3,1},{5,7},{7,5},{8,10},{10,8},{12,... | collective-permute-start | bytes 786440 | tf_op jit(solution)/shard_map/ppermute | solution.py:530
  18.6 1.8 %collective-permute-done.6.refs_1_ = f32[2,2,128,128]{3,2,1,0:T(8,128)S(1)} collective-permute-done((f32[2,2,128,128]{3,2,1,0:T(8,128)S(1)}, f32[2,2,128,128]{3,2,1,0:T(8,128)S(1)}, u32[]{:S(2)}, u32[]{:S(2)}) %collective-permute-start.6) | collective-permute-done | bytes 262176 | tf_op jit(solution)/shard_map/ppermute | solution.py:492
  20.3 2.2 %collective-permute-done.7.refs_2_ = f32[2,2,128,128]{3,2,1,0:T(8,128)S(1)} collective-permute-done((f32[2,2,128,128]{3,2,1,0:T(8,128)S(1)}, f32[2,2,128,128]{3,2,1,0:T(8,128)S(1)}, u32[]{:S(2)}, u32[]{:S(2)}) %collective-permute-start.7) | collective-permute-done | bytes 262176 | tf_op jit(solution)/shard_map/ppermute | solution.py:492
  22.5 4.6 %collective-permute-done.8.refs_3_ = f32[2,2,128,128]{3,2,1,0:T(8,128)S(1)} collective-permute-done((f32[2,2,128,128]{3,2,1,0:T(8,128)S(1)}, f32[2,2,128,128]{3,2,1,0:T(8,128)S(1)}, u32[]{:S(2)}, u32[]{:S(2)}) %collective-permute-start.8) | collective-permute-done | bytes 262176 | tf_op jit(solution)/shard_map/ppermute | solution.py:492
  27.8 1.9 %collective-permute-done.9.other_ref = f32[4,2,128,128]{3,2,1,0:T(8,128)S(1)} collective-permute-done((f32[4,2,128,128]{3,2,1,0:T(8,128)S(1)}, f32[4,2,128,128]{3,2,1,0:T(8,128)S(1)}, u32[]{:S(2)}, u32[]{:S(2)}) %collective-permute-start.9) | collective-permute-done | bytes 524320 | tf_op jit(solution)/shard_map/ppermute | solution.py:537
  30.5 1.8 %collective-permute-start.10 = (f32[4,5,32,128]{3,2,1,0:T(8,128)S(1)}, f32[4,5,32,128]{3,2,1,0:T(8,128)S(1)}, u32[]{:S(2)}, u32[]{:S(2)}) collective-permute-start(f32[4,5,32,128]{3,2,1,0:T(8,128)S(1)} %get-tuple-element.57), channel_id=1, source_target_pairs={{0,2},{2,0},{4,6},{6,4},{1,3},{3,1},{5,7},{7,5},{8,10},{10,8},{12,... | collective-permute-start | bytes 983048 | tf_op jit(solution)/shard_map/ppermute | solution.py:542
  33.0 3.9 %inner_steps.1 = (f32[4,26,48,128]{3,2,1,0:T(8,128)S(1)}, f32[4,24,48,128]{3,2,1,0:T(8,128)S(1)}, f32[4,22,48,128]{3,2,1,0:T(8,128)S(1)}, f32[4,20,48,128]{3,2,1,0:T(8,128)S(1)}, f32[4,26,48,128]{3,2,1,0:T(8,128)S(1)}) custom-call(s32[6]{0:T(128)S(1)} %stack.35.spot_ref, f32[4,2,128,128]{3,2,1,0:T(8,128)S(1)} %get-tuple-element.49.mine_ref, ...), custom_call_target="tpu_custom_call" | custom-call | flops 8388608 | bytes 4194304 | tf_op jit(solution)/shard_map/inner_steps/pallas_call | solution.py:552
  36.9 3.4 %collective-permute-done.10.even_ref = f32[4,5,32,128]{3,2,1,0:T(8,128)S(1)} collective-permute-done((f32[4,5,32,128]{3,2,1,0:T(8,128)S(1)}, f32[4,5,32,128]{3,2,1,0:T(8,128)S(1)}, u32[]{:S(2)}, u32[]{:S(2)}) %collective-permute-start.10) | collective-permute-done | bytes 327712 | tf_op jit(solution)/shard_map/ppermute | solution.py:542
  40.3 2.7 %first_steps.1 = (f32[4,26,48,128]{3,2,1,0:T(8,128)S(1)}, f32[4,24,48,128]{3,2,1,0:T(8,128)S(1)}, f32[4,24,48,128]{3,2,1,0:T(8,128)S(1)}, f32[4,22,48,128]{3,2,1...) custom-call(s32[6]{0:T(128)S(1)} %stack.35.spot_ref, ...), custom_call_target="tpu_custom_call", output_to_operand_aliasing={{0}: (1, {}), {1}: (2, {}), {2}: (3, {}), {3}: (4, {}), {4}... | custom-call | tf_op jit(solution)/shard_map/first_steps/pallas_call | solution.py:562
  43.0 4.8 %collective-permute-start.12 = (f32[4,5,32,128]{3,2,1,0:T(8,128)S(1)}, f32[4,5,32,128]{3,2,1,0:T(8,128)S(1)}, u32[]{:S(2)}, u32[]{:S(2)}) collective-permute-start(f32[4,5,32,128]{3,2,1,0:T(8,128)S(1)} %get-tuple-element.69), channel_id=1, source_target_pairs={{0,2},{2,0},{4,6},{6,4},{1,3},{3,1},{5,7},{7,5},{8,10},{10,8},{12,... | collective-permute-start | bytes 983048 | tf_op jit(solution)/shard_map/ppermute | solution.py:572
  49.9 3.1 %collective-permute-start.14 = (f32[8,128]{1,0:T(8,128)S(1)}, f32[8,128]{1,0:T(8,128)S(1)}, u32[]{:S(2)}, u32[]{:S(2)}) collective-permute-start(f32[8,128]{1,0:T(8,128)S(1)} %get-tuple-element.76.rest_0_), channel_id=1, source_target_pairs={{0,2},{2,0},{4,6},{6,4},{1,3},{3,1},{5,7},{7,5},{8,10},{10,8},{12,... | collective-permute-start | bytes 12296 | tf_op jit(solution)/shard_map/ppermute | solution.py:585
  53.2 2.2 %collective-permute-start.16 = (f32[8,128]{1,0:T(8,128)S(1)}, f32[8,128]{1,0:T(8,128)S(1)}, u32[]{:S(2)}, u32[]{:S(2)}) collective-permute-start(f32[8,128]{1,0:T(8,128)S(1)} %get-tuple-element.76.rest_0_), channel_id=1, source_target_pairs={{0,6},{2,4},{4,2},{6,0},{1,7},{3,5},{5,3},{7,1},{8,14},{10,12},{12... | collective-permute-start | bytes 12296 | tf_op jit(solution)/shard_map/ppermute | solution.py:585
  55.4 2.3 %second_inner_steps.1 = (f32[4,22,48,128]{3,2,1,0:T(8,128)S(1)}, f32[4,20,48,128]{3,2,1,0:T(8,128)S(1)}, f32[4,18,48,128]{3,2,1,0:T(8,128)S(1)}) custom-call(f32[4,24,48,128]{3,2,1,0:T(8,128)S(1)} %get-tuple-element.60.diagonal_ref, f32[4,26,48,128]{3,2,1,0:T(8,128)S(1)} %get-tuple-element.64.c2_ref.c2_in, f32[4,24,48,128]{3,2,1,0:T(8,128)S(1)} %get-tuple-element.65.d2_ref.d2_in), custom_call_target="tpu_custom_call" | custom-call | flops 7864320 | bytes 4194304 | tf_op jit(solution)/shard_map/second_inner_steps/pallas_call | solution.py:587
  57.8 2.4 %third_steps.1 = (f32[4,26,48,128]{3,2,1,0:T(8,128)S(1)}, f32[4,24,48,128]{3,2,1,0:T(8,128)S(1)}, f32[4,22,48,128]{3,2,1,0:T(8,128)S(1)}, f32[4,20,48,128]{3,2,1,0:T(8,128)S(1)}, f32[4,18,48,128]{3,2,1,0:T(8,128)S(1)}) custom-call(s32[6]{0:T(128)S(1)} %stack.35.spot_ref, ...), custom_call_target="tpu_custom_call", output_to_operand_aliasing={{0}: (2, {}), {1}: (3, {}), {2}: (4, {}), {3}: (5, {}), {4}... | custom-call | flops 5242880 | bytes 4194304 | tf_op jit(solution)/shard_map/third_steps/pallas_call | solution.py:597
  60.2 2.0 %last_step_given.1 = f32[4,2,128,128]{3,2,1,0:T(8,128)S(1)} custom-call(s32[6]{0:T(128)S(1)} %stack.35.spot_ref, f32[5,8]{1,0:T(8,128)S(1)} %copy-done, f32[4,26,48,128]{3,2,1,0:T(8,128)S(1)} %get-tuple-element.59.c0_ref, f32[4,24,48,128]{3,2,1,0:T(8,128)S(1)} %get-tuple-element.60.diagonal_ref, f32[4,24,48,128]{3,2,1,0:T(8,128)S(1)} %get-tuple-element.61.d0_ref, ...), custom_call_target="tpu_custom_call" | custom-call | flops 5242880 | bytes 4194304 | tf_op jit(solution)/shard_map/last_step_given/pallas_call | solution.py:613
  62.3 2.0 %last_step_kept.1.kept_ref = f32[4,2,128,128]{3,2,1,0:T(8,128)S(1)} custom-call(s32[6]{0:T(128)S(1)} %stack.35.spot_ref, f32[5,8]{1,0:T(8,128)S(1)} %copy-done, f32[4,26,48,128]{3,2,1,0:T(8,128)S(1)} %get-tuple-element.59.c0_ref, f32[4,24,48,128]{3,2,1,0:T(8,128)S(1)} %get-tuple-element.60.diagonal_ref, f32[4,24,48,128]{3,2,1,0:T(8,128)S(1)} %get-tuple-element.61.d0_ref, ...), custom_call_target="tpu_custom_call" | custom-call | flops 5242880 | bytes 4194304 | tf_op jit(solution)/shard_map/last_step_kept/pallas_call | solution.py:613
  65.0 2.5 %collective-permute-start.18 = (f32[2,128,128]{2,1,0:T(8,128)S(1)}, f32[2,128,128]{2,1,0:T(8,128)S(1)}, u32[]{:S(2)}, u32[]{:S(2)}) collective-permute-start(f32[2,128,128]{2,1,0:T(8,128)S(1)} %get-tuple-element.78), channel_id=1, source_target_pairs={{0,17},{1,16},{16,1},{17,0},{2,19},{3,18},{18,3},{19,2},{4,21},{5,... | collective-permute-start | bytes 393224 | tf_op jit(solution)/shard_map/ppermute | solution.py:492
  68.5 3.7 %collective-permute-done.18.refs_1_ = f32[2,128,128]{2,1,0:T(8,128)S(1)} collective-permute-done((f32[2,128,128]{2,1,0:T(8,128)S(1)}, f32[2,128,128]{2,1,0:T(8,128)S(1)}, u32[]{:S(2)}, u32[]{:S(2)}) %collective-permute-start.18) | collective-permute-done | bytes 131104 | tf_op jit(solution)/shard_map/ppermute | solution.py:492
  72.2 2.5 %collective-permute-done.19.refs_2_ = f32[2,128,128]{2,1,0:T(8,128)S(1)} collective-permute-done((f32[2,128,128]{2,1,0:T(8,128)S(1)}, f32[2,128,128]{2,1,0:T(8,128)S(1)}, u32[]{:S(2)}, u32[]{:S(2)}) %collective-permute-start.19) | collective-permute-done | bytes 131104 | tf_op jit(solution)/shard_map/ppermute | solution.py:492
  (36 shorter events, 12.6 us)
Async XLA Ops:
  0.9 6.6 %collective-permute-start = (f32[2,128,128]{2,1,0:T(8,128)S(1)}, f32[2,128,128]{2,1,0:T(8,128)S(1)}, u32[]{:S(2)}, u32[]{:S(2)}) collective-permute-start(f32[2,128,128]{2,1,0:T(8,128)S(1)} %pack_kappa.1.after_ref.refs_0_), channel_id=1, source_target_pairs={{0,1},{1,0},{16,17},{17,16},{2,3},{3,2},{18,19},{19,18},{4,5},{5,4... | collective-permute-start | bytes 393224 | tf_op jit(solution)/shard_map/ppermute | solution.py:492
  3.9 6.4 %collective-permute-start.1 = (f32[2,128,128]{2,1,0:T(8,128)S(1)}, f32[2,128,128]{2,1,0:T(8,128)S(1)}, u32[]{:S(2)}, u32[]{:S(2)}) collective-permute-start(f32[2,128,128]{2,1,0:T(8,128)S(1)} %pack_kappa.1.after_ref.refs_0_), channel_id=1, source_target_pairs={{0,16},{1,17},{16,0},{17,1},{2,18},{3,19},{18,2},{19,3},{4,20},{5,... | collective-permute-start | bytes 393224 | tf_op jit(solution)/shard_map/ppermute | solution.py:492
  5.4 6.1 %collective-permute-start.2 = (f32[2,128,128]{2,1,0:T(8,128)S(1)}, f32[2,128,128]{2,1,0:T(8,128)S(1)}, u32[]{:S(2)}, u32[]{:S(2)}) collective-permute-start(f32[2,128,128]{2,1,0:T(8,128)S(1)} %pack_kappa.1.after_ref.refs_0_), channel_id=1, source_target_pairs={{0,17},{1,16},{16,1},{17,0},{2,19},{3,18},{18,3},{19,2},{4,21},{5,... | collective-permute-start | bytes 393224 | tf_op jit(solution)/shard_map/ppermute | solution.py:492
  11.5 3.6 %collective-permute-start.3 = (f32[4,2,128,128]{3,2,1,0:T(8,128)S(1)}, f32[4,2,128,128]{3,2,1,0:T(8,128)S(1)}, u32[]{:S(2)}, u32[]{:S(2)}) collective-permute-start(f32[4,2,128,128]{3,2,1,0:T(8,128)S(1)} %stack_kappa.1.mine_ref), channel_id=1, source_target_pairs={{0,8},{8,0},{1,9},{9,1},{2,10},{10,2},{3,11},{11,3},{4,12},{12,4},... | collective-permute-start | bytes 1572872 | tf_op jit(solution)/shard_map/ppermute | solution.py:524
  11.6 8.7 %collective-permute-start.6 = (f32[2,2,128,128]{3,2,1,0:T(8,128)S(1)}, f32[2,2,128,128]{3,2,1,0:T(8,128)S(1)}, u32[]{:S(2)}, u32[]{:S(2)}) collective-permute-start(f32[2,2,128,128]{3,2,1,0:T(8,128)S(1)} %get-tuple-element.46), channel_id=1, source_target_pairs={{0,1},{1,0},{16,17},{17,16},{2,3},{3,2},{18,19},{19,18},{4,5},{5,4... | collective-permute-start | bytes 786440 | tf_op jit(solution)/shard_map/ppermute | solution.py:492
  13.3 9.2 %collective-permute-start.7 = (f32[2,2,128,128]{3,2,1,0:T(8,128)S(1)}, f32[2,2,128,128]{3,2,1,0:T(8,128)S(1)}, u32[]{:S(2)}, u32[]{:S(2)}) collective-permute-start(f32[2,2,128,128]{3,2,1,0:T(8,128)S(1)} %get-tuple-element.47), channel_id=1, source_target_pairs={{0,16},{1,17},{16,0},{17,1},{2,18},{3,19},{18,2},{19,3},{4,20},{5,... | collective-permute-start | bytes 786440 | tf_op jit(solution)/shard_map/ppermute | solution.py:492
  14.8 12.3 %collective-permute-start.8 = (f32[2,2,128,128]{3,2,1,0:T(8,128)S(1)}, f32[2,2,128,128]{3,2,1,0:T(8,128)S(1)}, u32[]{:S(2)}, u32[]{:S(2)}) collective-permute-start(f32[2,2,128,128]{3,2,1,0:T(8,128)S(1)} %get-tuple-element.48), channel_id=1, source_target_pairs={{0,17},{1,16},{16,1},{17,0},{2,19},{3,18},{18,3},{19,2},{4,21},{5,... | collective-permute-start | bytes 786440 | tf_op jit(solution)/shard_map/ppermute | solution.py:492
  16.1 11.0 %collective-permute-start.4 = (f32[4,4,32,128]{3,2,1,0:T(8,128)S(1)}, f32[4,4,32,128]{3,2,1,0:T(8,128)S(1)}, u32[]{:S(2)}, u32[]{:S(2)}) collective-permute-start(f32[4,4,32,128]{3,2,1,0:T(8,128)S(1)} %get-tuple-element.44), channel_id=1, source_target_pairs={{0,2},{2,0},{4,6},{6,4},{1,3},{3,1},{5,7},{7,5},{8,10},{10,8},{12,... | collective-permute-start | bytes 786440 | tf_op jit(solution)/shard_map/ppermute | solution.py:530
  17.9 9.2 %collective-permute-start.5 = (f32[4,4,32,128]{3,2,1,0:T(8,128)S(1)}, f32[4,4,32,128]{3,2,1,0:T(8,128)S(1)}, u32[]{:S(2)}, u32[]{:S(2)}) collective-permute-start(f32[4,4,32,128]{3,2,1,0:T(8,128)S(1)} %get-tuple-element.45), channel_id=1, source_target_pairs={{2,4},{4,2},{3,5},{5,3},{10,12},{12,10},{11,13},{13,11},{18,20},{2... | collective-permute-start | bytes 786440 | tf_op jit(solution)/shard_map/ppermute | solution.py:531
  27.8 2.0 %collective-permute-start.9 = (f32[4,2,128,128]{3,2,1,0:T(8,128)S(1)}, f32[4,2,128,128]{3,2,1,0:T(8,128)S(1)}, u32[]{:S(2)}, u32[]{:S(2)}) collective-permute-start(f32[4,2,128,128]{3,2,1,0:T(8,128)S(1)} %get-tuple-element.50), channel_id=1, source_target_pairs={{0,8},{8,0},{1,9},{9,1},{2,10},{10,2},{3,11},{11,3},{4,12},{12,4},... | collective-permute-start | bytes 1572872 | tf_op jit(solution)/shard_map/ppermute | solution.py:537
  30.5 9.8 %collective-permute-start.10 = (f32[4,5,32,128]{3,2,1,0:T(8,128)S(1)}, f32[4,5,32,128]{3,2,1,0:T(8,128)S(1)}, u32[]{:S(2)}, u32[]{:S(2)}) collective-permute-start(f32[4,5,32,128]{3,2,1,0:T(8,128)S(1)} %get-tuple-element.57), channel_id=1, source_target_pairs={{0,2},{2,0},{4,6},{6,4},{1,3},{3,1},{5,7},{7,5},{8,10},{10,8},{12,... | collective-permute-start | bytes 983048 | tf_op jit(solution)/shard_map/ppermute | solution.py:542
  32.3 8.0 %collective-permute-start.11 = (f32[4,5,32,128]{3,2,1,0:T(8,128)S(1)}, f32[4,5,32,128]{3,2,1,0:T(8,128)S(1)}, u32[]{:S(2)}, u32[]{:S(2)}) collective-permute-start(f32[4,5,32,128]{3,2,1,0:T(8,128)S(1)} %get-tuple-element.58), channel_id=1, source_target_pairs={{2,4},{4,2},{3,5},{5,3},{10,12},{12,10},{11,13},{13,11},{18,20},{2... | collective-permute-start | bytes 983048 | tf_op jit(solution)/shard_map/ppermute | solution.py:543
  43.0 14.8 %collective-permute-start.12 = (f32[4,5,32,128]{3,2,1,0:T(8,128)S(1)}, f32[4,5,32,128]{3,2,1,0:T(8,128)S(1)}, u32[]{:S(2)}, u32[]{:S(2)}) collective-permute-start(f32[4,5,32,128]{3,2,1,0:T(8,128)S(1)} %get-tuple-element.69), channel_id=1, source_target_pairs={{0,2},{2,0},{4,6},{6,4},{1,3},{3,1},{5,7},{7,5},{8,10},{10,8},{12,... | collective-permute-start | bytes 983048 | tf_op jit(solution)/shard_map/ppermute | solution.py:572
  47.8 10.0 %collective-permute-start.13 = (f32[4,5,32,128]{3,2,1,0:T(8,128)S(1)}, f32[4,5,32,128]{3,2,1,0:T(8,128)S(1)}, u32[]{:S(2)}, u32[]{:S(2)}) collective-permute-start(f32[4,5,32,128]{3,2,1,0:T(8,128)S(1)} %get-tuple-element.70), channel_id=1, source_target_pairs={{2,4},{4,2},{3,5},{5,3},{10,12},{12,10},{11,13},{13,11},{18,20},{2... | collective-permute-start | bytes 983048 | tf_op jit(solution)/shard_map/ppermute | solution.py:573
  49.9 10.2 %collective-permute-start.14 = (f32[8,128]{1,0:T(8,128)S(1)}, f32[8,128]{1,0:T(8,128)S(1)}, u32[]{:S(2)}, u32[]{:S(2)}) collective-permute-start(f32[8,128]{1,0:T(8,128)S(1)} %get-tuple-element.76.rest_0_), channel_id=1, source_target_pairs={{0,2},{2,0},{4,6},{6,4},{1,3},{3,1},{5,7},{7,5},{8,10},{10,8},{12,... | collective-permute-start | bytes 12296 | tf_op jit(solution)/shard_map/ppermute | solution.py:585
  53.0 7.2 %collective-permute-start.15 = (f32[8,128]{1,0:T(8,128)S(1)}, f32[8,128]{1,0:T(8,128)S(1)}, u32[]{:S(2)}, u32[]{:S(2)}) collective-permute-start(f32[8,128]{1,0:T(8,128)S(1)} %get-tuple-element.76.rest_0_), channel_id=1, source_target_pairs={{0,4},{2,6},{4,0},{6,2},{1,5},{3,7},{5,1},{7,3},{8,12},{10,14},{12... | collective-permute-start | bytes 12296 | tf_op jit(solution)/shard_map/ppermute | solution.py:585
  53.2 7.0 %collective-permute-start.16 = (f32[8,128]{1,0:T(8,128)S(1)}, f32[8,128]{1,0:T(8,128)S(1)}, u32[]{:S(2)}, u32[]{:S(2)}) collective-permute-start(f32[8,128]{1,0:T(8,128)S(1)} %get-tuple-element.76.rest_0_), channel_id=1, source_target_pairs={{0,6},{2,4},{4,2},{6,0},{1,7},{3,5},{5,3},{7,1},{8,14},{10,12},{12... | collective-permute-start | bytes 12296 | tf_op jit(solution)/shard_map/ppermute | solution.py:585
  57.8 2.4 %copy-start = (f32[5,8]{1,0:T(8,128)S(1)}, f32[5,8]{1,0:T(8,128)}, u32[]{:S(2)}) copy-start(f32[5,8]{1,0:T(8,128)} %weights_ref.3) | copy-start | bytes 484
  62.2 2.1 %collective-permute-start.17 = (f32[4,2,128,128]{3,2,1,0:T(8,128)S(1)}, f32[4,2,128,128]{3,2,1,0:T(8,128)S(1)}, u32[]{:S(2)}, u32[]{:S(2)}) collective-permute-start(f32[4,2,128,128]{3,2,1,0:T(8,128)S(1)} %last_step_given.1), channel_id=1, source_target_pairs={{0,8},{8,0},{1,9},{9,1},{2,10},{10,2},{3,11},{11,3},{4,12},{12,4},... | collective-permute-start | bytes 1572872 | tf_op jit(solution)/shard_map/ppermute | solution.py:623
  65.0 7.3 %collective-permute-start.18 = (f32[2,128,128]{2,1,0:T(8,128)S(1)}, f32[2,128,128]{2,1,0:T(8,128)S(1)}, u32[]{:S(2)}, u32[]{:S(2)}) collective-permute-start(f32[2,128,128]{2,1,0:T(8,128)S(1)} %get-tuple-element.78), channel_id=1, source_target_pairs={{0,17},{1,16},{16,1},{17,0},{2,19},{3,18},{18,3},{19,2},{4,21},{5,... | collective-permute-start | bytes 393224 | tf_op jit(solution)/shard_map/ppermute | solution.py:492
  67.5 7.3 %collective-permute-start.19 = (f32[2,128,128]{2,1,0:T(8,128)S(1)}, f32[2,128,128]{2,1,0:T(8,128)S(1)}, u32[]{:S(2)}, u32[]{:S(2)}) collective-permute-start(f32[2,128,128]{2,1,0:T(8,128)S(1)} %get-tuple-element.79), channel_id=1, source_target_pairs={{0,16},{1,17},{16,0},{17,1},{2,18},{3,19},{18,2},{19,3},{4,20},{5,... | collective-permute-start | bytes 393224 | tf_op jit(solution)/shard_map/ppermute | solution.py:492
  68.0 6.7 %collective-permute-start.20 = (f32[2,128,128]{2,1,0:T(8,128)S(1)}, f32[2,128,128]{2,1,0:T(8,128)S(1)}, u32[]{:S(2)}, u32[]{:S(2)}) collective-permute-start(f32[2,128,128]{2,1,0:T(8,128)S(1)} %get-tuple-element.80), channel_id=1, source_target_pairs={{0,1},{1,0},{16,17},{17,16},{2,3},{3,2},{18,19},{19,18},{4,5},{5,4... | collective-permute-start | bytes 393224 | tf_op jit(solution)/shard_map/ppermute | solution.py:492

commit v12 on v11

--- a/solution.py
+++ b/solution.py
@@ -235,12 +235,13 @@
 
 def fill_halo(spot_ref, field, own, even_ref, odd_ref):
     odd = spot_ref[5] == 1
+    inside = [1.0 - spot_ref[end].astype(jnp.float32) for end in range(2)]
     for c in range(field.columns):
         for y in range(field.halo):
             for x in range(0, field.cells, 8):
                 even, other = even_ref[c, y, pl.ds(x, 8), :], odd_ref[c, y, pl.ds(x, 8), :]
-                field.store(c, y - field.halo, x, jnp.where(odd, even, other))
-                field.store(c, own + y, x, jnp.where(odd, other, even))
+                field.store(c, y - field.halo, x, jnp.where(odd, even, other) * inside[0])
+                field.store(c, own + y, x, jnp.where(odd, other, even) * inside[1])
 
 
 def inner_kernel(
@@ -470,7 +471,7 @@
     mine = place % count
     assert ny & (ny - 1) == 0
     even = [(i, i ^ 1) for i in range(ny)]
-    odd = [(i, i + 1 if i % 2 else i - 1) for i in range(1, ny - 1)]
+    odd = [(i, min(max(i + 1 if i % 2 else i - 1, 0), ny - 1)) for i in range(ny)]
     swap = [(0, 1), (1, 0)]
 
     def edge(halo):

time: 75.7 us -> 75.7 us (level)
  no operation moved by 1% of the time
where the time goes in v12:
time: 75.7 us; the launch traced here: 75.5 us
  starting transfers between devices  27.8 us (37%)
  waiting for transfers between devices  24.1 us (32%)
  Pallas kernels  23.2 us (31%)
    ppermute x9, waiting for transfers between devices, to_chip(): return lax.ppermute(value, ('chip', 'gz'), pairs)  18.8 us
    ppermute x9, starting transfers between devices, to_chip(): return lax.ppermute(value, ('chip', 'gz'), pairs)  11.7 us
    pallas_call x8, Pallas kernels, plain(): pl.pallas_call(kernel, out_shape=out_shape, in_specs=specs, out_specs=(vm...  6.42 us
    ppermute x3, starting transfers between devices, body(): lax.ppermute(moments, 'gy', [(i, i ^ step) for i in range(ny)])  5.49 us
    ppermute x1, starting transfers between devices, body(): even2 = lax.ppermute(even_edge, 'gy', even)  4.81 us
    pallas_call x2, Pallas kernels, last_step(): pl.pallas_call(functools.partial(last_kernel, grid, inverse_count, flip),...  4.06 us
    pallas_call x1, Pallas kernels, body(): pl.pallas_call(functools.partial(inner_kernel, grid), out_shape=tuple((ve...  3.91 us
    ppermute x1, waiting for transfers between devices, body(): even1 = lax.ppermute(even_edge, 'gy', even)  3.42 us
  transfers between devices with their start and end apart: 21, of which 9 were waited for; matrix products, arithmetic and copies ran while one was open for 0% of the time, Pallas kernels for 20%

profile of v12, /device:TPU:0, one launch (start us, length us, event | category | flops | bytes accessed | tf_op | source)
XLA Modules:
  0.0 75.5 jit_solution(8545950945389751470)
XLA Ops:
  0.9 3.0 %collective-permute-start = (f32[2,128,128]{2,1,0:T(8,128)S(1)}, f32[2,128,128]{2,1,0:T(8,128)S(1)}, u32[]{:S(2)}, u32[]{:S(2)}) collective-permute-start(f32[2,128,128]{2,1,0:T(8,128)S(1)} %pack_kappa.1.after_ref.refs_0_), channel_id=1, source_target_pairs={{0,1},{1,0},{16,17},{17,16},{2,3},{3,2},{18,19},{19,18},{4,5},{5,4... | collective-permute-start | bytes 393224 | tf_op jit(solution)/shard_map/ppermute | solution.py:493
  5.6 1.9 %pack_probes.1 = (f32[2,2,128,128]{3,2,1,0:T(8,128)S(1)}, f32[2,2,128,128]{3,2,1,0:T(8,128)S(1)}, f32[2,2,128,128]{3,2,1,0:T(8,128)S(1)}, f32[2,2,128,128]{3,2,1,0:T(8,128)S(1)}) custom-call(s32[6]{0:T(128)S(1)} %stack.35.spot_ref, f32[2,128,128]{2,1,0:T(8,128)S(1)} %pack_kappa.1.after_ref.refs_0_, f32[1024,256]{1,0:T(8,128)} %bitcast.8), custom_call_target="tpu_custom_call" | custom-call | tf_op jit(solution)/shard_map/pack_probes/pallas_call | solution.py:496
  7.5 2.8 %collective-permute-done.1.refs_2_ = f32[2,128,128]{2,1,0:T(8,128)S(1)} collective-permute-done((f32[2,128,128]{2,1,0:T(8,128)S(1)}, f32[2,128,128]{2,1,0:T(8,128)S(1)}, u32[]{:S(2)}, u32[]{:S(2)}) %collective-permute-start.1) | collective-permute-done | bytes 131104 | tf_op jit(solution)/shard_map/ppermute | solution.py:493
  11.6 1.7 %collective-permute-start.6 = (f32[2,2,128,128]{3,2,1,0:T(8,128)S(1)}, f32[2,2,128,128]{3,2,1,0:T(8,128)S(1)}, u32[]{:S(2)}, u32[]{:S(2)}) collective-permute-start(f32[2,2,128,128]{3,2,1,0:T(8,128)S(1)} %get-tuple-element.46), channel_id=1, source_target_pairs={{0,1},{1,0},{16,17},{17,16},{2,3},{3,2},{18,19},{19,18},{4,5},{5,4... | collective-permute-start | bytes 786440 | tf_op jit(solution)/shard_map/ppermute | solution.py:493
  13.3 1.5 %collective-permute-start.7 = (f32[2,2,128,128]{3,2,1,0:T(8,128)S(1)}, f32[2,2,128,128]{3,2,1,0:T(8,128)S(1)}, u32[]{:S(2)}, u32[]{:S(2)}) collective-permute-start(f32[2,2,128,128]{3,2,1,0:T(8,128)S(1)} %get-tuple-element.47), channel_id=1, source_target_pairs={{0,16},{1,17},{16,0},{17,1},{2,18},{3,19},{18,2},{19,3},{4,20},{5,... | collective-permute-start | bytes 786440 | tf_op jit(solution)/shard_map/ppermute | solution.py:493
  16.1 1.8 %collective-permute-start.4 = (f32[4,4,32,128]{3,2,1,0:T(8,128)S(1)}, f32[4,4,32,128]{3,2,1,0:T(8,128)S(1)}, u32[]{:S(2)}, u32[]{:S(2)}) collective-permute-start(f32[4,4,32,128]{3,2,1,0:T(8,128)S(1)} %get-tuple-element.44), channel_id=1, source_target_pairs={{0,2},{2,0},{4,6},{6,4},{1,3},{3,1},{5,7},{7,5},{8,10},{10,8},{12,... | collective-permute-start | bytes 786440 | tf_op jit(solution)/shard_map/ppermute | solution.py:531
  18.6 1.8 %collective-permute-done.6.refs_1_ = f32[2,2,128,128]{3,2,1,0:T(8,128)S(1)} collective-permute-done((f32[2,2,128,128]{3,2,1,0:T(8,128)S(1)}, f32[2,2,128,128]{3,2,1,0:T(8,128)S(1)}, u32[]{:S(2)}, u32[]{:S(2)}) %collective-permute-start.6) | collective-permute-done | bytes 262176 | tf_op jit(solution)/shard_map/ppermute | solution.py:493
  20.3 2.2 %collective-permute-done.7.refs_2_ = f32[2,2,128,128]{3,2,1,0:T(8,128)S(1)} collective-permute-done((f32[2,2,128,128]{3,2,1,0:T(8,128)S(1)}, f32[2,2,128,128]{3,2,1,0:T(8,128)S(1)}, u32[]{:S(2)}, u32[]{:S(2)}) %collective-permute-start.7) | collective-permute-done | bytes 262176 | tf_op jit(solution)/shard_map/ppermute | solution.py:493
  22.5 4.6 %collective-permute-done.8.refs_3_ = f32[2,2,128,128]{3,2,1,0:T(8,128)S(1)} collective-permute-done((f32[2,2,128,128]{3,2,1,0:T(8,128)S(1)}, f32[2,2,128,128]{3,2,1,0:T(8,128)S(1)}, u32[]{:S(2)}, u32[]{:S(2)}) %collective-permute-start.8) | collective-permute-done | bytes 262176 | tf_op jit(solution)/shard_map/ppermute | solution.py:493
  27.8 1.9 %collective-permute-done.9.other_ref = f32[4,2,128,128]{3,2,1,0:T(8,128)S(1)} collective-permute-done((f32[4,2,128,128]{3,2,1,0:T(8,128)S(1)}, f32[4,2,128,128]{3,2,1,0:T(8,128)S(1)}, u32[]{:S(2)}, u32[]{:S(2)}) %collective-permute-start.9) | collective-permute-done | bytes 524320 | tf_op jit(solution)/shard_map/ppermute | solution.py:538
  30.5 1.8 %collective-permute-start.10 = (f32[4,5,32,128]{3,2,1,0:T(8,128)S(1)}, f32[4,5,32,128]{3,2,1,0:T(8,128)S(1)}, u32[]{:S(2)}, u32[]{:S(2)}) collective-permute-start(f32[4,5,32,128]{3,2,1,0:T(8,128)S(1)} %get-tuple-element.57), channel_id=1, source_target_pairs={{0,2},{2,0},{4,6},{6,4},{1,3},{3,1},{5,7},{7,5},{8,10},{10,8},{12,... | collective-permute-start | bytes 983048 | tf_op jit(solution)/shard_map/ppermute | solution.py:543
  33.0 3.9 %inner_steps.1 = (f32[4,26,48,128]{3,2,1,0:T(8,128)S(1)}, f32[4,24,48,128]{3,2,1,0:T(8,128)S(1)}, f32[4,22,48,128]{3,2,1,0:T(8,128)S(1)}, f32[4,20,48,128]{3,2,1,0:T(8,128)S(1)}, f32[4,26,48,128]{3,2,1,0:T(8,128)S(1)}) custom-call(s32[6]{0:T(128)S(1)} %stack.35.spot_ref, f32[4,2,128,128]{3,2,1,0:T(8,128)S(1)} %get-tuple-element.49.mine_ref, ...), custom_call_target="tpu_custom_call" | custom-call | flops 8388608 | bytes 4194304 | tf_op jit(solution)/shard_map/inner_steps/pallas_call | solution.py:553
  36.9 3.4 %collective-permute-done.10.even_ref = f32[4,5,32,128]{3,2,1,0:T(8,128)S(1)} collective-permute-done((f32[4,5,32,128]{3,2,1,0:T(8,128)S(1)}, f32[4,5,32,128]{3,2,1,0:T(8,128)S(1)}, u32[]{:S(2)}, u32[]{:S(2)}) %collective-permute-start.10) | collective-permute-done | bytes 327712 | tf_op jit(solution)/shard_map/ppermute | solution.py:543
  40.3 2.7 %first_steps.1 = (f32[4,26,48,128]{3,2,1,0:T(8,128)S(1)}, f32[4,24,48,128]{3,2,1,0:T(8,128)S(1)}, f32[4,24,48,128]{3,2,1,0:T(8,128)S(1)}, f32[4,22,48,128]{3,2,1...) custom-call(s32[6]{0:T(128)S(1)} %stack.35.spot_ref, ...), custom_call_target="tpu_custom_call", output_to_operand_aliasing={{0}: (1, {}), {1}: (2, {}), {2}: (3, {}), {3}: (4, {}), {4}... | custom-call | tf_op jit(solution)/shard_map/first_steps/pallas_call | solution.py:563
  43.0 4.8 %collective-permute-start.12 = (f32[4,5,32,128]{3,2,1,0:T(8,128)S(1)}, f32[4,5,32,128]{3,2,1,0:T(8,128)S(1)}, u32[]{:S(2)}, u32[]{:S(2)}) collective-permute-start(f32[4,5,32,128]{3,2,1,0:T(8,128)S(1)} %get-tuple-element.69), channel_id=1, source_target_pairs={{0,2},{2,0},{4,6},{6,4},{1,3},{3,1},{5,7},{7,5},{8,10},{10,8},{12,... | collective-permute-start | bytes 983048 | tf_op jit(solution)/shard_map/ppermute | solution.py:573
  50.0 3.1 %collective-permute-start.14 = (f32[8,128]{1,0:T(8,128)S(1)}, f32[8,128]{1,0:T(8,128)S(1)}, u32[]{:S(2)}, u32[]{:S(2)}) collective-permute-start(f32[8,128]{1,0:T(8,128)S(1)} %get-tuple-element.76.rest_0_), channel_id=1, source_target_pairs={{0,2},{2,0},{4,6},{6,4},{1,3},{3,1},{5,7},{7,5},{8,10},{10,8},{12,... | collective-permute-start | bytes 12296 | tf_op jit(solution)/shard_map/ppermute | solution.py:586
  53.2 2.2 %collective-permute-start.16 = (f32[8,128]{1,0:T(8,128)S(1)}, f32[8,128]{1,0:T(8,128)S(1)}, u32[]{:S(2)}, u32[]{:S(2)}) collective-permute-start(f32[8,128]{1,0:T(8,128)S(1)} %get-tuple-element.76.rest_0_), channel_id=1, source_target_pairs={{0,6},{2,4},{4,2},{6,0},{1,7},{3,5},{5,3},{7,1},{8,14},{10,12},{12... | collective-permute-start | bytes 12296 | tf_op jit(solution)/shard_map/ppermute | solution.py:586
  55.5 2.3 %second_inner_steps.1 = (f32[4,22,48,128]{3,2,1,0:T(8,128)S(1)}, f32[4,20,48,128]{3,2,1,0:T(8,128)S(1)}, f32[4,18,48,128]{3,2,1,0:T(8,128)S(1)}) custom-call(f32[4,24,48,128]{3,2,1,0:T(8,128)S(1)} %get-tuple-element.60.diagonal_ref, f32[4,26,48,128]{3,2,1,0:T(8,128)S(1)} %get-tuple-element.64.c2_ref.c2_in, f32[4,24,48,128]{3,2,1,0:T(8,128)S(1)} %get-tuple-element.65.d2_ref.d2_in), custom_call_target="tpu_custom_call" | custom-call | flops 7864320 | bytes 4194304 | tf_op jit(solution)/shard_map/second_inner_steps/pallas_call | solution.py:588
  57.8 2.4 %third_steps.1 = (f32[4,26,48,128]{3,2,1,0:T(8,128)S(1)}, f32[4,24,48,128]{3,2,1,0:T(8,128)S(1)}, f32[4,22,48,128]{3,2,1,0:T(8,128)S(1)}, f32[4,20,48,128]{3,2,1,0:T(8,128)S(1)}, f32[4,18,48,128]{3,2,1,0:T(8,128)S(1)}) custom-call(s32[6]{0:T(128)S(1)} %stack.35.spot_ref, ...), custom_call_target="tpu_custom_call", output_to_operand_aliasing={{0}: (2, {}), {1}: (3, {}), {2}: (4, {}), {3}: (5, {}), {4}... | custom-call | flops 5242880 | bytes 4194304 | tf_op jit(solution)/shard_map/third_steps/pallas_call | solution.py:598
  60.2 2.0 %last_step_given.1 = f32[4,2,128,128]{3,2,1,0:T(8,128)S(1)} custom-call(s32[6]{0:T(128)S(1)} %stack.35.spot_ref, f32[5,8]{1,0:T(8,128)S(1)} %copy-done, f32[4,26,48,128]{3,2,1,0:T(8,128)S(1)} %get-tuple-element.59.c0_ref, f32[4,24,48,128]{3,2,1,0:T(8,128)S(1)} %get-tuple-element.60.diagonal_ref, f32[4,24,48,128]{3,2,1,0:T(8,128)S(1)} %get-tuple-element.61.d0_ref, ...), custom_call_target="tpu_custom_call" | custom-call | flops 5242880 | bytes 4194304 | tf_op jit(solution)/shard_map/last_step_given/pallas_call | solution.py:614
  62.4 2.0 %last_step_kept.1.kept_ref = f32[4,2,128,128]{3,2,1,0:T(8,128)S(1)} custom-call(s32[6]{0:T(128)S(1)} %stack.35.spot_ref, f32[5,8]{1,0:T(8,128)S(1)} %copy-done, f32[4,26,48,128]{3,2,1,0:T(8,128)S(1)} %get-tuple-element.59.c0_ref, f32[4,24,48,128]{3,2,1,0:T(8,128)S(1)} %get-tuple-element.60.diagonal_ref, f32[4,24,48,128]{3,2,1,0:T(8,128)S(1)} %get-tuple-element.61.d0_ref, ...), custom_call_target="tpu_custom_call" | custom-call | flops 5242880 | bytes 4194304 | tf_op jit(solution)/shard_map/last_step_kept/pallas_call | solution.py:614
  65.0 2.5 %collective-permute-start.18 = (f32[2,128,128]{2,1,0:T(8,128)S(1)}, f32[2,128,128]{2,1,0:T(8,128)S(1)}, u32[]{:S(2)}, u32[]{:S(2)}) collective-permute-start(f32[2,128,128]{2,1,0:T(8,128)S(1)} %get-tuple-element.78), channel_id=1, source_target_pairs={{0,17},{1,16},{16,1},{17,0},{2,19},{3,18},{18,3},{19,2},{4,21},{5,... | collective-permute-start | bytes 393224 | tf_op jit(solution)/shard_map/ppermute | solution.py:493
  68.6 3.7 %collective-permute-done.18.refs_1_ = f32[2,128,128]{2,1,0:T(8,128)S(1)} collective-permute-done((f32[2,128,128]{2,1,0:T(8,128)S(1)}, f32[2,128,128]{2,1,0:T(8,128)S(1)}, u32[]{:S(2)}, u32[]{:S(2)}) %collective-permute-start.18) | collective-permute-done | bytes 131104 | tf_op jit(solution)/shard_map/ppermute | solution.py:493
  72.3 2.5 %collective-permute-done.19.refs_2_ = f32[2,128,128]{2,1,0:T(8,128)S(1)} collective-permute-done((f32[2,128,128]{2,1,0:T(8,128)S(1)}, f32[2,128,128]{2,1,0:T(8,128)S(1)}, u32[]{:S(2)}, u32[]{:S(2)}) %collective-permute-start.19) | collective-permute-done | bytes 131104 | tf_op jit(solution)/shard_map/ppermute | solution.py:493
  (36 shorter events, 12.6 us)
Async XLA Ops:
  0.9 6.6 %collective-permute-start = (f32[2,128,128]{2,1,0:T(8,128)S(1)}, f32[2,128,128]{2,1,0:T(8,128)S(1)}, u32[]{:S(2)}, u32[]{:S(2)}) collective-permute-start(f32[2,128,128]{2,1,0:T(8,128)S(1)} %pack_kappa.1.after_ref.refs_0_), channel_id=1, source_target_pairs={{0,1},{1,0},{16,17},{17,16},{2,3},{3,2},{18,19},{19,18},{4,5},{5,4... | collective-permute-start | bytes 393224 | tf_op jit(solution)/shard_map/ppermute | solution.py:493
  3.9 6.4 %collective-permute-start.1 = (f32[2,128,128]{2,1,0:T(8,128)S(1)}, f32[2,128,128]{2,1,0:T(8,128)S(1)}, u32[]{:S(2)}, u32[]{:S(2)}) collective-permute-start(f32[2,128,128]{2,1,0:T(8,128)S(1)} %pack_kappa.1.after_ref.refs_0_), channel_id=1, source_target_pairs={{0,16},{1,17},{16,0},{17,1},{2,18},{3,19},{18,2},{19,3},{4,20},{5,... | collective-permute-start | bytes 393224 | tf_op jit(solution)/shard_map/ppermute | solution.py:493
  5.4 6.1 %collective-permute-start.2 = (f32[2,128,128]{2,1,0:T(8,128)S(1)}, f32[2,128,128]{2,1,0:T(8,128)S(1)}, u32[]{:S(2)}, u32[]{:S(2)}) collective-permute-start(f32[2,128,128]{2,1,0:T(8,128)S(1)} %pack_kappa.1.after_ref.refs_0_), channel_id=1, source_target_pairs={{0,17},{1,16},{16,1},{17,0},{2,19},{3,18},{18,3},{19,2},{4,21},{5,... | collective-permute-start | bytes 393224 | tf_op jit(solution)/shard_map/ppermute | solution.py:493
  11.5 3.6 %collective-permute-start.3 = (f32[4,2,128,128]{3,2,1,0:T(8,128)S(1)}, f32[4,2,128,128]{3,2,1,0:T(8,128)S(1)}, u32[]{:S(2)}, u32[]{:S(2)}) collective-permute-start(f32[4,2,128,128]{3,2,1,0:T(8,128)S(1)} %stack_kappa.1.mine_ref), channel_id=1, source_target_pairs={{0,8},{8,0},{1,9},{9,1},{2,10},{10,2},{3,11},{11,3},{4,12},{12,4},... | collective-permute-start | bytes 1572872 | tf_op jit(solution)/shard_map/ppermute | solution.py:525
  11.6 8.7 %collective-permute-start.6 = (f32[2,2,128,128]{3,2,1,0:T(8,128)S(1)}, f32[2,2,128,128]{3,2,1,0:T(8,128)S(1)}, u32[]{:S(2)}, u32[]{:S(2)}) collective-permute-start(f32[2,2,128,128]{3,2,1,0:T(8,128)S(1)} %get-tuple-element.46), channel_id=1, source_target_pairs={{0,1},{1,0},{16,17},{17,16},{2,3},{3,2},{18,19},{19,18},{4,5},{5,4... | collective-permute-start | bytes 786440 | tf_op jit(solution)/shard_map/ppermute | solution.py:493
  13.3 9.2 %collective-permute-start.7 = (f32[2,2,128,128]{3,2,1,0:T(8,128)S(1)}, f32[2,2,128,128]{3,2,1,0:T(8,128)S(1)}, u32[]{:S(2)}, u32[]{:S(2)}) collective-permute-start(f32[2,2,128,128]{3,2,1,0:T(8,128)S(1)} %get-tuple-element.47), channel_id=1, source_target_pairs={{0,16},{1,17},{16,0},{17,1},{2,18},{3,19},{18,2},{19,3},{4,20},{5,... | collective-permute-start | bytes 786440 | tf_op jit(solution)/shard_map/ppermute | solution.py:493
  14.8 12.3 %collective-permute-start.8 = (f32[2,2,128,128]{3,2,1,0:T(8,128)S(1)}, f32[2,2,128,128]{3,2,1,0:T(8,128)S(1)}, u32[]{:S(2)}, u32[]{:S(2)}) collective-permute-start(f32[2,2,128,128]{3,2,1,0:T(8,128)S(1)} %get-tuple-element.48), channel_id=1, source_target_pairs={{0,17},{1,16},{16,1},{17,0},{2,19},{3,18},{18,3},{19,2},{4,21},{5,... | collective-permute-start | bytes 786440 | tf_op jit(solution)/shard_map/ppermute | solution.py:493
  16.1 11.0 %collective-permute-start.4 = (f32[4,4,32,128]{3,2,1,0:T(8,128)S(1)}, f32[4,4,32,128]{3,2,1,0:T(8,128)S(1)}, u32[]{:S(2)}, u32[]{:S(2)}) collective-permute-start(f32[4,4,32,128]{3,2,1,0:T(8,128)S(1)} %get-tuple-element.44), channel_id=1, source_target_pairs={{0,2},{2,0},{4,6},{6,4},{1,3},{3,1},{5,7},{7,5},{8,10},{10,8},{12,... | collective-permute-start | bytes 786440 | tf_op jit(solution)/shard_map/ppermute | solution.py:531
  17.9 9.2 %collective-permute-start.5 = (f32[4,4,32,128]{3,2,1,0:T(8,128)S(1)}, f32[4,4,32,128]{3,2,1,0:T(8,128)S(1)}, u32[]{:S(2)}, u32[]{:S(2)}) collective-permute-start(f32[4,4,32,128]{3,2,1,0:T(8,128)S(1)} %get-tuple-element.45), channel_id=1, source_target_pairs={{0,0},{2,4},{4,2},{6,6},{1,1},{3,5},{5,3},{7,7},{8,8},{10,12},{12,... | collective-permute-start | bytes 786440 | tf_op jit(solution)/shard_map/ppermute | solution.py:532
  27.8 2.0 %collective-permute-start.9 = (f32[4,2,128,128]{3,2,1,0:T(8,128)S(1)}, f32[4,2,128,128]{3,2,1,0:T(8,128)S(1)}, u32[]{:S(2)}, u32[]{:S(2)}) collective-permute-start(f32[4,2,128,128]{3,2,1,0:T(8,128)S(1)} %get-tuple-element.50), channel_id=1, source_target_pairs={{0,8},{8,0},{1,9},{9,1},{2,10},{10,2},{3,11},{11,3},{4,12},{12,4},... | collective-permute-start | bytes 1572872 | tf_op jit(solution)/shard_map/ppermute | solution.py:538
  30.5 9.8 %collective-permute-start.10 = (f32[4,5,32,128]{3,2,1,0:T(8,128)S(1)}, f32[4,5,32,128]{3,2,1,0:T(8,128)S(1)}, u32[]{:S(2)}, u32[]{:S(2)}) collective-permute-start(f32[4,5,32,128]{3,2,1,0:T(8,128)S(1)} %get-tuple-element.57), channel_id=1, source_target_pairs={{0,2},{2,0},{4,6},{6,4},{1,3},{3,1},{5,7},{7,5},{8,10},{10,8},{12,... | collective-permute-start | bytes 983048 | tf_op jit(solution)/shard_map/ppermute | solution.py:543
  32.3 8.0 %collective-permute-start.11 = (f32[4,5,32,128]{3,2,1,0:T(8,128)S(1)}, f32[4,5,32,128]{3,2,1,0:T(8,128)S(1)}, u32[]{:S(2)}, u32[]{:S(2)}) collective-permute-start(f32[4,5,32,128]{3,2,1,0:T(8,128)S(1)} %get-tuple-element.58), channel_id=1, source_target_pairs={{0,0},{2,4},{4,2},{6,6},{1,1},{3,5},{5,3},{7,7},{8,8},{10,12},{12,... | collective-permute-start | bytes 983048 | tf_op jit(solution)/shard_map/ppermute | solution.py:544
  43.0 14.8 %collective-permute-start.12 = (f32[4,5,32,128]{3,2,1,0:T(8,128)S(1)}, f32[4,5,32,128]{3,2,1,0:T(8,128)S(1)}, u32[]{:S(2)}, u32[]{:S(2)}) collective-permute-start(f32[4,5,32,128]{3,2,1,0:T(8,128)S(1)} %get-tuple-element.69), channel_id=1, source_target_pairs={{0,2},{2,0},{4,6},{6,4},{1,3},{3,1},{5,7},{7,5},{8,10},{10,8},{12,... | collective-permute-start | bytes 983048 | tf_op jit(solution)/shard_map/ppermute | solution.py:573
  47.8 10.0 %collective-permute-start.13 = (f32[4,5,32,128]{3,2,1,0:T(8,128)S(1)}, f32[4,5,32,128]{3,2,1,0:T(8,128)S(1)}, u32[]{:S(2)}, u32[]{:S(2)}) collective-permute-start(f32[4,5,32,128]{3,2,1,0:T(8,128)S(1)} %get-tuple-element.70), channel_id=1, source_target_pairs={{0,0},{2,4},{4,2},{6,6},{1,1},{3,5},{5,3},{7,7},{8,8},{10,12},{12,... | collective-permute-start | bytes 983048 | tf_op jit(solution)/shard_map/ppermute | solution.py:574
  50.0 10.2 %collective-permute-start.14 = (f32[8,128]{1,0:T(8,128)S(1)}, f32[8,128]{1,0:T(8,128)S(1)}, u32[]{:S(2)}, u32[]{:S(2)}) collective-permute-start(f32[8,128]{1,0:T(8,128)S(1)} %get-tuple-element.76.rest_0_), channel_id=1, source_target_pairs={{0,2},{2,0},{4,6},{6,4},{1,3},{3,1},{5,7},{7,5},{8,10},{10,8},{12,... | collective-permute-start | bytes 12296 | tf_op jit(solution)/shard_map/ppermute | solution.py:586
  53.0 7.2 %collective-permute-start.15 = (f32[8,128]{1,0:T(8,128)S(1)}, f32[8,128]{1,0:T(8,128)S(1)}, u32[]{:S(2)}, u32[]{:S(2)}) collective-permute-start(f32[8,128]{1,0:T(8,128)S(1)} %get-tuple-element.76.rest_0_), channel_id=1, source_target_pairs={{0,4},{2,6},{4,0},{6,2},{1,5},{3,7},{5,1},{7,3},{8,12},{10,14},{12... | collective-permute-start | bytes 12296 | tf_op jit(solution)/shard_map/ppermute | solution.py:586
  53.2 7.0 %collective-permute-start.16 = (f32[8,128]{1,0:T(8,128)S(1)}, f32[8,128]{1,0:T(8,128)S(1)}, u32[]{:S(2)}, u32[]{:S(2)}) collective-permute-start(f32[8,128]{1,0:T(8,128)S(1)} %get-tuple-element.76.rest_0_), channel_id=1, source_target_pairs={{0,6},{2,4},{4,2},{6,0},{1,7},{3,5},{5,3},{7,1},{8,14},{10,12},{12... | collective-permute-start | bytes 12296 | tf_op jit(solution)/shard_map/ppermute | solution.py:586
  57.8 2.4 %copy-start = (f32[5,8]{1,0:T(8,128)S(1)}, f32[5,8]{1,0:T(8,128)}, u32[]{:S(2)}) copy-start(f32[5,8]{1,0:T(8,128)} %weights_ref.3) | copy-start | bytes 484
  62.3 2.1 %collective-permute-start.17 = (f32[4,2,128,128]{3,2,1,0:T(8,128)S(1)}, f32[4,2,128,128]{3,2,1,0:T(8,128)S(1)}, u32[]{:S(2)}, u32[]{:S(2)}) collective-permute-start(f32[4,2,128,128]{3,2,1,0:T(8,128)S(1)} %last_step_given.1), channel_id=1, source_target_pairs={{0,8},{8,0},{1,9},{9,1},{2,10},{10,2},{3,11},{11,3},{4,12},{12,4},... | collective-permute-start | bytes 1572872 | tf_op jit(solution)/shard_map/ppermute | solution.py:624
  65.0 7.3 %collective-permute-start.18 = (f32[2,128,128]{2,1,0:T(8,128)S(1)}, f32[2,128,128]{2,1,0:T(8,128)S(1)}, u32[]{:S(2)}, u32[]{:S(2)}) collective-permute-start(f32[2,128,128]{2,1,0:T(8,128)S(1)} %get-tuple-element.78), channel_id=1, source_target_pairs={{0,17},{1,16},{16,1},{17,0},{2,19},{3,18},{18,3},{19,2},{4,21},{5,... | collective-permute-start | bytes 393224 | tf_op jit(solution)/shard_map/ppermute | solution.py:493
  67.5 7.3 %collective-permute-start.19 = (f32[2,128,128]{2,1,0:T(8,128)S(1)}, f32[2,128,128]{2,1,0:T(8,128)S(1)}, u32[]{:S(2)}, u32[]{:S(2)}) collective-permute-start(f32[2,128,128]{2,1,0:T(8,128)S(1)} %get-tuple-element.79), channel_id=1, source_target_pairs={{0,16},{1,17},{16,0},{17,1},{2,18},{3,19},{18,2},{19,3},{4,20},{5,... | collective-permute-start | bytes 393224 | tf_op jit(solution)/shard_map/ppermute | solution.py:493
  68.0 6.7 %collective-permute-start.20 = (f32[2,128,128]{2,1,0:T(8,128)S(1)}, f32[2,128,128]{2,1,0:T(8,128)S(1)}, u32[]{:S(2)}, u32[]{:S(2)}) collective-permute-start(f32[2,128,128]{2,1,0:T(8,128)S(1)} %get-tuple-element.80), channel_id=1, source_target_pairs={{0,1},{1,0},{16,17},{17,16},{2,3},{3,2},{18,19},{19,18},{4,5},{5,4... | collective-permute-start | bytes 393224 | tf_op jit(solution)/shard_map/ppermute | solution.py:493

commit v13 on v11

--- a/solution.py
+++ b/solution.py
@@ -209,38 +209,38 @@
         field.ref[z, y + field.halo, at, :] = value
 
 
-def store_edges(spot_ref, even_ref, odd_ref, x, z, first, last):
+def store_edges(spot_ref, one_ref, two_ref, x, z, first, last):
     at = pl.ds(pl.multiple_of(x, 8), 8)
-    odd = spot_ref[5] == 1
+    below_first = spot_ref[5] == 1
     for y, (below, above) in enumerate(zip(first, last)):
-        even_ref[z, y, at, :] = jnp.where(odd, below, above)
-        odd_ref[z, y, at, :] = jnp.where(odd, above, below)
-
-
-def edge_kernel(grid, spot_ref, mine_ref, other_ref, even_ref, odd_ref):
+        one_ref[z, y, at, :] = jnp.where(below_first, below, above)
+        two_ref[z, y, at, :] = jnp.where(below_first, above, below)
+
+
+def edge_kernel(grid, spot_ref, mine_ref, other_ref, one_ref, two_ref):
     by = grid[3]
     rows = list(range(HALO)) + list(range(by - HALO, by))
     for x, z, values in block_rows(grid, spot_ref, mine_ref, other_ref, rows):
-        store_edges(spot_ref, even_ref, odd_ref, x, z, values[:HALO], values[HALO:])
-
-
-def diagonal_kernel(grid, spot_ref, mine_ref, other_ref, own_ref, even_ref, odd_ref):
+        store_edges(spot_ref, one_ref, two_ref, x, z, values[:HALO], values[HALO:])
+
+
+def diagonal_kernel(grid, spot_ref, mine_ref, other_ref, own_ref, one_ref, two_ref):
     own = Field(own_ref, DIAGONAL_HALO)
     for x, z, values in block_rows(grid, spot_ref, mine_ref, other_ref, range(grid[3])):
         values = [6.0 + value for value in values]
         store_own(own, x, z, values)
         first, last = values[:DIAGONAL_HALO], values[-DIAGONAL_HALO:]
-        store_edges(spot_ref, even_ref, odd_ref, x, z, first, last)
-
-
-def fill_halo(spot_ref, field, own, even_ref, odd_ref):
-    odd = spot_ref[5] == 1
+        store_edges(spot_ref, one_ref, two_ref, x, z, first, last)
+
+
+def fill_halo(spot_ref, field, own, one_ref, two_ref):
+    below_first = spot_ref[5] == 1
     for c in range(field.columns):
         for y in range(field.halo):
             for x in range(0, field.cells, 8):
-                even, other = even_ref[c, y, pl.ds(x, 8), :], odd_ref[c, y, pl.ds(x, 8), :]
-                field.store(c, y - field.halo, x, jnp.where(odd, even, other))
-                field.store(c, own + y, x, jnp.where(odd, other, even))
+                one, two = one_ref[c, y, pl.ds(x, 8), :], two_ref[c, y, pl.ds(x, 8), :]
+                field.store(c, y - field.halo, x, jnp.where(below_first, one, two))
+                field.store(c, own + y, x, jnp.where(below_first, two, one))
 
 
 def inner_kernel(
@@ -266,8 +266,8 @@
 def first_kernel(
     own,
     spot_ref, c0_in, diagonal_in, d0_in, c1_in, d1_in, c2_in,
-    even_ref, odd_ref, even_diagonal_ref, odd_diagonal_ref,
-    c0_ref, diagonal_ref, d0_ref, c1_ref, d1_ref, c2_ref, even_out, odd_out,
+    one_ref, two_ref, one_diagonal_ref, two_diagonal_ref,
+    c0_ref, diagonal_ref, d0_ref, c1_ref, d1_ref, c2_ref, one_out, two_out,
 ):
     c0 = Field(c0_ref, HALO)
     diagonal = Field(diagonal_ref, DIAGONAL_HALO)
@@ -275,8 +275,8 @@
     c1 = Field(c1_ref, 3)
     d1 = Field(d1_ref, 2)
     c2 = Field(c2_ref, HALO)
-    fill_halo(spot_ref, c0, own, even_ref, odd_ref)
-    fill_halo(spot_ref, diagonal, own, even_diagonal_ref, odd_diagonal_ref)
+    fill_halo(spot_ref, c0, own, one_ref, two_ref)
+    fill_halo(spot_ref, diagonal, own, one_diagonal_ref, two_diagonal_ref)
     strips = functools.partial(apply_strips, spot_ref, own)
     strips(d0, c0, diagonal, 4, HALO)
     strips(c1, d0, diagonal, 3, HALO, c0)
@@ -286,7 +286,7 @@
         for x in range(0, c2.cells, 8):
             first = [c2.load(c, y, x) for y in range(HALO)]
             last = [c2.load(c, own - HALO + y, x) for y in range(HALO)]
-            store_edges(spot_ref, even_out, odd_out, x, c, first, last)
+            store_edges(spot_ref, one_out, two_out, x, c, first, last)
 
 
 def middle_kernel(own, c0_ref, c1_ref, c2_ref, diagonal_ref, d2_ref, moments_ref):
@@ -341,7 +341,7 @@
 
 def third_kernel(
     own,
-    spot_ref, diagonal_ref, c2_in, d2_in, c3_in, d3_in, c4_in, even_ref, odd_ref,
+    spot_ref, diagonal_ref, c2_in, d2_in, c3_in, d3_in, c4_in, one_ref, two_ref,
     c2_ref, d2_ref, c3_ref, d3_ref, c4_ref,
 ):
     diagonal = Field(diagonal_ref, DIAGONAL_HALO)
@@ -350,7 +350,7 @@
     c3 = Field(c3_ref, 3)
     d3 = Field(d3_ref, 2)
     c4 = Field(c4_ref, 1)
-    fill_halo(spot_ref, c2, own, even_ref, odd_ref)
+    fill_halo(spot_ref, c2, own, one_ref, two_ref)
     strips = functools.partial(apply_strips, spot_ref, own)
     strips(d2, c2, diagonal, 4, 4)
     strips(c3, d2, diagonal, 3, 4, c2)
@@ -471,6 +471,11 @@
     assert ny & (ny - 1) == 0
     even = [(i, i ^ 1) for i in range(ny)]
     odd = [(i, i + 1 if i % 2 else i - 1) for i in range(1, ny - 1)]
+
+    def both_cores(first, second):
+        return first + [(ny + i, ny + j) for i, j in second]
+
+    first_pairs, second_pairs = both_cores(even, odd), both_cores(odd, even)
     swap = [(0, 1), (1, 0)]
 
     def edge(halo):
@@ -485,7 +490,7 @@
     chips = nx // 2 * nz
     assert chips & (chips - 1) == 0
     chip = lax.axis_index("chip") * nz + lax.axis_index("gz")
-    spot = jnp.stack([gy == 0, gy == ny - 1, mine, core, chip, gy % 2]).astype(jnp.int32)
+    spot = jnp.stack([gy == 0, gy == ny - 1, mine, core, chip, (gy + core) % 2]).astype(jnp.int32)
 
     def to_chip(value, k):
         pairs = [(i, i ^ k) for i in range(chips)]
@@ -522,25 +527,25 @@
         [vmem()] * (chips + 1), packed[0], *kappas,
     )
     other = lax.ppermute(kappa, "core", swap)
-    diagonal, even_edge, odd_edge = plain(
+    diagonal, one_edge, two_edge = plain(
         functools.partial(diagonal_kernel, grid), "diagonal_rows",
         (vector(DIAGONAL_HALO), edge(DIAGONAL_HALO), edge(DIAGONAL_HALO)),
         [smem(), vmem(), vmem()], spot, kappa, other,
     )
-    even_diagonal = lax.ppermute(even_edge, "gy", even)
-    odd_diagonal = lax.ppermute(odd_edge, "gy", odd)
+    one_diagonal = lax.ppermute(one_edge, ("core", "gy"), first_pairs)
+    two_diagonal = lax.ppermute(two_edge, ("core", "gy"), second_pairs)
 
     probe, give = plain(
         sort_probes_kernel, "sort_probes", (stacked, stacked),
-        [smem()] + [vmem()] * (chips + 2), spot, even_diagonal, odd_diagonal, *probes,
+        [smem()] + [vmem()] * (chips + 2), spot, one_diagonal, two_diagonal, *probes,
     )
     other = lax.ppermute(give, "core", swap)
-    even_edge, odd_edge = plain(
+    one_edge, two_edge = plain(
         functools.partial(edge_kernel, grid), "probe_edges", (edge(HALO), edge(HALO)),
         [smem(), vmem(), vmem()], spot, probe, other,
     )
-    even1 = lax.ppermute(even_edge, "gy", even)
-    odd1 = lax.ppermute(odd_edge, "gy", odd)
+    one1 = lax.ppermute(one_edge, ("core", "gy"), first_pairs)
+    two1 = lax.ppermute(two_edge, ("core", "gy"), second_pairs)
 
     cells = by * X * columns * 128
 
@@ -559,7 +564,7 @@
         name="inner_steps",
     )(spot, probe, other, here(diagonal))
     vectors = [here(value) for value in (inner[0], diagonal) + tuple(inner[1:])]
-    c0, diagonal, d0, c1, d1, c2, even_edge, odd_edge = pl.pallas_call(
+    c0, diagonal, d0, c1, d1, c2, one_edge, two_edge = pl.pallas_call(
         functools.partial(first_kernel, by),
         out_shape=tuple(vector(h) for h in (HALO, DIAGONAL_HALO, 4, 3, 2, HALO))
         + (edge(HALO), edge(HALO)),
@@ -568,9 +573,9 @@
         input_output_aliases={i + 1: i for i in range(6)},
         compiler_params=params(),
         name="first_steps",
-    )(spot, *vectors, even1, odd1, even_diagonal, odd_diagonal)
-    even2 = lax.ppermute(even_edge, "gy", even)
-    odd2 = lax.ppermute(odd_edge, "gy", odd)
+    )(spot, *vectors, one1, two1, one_diagonal, two_diagonal)
+    one2 = lax.ppermute(one_edge, ("core", "gy"), first_pairs)
+    two2 = lax.ppermute(two_edge, ("core", "gy"), second_pairs)
     d2, moments = pl.pallas_call(
         functools.partial(middle_kernel, by),
         out_shape=(vector(4), f32(8, 128)),
@@ -603,7 +608,7 @@
         compiler_params=params(),
         cost_estimate=cost(20),
         name="third_steps",
-    )(spot, *vectors, even2, odd2)
+    )(spot, *vectors, one2, two2)
     inverse_count = 1.0 / (ny * cells)
     vectors = [here(value) for value in (c0, diagonal, d0, c1, d1, c2, d2, c3, d3, c4)]
     if group > count:

time: 75.7 us -> 78.2 us (1.033)
  starting transfers between devices: 27.8 us -> 34.8 us
  waiting for transfers between devices: 24.1 us -> 19.5 us
    ppermute x6, starting transfers between devices: 10.4 us -> 16.1 us  [the longest x1 6.53 us: body(): one2 = lax.ppermute(one_edge, ('core', 'gy'), first_pairs)]
    ppermute x6, waiting for transfers between devices: 3.44 us -> 0.79 us  [the longest x1 0.78 us: body(): one1 = lax.ppermute(one_edge, ('core', 'gy'), first_pairs)]
    ppermute x9, waiting for transfers between devices: 18.8 us -> 16.9 us  [to_chip(): return lax.ppermute(value, ('chip', 'gz'), pairs)]
    ppermute x3, starting transfers between devices: 5.49 us -> 6.7 us  [body(): lax.ppermute(moments, 'gy', [(i, i ^ step) for i in range(ny)])]
  transfers between devices with their start and end apart: 21 -> 21, of which waited for: 9 -> 8; matrix products, arithmetic and copies ran while one was open for 0% -> 0% of each run, Pallas kernels for 20% -> 19%
where the time goes in v13:
time: 78.2 us; the launch traced here: 77.9 us
  starting transfers between devices  34.8 us (45%)
  Pallas kernels  23.2 us (30%)
  waiting for transfers between devices  19.5 us (25%)
    ppermute x9, waiting for transfers between devices, to_chip(): return lax.ppermute(value, ('chip', 'gz'), pairs)  16.9 us
    ppermute x9, starting transfers between devices, to_chip(): return lax.ppermute(value, ('chip', 'gz'), pairs)  11.7 us
    ppermute x3, starting transfers between devices, body(): lax.ppermute(moments, 'gy', [(i, i ^ step) for i in range(ny)])  6.7 us
    ppermute x1, starting transfers between devices, body(): one2 = lax.ppermute(one_edge, ('core', 'gy'), first_pairs)  6.53 us
    pallas_call x8, Pallas kernels, plain(): pl.pallas_call(kernel, out_shape=out_shape, in_specs=specs, out_specs=(vm...  6.42 us
    pallas_call x2, Pallas kernels, last_step(): pl.pallas_call(functools.partial(last_kernel, grid, inverse_count, flip),...  4.06 us
    ppermute x1, starting transfers between devices, body(): one1 = lax.ppermute(one_edge, ('core', 'gy'), first_pairs)  3.92 us
    pallas_call x1, Pallas kernels, body(): pl.pallas_call(functools.partial(inner_kernel, grid), out_shape=tuple((ve...  3.91 us
  transfers between devices with their start and end apart: 21, of which 8 were waited for; matrix products, arithmetic and copies ran while one was open for 0% of the time, Pallas kernels for 19%

profile of v13, /device:TPU:0, one launch (start us, length us, event | category | flops | bytes accessed | tf_op | source)
XLA Modules:
  0.0 77.9 jit_solution(11521936460346338414)
XLA Ops:
  0.9 3.0 %collective-permute-start = (f32[2,128,128]{2,1,0:T(8,128)S(1)}, f32[2,128,128]{2,1,0:T(8,128)S(1)}, u32[]{:S(2)}, u32[]{:S(2)}) collective-permute-start(f32[2,128,128]{2,1,0:T(8,128)S(1)} %pack_kappa.1.after_ref.refs_0_), channel_id=1, source_target_pairs={{0,1},{1,0},{16,17},{17,16},{2,3},{3,2},{18,19},{19,18},{4,5},{5,4... | collective-permute-start | bytes 393224 | tf_op jit(solution)/shard_map/ppermute | solution.py:497
  3.9 1.5 %collective-permute-start.1 = (f32[2,128,128]{2,1,0:T(8,128)S(1)}, f32[2,128,128]{2,1,0:T(8,128)S(1)}, u32[]{:S(2)}, u32[]{:S(2)}) collective-permute-start(f32[2,128,128]{2,1,0:T(8,128)S(1)} %pack_kappa.1.after_ref.refs_0_), channel_id=1, source_target_pairs={{0,16},{1,17},{16,0},{17,1},{2,18},{3,19},{18,2},{19,3},{4,20},{5,... | collective-permute-start | bytes 393224 | tf_op jit(solution)/shard_map/ppermute | solution.py:497
  5.6 1.9 %pack_probes.1 = (f32[2,2,128,128]{3,2,1,0:T(8,128)S(1)}, f32[2,2,128,128]{3,2,1,0:T(8,128)S(1)}, f32[2,2,128,128]{3,2,1,0:T(8,128)S(1)}, f32[2,2,128,128]{3,2,1,0:T(8,128)S(1)}) custom-call(s32[6]{0:T(128)S(1)} %stack.35.spot_ref, f32[2,128,128]{2,1,0:T(8,128)S(1)} %pack_kappa.1.after_ref.refs_0_, f32[1024,256]{1,0:T(8,128)} %bitcast.8), custom_call_target="tpu_custom_call" | custom-call | tf_op jit(solution)/shard_map/pack_probes/pallas_call | solution.py:500
  7.5 2.8 %collective-permute-done.1.refs_2_ = f32[2,128,128]{2,1,0:T(8,128)S(1)} collective-permute-done((f32[2,128,128]{2,1,0:T(8,128)S(1)}, f32[2,128,128]{2,1,0:T(8,128)S(1)}, u32[]{:S(2)}, u32[]{:S(2)}) %collective-permute-start.1) | collective-permute-done | bytes 131104 | tf_op jit(solution)/shard_map/ppermute | solution.py:497
  11.6 1.7 %collective-permute-start.6 = (f32[2,2,128,128]{3,2,1,0:T(8,128)S(1)}, f32[2,2,128,128]{3,2,1,0:T(8,128)S(1)}, u32[]{:S(2)}, u32[]{:S(2)}) collective-permute-start(f32[2,2,128,128]{3,2,1,0:T(8,128)S(1)} %get-tuple-element.46), channel_id=1, source_target_pairs={{0,1},{1,0},{16,17},{17,16},{2,3},{3,2},{18,19},{19,18},{4,5},{5,4... | collective-permute-start | bytes 786440 | tf_op jit(solution)/shard_map/ppermute | solution.py:497
  13.3 1.5 %collective-permute-start.7 = (f32[2,2,128,128]{3,2,1,0:T(8,128)S(1)}, f32[2,2,128,128]{3,2,1,0:T(8,128)S(1)}, u32[]{:S(2)}, u32[]{:S(2)}) collective-permute-start(f32[2,2,128,128]{3,2,1,0:T(8,128)S(1)} %get-tuple-element.47), channel_id=1, source_target_pairs={{0,16},{1,17},{16,0},{17,1},{2,18},{3,19},{18,2},{19,3},{4,20},{5,... | collective-permute-start | bytes 786440 | tf_op jit(solution)/shard_map/ppermute | solution.py:497
  16.1 3.6 %collective-permute-start.4 = (f32[4,4,32,128]{3,2,1,0:T(8,128)S(1)}, f32[4,4,32,128]{3,2,1,0:T(8,128)S(1)}, u32[]{:S(2)}, u32[]{:S(2)}) collective-permute-start(f32[4,4,32,128]{3,2,1,0:T(8,128)S(1)} %get-tuple-element.44), channel_id=1, source_target_pairs={{0,2},{2,0},{4,6},{6,4},{10,12},{12,10},{1,3},{3,1},{5,7},{7,5},{1... | collective-permute-start | bytes 786440 | tf_op jit(solution)/shard_map/ppermute | solution.py:535
  20.4 2.0 %collective-permute-done.7.refs_2_ = f32[2,2,128,128]{3,2,1,0:T(8,128)S(1)} collective-permute-done((f32[2,2,128,128]{3,2,1,0:T(8,128)S(1)}, f32[2,2,128,128]{3,2,1,0:T(8,128)S(1)}, u32[]{:S(2)}, u32[]{:S(2)}) %collective-permute-start.7) | collective-permute-done | bytes 262176 | tf_op jit(solution)/shard_map/ppermute | solution.py:497
  22.5 4.6 %collective-permute-done.8.refs_3_ = f32[2,2,128,128]{3,2,1,0:T(8,128)S(1)} collective-permute-done((f32[2,2,128,128]{3,2,1,0:T(8,128)S(1)}, f32[2,2,128,128]{3,2,1,0:T(8,128)S(1)}, u32[]{:S(2)}, u32[]{:S(2)}) %collective-permute-start.8) | collective-permute-done | bytes 262176 | tf_op jit(solution)/shard_map/ppermute | solution.py:497
  27.9 1.8 %collective-permute-done.9.other_ref = f32[4,2,128,128]{3,2,1,0:T(8,128)S(1)} collective-permute-done((f32[4,2,128,128]{3,2,1,0:T(8,128)S(1)}, f32[4,2,128,128]{3,2,1,0:T(8,128)S(1)}, u32[]{:S(2)}, u32[]{:S(2)}) %collective-permute-start.9) | collective-permute-done | bytes 524320 | tf_op jit(solution)/shard_map/ppermute | solution.py:542
  30.5 3.9 %collective-permute-start.10 = (f32[4,5,32,128]{3,2,1,0:T(8,128)S(1)}, f32[4,5,32,128]{3,2,1,0:T(8,128)S(1)}, u32[]{:S(2)}, u32[]{:S(2)}) collective-permute-start(f32[4,5,32,128]{3,2,1,0:T(8,128)S(1)} %get-tuple-element.57), channel_id=1, source_target_pairs={{0,2},{2,0},{4,6},{6,4},{10,12},{12,10},{1,3},{3,1},{5,7},{7,5},{1... | collective-permute-start | bytes 983048 | tf_op jit(solution)/shard_map/ppermute | solution.py:547
  35.1 3.9 %inner_steps.1 = (f32[4,26,48,128]{3,2,1,0:T(8,128)S(1)}, f32[4,24,48,128]{3,2,1,0:T(8,128)S(1)}, f32[4,22,48,128]{3,2,1,0:T(8,128)S(1)}, f32[4,20,48,128]{3,2,1,0:T(8,128)S(1)}, f32[4,26,48,128]{3,2,1,0:T(8,128)S(1)}) custom-call(s32[6]{0:T(128)S(1)} %stack.35.spot_ref, f32[4,2,128,128]{3,2,1,0:T(8,128)S(1)} %get-tuple-element.49.mine_ref, ...), custom_call_target="tpu_custom_call" | custom-call | flops 8388608 | bytes 4194304 | tf_op jit(solution)/shard_map/inner_steps/pallas_call | solution.py:557
  39.8 2.7 %first_steps.1 = (f32[4,26,48,128]{3,2,1,0:T(8,128)S(1)}, f32[4,24,48,128]{3,2,1,0:T(8,128)S(1)}, f32[4,24,48,128]{3,2,1,0:T(8,128)S(1)}, f32[4,22,48,128]{3,2,1...) custom-call(s32[6]{0:T(128)S(1)} %stack.35.spot_ref, ...), custom_call_target="tpu_custom_call", output_to_operand_aliasing={{0}: (1, {}), {1}: (2, {}), {2}: (3, {}), {3}: (4, {}), {4}... | custom-call | tf_op jit(solution)/shard_map/first_steps/pallas_call | solution.py:567
  42.5 6.5 %collective-permute-start.12 = (f32[4,5,32,128]{3,2,1,0:T(8,128)S(1)}, f32[4,5,32,128]{3,2,1,0:T(8,128)S(1)}, u32[]{:S(2)}, u32[]{:S(2)}) collective-permute-start(f32[4,5,32,128]{3,2,1,0:T(8,128)S(1)} %get-tuple-element.69), channel_id=1, source_target_pairs={{0,2},{2,0},{4,6},{6,4},{10,12},{12,10},{1,3},{3,1},{5,7},{7,5},{1... | collective-permute-start | bytes 983048 | tf_op jit(solution)/shard_map/ppermute | solution.py:577
  49.7 1.5 %middle_step.1 = (f32[4,24,48,128]{3,2,1,0:T(8,128)S(1)}, f32[8,128]{1,0:T(8,128)S(1)}) custom-call(f32[4,26,48,128]{3,2,1,0:T(8,128)S(1)} %get-tuple-element.59.c0_ref, f32[4,22,48,128]{3,2,1,0:T(8,128)S(1)} %get-tuple-element.62.c1_ref, f32[4,26,48,128]{3,2,1,0:T(8,128)S(1)} %get-tuple-element.64.c2_ref.c2_in, ...), custom_call_target="tpu_custom_call" | custom-call | flops 6291456 | bytes 4194304 | tf_op jit(solution)/shard_map/middle_step/pallas_call | solution.py:579
  51.2 4.3 %collective-permute-start.14 = (f32[8,128]{1,0:T(8,128)S(1)}, f32[8,128]{1,0:T(8,128)S(1)}, u32[]{:S(2)}, u32[]{:S(2)}) collective-permute-start(f32[8,128]{1,0:T(8,128)S(1)} %get-tuple-element.76.rest_0_), channel_id=1, source_target_pairs={{0,2},{2,0},{4,6},{6,4},{1,3},{3,1},{5,7},{7,5},{8,10},{10,8},{12,... | collective-permute-start | bytes 12296 | tf_op jit(solution)/shard_map/ppermute | solution.py:590
  55.4 2.4 %collective-permute-start.16 = (f32[8,128]{1,0:T(8,128)S(1)}, f32[8,128]{1,0:T(8,128)S(1)}, u32[]{:S(2)}, u32[]{:S(2)}) collective-permute-start(f32[8,128]{1,0:T(8,128)S(1)} %get-tuple-element.76.rest_0_), channel_id=1, source_target_pairs={{0,6},{2,4},{4,2},{6,0},{1,7},{3,5},{5,3},{7,1},{8,14},{10,12},{12... | collective-permute-start | bytes 12296 | tf_op jit(solution)/shard_map/ppermute | solution.py:590
  57.9 2.3 %second_inner_steps.1 = (f32[4,22,48,128]{3,2,1,0:T(8,128)S(1)}, f32[4,20,48,128]{3,2,1,0:T(8,128)S(1)}, f32[4,18,48,128]{3,2,1,0:T(8,128)S(1)}) custom-call(f32[4,24,48,128]{3,2,1,0:T(8,128)S(1)} %get-tuple-element.60.diagonal_ref, f32[4,26,48,128]{3,2,1,0:T(8,128)S(1)} %get-tuple-element.64.c2_ref.c2_in, f32[4,24,48,128]{3,2,1,0:T(8,128)S(1)} %get-tuple-element.65.d2_ref.d2_in), custom_call_target="tpu_custom_call" | custom-call | flops 7864320 | bytes 4194304 | tf_op jit(solution)/shard_map/second_inner_steps/pallas_call | solution.py:592
  60.2 2.4 %third_steps.1 = (f32[4,26,48,128]{3,2,1,0:T(8,128)S(1)}, f32[4,24,48,128]{3,2,1,0:T(8,128)S(1)}, f32[4,22,48,128]{3,2,1,0:T(8,128)S(1)}, f32[4,20,48,128]{3,2,1,0:T(8,128)S(1)}, f32[4,18,48,128]{3,2,1,0:T(8,128)S(1)}) custom-call(s32[6]{0:T(128)S(1)} %stack.35.spot_ref, ...), custom_call_target="tpu_custom_call", output_to_operand_aliasing={{0}: (2, {}), {1}: (3, {}), {2}: (4, {}), {3}: (5, {}), {4}... | custom-call | flops 5242880 | bytes 4194304 | tf_op jit(solution)/shard_map/third_steps/pallas_call | solution.py:602
  62.6 2.0 %last_step_given.1 = f32[4,2,128,128]{3,2,1,0:T(8,128)S(1)} custom-call(s32[6]{0:T(128)S(1)} %stack.35.spot_ref, f32[5,8]{1,0:T(8,128)S(1)} %copy-done, f32[4,26,48,128]{3,2,1,0:T(8,128)S(1)} %get-tuple-element.59.c0_ref, f32[4,24,48,128]{3,2,1,0:T(8,128)S(1)} %get-tuple-element.60.diagonal_ref, f32[4,24,48,128]{3,2,1,0:T(8,128)S(1)} %get-tuple-element.61.d0_ref, ...), custom_call_target="tpu_custom_call" | custom-call | flops 5242880 | bytes 4194304 | tf_op jit(solution)/shard_map/last_step_given/pallas_call | solution.py:618
  64.8 2.0 %last_step_kept.1.kept_ref = f32[4,2,128,128]{3,2,1,0:T(8,128)S(1)} custom-call(s32[6]{0:T(128)S(1)} %stack.35.spot_ref, f32[5,8]{1,0:T(8,128)S(1)} %copy-done, f32[4,26,48,128]{3,2,1,0:T(8,128)S(1)} %get-tuple-element.59.c0_ref, f32[4,24,48,128]{3,2,1,0:T(8,128)S(1)} %get-tuple-element.60.diagonal_ref, f32[4,24,48,128]{3,2,1,0:T(8,128)S(1)} %get-tuple-element.61.d0_ref, ...), custom_call_target="tpu_custom_call" | custom-call | flops 5242880 | bytes 4194304 | tf_op jit(solution)/shard_map/last_step_kept/pallas_call | solution.py:618
  67.4 2.5 %collective-permute-start.18 = (f32[2,128,128]{2,1,0:T(8,128)S(1)}, f32[2,128,128]{2,1,0:T(8,128)S(1)}, u32[]{:S(2)}, u32[]{:S(2)}) collective-permute-start(f32[2,128,128]{2,1,0:T(8,128)S(1)} %get-tuple-element.78), channel_id=1, source_target_pairs={{0,17},{1,16},{16,1},{17,0},{2,19},{3,18},{18,3},{19,2},{4,21},{5,... | collective-permute-start | bytes 393224 | tf_op jit(solution)/shard_map/ppermute | solution.py:497
  71.0 3.7 %collective-permute-done.18.refs_1_ = f32[2,128,128]{2,1,0:T(8,128)S(1)} collective-permute-done((f32[2,128,128]{2,1,0:T(8,128)S(1)}, f32[2,128,128]{2,1,0:T(8,128)S(1)}, u32[]{:S(2)}, u32[]{:S(2)}) %collective-permute-start.18) | collective-permute-done | bytes 131104 | tf_op jit(solution)/shard_map/ppermute | solution.py:497
  74.7 2.5 %collective-permute-done.19.refs_2_ = f32[2,128,128]{2,1,0:T(8,128)S(1)} collective-permute-done((f32[2,128,128]{2,1,0:T(8,128)S(1)}, f32[2,128,128]{2,1,0:T(8,128)S(1)}, u32[]{:S(2)}, u32[]{:S(2)}) %collective-permute-start.19) | collective-permute-done | bytes 131104 | tf_op jit(solution)/shard_map/ppermute | solution.py:497
  (36 shorter events, 10.4 us)
Async XLA Ops:
  0.9 6.6 %collective-permute-start = (f32[2,128,128]{2,1,0:T(8,128)S(1)}, f32[2,128,128]{2,1,0:T(8,128)S(1)}, u32[]{:S(2)}, u32[]{:S(2)}) collective-permute-start(f32[2,128,128]{2,1,0:T(8,128)S(1)} %pack_kappa.1.after_ref.refs_0_), channel_id=1, source_target_pairs={{0,1},{1,0},{16,17},{17,16},{2,3},{3,2},{18,19},{19,18},{4,5},{5,4... | collective-permute-start | bytes 393224 | tf_op jit(solution)/shard_map/ppermute | solution.py:497
  3.9 6.4 %collective-permute-start.1 = (f32[2,128,128]{2,1,0:T(8,128)S(1)}, f32[2,128,128]{2,1,0:T(8,128)S(1)}, u32[]{:S(2)}, u32[]{:S(2)}) collective-permute-start(f32[2,128,128]{2,1,0:T(8,128)S(1)} %pack_kappa.1.after_ref.refs_0_), channel_id=1, source_target_pairs={{0,16},{1,17},{16,0},{17,1},{2,18},{3,19},{18,2},{19,3},{4,20},{5,... | collective-permute-start | bytes 393224 | tf_op jit(solution)/shard_map/ppermute | solution.py:497
  5.4 6.1 %collective-permute-start.2 = (f32[2,128,128]{2,1,0:T(8,128)S(1)}, f32[2,128,128]{2,1,0:T(8,128)S(1)}, u32[]{:S(2)}, u32[]{:S(2)}) collective-permute-start(f32[2,128,128]{2,1,0:T(8,128)S(1)} %pack_kappa.1.after_ref.refs_0_), channel_id=1, source_target_pairs={{0,17},{1,16},{16,1},{17,0},{2,19},{3,18},{18,3},{19,2},{4,21},{5,... | collective-permute-start | bytes 393224 | tf_op jit(solution)/shard_map/ppermute | solution.py:497
  11.5 3.6 %collective-permute-start.3 = (f32[4,2,128,128]{3,2,1,0:T(8,128)S(1)}, f32[4,2,128,128]{3,2,1,0:T(8,128)S(1)}, u32[]{:S(2)}, u32[]{:S(2)}) collective-permute-start(f32[4,2,128,128]{3,2,1,0:T(8,128)S(1)} %stack_kappa.1.mine_ref), channel_id=1, source_target_pairs={{0,8},{8,0},{1,9},{9,1},{2,10},{10,2},{3,11},{11,3},{4,12},{12,4},... | collective-permute-start | bytes 1572872 | tf_op jit(solution)/shard_map/ppermute | solution.py:529
  11.6 8.8 %collective-permute-start.6 = (f32[2,2,128,128]{3,2,1,0:T(8,128)S(1)}, f32[2,2,128,128]{3,2,1,0:T(8,128)S(1)}, u32[]{:S(2)}, u32[]{:S(2)}) collective-permute-start(f32[2,2,128,128]{3,2,1,0:T(8,128)S(1)} %get-tuple-element.46), channel_id=1, source_target_pairs={{0,1},{1,0},{16,17},{17,16},{2,3},{3,2},{18,19},{19,18},{4,5},{5,4... | collective-permute-start | bytes 786440 | tf_op jit(solution)/shard_map/ppermute | solution.py:497
  13.3 9.2 %collective-permute-start.7 = (f32[2,2,128,128]{3,2,1,0:T(8,128)S(1)}, f32[2,2,128,128]{3,2,1,0:T(8,128)S(1)}, u32[]{:S(2)}, u32[]{:S(2)}) collective-permute-start(f32[2,2,128,128]{3,2,1,0:T(8,128)S(1)} %get-tuple-element.47), channel_id=1, source_target_pairs={{0,16},{1,17},{16,0},{17,1},{2,18},{3,19},{18,2},{19,3},{4,20},{5,... | collective-permute-start | bytes 786440 | tf_op jit(solution)/shard_map/ppermute | solution.py:497
  14.8 12.3 %collective-permute-start.8 = (f32[2,2,128,128]{3,2,1,0:T(8,128)S(1)}, f32[2,2,128,128]{3,2,1,0:T(8,128)S(1)}, u32[]{:S(2)}, u32[]{:S(2)}) collective-permute-start(f32[2,2,128,128]{3,2,1,0:T(8,128)S(1)} %get-tuple-element.48), channel_id=1, source_target_pairs={{0,17},{1,16},{16,1},{17,0},{2,19},{3,18},{18,3},{19,2},{4,21},{5,... | collective-permute-start | bytes 786440 | tf_op jit(solution)/shard_map/ppermute | solution.py:497
  16.1 11.0 %collective-permute-start.4 = (f32[4,4,32,128]{3,2,1,0:T(8,128)S(1)}, f32[4,4,32,128]{3,2,1,0:T(8,128)S(1)}, u32[]{:S(2)}, u32[]{:S(2)}) collective-permute-start(f32[4,4,32,128]{3,2,1,0:T(8,128)S(1)} %get-tuple-element.44), channel_id=1, source_target_pairs={{0,2},{2,0},{4,6},{6,4},{10,12},{12,10},{1,3},{3,1},{5,7},{7,5},{1... | collective-permute-start | bytes 786440 | tf_op jit(solution)/shard_map/ppermute | solution.py:535
  19.7 7.4 %collective-permute-start.5 = (f32[4,4,32,128]{3,2,1,0:T(8,128)S(1)}, f32[4,4,32,128]{3,2,1,0:T(8,128)S(1)}, u32[]{:S(2)}, u32[]{:S(2)}) collective-permute-start(f32[4,4,32,128]{3,2,1,0:T(8,128)S(1)} %get-tuple-element.45), channel_id=1, source_target_pairs={{2,4},{4,2},{8,10},{10,8},{12,14},{14,12},{3,5},{5,3},{9,11},{11,9... | collective-permute-start | bytes 786440 | tf_op jit(solution)/shard_map/ppermute | solution.py:536
  27.8 2.0 %collective-permute-start.9 = (f32[4,2,128,128]{3,2,1,0:T(8,128)S(1)}, f32[4,2,128,128]{3,2,1,0:T(8,128)S(1)}, u32[]{:S(2)}, u32[]{:S(2)}) collective-permute-start(f32[4,2,128,128]{3,2,1,0:T(8,128)S(1)} %get-tuple-element.50), channel_id=1, source_target_pairs={{0,8},{8,0},{1,9},{9,1},{2,10},{10,2},{3,11},{11,3},{4,12},{12,4},... | collective-permute-start | bytes 1572872 | tf_op jit(solution)/shard_map/ppermute | solution.py:542
  30.5 9.3 %collective-permute-start.10 = (f32[4,5,32,128]{3,2,1,0:T(8,128)S(1)}, f32[4,5,32,128]{3,2,1,0:T(8,128)S(1)}, u32[]{:S(2)}, u32[]{:S(2)}) collective-permute-start(f32[4,5,32,128]{3,2,1,0:T(8,128)S(1)} %get-tuple-element.57), channel_id=1, source_target_pairs={{0,2},{2,0},{4,6},{6,4},{10,12},{12,10},{1,3},{3,1},{5,7},{7,5},{1... | collective-permute-start | bytes 983048 | tf_op jit(solution)/shard_map/ppermute | solution.py:547
  34.4 5.4 %collective-permute-start.11 = (f32[4,5,32,128]{3,2,1,0:T(8,128)S(1)}, f32[4,5,32,128]{3,2,1,0:T(8,128)S(1)}, u32[]{:S(2)}, u32[]{:S(2)}) collective-permute-start(f32[4,5,32,128]{3,2,1,0:T(8,128)S(1)} %get-tuple-element.58), channel_id=1, source_target_pairs={{2,4},{4,2},{8,10},{10,8},{12,14},{14,12},{3,5},{5,3},{9,11},{11,9... | collective-permute-start | bytes 983048 | tf_op jit(solution)/shard_map/ppermute | solution.py:548
  42.5 17.7 %collective-permute-start.12 = (f32[4,5,32,128]{3,2,1,0:T(8,128)S(1)}, f32[4,5,32,128]{3,2,1,0:T(8,128)S(1)}, u32[]{:S(2)}, u32[]{:S(2)}) collective-permute-start(f32[4,5,32,128]{3,2,1,0:T(8,128)S(1)} %get-tuple-element.69), channel_id=1, source_target_pairs={{0,2},{2,0},{4,6},{6,4},{10,12},{12,10},{1,3},{3,1},{5,7},{7,5},{1... | collective-permute-start | bytes 983048 | tf_op jit(solution)/shard_map/ppermute | solution.py:577
  49.0 11.2 %collective-permute-start.13 = (f32[4,5,32,128]{3,2,1,0:T(8,128)S(1)}, f32[4,5,32,128]{3,2,1,0:T(8,128)S(1)}, u32[]{:S(2)}, u32[]{:S(2)}) collective-permute-start(f32[4,5,32,128]{3,2,1,0:T(8,128)S(1)} %get-tuple-element.70), channel_id=1, source_target_pairs={{2,4},{4,2},{8,10},{10,8},{12,14},{14,12},{3,5},{5,3},{9,11},{11,9... | collective-permute-start | bytes 983048 | tf_op jit(solution)/shard_map/ppermute | solution.py:578
  51.2 11.4 %collective-permute-start.14 = (f32[8,128]{1,0:T(8,128)S(1)}, f32[8,128]{1,0:T(8,128)S(1)}, u32[]{:S(2)}, u32[]{:S(2)}) collective-permute-start(f32[8,128]{1,0:T(8,128)S(1)} %get-tuple-element.76.rest_0_), channel_id=1, source_target_pairs={{0,2},{2,0},{4,6},{6,4},{1,3},{3,1},{5,7},{7,5},{8,10},{10,8},{12,... | collective-permute-start | bytes 12296 | tf_op jit(solution)/shard_map/ppermute | solution.py:590
  55.4 7.2 %collective-permute-start.15 = (f32[8,128]{1,0:T(8,128)S(1)}, f32[8,128]{1,0:T(8,128)S(1)}, u32[]{:S(2)}, u32[]{:S(2)}) collective-permute-start(f32[8,128]{1,0:T(8,128)S(1)} %get-tuple-element.76.rest_0_), channel_id=1, source_target_pairs={{0,4},{2,6},{4,0},{6,2},{1,5},{3,7},{5,1},{7,3},{8,12},{10,14},{12... | collective-permute-start | bytes 12296 | tf_op jit(solution)/shard_map/ppermute | solution.py:590
  55.4 7.2 %collective-permute-start.16 = (f32[8,128]{1,0:T(8,128)S(1)}, f32[8,128]{1,0:T(8,128)S(1)}, u32[]{:S(2)}, u32[]{:S(2)}) collective-permute-start(f32[8,128]{1,0:T(8,128)S(1)} %get-tuple-element.76.rest_0_), channel_id=1, source_target_pairs={{0,6},{2,4},{4,2},{6,0},{1,7},{3,5},{5,3},{7,1},{8,14},{10,12},{12... | collective-permute-start | bytes 12296 | tf_op jit(solution)/shard_map/ppermute | solution.py:590
  60.2 2.4 %copy-start = (f32[5,8]{1,0:T(8,128)S(1)}, f32[5,8]{1,0:T(8,128)}, u32[]{:S(2)}) copy-start(f32[5,8]{1,0:T(8,128)} %weights_ref.3) | copy-start | bytes 484
  64.7 2.1 %collective-permute-start.17 = (f32[4,2,128,128]{3,2,1,0:T(8,128)S(1)}, f32[4,2,128,128]{3,2,1,0:T(8,128)S(1)}, u32[]{:S(2)}, u32[]{:S(2)}) collective-permute-start(f32[4,2,128,128]{3,2,1,0:T(8,128)S(1)} %last_step_given.1), channel_id=1, source_target_pairs={{0,8},{8,0},{1,9},{9,1},{2,10},{10,2},{3,11},{11,3},{4,12},{12,4},... | collective-permute-start | bytes 1572872 | tf_op jit(solution)/shard_map/ppermute | solution.py:628
  67.4 7.3 %collective-permute-start.18 = (f32[2,128,128]{2,1,0:T(8,128)S(1)}, f32[2,128,128]{2,1,0:T(8,128)S(1)}, u32[]{:S(2)}, u32[]{:S(2)}) collective-permute-start(f32[2,128,128]{2,1,0:T(8,128)S(1)} %get-tuple-element.78), channel_id=1, source_target_pairs={{0,17},{1,16},{16,1},{17,0},{2,19},{3,18},{18,3},{19,2},{4,21},{5,... | collective-permute-start | bytes 393224 | tf_op jit(solution)/shard_map/ppermute | solution.py:497
  69.9 7.3 %collective-permute-start.19 = (f32[2,128,128]{2,1,0:T(8,128)S(1)}, f32[2,128,128]{2,1,0:T(8,128)S(1)}, u32[]{:S(2)}, u32[]{:S(2)}) collective-permute-start(f32[2,128,128]{2,1,0:T(8,128)S(1)} %get-tuple-element.79), channel_id=1, source_target_pairs={{0,16},{1,17},{16,0},{17,1},{2,18},{3,19},{18,2},{19,3},{4,20},{5,... | collective-permute-start | bytes 393224 | tf_op jit(solution)/shard_map/ppermute | solution.py:497
  70.4 6.7 %collective-permute-start.20 = (f32[2,128,128]{2,1,0:T(8,128)S(1)}, f32[2,128,128]{2,1,0:T(8,128)S(1)}, u32[]{:S(2)}, u32[]{:S(2)}) collective-permute-start(f32[2,128,128]{2,1,0:T(8,128)S(1)} %get-tuple-element.80), channel_id=1, source_target_pairs={{0,1},{1,0},{16,17},{17,16},{2,3},{3,2},{18,19},{19,18},{4,5},{5,4... | collective-permute-start | bytes 393224 | tf_op jit(solution)/shard_map/ppermute | solution.py:497

commit v14 on v11

--- a/solution.py
+++ b/solution.py
@@ -263,11 +263,10 @@
     apply_rows(c2, d1, diagonal, 4, own - 8, c1)
 
 
-def first_kernel(
-    own,
-    spot_ref, c0_in, diagonal_in, d0_in, c1_in, d1_in, c2_in,
-    even_ref, odd_ref, even_diagonal_ref, odd_diagonal_ref,
-    c0_ref, diagonal_ref, d0_ref, c1_ref, d1_ref, c2_ref, even_out, odd_out,
+def side_kernel(
+    own, which,
+    spot_ref, c0_in, diagonal_in, d0_in, c1_in, d1_in, c2_in, halo_ref, halo_diagonal_ref,
+    c0_ref, diagonal_ref, d0_ref, c1_ref, d1_ref, c2_ref, edge_out,
 ):
     c0 = Field(c0_ref, HALO)
     diagonal = Field(diagonal_ref, DIAGONAL_HALO)
@@ -275,18 +274,29 @@
     c1 = Field(c1_ref, 3)
     d1 = Field(d1_ref, 2)
     c2 = Field(c2_ref, HALO)
-    fill_halo(spot_ref, c0, own, even_ref, odd_ref)
-    fill_halo(spot_ref, diagonal, own, even_diagonal_ref, odd_diagonal_ref)
-    strips = functools.partial(apply_strips, spot_ref, own)
-    strips(d0, c0, diagonal, 4, HALO)
-    strips(c1, d0, diagonal, 3, HALO, c0)
-    strips(d1, c1, diagonal, 2, HALO)
-    strips(c2, d1, diagonal, 1, HALO, c1)
+    masks = lane_masks()
+    above = jnp.where(spot_ref[5] == which, 1, 0)
+    for field, ref in ((c0, halo_ref), (diagonal, halo_diagonal_ref)):
+        base = above * (own + field.halo)
+        for c in range(field.columns):
+            for y in range(field.halo):
+                for x in range(0, field.cells, 8):
+                    field.store(c, base + (y - field.halo), x, ref[c, y, pl.ds(x, 8), :])
+
+    def strip(target, source, halo, minus=None):
+        row = above * (own - HALO + 2 * halo) - halo
+        apply_block(target, source, diagonal, row, HALO, minus, masks)
+        clear_outside(spot_ref, own, target)
+
+    strip(d0, c0, 4)
+    strip(c1, d0, 3, c0)
+    strip(d1, c1, 2)
+    strip(c2, d1, 1, c1)
+    base = above * (own - HALO)
     for c in range(c2.columns):
         for x in range(0, c2.cells, 8):
-            first = [c2.load(c, y, x) for y in range(HALO)]
-            last = [c2.load(c, own - HALO + y, x) for y in range(HALO)]
-            store_edges(spot_ref, even_out, odd_out, x, c, first, last)
+            for y in range(HALO):
+                edge_out[c, y, pl.ds(x, 8), :] = c2.load(c, base + y, x)
 
 
 def middle_kernel(own, c0_ref, c1_ref, c2_ref, diagonal_ref, d2_ref, moments_ref):
@@ -559,18 +569,25 @@
         name="inner_steps",
     )(spot, probe, other, here(diagonal))
     vectors = [here(value) for value in (inner[0], diagonal) + tuple(inner[1:])]
-    c0, diagonal, d0, c1, d1, c2, even_edge, odd_edge = pl.pallas_call(
-        functools.partial(first_kernel, by),
-        out_shape=tuple(vector(h) for h in (HALO, DIAGONAL_HALO, 4, 3, 2, HALO))
-        + (edge(HALO), edge(HALO)),
-        in_specs=[smem()] + [vmem()] * 10,
-        out_specs=(vmem(),) * 8,
-        input_output_aliases={i + 1: i for i in range(6)},
-        compiler_params=params(),
-        name="first_steps",
-    )(spot, *vectors, even1, odd1, even_diagonal, odd_diagonal)
-    even2 = lax.ppermute(even_edge, "gy", even)
-    odd2 = lax.ppermute(odd_edge, "gy", odd)
+    arrived = []
+    for which, (halo, halo_diagonal, pairs) in enumerate(
+        ((even1, even_diagonal, even), (odd1, odd_diagonal, odd))
+    ):
+        *vectors, edge_rows = pl.pallas_call(
+            functools.partial(side_kernel, by, which),
+            out_shape=tuple(vector(h) for h in (HALO, DIAGONAL_HALO, 4, 3, 2, HALO))
+            + (edge(HALO),),
+            in_specs=[smem()] + [vmem()] * 8,
+            out_specs=(vmem(),) * 7,
+            input_output_aliases={i + 1: i for i in range(6)},
+            compiler_params=params(),
+            cost_estimate=cost(8),
+            name="side_steps_%d" % which,
+        )(spot, *(here(value) for value in vectors), halo, halo_diagonal)
+        arrived.append(lax.ppermute(edge_rows, "gy", pairs))
+    c0, diagonal, d0, c1, d1, c2 = vectors
+    even2, odd2 = arrived
+
     d2, moments = pl.pallas_call(
         functools.partial(middle_kernel, by),
         out_shape=(vector(4), f32(8, 128)),

time: 75.7 us -> 74.7 us (0.987)
  starting transfers between devices: 27.8 us -> 26.2 us
    ppermute x2, starting transfers between devices: 5.48 us -> 2.46 us  [body(): arrived.append(lax.ppermute(edge_rows, 'gy', pairs))]
    ppermute x3, starting transfers between devices: 5.49 us -> 6.87 us  [body(): lax.ppermute(moments, 'gy', [(i, i ^ step) for i in range(ny)])]
    pallas_call x1 -> x2, Pallas kernels: 2.65 us -> 3.24 us  [body(): pl.pallas_call(functools.partial(side_kernel, by, which), out_shape=tuple...]
  transfers between devices with their start and end apart: 21 -> 21, of which waited for: 9 -> 9; matrix products, arithmetic and copies ran while one was open for 0% -> 0% of each run, Pallas kernels for 20% -> 25%
where the time goes in v14:
time: 74.7 us; the launch traced here: 74.4 us
  starting transfers between devices  26.2 us (35%)
  waiting for transfers between devices  24.1 us (32%)
  Pallas kernels  23.8 us (32%)
    ppermute x9, waiting for transfers between devices, to_chip(): return lax.ppermute(value, ('chip', 'gz'), pairs)  18.8 us
    ppermute x9, starting transfers between devices, to_chip(): return lax.ppermute(value, ('chip', 'gz'), pairs)  11.7 us
    ppermute x3, starting transfers between devices, body(): lax.ppermute(moments, 'gy', [(i, i ^ step) for i in range(ny)])  6.87 us
    pallas_call x8, Pallas kernels, plain(): pl.pallas_call(kernel, out_shape=out_shape, in_specs=specs, out_specs=(vm...  6.42 us
    pallas_call x2, Pallas kernels, last_step(): pl.pallas_call(functools.partial(last_kernel, grid, inverse_count, flip),...  4.06 us
    pallas_call x1, Pallas kernels, body(): pl.pallas_call(functools.partial(inner_kernel, grid), out_shape=tuple((ve...  3.93 us
    ppermute x1, waiting for transfers between devices, body(): even1 = lax.ppermute(even_edge, 'gy', even)  3.4 us
    pallas_call x2, Pallas kernels, body(): pl.pallas_call(functools.partial(side_kernel, by, which), out_shape=tuple...  3.24 us
  transfers between devices with their start and end apart: 21, of which 9 were waited for; matrix products, arithmetic and copies ran while one was open for 0% of the time, Pallas kernels for 25%

profile of v14, /device:TPU:0, one launch (start us, length us, event | category | flops | bytes accessed | tf_op | source)
XLA Modules:
  0.0 74.4 jit_solution(17940077079611914829)
XLA Ops:
  0.9 3.0 %collective-permute-start = (f32[2,128,128]{2,1,0:T(8,128)S(1)}, f32[2,128,128]{2,1,0:T(8,128)S(1)}, u32[]{:S(2)}, u32[]{:S(2)}) collective-permute-start(f32[2,128,128]{2,1,0:T(8,128)S(1)} %pack_kappa.1.after_ref.refs_0_), channel_id=1, source_target_pairs={{0,1},{1,0},{16,17},{17,16},{2,3},{3,2},{18,19},{19,18},{4,5},{5,4... | collective-permute-start | bytes 393224 | tf_op jit(solution)/shard_map/ppermute | solution.py:502
  5.6 1.9 %pack_probes.1 = (f32[2,2,128,128]{3,2,1,0:T(8,128)S(1)}, f32[2,2,128,128]{3,2,1,0:T(8,128)S(1)}, f32[2,2,128,128]{3,2,1,0:T(8,128)S(1)}, f32[2,2,128,128]{3,2,1,0:T(8,128)S(1)}) custom-call(s32[6]{0:T(128)S(1)} %stack.35.spot_ref, f32[2,128,128]{2,1,0:T(8,128)S(1)} %pack_kappa.1.after_ref.refs_0_, f32[1024,256]{1,0:T(8,128)} %bitcast.8), custom_call_target="tpu_custom_call" | custom-call | tf_op jit(solution)/shard_map/pack_probes/pallas_call | solution.py:505
  7.5 2.8 %collective-permute-done.1.refs_2_ = f32[2,128,128]{2,1,0:T(8,128)S(1)} collective-permute-done((f32[2,128,128]{2,1,0:T(8,128)S(1)}, f32[2,128,128]{2,1,0:T(8,128)S(1)}, u32[]{:S(2)}, u32[]{:S(2)}) %collective-permute-start.1) | collective-permute-done | bytes 131104 | tf_op jit(solution)/shard_map/ppermute | solution.py:502
  11.6 1.7 %collective-permute-start.6 = (f32[2,2,128,128]{3,2,1,0:T(8,128)S(1)}, f32[2,2,128,128]{3,2,1,0:T(8,128)S(1)}, u32[]{:S(2)}, u32[]{:S(2)}) collective-permute-start(f32[2,2,128,128]{3,2,1,0:T(8,128)S(1)} %get-tuple-element.52), channel_id=1, source_target_pairs={{0,1},{1,0},{16,17},{17,16},{2,3},{3,2},{18,19},{19,18},{4,5},{5,4... | collective-permute-start | bytes 786440 | tf_op jit(solution)/shard_map/ppermute | solution.py:502
  16.1 1.8 %collective-permute-start.4 = (f32[4,4,32,128]{3,2,1,0:T(8,128)S(1)}, f32[4,4,32,128]{3,2,1,0:T(8,128)S(1)}, u32[]{:S(2)}, u32[]{:S(2)}) collective-permute-start(f32[4,4,32,128]{3,2,1,0:T(8,128)S(1)} %get-tuple-element.50), channel_id=1, source_target_pairs={{0,2},{2,0},{4,6},{6,4},{1,3},{3,1},{5,7},{7,5},{8,10},{10,8},{12,... | collective-permute-start | bytes 786440 | tf_op jit(solution)/shard_map/ppermute | solution.py:540
  18.6 1.8 %collective-permute-done.6.refs_1_ = f32[2,2,128,128]{3,2,1,0:T(8,128)S(1)} collective-permute-done((f32[2,2,128,128]{3,2,1,0:T(8,128)S(1)}, f32[2,2,128,128]{3,2,1,0:T(8,128)S(1)}, u32[]{:S(2)}, u32[]{:S(2)}) %collective-permute-start.6) | collective-permute-done | bytes 262176 | tf_op jit(solution)/shard_map/ppermute | solution.py:502
  20.3 2.2 %collective-permute-done.7.refs_2_ = f32[2,2,128,128]{3,2,1,0:T(8,128)S(1)} collective-permute-done((f32[2,2,128,128]{3,2,1,0:T(8,128)S(1)}, f32[2,2,128,128]{3,2,1,0:T(8,128)S(1)}, u32[]{:S(2)}, u32[]{:S(2)}) %collective-permute-start.7) | collective-permute-done | bytes 262176 | tf_op jit(solution)/shard_map/ppermute | solution.py:502
  22.5 4.6 %collective-permute-done.8.refs_3_ = f32[2,2,128,128]{3,2,1,0:T(8,128)S(1)} collective-permute-done((f32[2,2,128,128]{3,2,1,0:T(8,128)S(1)}, f32[2,2,128,128]{3,2,1,0:T(8,128)S(1)}, u32[]{:S(2)}, u32[]{:S(2)}) %collective-permute-start.8) | collective-permute-done | bytes 262176 | tf_op jit(solution)/shard_map/ppermute | solution.py:502
  27.8 1.9 %collective-permute-done.9.other_ref = f32[4,2,128,128]{3,2,1,0:T(8,128)S(1)} collective-permute-done((f32[4,2,128,128]{3,2,1,0:T(8,128)S(1)}, f32[4,2,128,128]{3,2,1,0:T(8,128)S(1)}, u32[]{:S(2)}, u32[]{:S(2)}) %collective-permute-start.9) | collective-permute-done | bytes 524320 | tf_op jit(solution)/shard_map/ppermute | solution.py:547
  30.5 1.8 %collective-permute-start.10 = (f32[4,5,32,128]{3,2,1,0:T(8,128)S(1)}, f32[4,5,32,128]{3,2,1,0:T(8,128)S(1)}, u32[]{:S(2)}, u32[]{:S(2)}) collective-permute-start(f32[4,5,32,128]{3,2,1,0:T(8,128)S(1)} %get-tuple-element.63), channel_id=1, source_target_pairs={{0,2},{2,0},{4,6},{6,4},{1,3},{3,1},{5,7},{7,5},{8,10},{10,8},{12,... | collective-permute-start | bytes 983048 | tf_op jit(solution)/shard_map/ppermute | solution.py:552
  33.0 3.9 %inner_steps.1 = (f32[4,26,48,128]{3,2,1,0:T(8,128)S(1)}, f32[4,24,48,128]{3,2,1,0:T(8,128)S(1)}, f32[4,22,48,128]{3,2,1,0:T(8,128)S(1)}, f32[4,20,48,128]{3,2,1,0:T(8,128)S(1)}, f32[4,26,48,128]{3,2,1,0:T(8,128)S(1)}) custom-call(s32[6]{0:T(128)S(1)} %stack.35.spot_ref, f32[4,2,128,128]{3,2,1,0:T(8,128)S(1)} %get-tuple-element.55.mine_ref, ...), custom_call_target="tpu_custom_call" | custom-call | flops 8388608 | bytes 4194304 | tf_op jit(solution)/shard_map/inner_steps/pallas_call | solution.py:562
  36.9 3.4 %collective-permute-done.10.halo_ref = f32[4,5,32,128]{3,2,1,0:T(8,128)S(1)} collective-permute-done((f32[4,5,32,128]{3,2,1,0:T(8,128)S(1)}, f32[4,5,32,128]{3,2,1,0:T(8,128)S(1)}, u32[]{:S(2)}, u32[]{:S(2)}) %collective-permute-start.10) | collective-permute-done | bytes 327712 | tf_op jit(solution)/shard_map/ppermute | solution.py:552
  40.3 1.6 %side_steps_0.1 = (f32[4,26,48,128]{3,2,1,0:T(8,128)S(1)}, f32[4,24,48,128]{3,2,1,0:T(8,128)S(1)}, f32[4,24,48,128]{3,2,1,0:T(8,128)S(1)}, f32[4,22,48,128]{3,2,...) custom-call(s32[6]{0:T(128)S(1)} %stack.35.spot_ref, ...), custom_call_target="tpu_custom_call", output_to_operand_aliasing={{0}: (1, {}), {1}: (2, {}), {2}: (3, {}), {3}: (4, {}), {4}... | custom-call | flops 2097152 | bytes 4194304 | tf_op jit(solution)/shard_map/side_steps_0/pallas_call | solution.py:576
  41.9 1.8 %collective-permute-start.12 = (f32[4,5,32,128]{3,2,1,0:T(8,128)S(1)}, f32[4,5,32,128]{3,2,1,0:T(8,128)S(1)}, u32[]{:S(2)}, u32[]{:S(2)}) collective-permute-start(f32[4,5,32,128]{3,2,1,0:T(8,128)S(1)} %get-tuple-element.81), channel_id=1, source_target_pairs={{0,2},{2,0},{4,6},{6,4},{1,3},{3,1},{5,7},{7,5},{8,10},{10,8},{12,... | collective-permute-start | bytes 983048 | tf_op jit(solution)/shard_map/ppermute | solution.py:587
  43.7 1.6 %side_steps_1.1 = (f32[4,26,48,128]{3,2,1,0:T(8,128)S(1)}, f32[4,24,48,128]{3,2,1,0:T(8,128)S(1)}, f32[4,24,48,128]{3,2,1,0:T(8,128)S(1)}, f32[4,22,48,128]{3,2,...) custom-call(s32[6]{0:T(128)S(1)} %stack.35.spot_ref, ...), custom_call_target="tpu_custom_call", output_to_operand_aliasing={{0}: (1, {}), {1}: (2, {}), {2}: (3, {}), {3}: (4, {}), {4}... | custom-call | flops 2097152 | bytes 4194304 | tf_op jit(solution)/shard_map/side_steps_1/pallas_call | solution.py:576
  47.5 4.4 %collective-permute-start.14 = (f32[8,128]{1,0:T(8,128)S(1)}, f32[8,128]{1,0:T(8,128)S(1)}, u32[]{:S(2)}, u32[]{:S(2)}) collective-permute-start(f32[8,128]{1,0:T(8,128)S(1)} %get-tuple-element.88.rest_0_), channel_id=1, source_target_pairs={{0,2},{2,0},{4,6},{6,4},{1,3},{3,1},{5,7},{7,5},{8,10},{10,8},{12,... | collective-permute-start | bytes 12296 | tf_op jit(solution)/shard_map/ppermute | solution.py:602
  52.0 2.4 %collective-permute-start.16 = (f32[8,128]{1,0:T(8,128)S(1)}, f32[8,128]{1,0:T(8,128)S(1)}, u32[]{:S(2)}, u32[]{:S(2)}) collective-permute-start(f32[8,128]{1,0:T(8,128)S(1)} %get-tuple-element.88.rest_0_), channel_id=1, source_target_pairs={{0,6},{2,4},{4,2},{6,0},{1,7},{3,5},{5,3},{7,1},{8,14},{10,12},{12... | collective-permute-start | bytes 12296 | tf_op jit(solution)/shard_map/ppermute | solution.py:602
  54.4 2.3 %second_inner_steps.1 = (f32[4,22,48,128]{3,2,1,0:T(8,128)S(1)}, f32[4,20,48,128]{3,2,1,0:T(8,128)S(1)}, f32[4,18,48,128]{3,2,1,0:T(8,128)S(1)}) custom-call(f32[4,24,48,128]{3,2,1,0:T(8,128)S(1)} %get-tuple-element.72.diagonal_ref, f32[4,26,48,128]{3,2,1,0:T(8,128)S(1)} %get-tuple-element.76.c2_ref.c2_in, f32[4,24,48,128]{3,2,1,0:T(8,128)S(1)} %get-tuple-element.77.d2_ref.d2_in), custom_call_target="tpu_custom_call" | custom-call | flops 7864320 | bytes 4194304 | tf_op jit(solution)/shard_map/second_inner_steps/pallas_call | solution.py:604
  56.8 2.4 %third_steps.1 = (f32[4,26,48,128]{3,2,1,0:T(8,128)S(1)}, f32[4,24,48,128]{3,2,1,0:T(8,128)S(1)}, f32[4,22,48,128]{3,2,1,0:T(8,128)S(1)}, f32[4,20,48,128]{3,2,1,0:T(8,128)S(1)}, f32[4,18,48,128]{3,2,1,0:T(8,128)S(1)}) custom-call(s32[6]{0:T(128)S(1)} %stack.35.spot_ref, ...), custom_call_target="tpu_custom_call", output_to_operand_aliasing={{0}: (2, {}), {1}: (3, {}), {2}: (4, {}), {3}: (5, {}), {4}... | custom-call | flops 5242880 | bytes 4194304 | tf_op jit(solution)/shard_map/third_steps/pallas_call | solution.py:614
  59.2 2.0 %last_step_given.1 = f32[4,2,128,128]{3,2,1,0:T(8,128)S(1)} custom-call(s32[6]{0:T(128)S(1)} %stack.35.spot_ref, f32[5,8]{1,0:T(8,128)S(1)} %copy-done, f32[4,26,48,128]{3,2,1,0:T(8,128)S(1)} %get-tuple-element.71.c0_ref, f32[4,24,48,128]{3,2,1,0:T(8,128)S(1)} %get-tuple-element.72.diagonal_ref, f32[4,24,48,128]{3,2,1,0:T(8,128)S(1)} %get-tuple-element.73.d0_ref, ...), custom_call_target="tpu_custom_call" | custom-call | flops 5242880 | bytes 4194304 | tf_op jit(solution)/shard_map/last_step_given/pallas_call | solution.py:630
  61.3 2.0 %last_step_kept.1.kept_ref = f32[4,2,128,128]{3,2,1,0:T(8,128)S(1)} custom-call(s32[6]{0:T(128)S(1)} %stack.35.spot_ref, f32[5,8]{1,0:T(8,128)S(1)} %copy-done, f32[4,26,48,128]{3,2,1,0:T(8,128)S(1)} %get-tuple-element.71.c0_ref, f32[4,24,48,128]{3,2,1,0:T(8,128)S(1)} %get-tuple-element.72.diagonal_ref, f32[4,24,48,128]{3,2,1,0:T(8,128)S(1)} %get-tuple-element.73.d0_ref, ...), custom_call_target="tpu_custom_call" | custom-call | flops 5242880 | bytes 4194304 | tf_op jit(solution)/shard_map/last_step_kept/pallas_call | solution.py:630
  64.0 2.5 %collective-permute-start.18 = (f32[2,128,128]{2,1,0:T(8,128)S(1)}, f32[2,128,128]{2,1,0:T(8,128)S(1)}, u32[]{:S(2)}, u32[]{:S(2)}) collective-permute-start(f32[2,128,128]{2,1,0:T(8,128)S(1)} %get-tuple-element.90), channel_id=1, source_target_pairs={{0,17},{1,16},{16,1},{17,0},{2,19},{3,18},{18,3},{19,2},{4,21},{5,... | collective-permute-start | bytes 393224 | tf_op jit(solution)/shard_map/ppermute | solution.py:502
  67.5 3.7 %collective-permute-done.18.refs_1_ = f32[2,128,128]{2,1,0:T(8,128)S(1)} collective-permute-done((f32[2,128,128]{2,1,0:T(8,128)S(1)}, f32[2,128,128]{2,1,0:T(8,128)S(1)}, u32[]{:S(2)}, u32[]{:S(2)}) %collective-permute-start.18) | collective-permute-done | bytes 131104 | tf_op jit(solution)/shard_map/ppermute | solution.py:502
  71.2 2.5 %collective-permute-done.19.refs_2_ = f32[2,128,128]{2,1,0:T(8,128)S(1)} collective-permute-done((f32[2,128,128]{2,1,0:T(8,128)S(1)}, f32[2,128,128]{2,1,0:T(8,128)S(1)}, u32[]{:S(2)}, u32[]{:S(2)}) %collective-permute-start.19) | collective-permute-done | bytes 131104 | tf_op jit(solution)/shard_map/ppermute | solution.py:502
  (37 shorter events, 13.9 us)
Async XLA Ops:
  0.9 6.6 %collective-permute-start = (f32[2,128,128]{2,1,0:T(8,128)S(1)}, f32[2,128,128]{2,1,0:T(8,128)S(1)}, u32[]{:S(2)}, u32[]{:S(2)}) collective-permute-start(f32[2,128,128]{2,1,0:T(8,128)S(1)} %pack_kappa.1.after_ref.refs_0_), channel_id=1, source_target_pairs={{0,1},{1,0},{16,17},{17,16},{2,3},{3,2},{18,19},{19,18},{4,5},{5,4... | collective-permute-start | bytes 393224 | tf_op jit(solution)/shard_map/ppermute | solution.py:502
  3.9 6.4 %collective-permute-start.1 = (f32[2,128,128]{2,1,0:T(8,128)S(1)}, f32[2,128,128]{2,1,0:T(8,128)S(1)}, u32[]{:S(2)}, u32[]{:S(2)}) collective-permute-start(f32[2,128,128]{2,1,0:T(8,128)S(1)} %pack_kappa.1.after_ref.refs_0_), channel_id=1, source_target_pairs={{0,16},{1,17},{16,0},{17,1},{2,18},{3,19},{18,2},{19,3},{4,20},{5,... | collective-permute-start | bytes 393224 | tf_op jit(solution)/shard_map/ppermute | solution.py:502
  5.4 6.1 %collective-permute-start.2 = (f32[2,128,128]{2,1,0:T(8,128)S(1)}, f32[2,128,128]{2,1,0:T(8,128)S(1)}, u32[]{:S(2)}, u32[]{:S(2)}) collective-permute-start(f32[2,128,128]{2,1,0:T(8,128)S(1)} %pack_kappa.1.after_ref.refs_0_), channel_id=1, source_target_pairs={{0,17},{1,16},{16,1},{17,0},{2,19},{3,18},{18,3},{19,2},{4,21},{5,... | collective-permute-start | bytes 393224 | tf_op jit(solution)/shard_map/ppermute | solution.py:502
  11.5 3.6 %collective-permute-start.3 = (f32[4,2,128,128]{3,2,1,0:T(8,128)S(1)}, f32[4,2,128,128]{3,2,1,0:T(8,128)S(1)}, u32[]{:S(2)}, u32[]{:S(2)}) collective-permute-start(f32[4,2,128,128]{3,2,1,0:T(8,128)S(1)} %stack_kappa.1.mine_ref), channel_id=1, source_target_pairs={{0,8},{8,0},{1,9},{9,1},{2,10},{10,2},{3,11},{11,3},{4,12},{12,4},... | collective-permute-start | bytes 1572872 | tf_op jit(solution)/shard_map/ppermute | solution.py:534
  11.6 8.7 %collective-permute-start.6 = (f32[2,2,128,128]{3,2,1,0:T(8,128)S(1)}, f32[2,2,128,128]{3,2,1,0:T(8,128)S(1)}, u32[]{:S(2)}, u32[]{:S(2)}) collective-permute-start(f32[2,2,128,128]{3,2,1,0:T(8,128)S(1)} %get-tuple-element.52), channel_id=1, source_target_pairs={{0,1},{1,0},{16,17},{17,16},{2,3},{3,2},{18,19},{19,18},{4,5},{5,4... | collective-permute-start | bytes 786440 | tf_op jit(solution)/shard_map/ppermute | solution.py:502
  13.3 9.2 %collective-permute-start.7 = (f32[2,2,128,128]{3,2,1,0:T(8,128)S(1)}, f32[2,2,128,128]{3,2,1,0:T(8,128)S(1)}, u32[]{:S(2)}, u32[]{:S(2)}) collective-permute-start(f32[2,2,128,128]{3,2,1,0:T(8,128)S(1)} %get-tuple-element.53), channel_id=1, source_target_pairs={{0,16},{1,17},{16,0},{17,1},{2,18},{3,19},{18,2},{19,3},{4,20},{5,... | collective-permute-start | bytes 786440 | tf_op jit(solution)/shard_map/ppermute | solution.py:502
  14.8 12.3 %collective-permute-start.8 = (f32[2,2,128,128]{3,2,1,0:T(8,128)S(1)}, f32[2,2,128,128]{3,2,1,0:T(8,128)S(1)}, u32[]{:S(2)}, u32[]{:S(2)}) collective-permute-start(f32[2,2,128,128]{3,2,1,0:T(8,128)S(1)} %get-tuple-element.54), channel_id=1, source_target_pairs={{0,17},{1,16},{16,1},{17,0},{2,19},{3,18},{18,3},{19,2},{4,21},{5,... | collective-permute-start | bytes 786440 | tf_op jit(solution)/shard_map/ppermute | solution.py:502
  16.1 11.0 %collective-permute-start.4 = (f32[4,4,32,128]{3,2,1,0:T(8,128)S(1)}, f32[4,4,32,128]{3,2,1,0:T(8,128)S(1)}, u32[]{:S(2)}, u32[]{:S(2)}) collective-permute-start(f32[4,4,32,128]{3,2,1,0:T(8,128)S(1)} %get-tuple-element.50), channel_id=1, source_target_pairs={{0,2},{2,0},{4,6},{6,4},{1,3},{3,1},{5,7},{7,5},{8,10},{10,8},{12,... | collective-permute-start | bytes 786440 | tf_op jit(solution)/shard_map/ppermute | solution.py:540
  17.9 9.2 %collective-permute-start.5 = (f32[4,4,32,128]{3,2,1,0:T(8,128)S(1)}, f32[4,4,32,128]{3,2,1,0:T(8,128)S(1)}, u32[]{:S(2)}, u32[]{:S(2)}) collective-permute-start(f32[4,4,32,128]{3,2,1,0:T(8,128)S(1)} %get-tuple-element.51), channel_id=1, source_target_pairs={{2,4},{4,2},{3,5},{5,3},{10,12},{12,10},{11,13},{13,11},{18,20},{2... | collective-permute-start | bytes 786440 | tf_op jit(solution)/shard_map/ppermute | solution.py:541
  27.8 2.0 %collective-permute-start.9 = (f32[4,2,128,128]{3,2,1,0:T(8,128)S(1)}, f32[4,2,128,128]{3,2,1,0:T(8,128)S(1)}, u32[]{:S(2)}, u32[]{:S(2)}) collective-permute-start(f32[4,2,128,128]{3,2,1,0:T(8,128)S(1)} %get-tuple-element.56), channel_id=1, source_target_pairs={{0,8},{8,0},{1,9},{9,1},{2,10},{10,2},{3,11},{11,3},{4,12},{12,4},... | collective-permute-start | bytes 1572872 | tf_op jit(solution)/shard_map/ppermute | solution.py:547
  30.5 9.8 %collective-permute-start.10 = (f32[4,5,32,128]{3,2,1,0:T(8,128)S(1)}, f32[4,5,32,128]{3,2,1,0:T(8,128)S(1)}, u32[]{:S(2)}, u32[]{:S(2)}) collective-permute-start(f32[4,5,32,128]{3,2,1,0:T(8,128)S(1)} %get-tuple-element.63), channel_id=1, source_target_pairs={{0,2},{2,0},{4,6},{6,4},{1,3},{3,1},{5,7},{7,5},{8,10},{10,8},{12,... | collective-permute-start | bytes 983048 | tf_op jit(solution)/shard_map/ppermute | solution.py:552
  32.3 11.4 %collective-permute-start.11 = (f32[4,5,32,128]{3,2,1,0:T(8,128)S(1)}, f32[4,5,32,128]{3,2,1,0:T(8,128)S(1)}, u32[]{:S(2)}, u32[]{:S(2)}) collective-permute-start(f32[4,5,32,128]{3,2,1,0:T(8,128)S(1)} %get-tuple-element.70), channel_id=1, source_target_pairs={{2,4},{4,2},{3,5},{5,3},{10,12},{12,10},{11,13},{13,11},{18,20},{2... | collective-permute-start | bytes 983048 | tf_op jit(solution)/shard_map/ppermute | solution.py:553
  41.9 14.8 %collective-permute-start.12 = (f32[4,5,32,128]{3,2,1,0:T(8,128)S(1)}, f32[4,5,32,128]{3,2,1,0:T(8,128)S(1)}, u32[]{:S(2)}, u32[]{:S(2)}) collective-permute-start(f32[4,5,32,128]{3,2,1,0:T(8,128)S(1)} %get-tuple-element.81), channel_id=1, source_target_pairs={{0,2},{2,0},{4,6},{6,4},{1,3},{3,1},{5,7},{7,5},{8,10},{10,8},{12,... | collective-permute-start | bytes 983048 | tf_op jit(solution)/shard_map/ppermute | solution.py:587
  45.3 11.4 %collective-permute-start.13 = (f32[4,5,32,128]{3,2,1,0:T(8,128)S(1)}, f32[4,5,32,128]{3,2,1,0:T(8,128)S(1)}, u32[]{:S(2)}, u32[]{:S(2)}) collective-permute-start(f32[4,5,32,128]{3,2,1,0:T(8,128)S(1)} %get-tuple-element.82), channel_id=1, source_target_pairs={{2,4},{4,2},{3,5},{5,3},{10,12},{12,10},{11,13},{13,11},{18,20},{2... | collective-permute-start | bytes 983048 | tf_op jit(solution)/shard_map/ppermute | solution.py:587
  47.5 11.6 %collective-permute-start.14 = (f32[8,128]{1,0:T(8,128)S(1)}, f32[8,128]{1,0:T(8,128)S(1)}, u32[]{:S(2)}, u32[]{:S(2)}) collective-permute-start(f32[8,128]{1,0:T(8,128)S(1)} %get-tuple-element.88.rest_0_), channel_id=1, source_target_pairs={{0,2},{2,0},{4,6},{6,4},{1,3},{3,1},{5,7},{7,5},{8,10},{10,8},{12,... | collective-permute-start | bytes 12296 | tf_op jit(solution)/shard_map/ppermute | solution.py:602
  52.0 7.2 %collective-permute-start.15 = (f32[8,128]{1,0:T(8,128)S(1)}, f32[8,128]{1,0:T(8,128)S(1)}, u32[]{:S(2)}, u32[]{:S(2)}) collective-permute-start(f32[8,128]{1,0:T(8,128)S(1)} %get-tuple-element.88.rest_0_), channel_id=1, source_target_pairs={{0,4},{2,6},{4,0},{6,2},{1,5},{3,7},{5,1},{7,3},{8,12},{10,14},{12... | collective-permute-start | bytes 12296 | tf_op jit(solution)/shard_map/ppermute | solution.py:602
  52.0 7.2 %collective-permute-start.16 = (f32[8,128]{1,0:T(8,128)S(1)}, f32[8,128]{1,0:T(8,128)S(1)}, u32[]{:S(2)}, u32[]{:S(2)}) collective-permute-start(f32[8,128]{1,0:T(8,128)S(1)} %get-tuple-element.88.rest_0_), channel_id=1, source_target_pairs={{0,6},{2,4},{4,2},{6,0},{1,7},{3,5},{5,3},{7,1},{8,14},{10,12},{12... | collective-permute-start | bytes 12296 | tf_op jit(solution)/shard_map/ppermute | solution.py:602
  56.8 2.4 %copy-start = (f32[5,8]{1,0:T(8,128)S(1)}, f32[5,8]{1,0:T(8,128)}, u32[]{:S(2)}) copy-start(f32[5,8]{1,0:T(8,128)} %weights_ref.3) | copy-start | bytes 484
  61.2 2.1 %collective-permute-start.17 = (f32[4,2,128,128]{3,2,1,0:T(8,128)S(1)}, f32[4,2,128,128]{3,2,1,0:T(8,128)S(1)}, u32[]{:S(2)}, u32[]{:S(2)}) collective-permute-start(f32[4,2,128,128]{3,2,1,0:T(8,128)S(1)} %last_step_given.1), channel_id=1, source_target_pairs={{0,8},{8,0},{1,9},{9,1},{2,10},{10,2},{3,11},{11,3},{4,12},{12,4},... | collective-permute-start | bytes 1572872 | tf_op jit(solution)/shard_map/ppermute | solution.py:640
  64.0 7.3 %collective-permute-start.18 = (f32[2,128,128]{2,1,0:T(8,128)S(1)}, f32[2,128,128]{2,1,0:T(8,128)S(1)}, u32[]{:S(2)}, u32[]{:S(2)}) collective-permute-start(f32[2,128,128]{2,1,0:T(8,128)S(1)} %get-tuple-element.90), channel_id=1, source_target_pairs={{0,17},{1,16},{16,1},{17,0},{2,19},{3,18},{18,3},{19,2},{4,21},{5,... | collective-permute-start | bytes 393224 | tf_op jit(solution)/shard_map/ppermute | solution.py:502
  66.5 7.3 %collective-permute-start.19 = (f32[2,128,128]{2,1,0:T(8,128)S(1)}, f32[2,128,128]{2,1,0:T(8,128)S(1)}, u32[]{:S(2)}, u32[]{:S(2)}) collective-permute-start(f32[2,128,128]{2,1,0:T(8,128)S(1)} %get-tuple-element.91), channel_id=1, source_target_pairs={{0,16},{1,17},{16,0},{17,1},{2,18},{3,19},{18,2},{19,3},{4,20},{5,... | collective-permute-start | bytes 393224 | tf_op jit(solution)/shard_map/ppermute | solution.py:502
  67.0 6.7 %collective-permute-start.20 = (f32[2,128,128]{2,1,0:T(8,128)S(1)}, f32[2,128,128]{2,1,0:T(8,128)S(1)}, u32[]{:S(2)}, u32[]{:S(2)}) collective-permute-start(f32[2,128,128]{2,1,0:T(8,128)S(1)} %get-tuple-element.92), channel_id=1, source_target_pairs={{0,1},{1,0},{16,17},{17,16},{2,3},{3,2},{18,19},{19,18},{4,5},{5,4... | collective-permute-start | bytes 393224 | tf_op jit(solution)/shard_map/ppermute | solution.py:502

commit v15 on v14

--- a/solution.py
+++ b/solution.py
@@ -332,7 +332,7 @@
     weights = [weights_ref[k, probe] for k in range(5)]
     value, pullback = jax.vjp(lambda m: loss_of_moments(m, weights), moments)
     (slopes,) = pullback(jnp.full((8, 128), 2.0, jnp.float32))
-    return [slope[0, 0] for slope in slopes]
+    return slopes
 
 
 def second_inner_kernel(own, diagonal_ref, c2_ref, d2_ref, c3_ref, d3_ref, c4_ref):
@@ -370,12 +370,19 @@
 
 def last_kernel(
     grid, inverse_count, flip,
-    spot_ref, weights_ref, c0_ref, diagonal_ref, d0_ref, c1_ref, d1_ref,
+    spot_ref, c0_ref, diagonal_ref, d0_ref, c1_ref, d1_ref,
     c2_ref, d2_ref, c3_ref, d3_ref, c4_ref, *rest,
 ):
     nx, nz, bx, by, bz = grid
     per = bz // 128
-    moment_refs, out_ref = rest[:-1], rest[-1]
+    if flip:
+        weights_ref, *moment_refs, out_ref, slopes_ref = rest
+        slopes = moment_slopes(inverse_count, spot_ref[2], weights_ref, moment_refs)
+        for k, slope in enumerate(slopes):
+            slopes_ref[k] = slope
+    else:
+        slopes_ref, out_ref = rest
+        slopes = [slopes_ref[k] for k in range(6)]
     c0 = Field(c0_ref, HALO)
     diagonal = Field(diagonal_ref, DIAGONAL_HALO)
     d0 = Field(d0_ref, 4)
@@ -386,7 +393,6 @@
     c3 = Field(c3_ref, 3)
     d3 = Field(d3_ref, 2)
     c4 = Field(c4_ref, 1)
-    slopes = moment_slopes(inverse_count, spot_ref[2], weights_ref, moment_refs)
     masks = lane_masks()
     block = 2
 
@@ -626,21 +632,21 @@
     if group > count:
         cotangents = jnp.where(place < count, cotangents, 0.0)
 
-    def last_step(flip):
-        return pl.pallas_call(
+    def last_step(flip, out_shape, specs, *operands):
+        return plain(
             functools.partial(last_kernel, grid, inverse_count, flip),
-            out_shape=stacked,
-            in_specs=[smem(), smem()] + [vmem()] * (10 + ny),
-            out_specs=vmem(),
-            compiler_params=params(),
-            cost_estimate=cost(20),
-            name="last_step_given" if flip else "last_step_kept",
-        )(spot, cotangents, *vectors, *shares)
-
-    got = lax.ppermute(last_step(True), "core", swap)
+            "last_step_given" if flip else "last_step_kept", out_shape,
+            [smem()] + [vmem()] * 10 + specs, spot, *vectors, *operands,
+        )
+
+    given, slopes = last_step(
+        True, (stacked, f32(6, 8, 128)), [smem()] + [vmem()] * ny, cotangents, *shares
+    )
+    got = lax.ppermute(given, "core", swap)
+    kept = last_step(False, stacked, [vmem()], slopes)
     parts = plain(
         add_kernel, "add_cores", (block,) * chips, [smem(), vmem(), vmem()],
-        spot, last_step(False), got,
+        spot, kept, got,
     )
     parts = [parts[0]] + [to_chip(parts[k], k) for k in range(chips - 1, 0, -1)]
     return plain(

time: 74.7 us -> 74.4 us (level)
    pallas_call x2 -> x0, Pallas kernels: 4.06 us -> none  [last_step(): pl.pallas_call(functools.partial(last_kernel, grid, inverse_count, flip),...]
    pallas_call x8 -> x10, Pallas kernels: 6.42 us -> 10.1 us  [plain(): pl.pallas_call(kernel, out_shape=out_shape, in_specs=specs, out_specs=(vm...]
  transfers between devices with their start and end apart: 21 -> 21, of which waited for: 9 -> 10; matrix products, arithmetic and copies ran while one was open for 0% -> 0% of each run, Pallas kernels for 25% -> 24%
where the time goes in v15:
time: 74.4 us; the launch traced here: 74.1 us
  starting transfers between devices  26.2 us (35%)
  waiting for transfers between devices  24.1 us (32%)
  Pallas kernels  23.5 us (32%)
    ppermute x9, waiting for transfers between devices, to_chip(): return lax.ppermute(value, ('chip', 'gz'), pairs)  18.6 us
    ppermute x9, starting transfers between devices, to_chip(): return lax.ppermute(value, ('chip', 'gz'), pairs)  11.7 us
    pallas_call x10, Pallas kernels, plain(): pl.pallas_call(kernel, out_shape=out_shape, in_specs=specs, out_specs=(vm...  10.1 us
    ppermute x3, starting transfers between devices, body(): lax.ppermute(moments, 'gy', [(i, i ^ step) for i in range(ny)])  6.87 us
    pallas_call x1, Pallas kernels, body(): pl.pallas_call(functools.partial(inner_kernel, grid), out_shape=tuple((ve...  3.92 us
    ppermute x1, waiting for transfers between devices, body(): even1 = lax.ppermute(even_edge, 'gy', even)  3.41 us
    pallas_call x2, Pallas kernels, body(): pl.pallas_call(functools.partial(side_kernel, by, which), out_shape=tuple...  3.25 us
    ppermute x2, starting transfers between devices, body(): arrived.append(lax.ppermute(edge_rows, 'gy', pairs))  2.47 us
  transfers between devices with their start and end apart: 21, of which 10 were waited for; matrix products, arithmetic and copies ran while one was open for 0% of the time, Pallas kernels for 24%

profile of v15, /device:TPU:0, one launch (start us, length us, event | category | flops | bytes accessed | tf_op | source)
XLA Modules:
  0.0 74.1 jit_solution(14099922378633716074)
XLA Ops:
  0.9 3.0 %collective-permute-start = (f32[2,128,128]{2,1,0:T(8,128)S(1)}, f32[2,128,128]{2,1,0:T(8,128)S(1)}, u32[]{:S(2)}, u32[]{:S(2)}) collective-permute-start(f32[2,128,128]{2,1,0:T(8,128)S(1)} %pack_kappa.1.after_ref.refs_0_), channel_id=1, source_target_pairs={{0,1},{1,0},{16,17},{17,16},{2,3},{3,2},{18,19},{19,18},{4,5},{5,4... | collective-permute-start | bytes 393224 | tf_op jit(solution)/shard_map/ppermute | solution.py:508
  5.6 1.9 %pack_probes.1 = (f32[2,2,128,128]{3,2,1,0:T(8,128)S(1)}, f32[2,2,128,128]{3,2,1,0:T(8,128)S(1)}, f32[2,2,128,128]{3,2,1,0:T(8,128)S(1)}, f32[2,2,128,128]{3,2,1,0:T(8,128)S(1)}) custom-call(s32[6]{0:T(128)S(1)} %stack.35.spot_ref, f32[2,128,128]{2,1,0:T(8,128)S(1)} %pack_kappa.1.after_ref.refs_0_, f32[1024,256]{1,0:T(8,128)} %bitcast.8), custom_call_target="tpu_custom_call" | custom-call | tf_op jit(solution)/shard_map/pack_probes/pallas_call | solution.py:511
  7.5 2.8 %collective-permute-done.1.refs_2_ = f32[2,128,128]{2,1,0:T(8,128)S(1)} collective-permute-done((f32[2,128,128]{2,1,0:T(8,128)S(1)}, f32[2,128,128]{2,1,0:T(8,128)S(1)}, u32[]{:S(2)}, u32[]{:S(2)}) %collective-permute-start.1) | collective-permute-done | bytes 131104 | tf_op jit(solution)/shard_map/ppermute | solution.py:508
  11.6 1.7 %collective-permute-start.6 = (f32[2,2,128,128]{3,2,1,0:T(8,128)S(1)}, f32[2,2,128,128]{3,2,1,0:T(8,128)S(1)}, u32[]{:S(2)}, u32[]{:S(2)}) collective-permute-start(f32[2,2,128,128]{3,2,1,0:T(8,128)S(1)} %get-tuple-element.54), channel_id=1, source_target_pairs={{0,1},{1,0},{16,17},{17,16},{2,3},{3,2},{18,19},{19,18},{4,5},{5,4... | collective-permute-start | bytes 786440 | tf_op jit(solution)/shard_map/ppermute | solution.py:508
  16.1 1.8 %collective-permute-start.4 = (f32[4,4,32,128]{3,2,1,0:T(8,128)S(1)}, f32[4,4,32,128]{3,2,1,0:T(8,128)S(1)}, u32[]{:S(2)}, u32[]{:S(2)}) collective-permute-start(f32[4,4,32,128]{3,2,1,0:T(8,128)S(1)} %get-tuple-element.52), channel_id=1, source_target_pairs={{0,2},{2,0},{4,6},{6,4},{1,3},{3,1},{5,7},{7,5},{8,10},{10,8},{12,... | collective-permute-start | bytes 786440 | tf_op jit(solution)/shard_map/ppermute | solution.py:546
  18.6 1.8 %collective-permute-done.6.refs_1_ = f32[2,2,128,128]{3,2,1,0:T(8,128)S(1)} collective-permute-done((f32[2,2,128,128]{3,2,1,0:T(8,128)S(1)}, f32[2,2,128,128]{3,2,1,0:T(8,128)S(1)}, u32[]{:S(2)}, u32[]{:S(2)}) %collective-permute-start.6) | collective-permute-done | bytes 262176 | tf_op jit(solution)/shard_map/ppermute | solution.py:508
  20.3 2.2 %collective-permute-done.7.refs_2_ = f32[2,2,128,128]{3,2,1,0:T(8,128)S(1)} collective-permute-done((f32[2,2,128,128]{3,2,1,0:T(8,128)S(1)}, f32[2,2,128,128]{3,2,1,0:T(8,128)S(1)}, u32[]{:S(2)}, u32[]{:S(2)}) %collective-permute-start.7) | collective-permute-done | bytes 262176 | tf_op jit(solution)/shard_map/ppermute | solution.py:508
  22.5 4.6 %collective-permute-done.8.refs_3_ = f32[2,2,128,128]{3,2,1,0:T(8,128)S(1)} collective-permute-done((f32[2,2,128,128]{3,2,1,0:T(8,128)S(1)}, f32[2,2,128,128]{3,2,1,0:T(8,128)S(1)}, u32[]{:S(2)}, u32[]{:S(2)}) %collective-permute-start.8) | collective-permute-done | bytes 262176 | tf_op jit(solution)/shard_map/ppermute | solution.py:508
  27.8 1.9 %collective-permute-done.9.other_ref = f32[4,2,128,128]{3,2,1,0:T(8,128)S(1)} collective-permute-done((f32[4,2,128,128]{3,2,1,0:T(8,128)S(1)}, f32[4,2,128,128]{3,2,1,0:T(8,128)S(1)}, u32[]{:S(2)}, u32[]{:S(2)}) %collective-permute-start.9) | collective-permute-done | bytes 524320 | tf_op jit(solution)/shard_map/ppermute | solution.py:553
  30.5 1.8 %collective-permute-start.10 = (f32[4,5,32,128]{3,2,1,0:T(8,128)S(1)}, f32[4,5,32,128]{3,2,1,0:T(8,128)S(1)}, u32[]{:S(2)}, u32[]{:S(2)}) collective-permute-start(f32[4,5,32,128]{3,2,1,0:T(8,128)S(1)} %get-tuple-element.65), channel_id=1, source_target_pairs={{0,2},{2,0},{4,6},{6,4},{1,3},{3,1},{5,7},{7,5},{8,10},{10,8},{12,... | collective-permute-start | bytes 983048 | tf_op jit(solution)/shard_map/ppermute | solution.py:558
  33.0 3.9 %inner_steps.1 = (f32[4,26,48,128]{3,2,1,0:T(8,128)S(1)}, f32[4,24,48,128]{3,2,1,0:T(8,128)S(1)}, f32[4,22,48,128]{3,2,1,0:T(8,128)S(1)}, f32[4,20,48,128]{3,2,1,0:T(8,128)S(1)}, f32[4,26,48,128]{3,2,1,0:T(8,128)S(1)}) custom-call(s32[6]{0:T(128)S(1)} %stack.35.spot_ref, f32[4,2,128,128]{3,2,1,0:T(8,128)S(1)} %get-tuple-element.57.mine_ref, ...), custom_call_target="tpu_custom_call" | custom-call | flops 8388608 | bytes 4194304 | tf_op jit(solution)/shard_map/inner_steps/pallas_call | solution.py:568
  36.9 3.4 %collective-permute-done.10.halo_ref = f32[4,5,32,128]{3,2,1,0:T(8,128)S(1)} collective-permute-done((f32[4,5,32,128]{3,2,1,0:T(8,128)S(1)}, f32[4,5,32,128]{3,2,1,0:T(8,128)S(1)}, u32[]{:S(2)}, u32[]{:S(2)}) %collective-permute-start.10) | collective-permute-done | bytes 327712 | tf_op jit(solution)/shard_map/ppermute | solution.py:558
  40.3 1.6 %side_steps_0.1 = (f32[4,26,48,128]{3,2,1,0:T(8,128)S(1)}, f32[4,24,48,128]{3,2,1,0:T(8,128)S(1)}, f32[4,24,48,128]{3,2,1,0:T(8,128)S(1)}, f32[4,22,48,128]{3,2,...) custom-call(s32[6]{0:T(128)S(1)} %stack.35.spot_ref, ...), custom_call_target="tpu_custom_call", output_to_operand_aliasing={{0}: (1, {}), {1}: (2, {}), {2}: (3, {}), {3}: (4, {}), {4}... | custom-call | flops 2097152 | bytes 4194304 | tf_op jit(solution)/shard_map/side_steps_0/pallas_call | solution.py:582
  41.9 1.8 %collective-permute-start.12 = (f32[4,5,32,128]{3,2,1,0:T(8,128)S(1)}, f32[4,5,32,128]{3,2,1,0:T(8,128)S(1)}, u32[]{:S(2)}, u32[]{:S(2)}) collective-permute-start(f32[4,5,32,128]{3,2,1,0:T(8,128)S(1)} %get-tuple-element.83), channel_id=1, source_target_pairs={{0,2},{2,0},{4,6},{6,4},{1,3},{3,1},{5,7},{7,5},{8,10},{10,8},{12,... | collective-permute-start | bytes 983048 | tf_op jit(solution)/shard_map/ppermute | solution.py:593
  43.7 1.6 %side_steps_1.1 = (f32[4,26,48,128]{3,2,1,0:T(8,128)S(1)}, f32[4,24,48,128]{3,2,1,0:T(8,128)S(1)}, f32[4,24,48,128]{3,2,1,0:T(8,128)S(1)}, f32[4,22,48,128]{3,2,...) custom-call(s32[6]{0:T(128)S(1)} %stack.35.spot_ref, ...), custom_call_target="tpu_custom_call", output_to_operand_aliasing={{0}: (1, {}), {1}: (2, {}), {2}: (3, {}), {3}: (4, {}), {4}... | custom-call | flops 2097152 | bytes 4194304 | tf_op jit(solution)/shard_map/side_steps_1/pallas_call | solution.py:582
  47.5 4.4 %collective-permute-start.14 = (f32[8,128]{1,0:T(8,128)S(1)}, f32[8,128]{1,0:T(8,128)S(1)}, u32[]{:S(2)}, u32[]{:S(2)}) collective-permute-start(f32[8,128]{1,0:T(8,128)S(1)} %get-tuple-element.90.rest_1_), channel_id=1, source_target_pairs={{0,2},{2,0},{4,6},{6,4},{1,3},{3,1},{5,7},{7,5},{8,10},{10,8},{12,... | collective-permute-start | bytes 12296 | tf_op jit(solution)/shard_map/ppermute | solution.py:608
  51.9 2.4 %collective-permute-start.16 = (f32[8,128]{1,0:T(8,128)S(1)}, f32[8,128]{1,0:T(8,128)S(1)}, u32[]{:S(2)}, u32[]{:S(2)}) collective-permute-start(f32[8,128]{1,0:T(8,128)S(1)} %get-tuple-element.90.rest_1_), channel_id=1, source_target_pairs={{0,6},{2,4},{4,2},{6,0},{1,7},{3,5},{5,3},{7,1},{8,14},{10,12},{12... | collective-permute-start | bytes 12296 | tf_op jit(solution)/shard_map/ppermute | solution.py:608
  54.4 2.4 %second_inner_steps.1 = (f32[4,22,48,128]{3,2,1,0:T(8,128)S(1)}, f32[4,20,48,128]{3,2,1,0:T(8,128)S(1)}, f32[4,18,48,128]{3,2,1,0:T(8,128)S(1)}) custom-call(f32[4,24,48,128]{3,2,1,0:T(8,128)S(1)} %get-tuple-element.74.diagonal_ref, f32[4,26,48,128]{3,2,1,0:T(8,128)S(1)} %get-tuple-element.78.c2_ref.c2_in, f32[4,24,48,128]{3,2,1,0:T(8,128)S(1)} %get-tuple-element.79.d2_ref.d2_in), custom_call_target="tpu_custom_call" | custom-call | flops 7864320 | bytes 4194304 | tf_op jit(solution)/shard_map/second_inner_steps/pallas_call | solution.py:610
  56.8 2.4 %third_steps.1 = (f32[4,26,48,128]{3,2,1,0:T(8,128)S(1)}, f32[4,24,48,128]{3,2,1,0:T(8,128)S(1)}, f32[4,22,48,128]{3,2,1,0:T(8,128)S(1)}, f32[4,20,48,128]{3,2,1,0:T(8,128)S(1)}, f32[4,18,48,128]{3,2,1,0:T(8,128)S(1)}) custom-call(s32[6]{0:T(128)S(1)} %stack.35.spot_ref, ...), custom_call_target="tpu_custom_call", output_to_operand_aliasing={{0}: (2, {}), {1}: (3, {}), {2}: (4, {}), {3}: (5, {}), {4}... | custom-call | flops 5242880 | bytes 4194304 | tf_op jit(solution)/shard_map/third_steps/pallas_call | solution.py:620
  59.2 2.0 %last_step_given.1 = (f32[4,2,128,128]{3,2,1,0:T(8,128)S(1)}, f32[6,8,128]{2,1,0:T(8,128)S(1)}) custom-call(s32[6]{0:T(128)S(1)} %stack.35.spot_ref, f32[4,26,48,128]{3,2,1,0:T(8,128)S(1)} %get-tuple-element.73.c0_ref, f32[4,24,48,128]{3,2,1,0:T(8,128)S(1)} %get-tuple-element.74.diagonal_ref, f32[4,24,48,128]{3,2,1,0:T(8,128)S(1)} %get-tuple-element.75.d0_ref, ...), custom_call_target="tpu_custom_call" | custom-call | tf_op jit(solution)/shard_map/last_step_given/pallas_call | solution.py:511
  61.3 1.7 %last_step_kept.1.kept_ref = f32[4,2,128,128]{3,2,1,0:T(8,128)S(1)} custom-call(s32[6]{0:T(128)S(1)} %stack.35.spot_ref, f32[4,26,48,128]{3,2,1,0:T(8,128)S(1)} %get-tuple-element.73.c0_ref, f32[4,24,48,128]{3,2,1,0:T(8,128)S(1)} %get-tuple-element.74.diagonal_ref, f32[4,24,48,128]{3,2,1,0:T(8,128)S(1)} %get-tuple-element.75.d0_ref, ...), custom_call_target="tpu_custom_call" | custom-call | tf_op jit(solution)/shard_map/last_step_kept/pallas_call | solution.py:511
  63.8 2.5 %collective-permute-start.18 = (f32[2,128,128]{2,1,0:T(8,128)S(1)}, f32[2,128,128]{2,1,0:T(8,128)S(1)}, u32[]{:S(2)}, u32[]{:S(2)}) collective-permute-start(f32[2,128,128]{2,1,0:T(8,128)S(1)} %get-tuple-element.94), channel_id=1, source_target_pairs={{0,17},{1,16},{16,1},{17,0},{2,19},{3,18},{18,3},{19,2},{4,21},{5,... | collective-permute-start | bytes 393224 | tf_op jit(solution)/shard_map/ppermute | solution.py:508
  67.4 3.7 %collective-permute-done.18.refs_1_ = f32[2,128,128]{2,1,0:T(8,128)S(1)} collective-permute-done((f32[2,128,128]{2,1,0:T(8,128)S(1)}, f32[2,128,128]{2,1,0:T(8,128)S(1)}, u32[]{:S(2)}, u32[]{:S(2)}) %collective-permute-start.18) | collective-permute-done | bytes 131104 | tf_op jit(solution)/shard_map/ppermute | solution.py:508
  71.1 2.3 %collective-permute-done.19.refs_2_ = f32[2,128,128]{2,1,0:T(8,128)S(1)} collective-permute-done((f32[2,128,128]{2,1,0:T(8,128)S(1)}, f32[2,128,128]{2,1,0:T(8,128)S(1)}, u32[]{:S(2)}, u32[]{:S(2)}) %collective-permute-start.19) | collective-permute-done | bytes 131104 | tf_op jit(solution)/shard_map/ppermute | solution.py:508
  (37 shorter events, 14.0 us)
Async XLA Ops:
  0.9 6.6 %collective-permute-start = (f32[2,128,128]{2,1,0:T(8,128)S(1)}, f32[2,128,128]{2,1,0:T(8,128)S(1)}, u32[]{:S(2)}, u32[]{:S(2)}) collective-permute-start(f32[2,128,128]{2,1,0:T(8,128)S(1)} %pack_kappa.1.after_ref.refs_0_), channel_id=1, source_target_pairs={{0,1},{1,0},{16,17},{17,16},{2,3},{3,2},{18,19},{19,18},{4,5},{5,4... | collective-permute-start | bytes 393224 | tf_op jit(solution)/shard_map/ppermute | solution.py:508
  3.9 6.4 %collective-permute-start.1 = (f32[2,128,128]{2,1,0:T(8,128)S(1)}, f32[2,128,128]{2,1,0:T(8,128)S(1)}, u32[]{:S(2)}, u32[]{:S(2)}) collective-permute-start(f32[2,128,128]{2,1,0:T(8,128)S(1)} %pack_kappa.1.after_ref.refs_0_), channel_id=1, source_target_pairs={{0,16},{1,17},{16,0},{17,1},{2,18},{3,19},{18,2},{19,3},{4,20},{5,... | collective-permute-start | bytes 393224 | tf_op jit(solution)/shard_map/ppermute | solution.py:508
  5.4 6.1 %collective-permute-start.2 = (f32[2,128,128]{2,1,0:T(8,128)S(1)}, f32[2,128,128]{2,1,0:T(8,128)S(1)}, u32[]{:S(2)}, u32[]{:S(2)}) collective-permute-start(f32[2,128,128]{2,1,0:T(8,128)S(1)} %pack_kappa.1.after_ref.refs_0_), channel_id=1, source_target_pairs={{0,17},{1,16},{16,1},{17,0},{2,19},{3,18},{18,3},{19,2},{4,21},{5,... | collective-permute-start | bytes 393224 | tf_op jit(solution)/shard_map/ppermute | solution.py:508
  11.5 3.6 %collective-permute-start.3 = (f32[4,2,128,128]{3,2,1,0:T(8,128)S(1)}, f32[4,2,128,128]{3,2,1,0:T(8,128)S(1)}, u32[]{:S(2)}, u32[]{:S(2)}) collective-permute-start(f32[4,2,128,128]{3,2,1,0:T(8,128)S(1)} %stack_kappa.1.mine_ref), channel_id=1, source_target_pairs={{0,8},{8,0},{1,9},{9,1},{2,10},{10,2},{3,11},{11,3},{4,12},{12,4},... | collective-permute-start | bytes 1572872 | tf_op jit(solution)/shard_map/ppermute | solution.py:540
  11.6 8.7 %collective-permute-start.6 = (f32[2,2,128,128]{3,2,1,0:T(8,128)S(1)}, f32[2,2,128,128]{3,2,1,0:T(8,128)S(1)}, u32[]{:S(2)}, u32[]{:S(2)}) collective-permute-start(f32[2,2,128,128]{3,2,1,0:T(8,128)S(1)} %get-tuple-element.54), channel_id=1, source_target_pairs={{0,1},{1,0},{16,17},{17,16},{2,3},{3,2},{18,19},{19,18},{4,5},{5,4... | collective-permute-start | bytes 786440 | tf_op jit(solution)/shard_map/ppermute | solution.py:508
  13.3 9.2 %collective-permute-start.7 = (f32[2,2,128,128]{3,2,1,0:T(8,128)S(1)}, f32[2,2,128,128]{3,2,1,0:T(8,128)S(1)}, u32[]{:S(2)}, u32[]{:S(2)}) collective-permute-start(f32[2,2,128,128]{3,2,1,0:T(8,128)S(1)} %get-tuple-element.55), channel_id=1, source_target_pairs={{0,16},{1,17},{16,0},{17,1},{2,18},{3,19},{18,2},{19,3},{4,20},{5,... | collective-permute-start | bytes 786440 | tf_op jit(solution)/shard_map/ppermute | solution.py:508
  14.8 12.3 %collective-permute-start.8 = (f32[2,2,128,128]{3,2,1,0:T(8,128)S(1)}, f32[2,2,128,128]{3,2,1,0:T(8,128)S(1)}, u32[]{:S(2)}, u32[]{:S(2)}) collective-permute-start(f32[2,2,128,128]{3,2,1,0:T(8,128)S(1)} %get-tuple-element.56), channel_id=1, source_target_pairs={{0,17},{1,16},{16,1},{17,0},{2,19},{3,18},{18,3},{19,2},{4,21},{5,... | collective-permute-start | bytes 786440 | tf_op jit(solution)/shard_map/ppermute | solution.py:508
  16.1 11.0 %collective-permute-start.4 = (f32[4,4,32,128]{3,2,1,0:T(8,128)S(1)}, f32[4,4,32,128]{3,2,1,0:T(8,128)S(1)}, u32[]{:S(2)}, u32[]{:S(2)}) collective-permute-start(f32[4,4,32,128]{3,2,1,0:T(8,128)S(1)} %get-tuple-element.52), channel_id=1, source_target_pairs={{0,2},{2,0},{4,6},{6,4},{1,3},{3,1},{5,7},{7,5},{8,10},{10,8},{12,... | collective-permute-start | bytes 786440 | tf_op jit(solution)/shard_map/ppermute | solution.py:546
  17.9 9.2 %collective-permute-start.5 = (f32[4,4,32,128]{3,2,1,0:T(8,128)S(1)}, f32[4,4,32,128]{3,2,1,0:T(8,128)S(1)}, u32[]{:S(2)}, u32[]{:S(2)}) collective-permute-start(f32[4,4,32,128]{3,2,1,0:T(8,128)S(1)} %get-tuple-element.53), channel_id=1, source_target_pairs={{2,4},{4,2},{3,5},{5,3},{10,12},{12,10},{11,13},{13,11},{18,20},{2... | collective-permute-start | bytes 786440 | tf_op jit(solution)/shard_map/ppermute | solution.py:547
  27.8 2.0 %collective-permute-start.9 = (f32[4,2,128,128]{3,2,1,0:T(8,128)S(1)}, f32[4,2,128,128]{3,2,1,0:T(8,128)S(1)}, u32[]{:S(2)}, u32[]{:S(2)}) collective-permute-start(f32[4,2,128,128]{3,2,1,0:T(8,128)S(1)} %get-tuple-element.58), channel_id=1, source_target_pairs={{0,8},{8,0},{1,9},{9,1},{2,10},{10,2},{3,11},{11,3},{4,12},{12,4},... | collective-permute-start | bytes 1572872 | tf_op jit(solution)/shard_map/ppermute | solution.py:553
  30.5 9.8 %collective-permute-start.10 = (f32[4,5,32,128]{3,2,1,0:T(8,128)S(1)}, f32[4,5,32,128]{3,2,1,0:T(8,128)S(1)}, u32[]{:S(2)}, u32[]{:S(2)}) collective-permute-start(f32[4,5,32,128]{3,2,1,0:T(8,128)S(1)} %get-tuple-element.65), channel_id=1, source_target_pairs={{0,2},{2,0},{4,6},{6,4},{1,3},{3,1},{5,7},{7,5},{8,10},{10,8},{12,... | collective-permute-start | bytes 983048 | tf_op jit(solution)/shard_map/ppermute | solution.py:558
  32.3 11.4 %collective-permute-start.11 = (f32[4,5,32,128]{3,2,1,0:T(8,128)S(1)}, f32[4,5,32,128]{3,2,1,0:T(8,128)S(1)}, u32[]{:S(2)}, u32[]{:S(2)}) collective-permute-start(f32[4,5,32,128]{3,2,1,0:T(8,128)S(1)} %get-tuple-element.72), channel_id=1, source_target_pairs={{2,4},{4,2},{3,5},{5,3},{10,12},{12,10},{11,13},{13,11},{18,20},{2... | collective-permute-start | bytes 983048 | tf_op jit(solution)/shard_map/ppermute | solution.py:559
  41.9 14.8 %collective-permute-start.12 = (f32[4,5,32,128]{3,2,1,0:T(8,128)S(1)}, f32[4,5,32,128]{3,2,1,0:T(8,128)S(1)}, u32[]{:S(2)}, u32[]{:S(2)}) collective-permute-start(f32[4,5,32,128]{3,2,1,0:T(8,128)S(1)} %get-tuple-element.83), channel_id=1, source_target_pairs={{0,2},{2,0},{4,6},{6,4},{1,3},{3,1},{5,7},{7,5},{8,10},{10,8},{12,... | collective-permute-start | bytes 983048 | tf_op jit(solution)/shard_map/ppermute | solution.py:593
  45.4 11.4 %collective-permute-start.13 = (f32[4,5,32,128]{3,2,1,0:T(8,128)S(1)}, f32[4,5,32,128]{3,2,1,0:T(8,128)S(1)}, u32[]{:S(2)}, u32[]{:S(2)}) collective-permute-start(f32[4,5,32,128]{3,2,1,0:T(8,128)S(1)} %get-tuple-element.84), channel_id=1, source_target_pairs={{2,4},{4,2},{3,5},{5,3},{10,12},{12,10},{11,13},{13,11},{18,20},{2... | collective-permute-start | bytes 983048 | tf_op jit(solution)/shard_map/ppermute | solution.py:593
  47.5 11.7 %collective-permute-start.14 = (f32[8,128]{1,0:T(8,128)S(1)}, f32[8,128]{1,0:T(8,128)S(1)}, u32[]{:S(2)}, u32[]{:S(2)}) collective-permute-start(f32[8,128]{1,0:T(8,128)S(1)} %get-tuple-element.90.rest_1_), channel_id=1, source_target_pairs={{0,2},{2,0},{4,6},{6,4},{1,3},{3,1},{5,7},{7,5},{8,10},{10,8},{12,... | collective-permute-start | bytes 12296 | tf_op jit(solution)/shard_map/ppermute | solution.py:608
  51.9 7.3 %collective-permute-start.15 = (f32[8,128]{1,0:T(8,128)S(1)}, f32[8,128]{1,0:T(8,128)S(1)}, u32[]{:S(2)}, u32[]{:S(2)}) collective-permute-start(f32[8,128]{1,0:T(8,128)S(1)} %get-tuple-element.90.rest_1_), channel_id=1, source_target_pairs={{0,4},{2,6},{4,0},{6,2},{1,5},{3,7},{5,1},{7,3},{8,12},{10,14},{12... | collective-permute-start | bytes 12296 | tf_op jit(solution)/shard_map/ppermute | solution.py:608
  51.9 7.3 %collective-permute-start.16 = (f32[8,128]{1,0:T(8,128)S(1)}, f32[8,128]{1,0:T(8,128)S(1)}, u32[]{:S(2)}, u32[]{:S(2)}) collective-permute-start(f32[8,128]{1,0:T(8,128)S(1)} %get-tuple-element.90.rest_1_), channel_id=1, source_target_pairs={{0,6},{2,4},{4,2},{6,0},{1,7},{3,5},{5,3},{7,1},{8,14},{10,12},{12... | collective-permute-start | bytes 12296 | tf_op jit(solution)/shard_map/ppermute | solution.py:608
  56.8 2.5 %copy-start = (f32[5,8]{1,0:T(8,128)S(1)}, f32[5,8]{1,0:T(8,128)}, u32[]{:S(2)}) copy-start(f32[5,8]{1,0:T(8,128)} %rest_0_.1) | copy-start | bytes 484
  61.2 2.0 %collective-permute-start.17 = (f32[4,2,128,128]{3,2,1,0:T(8,128)S(1)}, f32[4,2,128,128]{3,2,1,0:T(8,128)S(1)}, u32[]{:S(2)}, u32[]{:S(2)}) collective-permute-start(f32[4,2,128,128]{3,2,1,0:T(8,128)S(1)} %get-tuple-element.92), channel_id=1, source_target_pairs={{0,8},{8,0},{1,9},{9,1},{2,10},{10,2},{3,11},{11,3},{4,12},{12,4},... | collective-permute-start | bytes 1572872 | tf_op jit(solution)/shard_map/ppermute | solution.py:645
  63.8 7.3 %collective-permute-start.18 = (f32[2,128,128]{2,1,0:T(8,128)S(1)}, f32[2,128,128]{2,1,0:T(8,128)S(1)}, u32[]{:S(2)}, u32[]{:S(2)}) collective-permute-start(f32[2,128,128]{2,1,0:T(8,128)S(1)} %get-tuple-element.94), channel_id=1, source_target_pairs={{0,17},{1,16},{16,1},{17,0},{2,19},{3,18},{18,3},{19,2},{4,21},{5,... | collective-permute-start | bytes 393224 | tf_op jit(solution)/shard_map/ppermute | solution.py:508
  66.3 7.1 %collective-permute-start.19 = (f32[2,128,128]{2,1,0:T(8,128)S(1)}, f32[2,128,128]{2,1,0:T(8,128)S(1)}, u32[]{:S(2)}, u32[]{:S(2)}) collective-permute-start(f32[2,128,128]{2,1,0:T(8,128)S(1)} %get-tuple-element.95), channel_id=1, source_target_pairs={{0,16},{1,17},{16,0},{17,1},{2,18},{3,19},{18,2},{19,3},{4,20},{5,... | collective-permute-start | bytes 393224 | tf_op jit(solution)/shard_map/ppermute | solution.py:508
  66.9 6.6 %collective-permute-start.20 = (f32[2,128,128]{2,1,0:T(8,128)S(1)}, f32[2,128,128]{2,1,0:T(8,128)S(1)}, u32[]{:S(2)}, u32[]{:S(2)}) collective-permute-start(f32[2,128,128]{2,1,0:T(8,128)S(1)} %get-tuple-element.96), channel_id=1, source_target_pairs={{0,1},{1,0},{16,17},{17,16},{2,3},{3,2},{18,19},{19,18},{4,5},{5,4... | collective-permute-start | bytes 393224 | tf_op jit(solution)/shard_map/ppermute | solution.py:508
